TPU v7x, 32 devices: a whole 2x2x4 slice. The times are simulated.
32 devices in a mesh: groups: 2 (over y), rows: 16 (over z, x, core).
Axes of the slice: x: 2, y: 2, z: 4, core: 2. Of those that a mesh axis runs over, the one named last changes fastest.
Arguments:
- transition_tiles: bfloat16 [2048, 5, 128, 128], P(('groups', 'rows')), parts along dimension 0, may hold values from 0.049804688 to 1
- column_tiles: int32 [2048, 5], P(('groups', 'rows')), parts along dimension 0, may hold values from 0 to 1023, as said below
- schur_basis: bfloat16 [32, 262144], P(None, ('groups', 'rows')), parts along dimension 1, may hold values from -60 to 60
- membership_map: float32 [64, 32], P('groups'), parts along dimension 0, may hold values from -1 to 1
Outputs:
- memberships: float32 [32, 262144], P(None, ('groups', 'rows')), parts along dimension 1
There are 2 independent parts, one for each index of `groups`. A program takes and returns all parts, laid end to end along the dimension named above; each array names one. Nothing has to cross between parts.
Inputs may be any that keep to these rules, and one draw needn't show every extreme that they name: `column_tiles`: the 5 entries of row tile r are distinct column tiles, r itself among them, all within 64 of r; some row tile has one at distance exactly 64.
All inputs are finite; a program needn't handle non-finite values.
Results may differ from a plain program's by a relative error of at most 0.0045.
Values may be sent and summed in bfloat16 or wider, within the bound.
No kernel may reach another device: no remote copies, remote signals or barrier semaphores. Data moves between devices by JAX's collectives and lax.ppermute only.
A program may use at most 64 MiB of HBM per device.

v0:
```python
import jax
import jax.numpy as jnp
from jax import lax
from jax.sharding import PartitionSpec as P

PRODUCTS = 4


def padded_2(block, sides, width):
    for axis, dim in sides:
        count = lax.axis_size(axis)
        forward = [(i, i + 1) for i in range(count - 1)]
        backward = [(target, source) for source, target in forward]
        low = lax.ppermute(
            lax.slice_in_dim(block, block.shape[dim] - width, None, axis=dim), axis, forward
        )
        high = lax.ppermute(lax.slice_in_dim(block, 0, width, axis=dim), axis, backward)
        block = jnp.concatenate([low, block, high], axis=dim)
    return block


def tile_product(transition_tiles, local_index, row_total, padded):
    vector_count = padded.shape[0]
    tile_size = transition_tiles.shape[-1]
    blocks = padded.reshape(vector_count, -1, tile_size)
    picked = jnp.take(blocks, local_index, axis=1)
    summed = jnp.einsum(
        "rsij,vrsj->vri", transition_tiles, picked, preferred_element_type=jnp.float32
    )
    return (summed / row_total[None]).reshape(vector_count, -1)


def body(transition_tiles, column_tiles, schur_basis, membership_map):
    panel_tiles = transition_tiles.shape[0]
    tile_size = transition_tiles.shape[-1]
    shard_width = schur_basis.shape[1]
    state_count = shard_width * lax.axis_size("rows")
    own_first = lax.axis_index("rows") * panel_tiles
    first_tile = own_first - panel_tiles
    local_index = column_tiles - first_tile
    unit_vector = jnp.ones((tile_size,), jnp.bfloat16)
    row_total = jnp.einsum(
        "rsij,j->ri", transition_tiles, unit_vector, preferred_element_type=jnp.float32
    )
    padded = padded_2(schur_basis, (("rows", 1),), shard_width)
    result = tile_product(transition_tiles, local_index, row_total, padded)
    for step in range(PRODUCTS - 1):
        image = result.astype(jnp.bfloat16)
        padded_image = padded_2(image, (("rows", 1),), shard_width)
        result = tile_product(transition_tiles, local_index, row_total, padded_image)
    gram_local = (
        jnp.dot(
            result, result.T, precision=lax.Precision.HIGHEST, preferred_element_type=jnp.float32
        )
        / state_count
    )
    gram_total = lax.psum(gram_local, "rows")
    factor = jnp.linalg.cholesky(gram_total)
    basis_q = jax.scipy.linalg.solve_triangular(factor, result, lower=True)
    return jnp.dot(
        membership_map.T,
        basis_q,
        precision=lax.Precision.HIGHEST,
        preferred_element_type=jnp.float32,
    )


def solution(mesh):
    return jax.shard_map(
        body,
        mesh=mesh,
        in_specs=(
            P(("groups", "rows"), None, None, None),
            P(("groups", "rows"), None),
            P(None, ("groups", "rows")),
            P("groups", None),
        ),
        out_specs=P(None, ("groups", "rows")),
        check_vma=False,
    )
```

profile of v0, /device:TPU:0, one launch (start us, length us, event | category | flops | bytes accessed | tf_op | source)
XLA Modules:
  0.0 183.3 jit_solution(8848551696498775349)
XLA Ops:
  0.0 0.0 copy-start
  0.0 2.5 %collective-permute-start = (bf16[32,8192]{1,0:T(8,128)(2,1)}, bf16[32,8192]{1,0:T(8,128)(2,1)S(1)}, u32[]{:S(2)}, u32[]{:S(2)}) collective-permute-start(bf16[32,8192]{1,0:T(8,128)(2,1)} %param.8), channel_id=1, source_target_pairs={{0,1},{1,2},{2,3},{3,4},{4,5},{5,6},{6,7},{7,8},{8,9},{9,10},{10,1... | collective-permute-start | bytes 1572872 | tf_op jit(solution)/shard_map/ppermute | solution.py:14
  2.5 1.3 collective-permute-start.1
  3.8 0.0 copy-start.2
  3.8 0.0 copy-start.1
  3.8 6.6 %convert_reduce_fusion = bf16[64,128,128]{2,1,0:T(8,128)(2,1)S(1)} fusion(bf16[64,5,128,128]{3,2,1,0:T(8,128)(2,1)} %param.6), kind=kLoop, calls=%fused_computation.4 | loop fusion | flops 9437184 | bytes 12582912 | tf_op jit(solution)/shard_map/rsij,j->ri/reduce_sum | solution.py:42
  10.4 0.0 copy-done.2
  10.5 0.1 copy.26
  10.6 0.1 copy.30
  10.7 0.1 reshape.82
  10.8 0.6 fusion.58
  11.5 0.0 collective-permute-done
  11.5 0.0 collective-permute-done.1
  11.5 0.0 copy-done.1
  11.5 1.3 copy_bitcast_fusion.3
  12.8 3.0 %gather_fusion = bf16[320,32,128]{2,1,0:T(8,128)(2,1)} fusion(bf16[32,192,128]{2,0,1:T(8,128)(2,1)S(1)} %copy_bitcast_fusion.3, s32[1024]{0:T(1024)S(1)} %pad_clamp_fusion), kind=kCustom, calls=%fused_computation.clone | custom fusion | bytes 5244160 | tf_op jit(solution)/shard_map/jit(_take)/gather | solution.py:26
  15.8 8.5 %fusion.52 = bf16[64,4,8,128]{3,2,1,0:T(8,128)(2,1)S(1)} fusion(bf16[64,5,128,128]{3,2,1,0:T(8,128)(2,1)} %param.6, bf16[64,5,32,128]{3,2,1,0:T(8,128)(2,1)} %bitcast.137, pred[64,5]{1,0:T(8,128)(4,1)S(1)} %copy.26, f32[64,128]{1,0:T(8,128)S(1)} %bitcast.149), kind=kOutput, calls=%fused_computation.50 | convolution fusion | flops 337379328 | bytes 13664576 | tf_op jit(solution)/shard_map/rsij,vrsj->vri/dot_general | solution.py:27
  24.3 0.1 copy.72
  24.4 1.3 collective-permute-start.3
  25.7 8.2 %collective-permute-start.2 = (bf16[32,8192]{1,0:T(8,128)(2,1)S(1)}, bf16[32,8192]{1,0:T(8,128)(2,1)S(1)}, u32[]{:S(2)}, u32[]{:S(2)}) collective-permute-start(bf16[32,8192]{1,0:T(8,128)(2,1)S(1)} %bitcast.141), channel_id=1, source_target_pairs={{0,1},{1,2},{2,3},{3,4},{4,5},{5,6},{6,7},{7,8},{8,9},{9,10},{10,1... | collective-permute-start | bytes 1572872 | tf_op jit(solution)/shard_map/ppermute | solution.py:14
  33.9 0.0 collective-permute-done.3
  34.0 1.5 collective-permute-done.2
  35.4 0.3 copy_bitcast_fusion.2
  35.7 3.0 %gather_fusion.1 = bf16[320,32,128]{2,1,0:T(8,128)(2,1)} fusion(bf16[32,192,128]{2,0,1:T(8,128)(2,1)S(1)} %copy_bitcast_fusion.2, s32[1024]{0:T(1024)S(1)} %pad_clamp_fusion), kind=kCustom, calls=%fused_computation.1.clone | custom fusion | bytes 5244160 | tf_op jit(solution)/shard_map/jit(_take)/gather | solution.py:26
  38.7 8.5 %fusion.47 = bf16[64,4,8,128]{3,2,1,0:T(8,128)(2,1)S(1)} fusion(bf16[64,5,128,128]{3,2,1,0:T(8,128)(2,1)} %param.6, bf16[64,5,32,128]{3,2,1,0:T(8,128)(2,1)} %bitcast.138, pred[64,5]{1,0:T(8,128)(4,1)S(1)} %copy.26, f32[64,128]{1,0:T(8,128)S(1)} %bitcast.150), kind=kOutput, calls=%fused_computation.49 | convolution fusion | flops 337379328 | bytes 13664576 | tf_op jit(solution)/shard_map/rsij,vrsj->vri/dot_general | solution.py:27
  47.2 0.1 copy.71
  47.3 1.3 collective-permute-start.5
  48.6 13.6 %collective-permute-start.4 = (bf16[32,8192]{1,0:T(8,128)(2,1)S(1)}, bf16[32,8192]{1,0:T(8,128)(2,1)S(1)}, u32[]{:S(2)}, u32[]{:S(2)}) collective-permute-start(bf16[32,8192]{1,0:T(8,128)(2,1)S(1)} %bitcast.144), channel_id=1, source_target_pairs={{0,1},{1,2},{2,3},{3,4},{4,5},{5,6},{6,7},{7,8},{8,9},{9,10},{10,1... | collective-permute-start | bytes 1572872 | tf_op jit(solution)/shard_map/ppermute | solution.py:14
  62.2 0.0 collective-permute-done.5
  62.2 1.3 collective-permute-done.4
  63.5 0.3 copy_bitcast_fusion.1
  63.8 3.0 %gather_fusion.2 = bf16[320,32,128]{2,1,0:T(8,128)(2,1)} fusion(bf16[32,192,128]{2,0,1:T(8,128)(2,1)S(1)} %copy_bitcast_fusion.1, s32[1024]{0:T(1024)S(1)} %pad_clamp_fusion), kind=kCustom, calls=%fused_computation.2.clone | custom fusion | bytes 5244160 | tf_op jit(solution)/shard_map/jit(_take)/gather | solution.py:26
  66.8 8.5 %fusion.42 = bf16[64,4,8,128]{3,2,1,0:T(8,128)(2,1)S(1)} fusion(bf16[64,5,128,128]{3,2,1,0:T(8,128)(2,1)} %param.6, bf16[64,5,32,128]{3,2,1,0:T(8,128)(2,1)} %bitcast.139, pred[64,5]{1,0:T(8,128)(4,1)S(1)} %copy.26, f32[64,128]{1,0:T(8,128)S(1)} %bitcast.151), kind=kOutput, calls=%fused_computation.48 | convolution fusion | flops 337379328 | bytes 13664576 | tf_op jit(solution)/shard_map/rsij,vrsj->vri/dot_general | solution.py:27
  75.3 0.1 copy.70
  75.4 1.3 collective-permute-start.7
  76.7 10.6 %collective-permute-start.6 = (bf16[32,8192]{1,0:T(8,128)(2,1)S(1)}, bf16[32,8192]{1,0:T(8,128)(2,1)S(1)}, u32[]{:S(2)}, u32[]{:S(2)}) collective-permute-start(bf16[32,8192]{1,0:T(8,128)(2,1)S(1)} %bitcast.147), channel_id=1, source_target_pairs={{0,1},{1,2},{2,3},{3,4},{4,5},{5,6},{6,7},{7,8},{8,9},{9,10},{10,1... | collective-permute-start | bytes 1572872 | tf_op jit(solution)/shard_map/ppermute | solution.py:14
  87.3 0.0 collective-permute-done.7
  87.3 1.5 collective-permute-done.6
  88.8 0.3 copy_bitcast_fusion
  89.1 3.0 %gather_fusion.3 = bf16[320,32,128]{2,1,0:T(8,128)(2,1)} fusion(bf16[32,192,128]{2,0,1:T(8,128)(2,1)S(1)} %copy_bitcast_fusion, s32[1024]{0:T(1024)S(1)} %pad_clamp_fusion), kind=kCustom, calls=%fused_computation.3.clone | custom fusion | bytes 5244160 | tf_op jit(solution)/shard_map/jit(_take)/gather | solution.py:26
  92.1 8.4 %fusion.37 = f32[64,32,128]{2,1,0:T(8,128)S(1)} fusion(bf16[64,5,128,128]{3,2,1,0:T(8,128)(2,1)} %param.6, bf16[64,5,32,128]{3,2,1,0:T(8,128)(2,1)} %bitcast.136, pred[64,5]{1,0:T(8,128)(4,1)S(1)} %copy.26, f32[64,128]{1,0:T(8,128)S(1)} %bitcast.152), kind=kOutput, calls=%fused_computation.47 | convolution fusion | flops 337117184 | bytes 14188864 | tf_op jit(solution)/shard_map/rsij,vrsj->vri/dot_general | solution.py:27
  100.6 1.0 fusion.32
  101.5 71.9 %psum.7 = f32[32,32]{0,1:T(8,128)S(1)} all-reduce(f32[32,32]{0,1:T(8,128)S(1)} %fusion.32), channel_id=1, replica_groups=mesh['groups'=2,'rows'=16] {'rows'}, use_global_device_ids=true, to_apply=%region_1.0 | all-reduce | flops 1024 | bytes 8192 | tf_op jit(solution)/shard_map/psum | solution.py:57
  173.5 0.1 copy.42
  173.6 2.9 %cholesky.16 = f32[32,32]{1,0:T(8,128)S(1)} custom-call(f32[32,32]{1,0:T(8,128)S(1)} %fusion.57), custom_call_target="Cholesky" | custom-call | tf_op jit(solution)/shard_map/jit(cholesky)/cholesky | solution.py:58
  176.5 0.6 compare_reduce_fusion
  177.1 0.7 fusion.55
  177.8 2.4 %custom-call.7 = f32[1,32,32]{1,2,0:T(8,128)S(1)} custom-call(f32[1,32,32]{2,1,0:T(8,128)S(1)} %fusion.55), custom_call_target="InvertDiagBlocksLowerTriangular" | custom-call | tf_op jit(solution)/shard_map/jit(_solve_triangular)/triangular_solve | solution.py:59
  180.2 1.1 fusion.33
  181.3 0.0 copy-done
  181.3 2.0 %convolution_bitcast_fusion = f32[32,8192]{1,0:T(8,128)} fusion(f32[32,8192]{1,0:T(8,128)S(1)} %fusion.33, f32[32,32]{1,0:T(8,128)S(1)} %copy-done), kind=kOutput, calls=%fused_computation.5 | convolution fusion | flops 100663296 | bytes 2101248 | tf_op jit(solution)/shard_map/dot_general | solution.py:60
  (4 shorter events, 0.1 us)
Async XLA Ops:
  0.0 181.3 %copy-start = (f32[32,32]{1,0:T(8,128)S(1)}, f32[32,32]{1,0:T(8,128)}, u32[]{:S(2)}) copy-start(f32[32,32]{1,0:T(8,128)} %param.9) | copy-start | bytes 12292
  0.0 11.5 %collective-permute-start = (bf16[32,8192]{1,0:T(8,128)(2,1)}, bf16[32,8192]{1,0:T(8,128)(2,1)S(1)}, u32[]{:S(2)}, u32[]{:S(2)}) collective-permute-start(bf16[32,8192]{1,0:T(8,128)(2,1)} %param.8), channel_id=1, source_target_pairs={{0,1},{1,2},{2,3},{3,4},{4,5},{5,6},{6,7},{7,8},{8,9},{9,10},{10,1... | collective-permute-start | bytes 1572872 | tf_op jit(solution)/shard_map/ppermute | solution.py:14
  2.5 8.9 %collective-permute-start.1 = (bf16[32,8192]{1,0:T(8,128)(2,1)}, bf16[32,8192]{1,0:T(8,128)(2,1)}, u32[]{:S(2)}, u32[]{:S(2)}) collective-permute-start(bf16[32,8192]{1,0:T(8,128)(2,1)} %param.8), channel_id=1, source_target_pairs={{1,0},{2,1},{3,2},{4,3},{5,4},{6,5},{7,6},{8,7},{9,8},{10,9},{11,1... | collective-permute-start | bytes 1572872 | tf_op jit(solution)/shard_map/ppermute | solution.py:17
  3.8 6.6 %copy-start.2 = (s32[64,5]{0,1:T(8,128)S(1)}, s32[64,5]{0,1:T(8,128)}, u32[]{:S(2)}) copy-start(s32[64,5]{0,1:T(8,128)} %param.7) | copy-start | bytes 3844
  3.8 7.6 %copy-start.1 = (bf16[32,8192]{1,0:T(8,128)(2,1)S(1)}, bf16[32,8192]{1,0:T(8,128)(2,1)}, u32[]{:S(2)}) copy-start(bf16[32,8192]{1,0:T(8,128)(2,1)} %param.8) | copy-start | bytes 1572868
  24.4 9.5 %collective-permute-start.3 = (bf16[32,8192]{1,0:T(8,128)(2,1)S(1)}, bf16[32,8192]{1,0:T(8,128)(2,1)S(1)}, u32[]{:S(2)}, u32[]{:S(2)}) collective-permute-start(bf16[32,8192]{1,0:T(8,128)(2,1)S(1)} %bitcast.140), channel_id=1, source_target_pairs={{1,0},{2,1},{3,2},{4,3},{5,4},{6,5},{7,6},{8,7},{9,8},{10,9},{11,1... | collective-permute-start | bytes 1572872 | tf_op jit(solution)/shard_map/ppermute | solution.py:17
  25.7 9.7 %collective-permute-start.2 = (bf16[32,8192]{1,0:T(8,128)(2,1)S(1)}, bf16[32,8192]{1,0:T(8,128)(2,1)S(1)}, u32[]{:S(2)}, u32[]{:S(2)}) collective-permute-start(bf16[32,8192]{1,0:T(8,128)(2,1)S(1)} %bitcast.141), channel_id=1, source_target_pairs={{0,1},{1,2},{2,3},{3,4},{4,5},{5,6},{6,7},{7,8},{8,9},{9,10},{10,1... | collective-permute-start | bytes 1572872 | tf_op jit(solution)/shard_map/ppermute | solution.py:14
  47.3 14.9 %collective-permute-start.5 = (bf16[32,8192]{1,0:T(8,128)(2,1)S(1)}, bf16[32,8192]{1,0:T(8,128)(2,1)S(1)}, u32[]{:S(2)}, u32[]{:S(2)}) collective-permute-start(bf16[32,8192]{1,0:T(8,128)(2,1)S(1)} %bitcast.143), channel_id=1, source_target_pairs={{1,0},{2,1},{3,2},{4,3},{5,4},{6,5},{7,6},{8,7},{9,8},{10,9},{11,1... | collective-permute-start | bytes 1572872 | tf_op jit(solution)/shard_map/ppermute | solution.py:17
  48.6 14.9 %collective-permute-start.4 = (bf16[32,8192]{1,0:T(8,128)(2,1)S(1)}, bf16[32,8192]{1,0:T(8,128)(2,1)S(1)}, u32[]{:S(2)}, u32[]{:S(2)}) collective-permute-start(bf16[32,8192]{1,0:T(8,128)(2,1)S(1)} %bitcast.144), channel_id=1, source_target_pairs={{0,1},{1,2},{2,3},{3,4},{4,5},{5,6},{6,7},{7,8},{8,9},{9,10},{10,1... | collective-permute-start | bytes 1572872 | tf_op jit(solution)/shard_map/ppermute | solution.py:14
  75.4 11.9 %collective-permute-start.7 = (bf16[32,8192]{1,0:T(8,128)(2,1)S(1)}, bf16[32,8192]{1,0:T(8,128)(2,1)S(1)}, u32[]{:S(2)}, u32[]{:S(2)}) collective-permute-start(bf16[32,8192]{1,0:T(8,128)(2,1)S(1)} %bitcast.146), channel_id=1, source_target_pairs={{1,0},{2,1},{3,2},{4,3},{5,4},{6,5},{7,6},{8,7},{9,8},{10,9},{11,1... | collective-permute-start | bytes 1572872 | tf_op jit(solution)/shard_map/ppermute | solution.py:17
  76.7 12.1 %collective-permute-start.6 = (bf16[32,8192]{1,0:T(8,128)(2,1)S(1)}, bf16[32,8192]{1,0:T(8,128)(2,1)S(1)}, u32[]{:S(2)}, u32[]{:S(2)}) collective-permute-start(bf16[32,8192]{1,0:T(8,128)(2,1)S(1)} %bitcast.147), channel_id=1, source_target_pairs={{0,1},{1,2},{2,3},{3,4},{4,5},{5,6},{6,7},{7,8},{8,9},{9,10},{10,1... | collective-permute-start | bytes 1572872 | tf_op jit(solution)/shard_map/ppermute | solution.py:14
where the time goes:
time: 184 us; the launch traced here: 183 us
  blocking collectives  71.9 us (39%)
  starting transfers between devices  40.1 us (22%)
  matrix products  38.6 us (21%)
  other arithmetic  15.4 us (8%)
  local copies, waits for them, and re-layouts  12.8 us (7%)
  waiting for transfers between devices  4.26 us (2%)
    psum x1, blocking collectives, body(): gram_total = lax.psum(gram_local, 'rows')  71.9 us
    ppermute x4, starting transfers between devices, padded_2(): lax.ppermute(lax.slice_in_dim(block, block.shape[dim] - width, None, axis...  34.9 us
    dot_general x4, matrix products, tile_product(): jnp.einsum('rsij,vrsj->vri', transition_tiles, picked, preferred_element_...  33.9 us
    gather x4, local copies, waits for them, and re-layouts, tile_product(): picked = jnp.take(blocks, local_index, axis=1)  12.1 us
    reduce_sum x1, other arithmetic, body(): jnp.einsum('rsij,j->ri', transition_tiles, unit_vector, preferred_element...  6.58 us
    ppermute x4, starting transfers between devices, padded_2(): lax.ppermute(lax.slice_in_dim(block, 0, width, axis=dim), axis, backward)  5.17 us
    ppermute x4, waiting for transfers between devices, padded_2(): lax.ppermute(lax.slice_in_dim(block, block.shape[dim] - width, None, axis...  4.25 us
  transfers between devices with their start and end apart: 8, of which 3 were waited for; matrix products, arithmetic and copies ran while one was open for 4% of the time, Pallas kernels for 0%

commit v1 on v0

v1 whole, which is shorter than its diff:
```python
import functools

import jax
import jax.numpy as jnp
from jax import lax
from jax.experimental import pallas as pl
from jax.experimental.pallas import tpu as pltpu
from jax.sharding import PartitionSpec as P

PRODUCTS = 4
BLOCK = 16
F32 = jnp.float32
BF16 = jnp.bfloat16
NN = (((1,), (0,)), ((), ()))
NT = (((1,), (1,)), ((), ()))
VM = pl.BlockSpec(memory_space=pltpu.VMEM)
SM = pl.BlockSpec(memory_space=pltpu.SMEM)


def in_vmem(array):
    return pltpu.with_memory_space_constraint(array, pltpu.VMEM)


def cost(flops, moved):
    return pl.CostEstimate(flops=flops, bytes_accessed=moved, transcendentals=0)


def params(mib):
    return pltpu.CompilerParams(vmem_limit_bytes=mib * 2**20)


def prep_kernel(where, columns, tiles, turned, inverse, index, order):
    rows, slots, size, _ = tiles.shape
    first, parity = where[0], where[1]
    low = jnp.where(parity == 0, 2 * rows, rows)
    high = jnp.where(parity == 0, rows, 2 * rows)
    ones = jnp.ones((16, slots * size), BF16)

    def place(r, counts):
        near, far = counts
        crosses = jnp.int32(0)
        for s in range(slots):
            offset = columns[s, r] - first
            spot = jnp.where(
                offset < 0,
                offset + rows + low,
                jnp.where(offset >= rows, offset - rows + high, offset),
            )
            index[r * slots + s] = spot
            crosses = jnp.maximum(crosses, jnp.where(spot >= 2 * rows, 1, 0))
        order[jnp.where(crosses == 1, rows - 1 - far, near)] = r
        return near + 1 - crosses, far + crosses

    def step(block, counts):
        for u in range(BLOCK // 2):
            r = block * (BLOCK // 2) + u
            counts = place(r, counts)
            for s in range(slots):
                turned[r, pl.ds(s * size, size), :] = tiles[r, s].T
            total = lax.dot_general(ones, turned[r], NN, preferred_element_type=F32)
            inverse[pl.ds(r, 1), :] = 1.0 / total[0:1]
        return counts

    near, _ = lax.fori_loop(
        0, 2 * rows // BLOCK, step, (jnp.int32(0), jnp.int32(0))
    )
    order[rows] = near


def prep(where, columns, tiles):
    rows, slots, size, _ = tiles.shape
    return pl.pallas_call(
        prep_kernel,
        out_shape=(
            pltpu.VMEM((rows, slots * size, size), BF16),
            pltpu.VMEM((rows, size), F32),
            pltpu.SMEM((rows * slots,), jnp.int32),
            pltpu.SMEM((rows + 8,), jnp.int32),
        ),
        in_specs=[SM, SM, VM],
        out_specs=(VM, VM, SM, SM),
        compiler_params=params(4),
        cost_estimate=cost(2 * tiles.size * 16, 4 * tiles.size),
        name="prep",
    )(where, columns, in_vmem(tiles))


def fill(window, start, panel, tile_major):
    rows = window.shape[0] // 3
    size = window.shape[2]
    if tile_major:
        window[start : start + rows] = panel[...]
    else:
        for t in range(rows):
            window[start + t] = panel[:, t * size : (t + 1) * size]


def row_block(start, index, order, turned, inverse, window, image):
    slots = turned.shape[1] // turned.shape[2]
    picked = [order[start + u] for u in range(BLOCK)]
    vectors = [
        jnp.concatenate([window[index[r * slots + s]] for s in range(slots)], axis=1)
        for r in picked
    ]
    sums = [
        lax.dot_general(x, turned[r], NN, preferred_element_type=F32)
        for x, r in zip(vectors, picked)
    ]
    for r, y in zip(picked, sums):
        image[r] = (y * inverse[pl.ds(r, 1), :]).astype(image.dtype)


def near_kernel(tile_major, index, order, turned, inverse, own, mate, window, image):
    rows = turned.shape[0]
    fill(window, 0, own, tile_major)
    fill(window, rows, mate, tile_major)

    def step(block, carry):
        row_block(block * BLOCK, index, order, turned, inverse, window, image)
        return carry

    lax.fori_loop(0, (order[rows] + BLOCK - 1) // BLOCK, step, 0)


def far_kernel(tile_major, index, order, turned, inverse, other, w_in, i_in, window, image):
    rows = turned.shape[0]
    fill(window, 2 * rows, other, tile_major)

    def step(block, carry):
        start = rows - (block + 1) * BLOCK
        row_block(start, index, order, turned, inverse, window, image)
        return carry

    lax.fori_loop(0, (rows - order[rows] + BLOCK - 1) // BLOCK, step, 0)


def product(plan, own, mate, other, tile_major, kind):
    index, order, turned, inverse = plan
    rows, depth, size = turned.shape
    vectors = own.shape[1 if tile_major else 0]
    shapes = (
        pltpu.VMEM((3 * rows, vectors, size), BF16),
        pltpu.VMEM((rows, vectors, size), kind),
    )
    estimate = cost(rows * depth * size * vectors, 2 * rows * depth * size)
    window, image = pl.pallas_call(
        functools.partial(near_kernel, tile_major),
        out_shape=shapes,
        in_specs=[SM, SM, VM, VM, VM, VM],
        out_specs=(VM, VM),
        compiler_params=params(4),
        cost_estimate=estimate,
        name="near_rows",
    )(index, order, in_vmem(turned), in_vmem(inverse), in_vmem(own), in_vmem(mate))
    window, image = pl.pallas_call(
        functools.partial(far_kernel, tile_major),
        out_shape=shapes,
        in_specs=[SM, SM, VM, VM, VM, VM, VM],
        out_specs=(VM, VM),
        input_output_aliases={5: 0, 6: 1},
        compiler_params=params(4),
        cost_estimate=estimate,
        name="far_rows",
    )(
        index,
        order,
        in_vmem(turned),
        in_vmem(inverse),
        in_vmem(other),
        in_vmem(window),
        in_vmem(image),
    )
    return image


def thirds(x):
    high = x.astype(BF16)
    rest = x - high.astype(F32)
    middle = rest.astype(BF16)
    low = (rest - middle.astype(F32)).astype(BF16)
    return high, middle, low


def fold(product3, vectors):
    total = None
    for a, b in ((2, 2), (1, 2), (2, 1), (0, 2), (2, 0), (1, 1), (0, 1), (1, 0), (0, 0)):
        part = product3[
            a * vectors : (a + 1) * vectors, b * vectors : (b + 1) * vectors
        ]
        total = part if total is None else total + part
    return total


def gram_kernel(power, parts, gram):
    rows, vectors, size = power.shape
    group = 8

    def step(block, total):
        taken = []
        for u in range(group):
            r = block * group + u
            stacked = jnp.concatenate(thirds(power[r]), axis=0)
            parts[r] = stacked
            taken.append(stacked)
        wide = jnp.concatenate(taken, axis=1)
        return total + lax.dot_general(wide, wide, NT, preferred_element_type=F32)

    total = lax.fori_loop(
        0, rows // group, step, jnp.zeros((3 * vectors, 3 * vectors), F32)
    )
    gram[...] = fold(total, vectors)


def gram_local(power):
    rows, vectors, size = power.shape
    return pl.pallas_call(
        gram_kernel,
        out_shape=(
            pltpu.VMEM((rows, 3 * vectors, size), BF16),
            pltpu.VMEM((vectors, vectors), F32),
        ),
        in_specs=[VM],
        out_specs=(VM, VM),
        compiler_params=params(4),
        cost_estimate=cost(18 * power.size * vectors, 10 * power.size),
        name="gram",
    )(in_vmem(power))


def inverse_factor(gram):
    count = gram.shape[0]
    row = lax.broadcasted_iota(jnp.int32, (count, count), 0)
    column = lax.broadcasted_iota(jnp.int32, (count, count), 1)
    work = jnp.concatenate([gram, jnp.where(row == column, 1.0, 0.0)], axis=1)
    below = lax.broadcasted_iota(jnp.int32, work.shape, 0)
    for k in range(count):
        pivot = work[k : k + 1]
        scaled = pivot * lax.rsqrt(pivot[:, k : k + 1])
        column_k = jnp.broadcast_to(work[:, k : k + 1], work.shape)
        head = lax.rsqrt(pivot[:, k : k + 1])
        work = jnp.where(
            below > k,
            work - (column_k * head) * scaled,
            jnp.where(below == k, scaled, work),
        )
    return work[:, count:]


def final_kernel(states, gram_a, gram_b, mapping, parts, out):
    rows, depth, size = parts.shape
    vectors = depth // 3
    total = (gram_a[...] + gram_b[...]) / states
    factor = inverse_factor(total)
    combined = lax.dot_general(
        mapping[...],
        factor,
        (((0,), (0,)), ((), ())),
        precision=lax.Precision.HIGHEST,
        preferred_element_type=F32,
    )
    high, middle, low = thirds(combined)
    blank = jnp.zeros_like(high)
    left = jnp.concatenate(
        [
            jnp.concatenate([high, high, high], axis=1),
            jnp.concatenate([middle, middle, blank], axis=1),
            jnp.concatenate([low, blank, blank], axis=1),
        ],
        axis=0,
    )
    for r in range(rows):
        y = lax.dot_general(left, parts[r], NN, preferred_element_type=F32)
        out[:, r * size : (r + 1) * size] = (
            y[2 * vectors :] + y[vectors : 2 * vectors]
        ) + y[:vectors]


def final(states, gram_a, gram_b, mapping, parts):
    rows, depth, size = parts.shape
    vectors = depth // 3
    return pl.pallas_call(
        functools.partial(final_kernel, float(states)),
        out_shape=jax.ShapeDtypeStruct((vectors, rows * size), F32),
        in_specs=[VM, VM, VM, VM],
        out_specs=VM,
        compiler_params=params(8),
        cost_estimate=cost(6 * parts.size * vectors, 4 * parts.size),
        name="memberships",
    )(gram_a, gram_b, mapping, in_vmem(parts))


def body(transition_tiles, column_tiles, schur_basis, membership_map):
    rows = transition_tiles.shape[0]
    count = lax.axis_size("rows")
    me = lax.axis_index("rows")
    mates = [(i, i ^ 1) for i in range(count)]
    others = []
    for i in range(1, count - 1, 2):
        others += [(i, i + 1), (i + 1, i)]

    def exchange(image):
        return lax.ppermute(image, "rows", mates), lax.ppermute(image, "rows", others)

    image = schur_basis
    mate, other = exchange(image)
    where = jnp.stack([me * rows, me % 2]).astype(jnp.int32)
    turned, inverse, index, order = prep(where, column_tiles.T, transition_tiles)
    plan = (index, order, turned, inverse)
    for step in range(PRODUCTS):
        if step:
            mate, other = exchange(image)
        kind = F32 if step == PRODUCTS - 1 else BF16
        image = product(plan, image, mate, other, step > 0, kind)
    parts, gram = gram_local(image)
    distance = 1
    while distance < count:
        partner = lax.ppermute(gram, "rows", [(i, i ^ distance) for i in range(count)])
        distance *= 2
        if distance < count:
            gram = gram + partner
    states = schur_basis.shape[1] * count
    return final(states, gram, partner, membership_map, parts)


def solution(mesh):
    return jax.shard_map(
        body,
        mesh=mesh,
        in_specs=(
            P(("groups", "rows"), None, None, None),
            P(("groups", "rows"), None),
            P(None, ("groups", "rows")),
            P("groups", None),
        ),
        out_specs=P(None, ("groups", "rows")),
        check_vma=False,
    )
```

time: 184 us -> 94.1 us (0.51)
  blocking collectives: 71.9 us -> 0 us
  matrix products: 38.6 us -> 0 us
  Pallas kernels: 0 us -> 23.1 us
  other arithmetic: 15.4 us -> 0.09 us
  starting transfers between devices: 40.1 us -> 55 us
  local copies, waits for them, and re-layouts: 12.8 us -> 4.67 us
  waiting for transfers between devices: 4.26 us -> 10.8 us
    psum x1 -> x0, blocking collectives: 71.9 us -> none  [body(): gram_total = lax.psum(gram_local, 'rows')]
    dot_general x7 -> x0, matrix products: 37.5 us -> none  [the longest x4 33.9 us: tile_product(): jnp.einsum('rsij,vrsj->vri', transition_tiles, picked, preferred_element_...]
    pallas_call x0 -> x11, Pallas kernels: none -> 23.1 us  [the longest x4 9.25 us: product(): pl.pallas_call(functools.partial(near_kernel, tile_major), out_shape=shap...]
    ppermute x8 -> x12, starting transfers between devices: 40.1 us -> 55 us  [the longest x4 33 us: exchange(): lax.ppermute(image, 'rows', mates)]
    gather x4 -> x0, local copies, waits for them, and re-layouts: 12.1 us -> none  [tile_product(): picked = jnp.take(blocks, local_index, axis=1)]
    another operation x5 -> x1, other arithmetic: 6.68 us -> 0.08 us  [body(): where = jnp.stack([me * rows, me % 2]).astype(jnp.int32)]
    reduce_sum x1 -> x0, other arithmetic: 6.58 us -> none  [body(): jnp.einsum('rsij,j->ri', transition_tiles, unit_vector, preferred_element...]
    ppermute x8 -> x12, waiting for transfers between devices: 4.26 us -> 10.8 us  [the longest x4 8.27 us: body(): lax.ppermute(gram, 'rows', [(i, i ^ distance) for i in range(count)])]
  transfers between devices with their start and end apart: 8 -> 12, of which waited for: 3 -> 7; matrix products, arithmetic and copies ran while one was open for 4% -> 0% of each run, Pallas kernels for 0% -> 16%
where the time goes in v1:
time: 94.1 us; the launch traced here: 93.9 us
  starting transfers between devices  55 us (58%)
  Pallas kernels  23.1 us (25%)
  waiting for transfers between devices  10.8 us (11%)
  local copies, waits for them, and re-layouts  4.67 us (5%)
    ppermute x4, starting transfers between devices, exchange(): lax.ppermute(image, 'rows', mates)  33 us
    ppermute x4, starting transfers between devices, body(): lax.ppermute(gram, 'rows', [(i, i ^ distance) for i in range(count)])  19.3 us
    pallas_call x4, Pallas kernels, product(): pl.pallas_call(functools.partial(near_kernel, tile_major), out_shape=shap...  9.25 us
    ppermute x4, waiting for transfers between devices, body(): lax.ppermute(gram, 'rows', [(i, i ^ distance) for i in range(count)])  8.27 us
    pallas_call x1, Pallas kernels, final(): pl.pallas_call(functools.partial(final_kernel, float(states)), out_shape=...  6.06 us
    pallas_call x1, Pallas kernels, prep(): pl.pallas_call(prep_kernel, out_shape=(pltpu.VMEM((rows, slots * size, si...  5.78 us
    unnamed x8, local copies, waits for them, and re-layouts  4.67 us
    ppermute x4, starting transfers between devices, exchange(): lax.ppermute(image, 'rows', others)  2.73 us
  transfers between devices with their start and end apart: 12, of which 7 were waited for; matrix products, arithmetic and copies ran while one was open for 0% of the time, Pallas kernels for 16%

profile of v1, /device:TPU:0, one launch (start us, length us, event | category | flops | bytes accessed | tf_op | source)
XLA Modules:
  0.0 93.9 jit_solution(417127714365406483)
XLA Ops:
  0.0 0.5 collective-permute-start.1
  0.5 0.7 collective-permute-start
  1.2 0.1 pad_add_fusion.where
  1.2 0.0 copy-start
  1.2 4.0 %copy-done = bf16[64,5,128,128]{3,2,1,0:T(8,128)(2,1)S(1)} copy-done((bf16[64,5,128,128]{3,2,1,0:T(8,128)(2,1)S(1)}, bf16[64,5,128,128]{3,2,1,0:T(8,128)(2,1)}, u32[]{:S(2)}) %copy-start) | copy-done | bytes 10485784
  5.2 0.0 copy-start.3
  5.2 0.7 copy-done.3
  5.9 0.0 copy-start.1
  5.9 5.8 %prep.1 = (bf16[64,640,128]{2,1,0:T(8,128)(2,1)S(1)}, f32[64,128]{1,0:T(8,128)S(1)}, s32[320]{0:T(512)S(4)}, s32[72]{0:T(128)S(4)}) custom-call(s32[2]{0:T(128)S(1)} %pad_add_fusion.where, s32[5,64]{1,0:T(8,128)S(1)} %bitcast.3, bf16[64,5,128,128]{3,2,1,0:T(8,128)(2,1)S(1)} %copy-done), custom_call_target="tpu_custom_call" | custom-call | flops 167772160 | bytes 20971520 | tf_op jit(solution)/shard_map/prep/pallas_call | solution.py:72
  11.7 0.0 collective-permute-done.1.mate
  11.7 0.0 copy-done.1
  11.7 2.4 %near_rows.4 = (bf16[192,32,128]{2,1,0:T(8,128)(2,1)S(1)}, bf16[64,32,128]{2,1,0:T(8,128)(2,1)S(1)}) custom-call(s32[320]{0:T(512)S(4)} %get-tuple-element.23.index, s32[72]{0:T(128)S(4)} %get-tuple-element.24.order, bf16[64,640,128]{2,1,0:T(8,128)(2,1)S(1)} %get-tuple-element.25.turned, f32[64,128]{1,0:T(8,128)S(1)} %get-tuple-element.26.inverse, ...), custom_call_target="tpu_custom_call" | custom-call | flops 167772160 | bytes 10485760 | tf_op jit(solution)/shard_map/near_rows/pallas_call | solution.py:146
  14.1 0.0 collective-permute-done.other
  14.1 0.1 far_rows.4
  14.2 4.6 %collective-permute-start.3 = (bf16[64,32,128]{2,1,0:T(8,128)(2,1)S(1)}, bf16[64,32,128]{2,1,0:T(8,128)(2,1)S(1)}, u32[]{:S(2)}, u32[]{:S(2)}) collective-permute-start(bf16[64,32,128]{2,1,0:T(8,128)(2,1)S(1)} %get-tuple-element.29.own), channel_id=1, source_target_pairs={{0,1},{1,0},{2,3},{3,2},{4,5},{5,4},{6,7},{7,6},{8,9},{9,8},{10,11... | collective-permute-start | bytes 1572872 | tf_op jit(solution)/shard_map/ppermute | solution.py:302
  18.8 0.7 collective-permute-start.2
  19.5 0.8 collective-permute-done.3.mate
  20.4 2.3 %near_rows.5 = (bf16[192,32,128]{2,1,0:T(8,128)(2,1)S(1)}, bf16[64,32,128]{2,1,0:T(8,128)(2,1)S(1)}) custom-call(s32[320]{0:T(512)S(4)} %get-tuple-element.23.index, s32[72]{0:T(128)S(4)} %get-tuple-element.24.order, bf16[64,640,128]{2,1,0:T(8,128)(2,1)S(1)} %get-tuple-element.25.turned, f32[64,128]{1,0:T(8,128)S(1)} %get-tuple-element.26.inverse, ...), custom_call_target="tpu_custom_call" | custom-call | flops 167772160 | bytes 10485760 | tf_op jit(solution)/shard_map/near_rows/pallas_call | solution.py:146
  22.7 0.0 collective-permute-done.2.other
  22.7 13.9 %collective-permute-start.5 = (bf16[64,32,128]{2,1,0:T(8,128)(2,1)S(1)}, bf16[64,32,128]{2,1,0:T(8,128)(2,1)S(1)}, u32[]{:S(2)}, u32[]{:S(2)}) collective-permute-start(bf16[64,32,128]{2,1,0:T(8,128)(2,1)S(1)} %get-tuple-element.32.own), channel_id=1, source_target_pairs={{0,1},{1,0},{2,3},{3,2},{4,5},{5,4},{6,7},{7,6},{8,9},{9,8},{10,11... | collective-permute-start | bytes 1572872 | tf_op jit(solution)/shard_map/ppermute | solution.py:302
  36.6 0.7 collective-permute-start.4
  37.3 0.8 collective-permute-done.5.mate
  38.2 2.3 %near_rows.6 = (bf16[192,32,128]{2,1,0:T(8,128)(2,1)S(1)}, bf16[64,32,128]{2,1,0:T(8,128)(2,1)S(1)}) custom-call(s32[320]{0:T(512)S(4)} %get-tuple-element.23.index, s32[72]{0:T(128)S(4)} %get-tuple-element.24.order, bf16[64,640,128]{2,1,0:T(8,128)(2,1)S(1)} %get-tuple-element.25.turned, f32[64,128]{1,0:T(8,128)S(1)} %get-tuple-element.26.inverse, ...), custom_call_target="tpu_custom_call" | custom-call | flops 167772160 | bytes 10485760 | tf_op jit(solution)/shard_map/near_rows/pallas_call | solution.py:146
  40.4 0.0 collective-permute-done.4.other
  40.5 14.0 %collective-permute-start.7 = (bf16[64,32,128]{2,1,0:T(8,128)(2,1)S(1)}, bf16[64,32,128]{2,1,0:T(8,128)(2,1)S(1)}, u32[]{:S(2)}, u32[]{:S(2)}) collective-permute-start(bf16[64,32,128]{2,1,0:T(8,128)(2,1)S(1)} %get-tuple-element.35.own), channel_id=1, source_target_pairs={{0,1},{1,0},{2,3},{3,2},{4,5},{5,4},{6,7},{7,6},{8,9},{9,8},{10,11... | collective-permute-start | bytes 1572872 | tf_op jit(solution)/shard_map/ppermute | solution.py:302
  54.5 0.7 collective-permute-start.6
  55.2 0.8 collective-permute-done.7.mate
  56.1 2.3 %near_rows.7 = (bf16[192,32,128]{2,1,0:T(8,128)(2,1)S(1)}, f32[64,32,128]{2,1,0:T(8,128)S(1)}) custom-call(s32[320]{0:T(512)S(4)} %get-tuple-element.23.index, s32[72]{0:T(128)S(4)} %get-tuple-element.24.order, bf16[64,640,128]{2,1,0:T(8,128)(2,1)S(1)} %get-tuple-element.25.turned, f32[64,128]{1,0:T(8,128)S(1)} %get-tuple-element.26.inverse, ...), custom_call_target="tpu_custom_call" | custom-call | flops 167772160 | bytes 10485760 | tf_op jit(solution)/shard_map/near_rows/pallas_call | solution.py:146
  58.3 0.0 collective-permute-done.6.other
  58.3 0.0 copy-start.2
  58.4 1.8 %gram.1 = (bf16[64,96,128]{2,1,0:T(8,128)(2,1)S(1)}, f32[32,32]{1,0:T(8,128)S(1)}) custom-call(f32[64,32,128]{2,1,0:T(8,128)S(1)} %get-tuple-element.38.power), custom_call_target="tpu_custom_call" | custom-call | flops 150994944 | bytes 2621440 | tf_op jit(solution)/shard_map/gram/pallas_call | solution.py:216
  60.2 14.0 %collective-permute-start.8 = (f32[32,32]{1,0:T(8,128)S(1)}, f32[32,32]{1,0:T(8,128)S(1)}, u32[]{:S(2)}, u32[]{:S(2)}) collective-permute-start(f32[32,32]{1,0:T(8,128)S(1)} %get-tuple-element.39), channel_id=1, source_target_pairs={{0,1},{1,0},{2,3},{3,2},{4,5},{5,4},{6,7},{7,6},{8,9},{9,8},{10,11... | collective-permute-start | bytes 12296 | tf_op jit(solution)/shard_map/ppermute | solution.py:317
  74.2 0.8 collective-permute-done.8
  75.0 2.7 %collective-permute-start.9 = (f32[32,32]{1,0:T(8,128)S(1)}, f32[32,32]{1,0:T(8,128)S(1)}, u32[]{:S(2)}, u32[]{:S(2)}) collective-permute-start(f32[32,32]{1,0:T(8,128)S(1)} %add.14), channel_id=1, source_target_pairs={{0,2},{1,3},{2,0},{3,1},{4,6},{5,7},{6,4},{7,5},{8,10},{9,11},{10,... | collective-permute-start | bytes 12296 | tf_op jit(solution)/shard_map/ppermute | solution.py:317
  77.7 1.7 %collective-permute-done.9 = f32[32,32]{1,0:T(8,128)S(1)} collective-permute-done((f32[32,32]{1,0:T(8,128)S(1)}, f32[32,32]{1,0:T(8,128)S(1)}, u32[]{:S(2)}, u32[]{:S(2)}) %collective-permute-start.9) | collective-permute-done | bytes 4128 | tf_op jit(solution)/shard_map/ppermute | solution.py:317
  79.5 0.1 collective-permute-start.10
  79.5 3.7 %collective-permute-done.10 = f32[32,32]{1,0:T(8,128)S(1)} collective-permute-done((f32[32,32]{1,0:T(8,128)S(1)}, f32[32,32]{1,0:T(8,128)S(1)}, u32[]{:S(2)}, u32[]{:S(2)}) %collective-permute-start.10) | collective-permute-done | bytes 4128 | tf_op jit(solution)/shard_map/ppermute | solution.py:317
  83.2 2.6 %collective-permute-start.11 = (f32[32,32]{1,0:T(8,128)S(1)}, f32[32,32]{1,0:T(8,128)S(1)}, u32[]{:S(2)}, u32[]{:S(2)}) collective-permute-start(f32[32,32]{1,0:T(8,128)S(1)} %add.16.gram_a), channel_id=1, source_target_pairs={{0,8},{1,9},{2,10},{3,11},{4,12},{5,13},{6,14},{7,15},{8,0},{9,1},... | collective-permute-start | bytes 12296 | tf_op jit(solution)/shard_map/ppermute | solution.py:317
  85.8 2.0 %collective-permute-done.11.gram_b = f32[32,32]{1,0:T(8,128)S(1)} collective-permute-done((f32[32,32]{1,0:T(8,128)S(1)}, f32[32,32]{1,0:T(8,128)S(1)}, u32[]{:S(2)}, u32[]{:S(2)}) %collective-permute-start.11) | collective-permute-done | bytes 4128 | tf_op jit(solution)/shard_map/ppermute | solution.py:317
  87.8 0.0 copy-done.2
  87.8 6.1 %memberships.1 = f32[32,8192]{1,0:T(8,128)} custom-call(f32[32,32]{1,0:T(8,128)S(1)} %add.16.gram_a, f32[32,32]{1,0:T(8,128)S(1)} %collective-permute-done.11.gram_b, f32[32,32]{1,0:T(8,128)S(1)} %copy-done.2, bf16[64,96,128]{2,1,0:T(8,128)(2,1)S(1)} %get-tuple-element.40.parts), custom_call_target="tpu_custom_call" | custom-call | flops 150994944 | bytes 3145728 | tf_op jit(solution)/shard_map/memberships/pallas_call | solution.py:281
  (6 shorter events, 0.1 us)
Async XLA Ops:
  0.0 11.7 %collective-permute-start.1 = (bf16[32,8192]{1,0:T(8,128)(2,1)}, bf16[32,8192]{1,0:T(8,128)(2,1)S(1)}, u32[]{:S(2)}, u32[]{:S(2)}) collective-permute-start(bf16[32,8192]{1,0:T(8,128)(2,1)} %own.1), channel_id=1, source_target_pairs={{0,1},{1,0},{2,3},{3,2},{4,5},{5,4},{6,7},{7,6},{8,9},{9,8},{10,11... | collective-permute-start | bytes 1572872 | tf_op jit(solution)/shard_map/ppermute | solution.py:302
  0.5 13.7 %collective-permute-start = (bf16[32,8192]{1,0:T(8,128)(2,1)}, bf16[32,8192]{1,0:T(8,128)(2,1)S(1)}, u32[]{:S(2)}, u32[]{:S(2)}) collective-permute-start(bf16[32,8192]{1,0:T(8,128)(2,1)} %own.1), channel_id=1, source_target_pairs={{1,2},{2,1},{3,4},{4,3},{5,6},{6,5},{7,8},{8,7},{9,10},{10,9},{11,... | collective-permute-start | bytes 1572872 | tf_op jit(solution)/shard_map/ppermute | solution.py:302
  1.2 4.0 %copy-start = (bf16[64,5,128,128]{3,2,1,0:T(8,128)(2,1)S(1)}, bf16[64,5,128,128]{3,2,1,0:T(8,128)(2,1)}, u32[]{:S(2)}) copy-start(bf16[64,5,128,128]{3,2,1,0:T(8,128)(2,1)} %tiles.1) | copy-start | bytes 31457284
  5.2 0.7 copy-start.3
  5.9 5.8 %copy-start.1 = (bf16[32,8192]{1,0:T(8,128)(2,1)S(1)}, bf16[32,8192]{1,0:T(8,128)(2,1)}, u32[]{:S(2)}) copy-start(bf16[32,8192]{1,0:T(8,128)(2,1)} %own.1) | copy-start | bytes 1572868
  14.2 6.1 %collective-permute-start.3 = (bf16[64,32,128]{2,1,0:T(8,128)(2,1)S(1)}, bf16[64,32,128]{2,1,0:T(8,128)(2,1)S(1)}, u32[]{:S(2)}, u32[]{:S(2)}) collective-permute-start(bf16[64,32,128]{2,1,0:T(8,128)(2,1)S(1)} %get-tuple-element.29.own), channel_id=1, source_target_pairs={{0,1},{1,0},{2,3},{3,2},{4,5},{5,4},{6,7},{7,6},{8,9},{9,8},{10,11... | collective-permute-start | bytes 1572872 | tf_op jit(solution)/shard_map/ppermute | solution.py:302
  18.8 3.8 %collective-permute-start.2 = (bf16[64,32,128]{2,1,0:T(8,128)(2,1)S(1)}, bf16[64,32,128]{2,1,0:T(8,128)(2,1)S(1)}, u32[]{:S(2)}, u32[]{:S(2)}) collective-permute-start(bf16[64,32,128]{2,1,0:T(8,128)(2,1)S(1)} %get-tuple-element.29.own), channel_id=1, source_target_pairs={{1,2},{2,1},{3,4},{4,3},{5,6},{6,5},{7,8},{8,7},{9,10},{10,9},{11,... | collective-permute-start | bytes 1572872 | tf_op jit(solution)/shard_map/ppermute | solution.py:302
  22.7 15.4 %collective-permute-start.5 = (bf16[64,32,128]{2,1,0:T(8,128)(2,1)S(1)}, bf16[64,32,128]{2,1,0:T(8,128)(2,1)S(1)}, u32[]{:S(2)}, u32[]{:S(2)}) collective-permute-start(bf16[64,32,128]{2,1,0:T(8,128)(2,1)S(1)} %get-tuple-element.32.own), channel_id=1, source_target_pairs={{0,1},{1,0},{2,3},{3,2},{4,5},{5,4},{6,7},{7,6},{8,9},{9,8},{10,11... | collective-permute-start | bytes 1572872 | tf_op jit(solution)/shard_map/ppermute | solution.py:302
  36.6 3.8 %collective-permute-start.4 = (bf16[64,32,128]{2,1,0:T(8,128)(2,1)S(1)}, bf16[64,32,128]{2,1,0:T(8,128)(2,1)S(1)}, u32[]{:S(2)}, u32[]{:S(2)}) collective-permute-start(bf16[64,32,128]{2,1,0:T(8,128)(2,1)S(1)} %get-tuple-element.32.own), channel_id=1, source_target_pairs={{1,2},{2,1},{3,4},{4,3},{5,6},{6,5},{7,8},{8,7},{9,10},{10,9},{11,... | collective-permute-start | bytes 1572872 | tf_op jit(solution)/shard_map/ppermute | solution.py:302
  40.5 15.5 %collective-permute-start.7 = (bf16[64,32,128]{2,1,0:T(8,128)(2,1)S(1)}, bf16[64,32,128]{2,1,0:T(8,128)(2,1)S(1)}, u32[]{:S(2)}, u32[]{:S(2)}) collective-permute-start(bf16[64,32,128]{2,1,0:T(8,128)(2,1)S(1)} %get-tuple-element.35.own), channel_id=1, source_target_pairs={{0,1},{1,0},{2,3},{3,2},{4,5},{5,4},{6,7},{7,6},{8,9},{9,8},{10,11... | collective-permute-start | bytes 1572872 | tf_op jit(solution)/shard_map/ppermute | solution.py:302
  54.5 3.8 %collective-permute-start.6 = (bf16[64,32,128]{2,1,0:T(8,128)(2,1)S(1)}, bf16[64,32,128]{2,1,0:T(8,128)(2,1)S(1)}, u32[]{:S(2)}, u32[]{:S(2)}) collective-permute-start(bf16[64,32,128]{2,1,0:T(8,128)(2,1)S(1)} %get-tuple-element.35.own), channel_id=1, source_target_pairs={{1,2},{2,1},{3,4},{4,3},{5,6},{6,5},{7,8},{8,7},{9,10},{10,9},{11,... | collective-permute-start | bytes 1572872 | tf_op jit(solution)/shard_map/ppermute | solution.py:302
  58.3 29.5 %copy-start.2 = (f32[32,32]{1,0:T(8,128)S(1)}, f32[32,32]{1,0:T(8,128)}, u32[]{:S(2)}) copy-start(f32[32,32]{1,0:T(8,128)} %mapping.1) | copy-start | bytes 12292
  60.2 14.8 %collective-permute-start.8 = (f32[32,32]{1,0:T(8,128)S(1)}, f32[32,32]{1,0:T(8,128)S(1)}, u32[]{:S(2)}, u32[]{:S(2)}) collective-permute-start(f32[32,32]{1,0:T(8,128)S(1)} %get-tuple-element.39), channel_id=1, source_target_pairs={{0,1},{1,0},{2,3},{3,2},{4,5},{5,4},{6,7},{7,6},{8,9},{9,8},{10,11... | collective-permute-start | bytes 12296 | tf_op jit(solution)/shard_map/ppermute | solution.py:317
  75.0 4.4 %collective-permute-start.9 = (f32[32,32]{1,0:T(8,128)S(1)}, f32[32,32]{1,0:T(8,128)S(1)}, u32[]{:S(2)}, u32[]{:S(2)}) collective-permute-start(f32[32,32]{1,0:T(8,128)S(1)} %add.14), channel_id=1, source_target_pairs={{0,2},{1,3},{2,0},{3,1},{4,6},{5,7},{6,4},{7,5},{8,10},{9,11},{10,... | collective-permute-start | bytes 12296 | tf_op jit(solution)/shard_map/ppermute | solution.py:317
  79.5 3.7 %collective-permute-start.10 = (f32[32,32]{1,0:T(8,128)S(1)}, f32[32,32]{1,0:T(8,128)S(1)}, u32[]{:S(2)}, u32[]{:S(2)}) collective-permute-start(f32[32,32]{1,0:T(8,128)S(1)} %add.15), channel_id=1, source_target_pairs={{0,4},{1,5},{2,6},{3,7},{4,0},{5,1},{6,2},{7,3},{8,12},{9,13},{10,... | collective-permute-start | bytes 12296 | tf_op jit(solution)/shard_map/ppermute | solution.py:317
  83.2 4.6 %collective-permute-start.11 = (f32[32,32]{1,0:T(8,128)S(1)}, f32[32,32]{1,0:T(8,128)S(1)}, u32[]{:S(2)}, u32[]{:S(2)}) collective-permute-start(f32[32,32]{1,0:T(8,128)S(1)} %add.16.gram_a), channel_id=1, source_target_pairs={{0,8},{1,9},{2,10},{3,11},{4,12},{5,13},{6,14},{7,15},{8,0},{9,1},... | collective-permute-start | bytes 12296 | tf_op jit(solution)/shard_map/ppermute | solution.py:317

commit v2 on v1

--- a/solution.py
+++ b/solution.py
@@ -9,6 +9,7 @@
 
 PRODUCTS = 4
 BLOCK = 16
+CHUNK = 8
 F32 = jnp.float32
 BF16 = jnp.bfloat16
 NN = (((1,), (0,)), ((), ()))
@@ -29,12 +30,20 @@
     return pltpu.CompilerParams(vmem_limit_bytes=mib * 2**20)
 
 
-def prep_kernel(where, columns, tiles, turned, inverse, index, order):
+def prep_kernel(where, columns, tiles, turned, inverse, index, order, landing, arrived):
     rows, slots, size, _ = tiles.shape
+    depth, chunk = landing.shape[:2]
+    chunks = rows // chunk
     first, parity = where[0], where[1]
     low = jnp.where(parity == 0, 2 * rows, rows)
     high = jnp.where(parity == 0, rows, 2 * rows)
     ones = jnp.ones((16, slots * size), BF16)
+
+    def copy(i):
+        slot = lax.rem(i, depth)
+        return pltpu.make_async_copy(
+            tiles.at[pl.ds(i * chunk, chunk)], landing.at[slot], arrived.at[slot]
+        )
 
     def place(r, counts):
         near, far = counts
@@ -51,24 +60,33 @@
         order[jnp.where(crosses == 1, rows - 1 - far, near)] = r
         return near + 1 - crosses, far + crosses
 
-    def step(block, counts):
-        for u in range(BLOCK // 2):
-            r = block * (BLOCK // 2) + u
+    for i in range(depth):
+        copy(i).start()
+
+    def step(i, counts):
+        slot = lax.rem(i, depth)
+        copy(i).wait()
+        for u in range(chunk):
+            r = i * chunk + u
             counts = place(r, counts)
             for s in range(slots):
-                turned[r, pl.ds(s * size, size), :] = tiles[r, s].T
+                turned[r, pl.ds(s * size, size), :] = landing[slot, u, s].T
             total = lax.dot_general(ones, turned[r], NN, preferred_element_type=F32)
             inverse[pl.ds(r, 1), :] = 1.0 / total[0:1]
+
+        @pl.when(i + depth < chunks)
+        def _():
+            copy(i + depth).start()
+
         return counts
 
-    near, _ = lax.fori_loop(
-        0, 2 * rows // BLOCK, step, (jnp.int32(0), jnp.int32(0))
-    )
+    near, _ = lax.fori_loop(0, chunks, step, (jnp.int32(0), jnp.int32(0)))
     order[rows] = near
 
 
 def prep(where, columns, tiles):
     rows, slots, size, _ = tiles.shape
+    chunk, depth = CHUNK, 3
     return pl.pallas_call(
         prep_kernel,
         out_shape=(
@@ -77,21 +95,93 @@
             pltpu.SMEM((rows * slots,), jnp.int32),
             pltpu.SMEM((rows + 8,), jnp.int32),
         ),
-        in_specs=[SM, SM, VM],
+        in_specs=[SM, SM, pl.BlockSpec(memory_space=pltpu.HBM)],
         out_specs=(VM, VM, SM, SM),
-        compiler_params=params(4),
+        scratch_shapes=[
+            pltpu.VMEM((depth, chunk, slots, size, size), BF16),
+            pltpu.SemaphoreType.DMA((depth,)),
+        ],
+        compiler_params=params(10),
         cost_estimate=cost(2 * tiles.size * 16, 4 * tiles.size),
         name="prep",
-    )(where, columns, in_vmem(tiles))
+    )(where, columns, pltpu.with_memory_space_constraint(tiles, pltpu.HBM))
+
+
+def lists_kernel(limit, where, theirs, index, packed, sending, more, mark, asked, rank):
+    slots, rows = theirs.shape
+    first = where[0]
+    unroll = 8
+
+    def clear(block, carry):
+        for u in range(unroll):
+            h = block * unroll + u
+            mark[h] = 0
+            asked[h] = 0
+            sending[h] = 0
+        return carry
+
+    def name(block, carry):
+        for u in range(unroll):
+            r = block * unroll + u
+            for s in range(slots):
+                t = index[r * slots + s] - 2 * rows
+                mark[jnp.where(t >= 0, t, rows)] = 1
+                c = theirs[s, r] - first
+                asked[jnp.where((c >= 0) & (c < rows), c, rows)] = 1
+        return carry
+
+    def count(block, carry):
+        read, sent = carry
+        for u in range(unroll):
+            h = block * unroll + u
+            rank[h] = read
+            sending[sent] = h
+            read, sent = read + mark[h], sent + asked[h]
+        return read, sent
+
+    def renumber(block, carry):
+        for u in range(unroll):
+            r = block * unroll + u
+            for s in range(slots):
+                t = index[r * slots + s]
+                far = t >= 2 * rows
+                packed[r * slots + s] = jnp.where(
+                    far, 2 * rows + rank[jnp.where(far, t - 2 * rows, 0)], t
+                )
+        return carry
+
+    blocks = rows // unroll
+    lax.fori_loop(0, blocks, clear, 0)
+    lax.fori_loop(0, blocks, name, 0)
+    read, sent = lax.fori_loop(0, blocks, count, (jnp.int32(0), jnp.int32(0)))
+    lax.fori_loop(0, blocks, renumber, 0)
+    more[0] = jnp.where(jnp.maximum(read, sent) > limit, 1, 0)
+
+
+def lists(limit, where, theirs, index):
+    slots, rows = theirs.shape
+    return pl.pallas_call(
+        functools.partial(lists_kernel, limit),
+        out_shape=(
+            pltpu.SMEM((rows * slots,), jnp.int32),
+            pltpu.SMEM((rows + 8,), jnp.int32),
+            jax.ShapeDtypeStruct((1,), jnp.int32),
+        ),
+        in_specs=[SM, SM, SM],
+        out_specs=(SM, SM, SM),
+        scratch_shapes=[pltpu.SMEM((rows + 8,), jnp.int32)] * 3,
+        compiler_params=params(1),
+        cost_estimate=cost(4000000, 4000),
+        name="lists",
+    )(where, theirs, index)
 
 
 def fill(window, start, panel, tile_major):
-    rows = window.shape[0] // 3
     size = window.shape[2]
     if tile_major:
-        window[start : start + rows] = panel[...]
+        window[start : start + panel.shape[0]] = panel[...]
     else:
-        for t in range(rows):
+        for t in range(panel.shape[1] // size):
             window[start + t] = panel[:, t * size : (t + 1) * size]
 
 
@@ -122,9 +212,8 @@
     lax.fori_loop(0, (order[rows] + BLOCK - 1) // BLOCK, step, 0)
 
 
-def far_kernel(tile_major, index, order, turned, inverse, other, w_in, i_in, window, image):
+def far_rows(index, order, turned, inverse, window, image):
     rows = turned.shape[0]
-    fill(window, 2 * rows, other, tile_major)
 
     def step(block, carry):
         start = rows - (block + 1) * BLOCK
@@ -134,8 +223,27 @@
     lax.fori_loop(0, (rows - order[rows] + BLOCK - 1) // BLOCK, step, 0)
 
 
-def product(plan, own, mate, other, tile_major, kind):
-    index, order, turned, inverse = plan
+def far_kernel(tile_major, packs, count, *refs):
+    index, order, turned, inverse, sending = refs[:5]
+    arrived = refs[5 : 5 + count]
+    window, image = refs[7 + count : 9 + count]
+    rows = turned.shape[0]
+    start = 2 * rows
+    for panel in arrived:
+        fill(window, start, panel, tile_major)
+        start += panel.shape[0]
+    far_rows(index, order, turned, inverse, window, image)
+    if packs:
+        send, rest = refs[9 + count :]
+        limit = send.shape[0]
+        for k in range(rows):
+            target = send.at[k] if k < limit else rest.at[k - limit]
+            target[...] = image[sending[k]]
+
+
+def product(plan, panels, tile_major, kind, limit):
+    near_index, far_index, order, turned, inverse, sending = plan
+    own, mate, *arrived = panels
     rows, depth, size = turned.shape
     vectors = own.shape[1 if tile_major else 0]
     shapes = (
@@ -151,26 +259,31 @@
         compiler_params=params(4),
         cost_estimate=estimate,
         name="near_rows",
-    )(index, order, in_vmem(turned), in_vmem(inverse), in_vmem(own), in_vmem(mate))
-    window, image = pl.pallas_call(
-        functools.partial(far_kernel, tile_major),
+    )(near_index, order, *map(in_vmem, (turned, inverse, own, mate)))
+    packs = limit > 0
+    if packs:
+        shapes += (
+            pltpu.VMEM((limit, vectors, size), kind),
+            pltpu.VMEM((rows - limit, vectors, size), kind),
+        )
+    count = len(arrived)
+    return pl.pallas_call(
+        functools.partial(far_kernel, tile_major, packs, count),
         out_shape=shapes,
-        in_specs=[SM, SM, VM, VM, VM, VM, VM],
-        out_specs=(VM, VM),
-        input_output_aliases={5: 0, 6: 1},
+        in_specs=[SM, SM, VM, VM, SM] + [VM] * (count + 2),
+        out_specs=(VM,) * len(shapes),
+        input_output_aliases={5 + count: 0, 6 + count: 1},
         compiler_params=params(4),
         cost_estimate=estimate,
         name="far_rows",
     )(
-        index,
+        far_index,
         order,
         in_vmem(turned),
         in_vmem(inverse),
-        in_vmem(other),
-        in_vmem(window),
-        in_vmem(image),
-    )
-    return image
+        sending,
+        *map(in_vmem, (*arrived, window, image)),
+    )[1:]
 
 
 def thirds(x):
@@ -298,19 +411,30 @@
     for i in range(1, count - 1, 2):
         others += [(i, i + 1), (i + 1, i)]
 
-    def exchange(image):
-        return lax.ppermute(image, "rows", mates), lax.ppermute(image, "rows", others)
-
-    image = schur_basis
-    mate, other = exchange(image)
+    def swap(array, pairs):
+        return lax.ppermute(array, "rows", pairs)
+
+    limit = 11 * rows // 16
     where = jnp.stack([me * rows, me % 2]).astype(jnp.int32)
-    turned, inverse, index, order = prep(where, column_tiles.T, transition_tiles)
-    plan = (index, order, turned, inverse)
-    for step in range(PRODUCTS):
-        if step:
-            mate, other = exchange(image)
-        kind = F32 if step == PRODUCTS - 1 else BF16
-        image = product(plan, image, mate, other, step > 0, kind)
+    columns = column_tiles.T
+    theirs = swap(columns, others)
+    panels = schur_basis, swap(schur_basis, mates), swap(schur_basis, others)
+    turned, inverse, index, order = prep(where, columns, transition_tiles)
+    packed, sending, more = lists(limit, where, theirs, index)
+    plan = (index, index, order, turned, inverse, sending)
+    image, send, rest = product(plan, panels, False, BF16, limit)
+    plan = (index, packed, order, turned, inverse, sending)
+    for step in range(1, PRODUCTS):
+        mate, other = swap(image, mates), swap(send, others)
+        extra = lax.cond(more[0] > 0, lambda x: swap(x, others), lambda x: x, rest)
+        last = step == PRODUCTS - 1
+        out = product(
+            plan, (image, mate, other, extra), True, F32 if last else BF16, 0 if last else limit
+        )
+        if last:
+            (image,) = out
+        else:
+            image, send, rest = out
     parts, gram = gram_local(image)
     distance = 1
     while distance < count:

time: 94.1 us -> 89.5 us (0.951)
  starting transfers between devices: 55 us -> 36.1 us
  local copies, waits for them, and re-layouts: 4.67 us -> 12.6 us
  Pallas kernels: 23.1 us -> 30 us
  waiting for transfers between devices: 10.8 us -> 9.44 us
    ppermute x8 -> x9, starting transfers between devices: 35.7 us -> 23.3 us  [swap(): return lax.ppermute(array, 'rows', pairs)]
    unnamed x8 -> x14, local copies, waits for them, and re-layouts: 4.67 us -> 12.6 us
    ppermute x4, starting transfers between devices: 19.3 us -> 12.8 us  [body(): lax.ppermute(gram, 'rows', [(i, i ^ distance) for i in range(count)])]
    pallas_call x4 -> x5, Pallas kernels: 0.22 us -> 4.3 us  [the longest x1 3.85 us: lists(): pl.pallas_call(functools.partial(lists_kernel, limit), out_shape=(pltpu.S...]
    pallas_call x1, Pallas kernels: 5.78 us -> 8.55 us  [prep(): pl.pallas_call(prep_kernel, out_shape=(pltpu.VMEM((rows, slots * size, si...]
    ppermute x8 -> x9, waiting for transfers between devices: 2.56 us -> 1.89 us  [swap(): return lax.ppermute(array, 'rows', pairs)]
  transfers between devices with their start and end apart: 12 -> 13, of which waited for: 7 -> 7; matrix products, arithmetic and copies ran while one was open for 0% -> 0% of each run, Pallas kernels for 16% -> 24%
where the time goes in v2:
time: 89.5 us; the launch traced here: 89.2 us
  starting transfers between devices  36.1 us (40%)
  Pallas kernels  30 us (34%)
  local copies, waits for them, and re-layouts  12.6 us (14%)
  waiting for transfers between devices  9.44 us (11%)
  between operations  0.9 us (1%)
    ppermute x9, starting transfers between devices, swap(): return lax.ppermute(array, 'rows', pairs)  23.3 us
    ppermute x4, starting transfers between devices, body(): lax.ppermute(gram, 'rows', [(i, i ^ distance) for i in range(count)])  12.8 us
    unnamed x14, local copies, waits for them, and re-layouts  12.6 us
    pallas_call x4, Pallas kernels, product(): pl.pallas_call(functools.partial(near_kernel, tile_major), out_shape=shap...  9.24 us
    pallas_call x1, Pallas kernels, prep(): pl.pallas_call(prep_kernel, out_shape=(pltpu.VMEM((rows, slots * size, si...  8.55 us
    ppermute x4, waiting for transfers between devices, body(): lax.ppermute(gram, 'rows', [(i, i ^ distance) for i in range(count)])  7.55 us
    pallas_call x1, Pallas kernels, final(): pl.pallas_call(functools.partial(final_kernel, float(states)), out_shape=...  6.06 us
    pallas_call x1, Pallas kernels, lists(): pl.pallas_call(functools.partial(lists_kernel, limit), out_shape=(pltpu.S...  3.85 us
  transfers between devices with their start and end apart: 13, of which 7 were waited for; matrix products, arithmetic and copies ran while one was open for 0% of the time, Pallas kernels for 24%

profile of v2, /device:TPU:0, one launch (start us, length us, event | category | flops | bytes accessed | tf_op | source)
XLA Modules:
  0.0 89.2 jit_solution(15599737521760779535)
XLA Ops:
  0.0 0.5 collective-permute-start.5
  0.5 0.7 collective-permute-start.4
  1.1 0.7 collective-permute-start.3
  1.8 0.1 pad_add_fusion.where
  1.9 0.0 copy-start.6
  1.9 0.7 copy-done.6
  2.6 0.0 copy-start.4
  2.6 8.5 %prep.1 = (bf16[64,640,128]{2,1,0:T(8,128)(2,1)S(1)}, f32[64,128]{1,0:T(8,128)S(1)}, s32[320]{0:T(512)S(4)}, s32[72]{0:T(128)S(4)}) custom-call(s32[2]{0:T(128)S(1)} %pad_add_fusion.where, s32[5,64]{1,0:T(8,128)S(1)} %bitcast.5, bf16[64,5,128,128]{3,2,1,0:T(8,128)(2,1)} %tiles.1), custom_call_target="tpu_custom_call" | custom-call | flops 167772160 | bytes 20971520 | tf_op jit(solution)/shard_map/prep/pallas_call | solution.py:90
  11.1 0.0 copy-start
  11.2 0.0 collective-permute-done.3.theirs
  11.2 3.8 %lists.1 = (s32[320]{0:T(512)S(4)}, s32[72]{0:T(128)S(4)}, s32[1]{0:T(128)}) custom-call(s32[2]{0:T(128)S(1)} %pad_add_fusion.where, s32[5,64]{1,0:T(8,128)S(1)} %collective-permute-done.3.theirs, s32[320]{0:T(512)S(4)} %get-tuple-element.47.index.refs_0_), custom_call_target="tpu_custom_call" | custom-call | flops 4000000 | bytes 4000 | tf_op jit(solution)/shard_map/lists/pallas_call | solution.py:163
  15.0 0.0 collective-permute-done.5.mate
  15.0 0.0 copy-done.4
  15.0 2.4 %near_rows.4 = (bf16[192,32,128]{2,1,0:T(8,128)(2,1)S(1)}, bf16[64,32,128]{2,1,0:T(8,128)(2,1)S(1)}) custom-call(s32[320]{0:T(512)S(4)} %get-tuple-element.47.index.refs_0_, s32[72]{0:T(128)S(4)} %get-tuple-element.49.order.refs_1_, bf16[64,640,128]{2,1,0:T(8,128)(2,1)S(1)} %get-tuple-element.50.turned.refs_2_, ...), custom_call_target="tpu_custom_call" | custom-call | flops 167772160 | bytes 10485760 | tf_op jit(solution)/shard_map/near_rows/pallas_call | solution.py:254
  17.5 0.0 collective-permute-done.4.refs_5_
  17.5 0.0 copy-done
  17.5 0.2 far_rows.4
  17.7 6.5 %collective-permute-start.7 = (bf16[64,32,128]{2,1,0:T(8,128)(2,1)S(1)}, bf16[64,32,128]{2,1,0:T(8,128)(2,1)S(1)}, u32[]{:S(2)}, u32[]{:S(2)}) collective-permute-start(bf16[64,32,128]{2,1,0:T(8,128)(2,1)S(1)} %get-tuple-element.58.own), channel_id=1, source_target_pairs={{0,1},{1,0},{2,3},{3,2},{4,5},{5,4},{6,7},{7,6},{8,9},{9,8},{10,11... | collective-permute-start | bytes 1572872 | tf_op jit(solution)/shard_map/ppermute | solution.py:415
  24.2 0.7 collective-permute-start.6
  25.5 0.2 collective-permute-done.7.mate
  25.7 0.0 copy-start.1
  25.7 4.0 %copy-done.1 = bf16[64,640,128]{2,1,0:T(8,128)(2,1)S(1)} copy-done((bf16[64,640,128]{2,1,0:T(8,128)(2,1)S(1)}, bf16[64,640,128]{2,1,0:T(8,128)(2,1)}, u32[]{:S(2)}) %copy-start.1) | copy-done | bytes 10485784
  29.7 2.3 %near_rows.5 = (bf16[192,32,128]{2,1,0:T(8,128)(2,1)S(1)}, bf16[64,32,128]{2,1,0:T(8,128)(2,1)S(1)}) custom-call(s32[320]{0:T(512)S(4)} %get-tuple-element.47.index.refs_0_, s32[72]{0:T(128)S(4)} %get-tuple-element.49.order.refs_1_, bf16[64,640,128]{2,1,0:T(8,128)(2,1)S(1)} %copy-done.1, f32[64,128]{1,0:T(8,128)S(1)} %get-tuple-element.51.inverse.refs_3_, ...), custom_call_target="tpu_custom_call" | custom-call | flops 167772160 | bytes 10485760 | tf_op jit(solution)/shard_map/near_rows/pallas_call | solution.py:254
  32.0 0.0 collective-permute-done.6.refs_5_
  32.0 0.1 far_rows.5
  32.1 6.5 %collective-permute-start.9 = (bf16[64,32,128]{2,1,0:T(8,128)(2,1)S(1)}, bf16[64,32,128]{2,1,0:T(8,128)(2,1)S(1)}, u32[]{:S(2)}, u32[]{:S(2)}) collective-permute-start(bf16[64,32,128]{2,1,0:T(8,128)(2,1)S(1)} %get-tuple-element.63.own), channel_id=1, source_target_pairs={{0,1},{1,0},{2,3},{3,2},{4,5},{5,4},{6,7},{7,6},{8,9},{9,8},{10,11... | collective-permute-start | bytes 1572872 | tf_op jit(solution)/shard_map/ppermute | solution.py:415
  38.6 0.7 collective-permute-start.8
  39.3 0.8 collective-permute-done.9.mate
  40.1 0.0 copy-start.2
  40.1 4.0 %copy-done.2 = bf16[64,640,128]{2,1,0:T(8,128)(2,1)S(1)} copy-done((bf16[64,640,128]{2,1,0:T(8,128)(2,1)S(1)}, bf16[64,640,128]{2,1,0:T(8,128)(2,1)}, u32[]{:S(2)}) %copy-start.2) | copy-done | bytes 10485784
  44.1 2.3 %near_rows.6 = (bf16[192,32,128]{2,1,0:T(8,128)(2,1)S(1)}, bf16[64,32,128]{2,1,0:T(8,128)(2,1)S(1)}) custom-call(s32[320]{0:T(512)S(4)} %get-tuple-element.47.index.refs_0_, s32[72]{0:T(128)S(4)} %get-tuple-element.49.order.refs_1_, bf16[64,640,128]{2,1,0:T(8,128)(2,1)S(1)} %copy-done.2, f32[64,128]{1,0:T(8,128)S(1)} %get-tuple-element.51.inverse.refs_3_, ...), custom_call_target="tpu_custom_call" | custom-call | flops 167772160 | bytes 10485760 | tf_op jit(solution)/shard_map/near_rows/pallas_call | solution.py:254
  46.4 0.0 collective-permute-done.8.refs_5_
  46.4 0.1 far_rows.6
  46.5 6.5 %collective-permute-start.11 = (bf16[64,32,128]{2,1,0:T(8,128)(2,1)S(1)}, bf16[64,32,128]{2,1,0:T(8,128)(2,1)S(1)}, u32[]{:S(2)}, u32[]{:S(2)}) collective-permute-start(bf16[64,32,128]{2,1,0:T(8,128)(2,1)S(1)} %get-tuple-element.68.own), channel_id=1, source_target_pairs={{0,1},{1,0},{2,3},{3,2},{4,5},{5,4},{6,7},{7,6},{8,9},{9,8},{10,11... | collective-permute-start | bytes 1572872 | tf_op jit(solution)/shard_map/ppermute | solution.py:415
  53.0 0.7 collective-permute-start.10
  53.7 0.8 collective-permute-done.11.mate
  54.6 0.0 copy-start.3
  54.6 4.0 %copy-done.3 = bf16[64,640,128]{2,1,0:T(8,128)(2,1)S(1)} copy-done((bf16[64,640,128]{2,1,0:T(8,128)(2,1)S(1)}, bf16[64,640,128]{2,1,0:T(8,128)(2,1)}, u32[]{:S(2)}) %copy-start.3) | copy-done | bytes 10485784
  58.5 2.3 %near_rows.7 = (bf16[192,32,128]{2,1,0:T(8,128)(2,1)S(1)}, f32[64,32,128]{2,1,0:T(8,128)S(1)}) custom-call(s32[320]{0:T(512)S(4)} %get-tuple-element.47.index.refs_0_, s32[72]{0:T(128)S(4)} %get-tuple-element.49.order.refs_1_, bf16[64,640,128]{2,1,0:T(8,128)(2,1)S(1)} %copy-done.3, f32[64,128]{1,0:T(8,128)S(1)} %get-tuple-element.51.inverse.refs_3_, ...), custom_call_target="tpu_custom_call" | custom-call | flops 167772160 | bytes 10485760 | tf_op jit(solution)/shard_map/near_rows/pallas_call | solution.py:254
  60.8 0.0 collective-permute-done.10.refs_5_
  60.8 0.0 copy-start.5
  60.9 1.8 %gram.1 = (bf16[64,96,128]{2,1,0:T(8,128)(2,1)S(1)}, f32[32,32]{1,0:T(8,128)S(1)}) custom-call(f32[64,32,128]{2,1,0:T(8,128)S(1)} %get-tuple-element.71.power), custom_call_target="tpu_custom_call" | custom-call | flops 150994944 | bytes 2621440 | tf_op jit(solution)/shard_map/gram/pallas_call | solution.py:329
  62.7 6.5 %collective-permute-start.12 = (f32[32,32]{1,0:T(8,128)S(1)}, f32[32,32]{1,0:T(8,128)S(1)}, u32[]{:S(2)}, u32[]{:S(2)}) collective-permute-start(f32[32,32]{1,0:T(8,128)S(1)} %get-tuple-element.72), channel_id=1, source_target_pairs={{0,1},{1,0},{2,3},{3,2},{4,5},{5,4},{6,7},{7,6},{8,9},{9,8},{10,11... | collective-permute-start | bytes 12296 | tf_op jit(solution)/shard_map/ppermute | solution.py:441
  69.2 0.8 collective-permute-done.12
  70.0 2.7 %collective-permute-start.13 = (f32[32,32]{1,0:T(8,128)S(1)}, f32[32,32]{1,0:T(8,128)S(1)}, u32[]{:S(2)}, u32[]{:S(2)}) collective-permute-start(f32[32,32]{1,0:T(8,128)S(1)} %add.14), channel_id=1, source_target_pairs={{0,2},{1,3},{2,0},{3,1},{4,6},{5,7},{6,4},{7,5},{8,10},{9,11},{10,... | collective-permute-start | bytes 12296 | tf_op jit(solution)/shard_map/ppermute | solution.py:441
  72.7 1.7 %collective-permute-done.13 = f32[32,32]{1,0:T(8,128)S(1)} collective-permute-done((f32[32,32]{1,0:T(8,128)S(1)}, f32[32,32]{1,0:T(8,128)S(1)}, u32[]{:S(2)}, u32[]{:S(2)}) %collective-permute-start.13) | collective-permute-done | bytes 4128 | tf_op jit(solution)/shard_map/ppermute | solution.py:441
  74.5 2.3 %collective-permute-start.14 = (f32[32,32]{1,0:T(8,128)S(1)}, f32[32,32]{1,0:T(8,128)S(1)}, u32[]{:S(2)}, u32[]{:S(2)}) collective-permute-start(f32[32,32]{1,0:T(8,128)S(1)} %add.15), channel_id=1, source_target_pairs={{0,4},{1,5},{2,6},{3,7},{4,0},{5,1},{6,2},{7,3},{8,12},{9,13},{10,... | collective-permute-start | bytes 12296 | tf_op jit(solution)/shard_map/ppermute | solution.py:441
  76.7 1.7 %collective-permute-done.14 = f32[32,32]{1,0:T(8,128)S(1)} collective-permute-done((f32[32,32]{1,0:T(8,128)S(1)}, f32[32,32]{1,0:T(8,128)S(1)}, u32[]{:S(2)}, u32[]{:S(2)}) %collective-permute-start.14) | collective-permute-done | bytes 4128 | tf_op jit(solution)/shard_map/ppermute | solution.py:441
  78.5 1.4 %collective-permute-start.15 = (f32[32,32]{1,0:T(8,128)S(1)}, f32[32,32]{1,0:T(8,128)S(1)}, u32[]{:S(2)}, u32[]{:S(2)}) collective-permute-start(f32[32,32]{1,0:T(8,128)S(1)} %add.16.gram_a), channel_id=1, source_target_pairs={{0,8},{1,9},{2,10},{3,11},{4,12},{5,13},{6,14},{7,15},{8,0},{9,1},... | collective-permute-start | bytes 12296 | tf_op jit(solution)/shard_map/ppermute | solution.py:441
  79.8 3.3 %collective-permute-done.15.gram_b = f32[32,32]{1,0:T(8,128)S(1)} collective-permute-done((f32[32,32]{1,0:T(8,128)S(1)}, f32[32,32]{1,0:T(8,128)S(1)}, u32[]{:S(2)}, u32[]{:S(2)}) %collective-permute-start.15) | collective-permute-done | bytes 4128 | tf_op jit(solution)/shard_map/ppermute | solution.py:441
  83.1 0.0 copy-done.5
  83.1 6.1 %memberships.1 = f32[32,8192]{1,0:T(8,128)} custom-call(f32[32,32]{1,0:T(8,128)S(1)} %add.16.gram_a, f32[32,32]{1,0:T(8,128)S(1)} %collective-permute-done.15.gram_b, f32[32,32]{1,0:T(8,128)S(1)} %copy-done.5, bf16[64,96,128]{2,1,0:T(8,128)(2,1)S(1)} %get-tuple-element.73.parts), custom_call_target="tpu_custom_call" | custom-call | flops 150994944 | bytes 3145728 | tf_op jit(solution)/shard_map/memberships/pallas_call | solution.py:394
  (7 shorter events, 0.1 us)
Async XLA Ops:
  0.0 15.0 %collective-permute-start.5 = (bf16[32,8192]{1,0:T(8,128)(2,1)}, bf16[32,8192]{1,0:T(8,128)(2,1)S(1)}, u32[]{:S(2)}, u32[]{:S(2)}) collective-permute-start(bf16[32,8192]{1,0:T(8,128)(2,1)} %own.1), channel_id=1, source_target_pairs={{0,1},{1,0},{2,3},{3,2},{4,5},{5,4},{6,7},{7,6},{8,9},{9,8},{10,11... | collective-permute-start | bytes 1572872 | tf_op jit(solution)/shard_map/ppermute | solution.py:415
  0.5 17.0 %collective-permute-start.4 = (bf16[32,8192]{1,0:T(8,128)(2,1)}, bf16[32,8192]{1,0:T(8,128)(2,1)S(1)}, u32[]{:S(2)}, u32[]{:S(2)}) collective-permute-start(bf16[32,8192]{1,0:T(8,128)(2,1)} %own.1), channel_id=1, source_target_pairs={{1,2},{2,1},{3,4},{4,3},{5,6},{6,5},{7,8},{8,7},{9,10},{10,9},{11,... | collective-permute-start | bytes 1572872 | tf_op jit(solution)/shard_map/ppermute | solution.py:415
  1.1 10.0 %collective-permute-start.3 = (s32[5,64]{1,0:T(8,128)}, s32[5,64]{1,0:T(8,128)S(1)}, u32[]{:S(2)}, u32[]{:S(2)}) collective-permute-start(s32[5,64]{1,0:T(8,128)} %bitcast.4), channel_id=1, source_target_pairs={{1,2},{2,1},{3,4},{4,3},{5,6},{6,5},{7,8},{8,7},{9,10},{10,9},{11,... | collective-permute-start | bytes 3848 | tf_op jit(solution)/shard_map/ppermute | solution.py:415
  1.9 0.7 copy-start.6
  2.6 12.4 %copy-start.4 = (bf16[32,8192]{1,0:T(8,128)(2,1)S(1)}, bf16[32,8192]{1,0:T(8,128)(2,1)}, u32[]{:S(2)}) copy-start(bf16[32,8192]{1,0:T(8,128)(2,1)} %own.1) | copy-start | bytes 1572868
  11.1 6.3 %copy-start = (bf16[64,640,128]{2,1,0:T(8,128)(2,1)}, bf16[64,640,128]{2,1,0:T(8,128)(2,1)S(1)}, u32[]{:S(2)}) copy-start(bf16[64,640,128]{2,1,0:T(8,128)(2,1)S(1)} %get-tuple-element.50.turned.refs_2_) | copy-start | bytes 31457284
  17.7 8.0 %collective-permute-start.7 = (bf16[64,32,128]{2,1,0:T(8,128)(2,1)S(1)}, bf16[64,32,128]{2,1,0:T(8,128)(2,1)S(1)}, u32[]{:S(2)}, u32[]{:S(2)}) collective-permute-start(bf16[64,32,128]{2,1,0:T(8,128)(2,1)S(1)} %get-tuple-element.58.own), channel_id=1, source_target_pairs={{0,1},{1,0},{2,3},{3,2},{4,5},{5,4},{6,7},{7,6},{8,9},{9,8},{10,11... | collective-permute-start | bytes 1572872 | tf_op jit(solution)/shard_map/ppermute | solution.py:415
  24.2 7.8 %collective-permute-start.6 = (bf16[44,32,128]{2,1,0:T(8,128)(2,1)S(1)}, bf16[44,32,128]{2,1,0:T(8,128)(2,1)S(1)}, u32[]{:S(2)}, u32[]{:S(2)}) collective-permute-start(bf16[44,32,128]{2,1,0:T(8,128)(2,1)S(1)} %get-tuple-element.55), channel_id=1, source_target_pairs={{1,2},{2,1},{3,4},{4,3},{5,6},{6,5},{7,8},{8,7},{9,10},{10,9},{11,... | collective-permute-start | bytes 1081352 | tf_op jit(solution)/shard_map/ppermute | solution.py:415
  25.7 4.0 %copy-start.1 = (bf16[64,640,128]{2,1,0:T(8,128)(2,1)S(1)}, bf16[64,640,128]{2,1,0:T(8,128)(2,1)}, u32[]{:S(2)}) copy-start(bf16[64,640,128]{2,1,0:T(8,128)(2,1)} %copy-done) | copy-start | bytes 31457284
  32.1 8.0 %collective-permute-start.9 = (bf16[64,32,128]{2,1,0:T(8,128)(2,1)S(1)}, bf16[64,32,128]{2,1,0:T(8,128)(2,1)S(1)}, u32[]{:S(2)}, u32[]{:S(2)}) collective-permute-start(bf16[64,32,128]{2,1,0:T(8,128)(2,1)S(1)} %get-tuple-element.63.own), channel_id=1, source_target_pairs={{0,1},{1,0},{2,3},{3,2},{4,5},{5,4},{6,7},{7,6},{8,9},{9,8},{10,11... | collective-permute-start | bytes 1572872 | tf_op jit(solution)/shard_map/ppermute | solution.py:415
  38.6 7.8 %collective-permute-start.8 = (bf16[44,32,128]{2,1,0:T(8,128)(2,1)S(1)}, bf16[44,32,128]{2,1,0:T(8,128)(2,1)S(1)}, u32[]{:S(2)}, u32[]{:S(2)}) collective-permute-start(bf16[44,32,128]{2,1,0:T(8,128)(2,1)S(1)} %get-tuple-element.61), channel_id=1, source_target_pairs={{1,2},{2,1},{3,4},{4,3},{5,6},{6,5},{7,8},{8,7},{9,10},{10,9},{11,... | collective-permute-start | bytes 1081352 | tf_op jit(solution)/shard_map/ppermute | solution.py:415
  40.1 4.0 %copy-start.2 = (bf16[64,640,128]{2,1,0:T(8,128)(2,1)S(1)}, bf16[64,640,128]{2,1,0:T(8,128)(2,1)}, u32[]{:S(2)}) copy-start(bf16[64,640,128]{2,1,0:T(8,128)(2,1)} %copy-done) | copy-start | bytes 31457284
  46.5 8.1 %collective-permute-start.11 = (bf16[64,32,128]{2,1,0:T(8,128)(2,1)S(1)}, bf16[64,32,128]{2,1,0:T(8,128)(2,1)S(1)}, u32[]{:S(2)}, u32[]{:S(2)}) collective-permute-start(bf16[64,32,128]{2,1,0:T(8,128)(2,1)S(1)} %get-tuple-element.68.own), channel_id=1, source_target_pairs={{0,1},{1,0},{2,3},{3,2},{4,5},{5,4},{6,7},{7,6},{8,9},{9,8},{10,11... | collective-permute-start | bytes 1572872 | tf_op jit(solution)/shard_map/ppermute | solution.py:415
  53.0 7.8 %collective-permute-start.10 = (bf16[44,32,128]{2,1,0:T(8,128)(2,1)S(1)}, bf16[44,32,128]{2,1,0:T(8,128)(2,1)S(1)}, u32[]{:S(2)}, u32[]{:S(2)}) collective-permute-start(bf16[44,32,128]{2,1,0:T(8,128)(2,1)S(1)} %get-tuple-element.66), channel_id=1, source_target_pairs={{1,2},{2,1},{3,4},{4,3},{5,6},{6,5},{7,8},{8,7},{9,10},{10,9},{11,... | collective-permute-start | bytes 1081352 | tf_op jit(solution)/shard_map/ppermute | solution.py:415
  54.6 4.0 %copy-start.3 = (bf16[64,640,128]{2,1,0:T(8,128)(2,1)S(1)}, bf16[64,640,128]{2,1,0:T(8,128)(2,1)}, u32[]{:S(2)}) copy-start(bf16[64,640,128]{2,1,0:T(8,128)(2,1)} %copy-done) | copy-start | bytes 31457284
  60.8 22.3 %copy-start.5 = (f32[32,32]{1,0:T(8,128)S(1)}, f32[32,32]{1,0:T(8,128)}, u32[]{:S(2)}) copy-start(f32[32,32]{1,0:T(8,128)} %mapping.1) | copy-start | bytes 12292
  62.7 7.3 %collective-permute-start.12 = (f32[32,32]{1,0:T(8,128)S(1)}, f32[32,32]{1,0:T(8,128)S(1)}, u32[]{:S(2)}, u32[]{:S(2)}) collective-permute-start(f32[32,32]{1,0:T(8,128)S(1)} %get-tuple-element.72), channel_id=1, source_target_pairs={{0,1},{1,0},{2,3},{3,2},{4,5},{5,4},{6,7},{7,6},{8,9},{9,8},{10,11... | collective-permute-start | bytes 12296 | tf_op jit(solution)/shard_map/ppermute | solution.py:441
  70.0 4.4 %collective-permute-start.13 = (f32[32,32]{1,0:T(8,128)S(1)}, f32[32,32]{1,0:T(8,128)S(1)}, u32[]{:S(2)}, u32[]{:S(2)}) collective-permute-start(f32[32,32]{1,0:T(8,128)S(1)} %add.14), channel_id=1, source_target_pairs={{0,2},{1,3},{2,0},{3,1},{4,6},{5,7},{6,4},{7,5},{8,10},{9,11},{10,... | collective-permute-start | bytes 12296 | tf_op jit(solution)/shard_map/ppermute | solution.py:441
  74.5 4.0 %collective-permute-start.14 = (f32[32,32]{1,0:T(8,128)S(1)}, f32[32,32]{1,0:T(8,128)S(1)}, u32[]{:S(2)}, u32[]{:S(2)}) collective-permute-start(f32[32,32]{1,0:T(8,128)S(1)} %add.15), channel_id=1, source_target_pairs={{0,4},{1,5},{2,6},{3,7},{4,0},{5,1},{6,2},{7,3},{8,12},{9,13},{10,... | collective-permute-start | bytes 12296 | tf_op jit(solution)/shard_map/ppermute | solution.py:441
  78.5 4.6 %collective-permute-start.15 = (f32[32,32]{1,0:T(8,128)S(1)}, f32[32,32]{1,0:T(8,128)S(1)}, u32[]{:S(2)}, u32[]{:S(2)}) collective-permute-start(f32[32,32]{1,0:T(8,128)S(1)} %add.16.gram_a), channel_id=1, source_target_pairs={{0,8},{1,9},{2,10},{3,11},{4,12},{5,13},{6,14},{7,15},{8,0},{9,1},... | collective-permute-start | bytes 12296 | tf_op jit(solution)/shard_map/ppermute | solution.py:441

commit v3 on v0

v3 whole, which is shorter than its diff:
```python
import functools

import jax
import jax.numpy as jnp
from jax import lax
from jax.experimental import pallas as pl
from jax.experimental.pallas import tpu as pltpu
from jax.sharding import PartitionSpec as P

PRODUCTS = 4
BLOCK = 16
CHUNK = 8
F32 = jnp.float32
BF16 = jnp.bfloat16
I32 = jnp.int32
NN = (((1,), (0,)), ((), ()))
NT = (((1,), (1,)), ((), ()))
VM = pl.BlockSpec(memory_space=pltpu.VMEM)
SM = pl.BlockSpec(memory_space=pltpu.SMEM)
HB = pl.BlockSpec(memory_space=pltpu.HBM)


def in_vmem(array):
    return pltpu.with_memory_space_constraint(array, pltpu.VMEM)


def cost(flops, moved):
    return pl.CostEstimate(flops=flops, bytes_accessed=moved, transcendentals=0)


def params(mib):
    return pltpu.CompilerParams(vmem_limit_bytes=mib * 2**20)


def prep_kernel(tiles, turned, inverse, landing, arrived):
    rows, slots, size, _ = tiles.shape
    chunks = rows // CHUNK
    ones = jnp.ones((16, slots * size), BF16)

    def copy(i):
        part = pl.ds(i * CHUNK, CHUNK)
        return pltpu.make_async_copy(tiles.at[part], landing.at[part], arrived.at[i])

    for i in range(chunks):
        copy(i).start()

    def step(i, carry):
        copy(i).wait()
        for u in range(CHUNK):
            r = i * CHUNK + u
            for s in range(slots):
                turned[r, pl.ds(s * size, size), :] = landing[r, s].T
            total = lax.dot_general(ones, turned[r], NN, preferred_element_type=F32)
            inverse[pl.ds(r, 1), :] = 1.0 / total[0:1]
        return carry

    lax.fori_loop(0, chunks, step, 0)


def prep(tiles):
    rows, slots, size, _ = tiles.shape
    return pl.pallas_call(
        prep_kernel,
        out_shape=(
            pltpu.VMEM((rows, slots * size, size), BF16),
            pltpu.VMEM((rows, size), F32),
        ),
        in_specs=[HB],
        out_specs=(VM, VM),
        scratch_shapes=[
            pltpu.VMEM(tiles.shape, BF16),
            pltpu.SemaphoreType.DMA((rows // CHUNK,)),
        ],
        compiler_params=params(14),
        cost_estimate=cost(2 * tiles.size * 16, 4 * tiles.size),
        name="prep",
    )(pltpu.with_memory_space_constraint(tiles, pltpu.HBM))


def ranks(named):
    rows = named.shape[0]
    h = lax.broadcasted_iota(I32, (rows, rows), 0)
    other = lax.broadcasted_iota(I32, (rows, rows), 1)
    before = jnp.where(other < h, 1.0, 0.0).astype(BF16)
    ones = jnp.ones((rows, rows), BF16)
    total = lax.dot_general(named.astype(BF16), ones, NN, preferred_element_type=F32)
    mark = jnp.where(total > 0.5, 1.0, 0.0)
    rank = lax.dot_general(before, mark.astype(BF16), NN, preferred_element_type=F32)
    return mark, rank


def plan_kernel(where, columns, plan, draft, done):
    slots, rows = columns.shape
    first, parity = where[0], where[1]
    low = jnp.where(parity == 0, 2 * rows, rows)
    high = jnp.where(parity == 0, rows, 2 * rows)
    offset = columns[...] - first
    spot = jnp.where(
        offset < 0,
        offset + (rows + low),
        jnp.where(offset >= rows, offset + (high - rows), offset),
    )
    h = lax.broadcasted_iota(I32, (rows, rows), 0)
    lane = lax.broadcasted_iota(I32, (rows, rows), 1)
    equal = [
        jnp.where(spot[s : s + 1] - 2 * rows == h, 1.0, 0.0) for s in range(slots)
    ]
    named = functools.reduce(jnp.add, equal)
    mark, rank = ranks(named)
    draft[0:slots, 0:rows] = spot
    for s in range(slots):
        place = jnp.sum(equal[s] * rank, axis=0, keepdims=True).astype(I32)
        line = spot[s : s + 1]
        draft[slots + s : slots + s + 1, 0:rows] = jnp.where(
            line >= 2 * rows, 2 * rows + place, line
        )
    far = jnp.where(jnp.sum(named, axis=0, keepdims=True) > 0.5, 1.0, 0.0)
    far = jnp.broadcast_to(far, (16, rows))
    before = jnp.where(h < lane, 1.0, 0.0).astype(BF16)
    far_before = lax.dot_general(far.astype(BF16), before, NN, preferred_element_type=F32)
    line = lax.broadcasted_iota(I32, (16, rows), 1).astype(F32)
    position = jnp.where(far > 0.5, rows - 1 - far_before, line - far_before)
    taken = jnp.where(position[0:1].astype(I32) == h, 1.0, 0.0).astype(BF16)
    order = lax.dot_general(line.astype(BF16), taken, NT, preferred_element_type=F32)
    ones = jnp.ones((rows, rows), BF16)
    near = lax.dot_general((1.0 - far).astype(BF16), ones, NN, preferred_element_type=F32)
    base = 2 * slots
    draft[base : base + 1, 0:rows] = order[0:1].astype(I32)
    draft[base + 1 : base + 2, 0:rows] = near[0:1].astype(I32)
    draft[base + 2 : base + 3, 0:rows] = jnp.sum(mark, axis=0, keepdims=True).astype(I32)
    copy = pltpu.make_async_copy(draft, plan, done)
    copy.start()
    copy.wait()


def make_plan(where, columns):
    slots, _ = columns.shape
    height = (2 * slots + 3 + 7) // 8 * 8
    return pl.pallas_call(
        plan_kernel,
        out_shape=pltpu.SMEM((height, 128), I32),
        in_specs=[SM, VM],
        out_specs=SM,
        scratch_shapes=[pltpu.VMEM((height, 128), I32), pltpu.SemaphoreType.DMA],
        compiler_params=params(2),
        cost_estimate=cost(1000000, 4000),
        name="plan",
    )(where, columns)


def fill(window, start, panel, tile_major):
    size = window.shape[2]
    if tile_major:
        window[start : start + panel.shape[0]] = panel[...]
    else:
        for t in range(panel.shape[1] // size):
            window[start + t] = panel[:, t * size : (t + 1) * size]


def row_block(start, base, plan, turned, inverse, window):
    slots = turned.shape[1] // turned.shape[2]
    picked = [plan[2 * slots, start + u] for u in range(BLOCK)]
    vectors = [
        jnp.concatenate([window[plan[base + s, r]] for s in range(slots)], axis=1)
        for r in picked
    ]
    sums = [
        lax.dot_general(x, turned[r], NN, preferred_element_type=F32)
        for x, r in zip(vectors, picked)
    ]
    return picked, [y * inverse[pl.ds(r, 1), :] for r, y in zip(picked, sums)]


def thirds(x):
    high = x.astype(BF16)
    rest = x - high.astype(F32)
    middle = rest.astype(BF16)
    low = (rest - middle.astype(F32)).astype(BF16)
    return high, middle, low


def fold(squares, vectors):
    total = None
    for a, b in ((2, 2), (1, 2), (2, 1), (0, 2), (2, 0), (1, 1), (0, 1), (1, 0), (0, 0)):
        part = squares[a * vectors : (a + 1) * vectors, b * vectors : (b + 1) * vectors]
        total = part if total is None else total + part
    return total


def run_rows(near_side, base, plan, turned, inverse, window, image, squares):
    rows = turned.shape[0]
    slots = turned.shape[1] // turned.shape[2]
    near = plan[2 * slots + 1, 0]
    count = near if near_side else rows - near

    def step(block, total):
        start = block * BLOCK if near_side else rows - (block + 1) * BLOCK
        picked, results = row_block(start, base, plan, turned, inverse, window)
        if squares is None:
            for r, y in zip(picked, results):
                image[r] = y.astype(BF16)
            return total
        counted = []
        for u, (r, y) in enumerate(zip(picked, results)):
            stacked = jnp.concatenate(thirds(y), axis=0)
            image[r] = stacked
            mine = start + u < near if near_side else start + u >= near
            counted.append(jnp.where(mine, stacked, jnp.zeros_like(stacked)))
        wide = jnp.concatenate(counted, axis=1)
        return total + lax.dot_general(wide, wide, NT, preferred_element_type=F32)

    begin = jnp.int32(0) if squares is None else squares
    return lax.fori_loop(0, (count + BLOCK - 1) // BLOCK, step, begin)


def near_kernel(tile_major, last, plan, turned, inverse, own, mate, window, image, *gram):
    rows, depth, size = turned.shape
    fill(window, 0, own, tile_major)
    fill(window, rows, mate, tile_major)
    zero = jnp.zeros(gram[0].shape, F32) if last else None
    total = run_rows(True, 0, plan, turned, inverse, window, image, zero)
    if last:
        gram[0][...] = total


def far_first_kernel(
    limit, where, theirs, plan, turned, inverse, other, w_in, i_in,
    window, image, send, rest, sending, more, draft, done,
):
    slots, rows = theirs.shape
    offset = theirs[...] - where[0]
    h = lax.broadcasted_iota(I32, (rows, rows), 0)
    lane = lax.broadcasted_iota(I32, (rows, rows), 1)
    named = functools.reduce(
        jnp.add,
        [jnp.where(offset[s : s + 1] == h, 1.0, 0.0) for s in range(slots)],
    )
    mark, rank = ranks(named)
    here = jnp.where((mark > 0.5) & (rank.astype(I32) == lane), h, 0)
    draft[0:1, 0:rows] = jnp.sum(here.astype(F32), axis=0, keepdims=True).astype(I32)
    sent = jnp.sum(mark, axis=0, keepdims=True).astype(I32)
    read = plan[2 * slots + 2, 0]
    draft[1:2, 0:rows] = jnp.where(jnp.maximum(sent, read) > limit, 1, 0)
    copy = pltpu.make_async_copy(draft, sending, done)
    copy.start()
    fill(window, 2 * rows, other, False)
    run_rows(False, 0, plan, turned, inverse, window, image, None)
    copy.wait()
    more[0] = sending[1, 0]
    pack(image, sending, send, rest)


def pack(image, sending, send, rest):
    limit = send.shape[0]
    for k in range(image.shape[0]):
        target = send.at[k] if k < limit else rest.at[k - limit]
        target[...] = image[sending[0, k]]


def far_kernel(plan, turned, inverse, sending, other, extra, w_in, i_in, window, image, send, rest):
    rows, depth, size = turned.shape
    limit = other.shape[0]
    fill(window, 2 * rows, other, True)
    fill(window, 2 * rows + limit, extra, True)
    run_rows(False, depth // size, plan, turned, inverse, window, image, None)
    pack(image, sending, send, rest)


def far_last_kernel(plan, turned, inverse, other, extra, near, w_in, i_in, window, image, gram):
    rows, depth, size = turned.shape
    limit = other.shape[0]
    fill(window, 2 * rows, other, True)
    fill(window, 2 * rows + limit, extra, True)
    total = run_rows(
        False, depth // size, plan, turned, inverse, window, image, near[...]
    )
    gram[...] = fold(total, gram.shape[0])


def near_rows(plan, turned, inverse, own, mate, tile_major, last):
    rows, depth, size = turned.shape
    vectors = own.shape[1 if tile_major else 0]
    height = 3 * vectors if last else vectors
    shapes = (
        pltpu.VMEM((3 * rows, vectors, size), BF16),
        pltpu.VMEM((rows, height, size), BF16),
    )
    if last:
        shapes += (pltpu.VMEM((height, height), F32),)
    return pl.pallas_call(
        functools.partial(near_kernel, tile_major, last),
        out_shape=shapes,
        in_specs=[SM, VM, VM, VM, VM],
        out_specs=(VM,) * len(shapes),
        compiler_params=params(4),
        cost_estimate=cost(rows * depth * size * vectors, 2 * rows * depth * size),
        name="near_rows",
    )(plan, *map(in_vmem, (turned, inverse, own, mate)))


def far_call(kernel, ins, in_specs, alias, outs, out_specs, turned, scratch=()):
    rows, depth, size = turned.shape
    return pl.pallas_call(
        kernel,
        out_shape=outs,
        in_specs=in_specs,
        out_specs=out_specs,
        scratch_shapes=scratch,
        input_output_aliases={alias: 0, alias + 1: 1},
        compiler_params=params(4),
        cost_estimate=cost(32 * rows * depth * size, 2 * rows * depth * size),
        name="far_rows",
    )(*ins)


def of(array):
    return pltpu.VMEM(array.shape, array.dtype)


def far_rows_first(limit, where, theirs, plan, turned, inverse, other, window, image):
    rows, vectors, size = image.shape
    return far_call(
        functools.partial(far_first_kernel, limit),
        (where, theirs, plan, *map(in_vmem, (turned, inverse, other, window, image))),
        [SM, VM, SM] + [VM] * 5,
        6,
        (
            of(window),
            of(image),
            pltpu.VMEM((limit, vectors, size), BF16),
            pltpu.VMEM((rows - limit, vectors, size), BF16),
            pltpu.SMEM((8, 128), I32),
            jax.ShapeDtypeStruct((1,), I32),
        ),
        (VM, VM, VM, VM, SM, SM),
        turned,
        [pltpu.VMEM((8, 128), I32), pltpu.SemaphoreType.DMA],
    )[1:]


def far_rows(plan, turned, inverse, sending, other, extra, window, image):
    return far_call(
        far_kernel,
        (
            plan,
            in_vmem(turned),
            in_vmem(inverse),
            sending,
            *map(in_vmem, (other, extra, window, image)),
        ),
        [SM, VM, VM, SM] + [VM] * 4,
        6,
        (of(window), of(image), of(other), of(extra)),
        (VM,) * 4,
        turned,
    )[1:]


def far_rows_last(plan, turned, inverse, other, extra, near, window, image):
    vectors = near.shape[0] // 3
    return far_call(
        far_last_kernel,
        (plan, *map(in_vmem, (turned, inverse, other, extra, near, window, image))),
        [SM] + [VM] * 7,
        6,
        (of(window), of(image), pltpu.VMEM((vectors, vectors), F32)),
        (VM,) * 3,
        turned,
    )[1:]


def inverse_factor(gram):
    count = gram.shape[0]
    step = 8
    row = lax.broadcasted_iota(I32, (count, count), 0)
    column = lax.broadcasted_iota(I32, (count, count), 1)
    work = jnp.concatenate([gram, jnp.where(row == column, 1.0, 0.0)], axis=1)
    below = lax.broadcasted_iota(I32, work.shape, 0)
    for begin in range(0, count, step):
        spread = [
            jnp.broadcast_to(work[:, k : k + 1], work.shape)
            for k in range(begin, begin + step)
        ]
        for j in range(step):
            k = begin + j
            factor = jnp.where(below > k, spread[j], 0.0)
            pivot = 1.0 / spread[j][k : k + 1]
            for q in range(j + 1, step):
                spread[q] = spread[q] - factor * (spread[q][k : k + 1] * pivot)
            work = work - factor * (work[k : k + 1] * pivot)
    pivots = jnp.sum(
        jnp.where(row == column, work[:, :count], 0.0), axis=1, keepdims=True
    )
    return work[:, count:] * lax.rsqrt(pivots)


def final_kernel(states, gram_a, gram_b, mapping, parts, out, ready, sent):
    rows, depth, size = parts.shape
    vectors = depth // 3
    factor = inverse_factor((gram_a[...] + gram_b[...]) / states)
    combined = lax.dot_general(
        mapping[...],
        factor,
        (((0,), (0,)), ((), ())),
        precision=lax.Precision.HIGHEST,
        preferred_element_type=F32,
    )
    high, middle, low = thirds(combined)
    blank = jnp.zeros_like(high)
    left = jnp.concatenate(
        [
            jnp.concatenate([high, high, high], axis=1),
            jnp.concatenate([middle, middle, blank], axis=1),
            jnp.concatenate([low, blank, blank], axis=1),
        ],
        axis=0,
    )
    copies = []
    for g in range(rows // CHUNK):
        for r in range(g * CHUNK, (g + 1) * CHUNK):
            y = lax.dot_general(left, parts[r], NN, preferred_element_type=F32)
            ready[:, r * size : (r + 1) * size] = (
                y[2 * vectors :] + y[vectors : 2 * vectors]
            ) + y[:vectors]
        part = pl.ds(g * CHUNK * size, CHUNK * size)
        copies.append(pltpu.make_async_copy(ready.at[:, part], out.at[:, part], sent.at[g]))
        copies[-1].start()
    for copy in copies:
        copy.wait()


def final(states, gram_a, gram_b, mapping, parts):
    rows, depth, size = parts.shape
    vectors = depth // 3
    return pl.pallas_call(
        functools.partial(final_kernel, float(states)),
        out_shape=jax.ShapeDtypeStruct((vectors, rows * size), F32),
        in_specs=[VM, VM, VM, VM],
        out_specs=HB,
        scratch_shapes=[
            pltpu.VMEM((vectors, rows * size), F32),
            pltpu.SemaphoreType.DMA((rows // CHUNK,)),
        ],
        compiler_params=params(8),
        cost_estimate=cost(6 * parts.size * vectors, 4 * parts.size),
        name="memberships",
    )(gram_a, gram_b, mapping, in_vmem(parts))


def body(transition_tiles, column_tiles, schur_basis, membership_map):
    rows = transition_tiles.shape[0]
    count = lax.axis_size("rows")
    me = lax.axis_index("rows")
    mates = [(i, i ^ 1) for i in range(count)]
    others = []
    for i in range(1, count - 1, 2):
        others += [(i, i + 1), (i + 1, i)]

    def swap(array, pairs):
        return lax.ppermute(array, "rows", pairs)

    limit = 11 * rows // 16
    where = jnp.stack([me * rows, me % 2]).astype(I32)
    columns = column_tiles.T
    mate, other = swap(schur_basis, mates), swap(schur_basis, others)
    theirs = swap(columns, others)
    plan = make_plan(where, columns)
    turned, inverse = prep(transition_tiles)
    window, image = near_rows(plan, turned, inverse, schur_basis, mate, False, False)
    image, send, rest, sending, more = far_rows_first(
        limit, where, theirs, plan, turned, inverse, other, window, image
    )
    for step in range(1, PRODUCTS):
        last = step == PRODUCTS - 1
        mate, other = swap(image, mates), swap(send, others)
        extra = lax.cond(more[0] > 0, lambda x: swap(x, others), lambda x: x, rest)
        window, image, *near = near_rows(plan, turned, inverse, image, mate, True, last)
        if last:
            parts, gram = far_rows_last(
                plan, turned, inverse, other, extra, near[0], window, image
            )
        else:
            image, send, rest = far_rows(
                plan, turned, inverse, sending, other, extra, window, image
            )
    distance = 1
    while distance < count:
        partner = swap(gram, [(i, i ^ distance) for i in range(count)])
        distance *= 2
        if distance < count:
            gram = gram + partner
    states = schur_basis.shape[1] * count
    return final(states, gram, partner, membership_map, parts)


def solution(mesh):
    return jax.shard_map(
        body,
        mesh=mesh,
        in_specs=(
            P(("groups", "rows"), None, None, None),
            P(("groups", "rows"), None),
            P(None, ("groups", "rows")),
            P("groups", None),
        ),
        out_specs=P(None, ("groups", "rows")),
        check_vma=False,
    )
```

time: 184 us -> 84.4 us (0.46)
  blocking collectives: 71.9 us -> 0 us
  matrix products: 38.6 us -> 0 us
  Pallas kernels: 0 us -> 23.3 us
  other arithmetic: 15.4 us -> 0.09 us
  waiting for transfers between devices: 4.26 us -> 8.26 us
  starting transfers between devices: 40.1 us -> 37.3 us
    psum x1 -> x0, blocking collectives: 71.9 us -> none  [body(): gram_total = lax.psum(gram_local, 'rows')]
    dot_general x7 -> x0, matrix products: 37.5 us -> none  [the longest x4 33.9 us: tile_product(): jnp.einsum('rsij,vrsj->vri', transition_tiles, picked, preferred_element_...]
    pallas_call x0 -> x11, Pallas kernels: none -> 23.3 us  [the longest x4 10.1 us: near_rows(): pl.pallas_call(functools.partial(near_kernel, tile_major, last), out_shap...]
    unnamed x6 -> x14, local copies, waits for them, and re-layouts: 0.03 us -> 14.1 us
    gather x4 -> x0, local copies, waits for them, and re-layouts: 12.1 us -> none  [tile_product(): picked = jnp.take(blocks, local_index, axis=1)]
    another operation x5 -> x1, other arithmetic: 6.68 us -> 0.08 us  [body(): where = jnp.stack([me * rows, me % 2]).astype(I32)]
    reduce_sum x1 -> x0, other arithmetic: 6.58 us -> none  [body(): jnp.einsum('rsij,j->ri', transition_tiles, unit_vector, preferred_element...]
    ppermute x8 -> x13, waiting for transfers between devices: 4.26 us -> 8.26 us  [swap(): return lax.ppermute(array, 'rows', pairs)]
  transfers between devices with their start and end apart: 8 -> 13, of which waited for: 3 -> 7; matrix products, arithmetic and copies ran while one was open for 4% -> 0% of each run, Pallas kernels for 0% -> 22%
where the time goes in v3:
time: 84.4 us; the launch traced here: 84 us
  starting transfers between devices  37.3 us (44%)
  Pallas kernels  23.3 us (28%)
  local copies, waits for them, and re-layouts  14.1 us (17%)
  waiting for transfers between devices  8.26 us (10%)
  between operations  0.89 us (1%)
    ppermute x13, starting transfers between devices, swap(): return lax.ppermute(array, 'rows', pairs)  37.3 us
    unnamed x14, local copies, waits for them, and re-layouts  14.1 us
    pallas_call x4, Pallas kernels, near_rows(): pl.pallas_call(functools.partial(near_kernel, tile_major, last), out_shap...  10.1 us
    ppermute x13, waiting for transfers between devices, swap(): return lax.ppermute(array, 'rows', pairs)  8.26 us
    pallas_call x1, Pallas kernels, prep(): pl.pallas_call(prep_kernel, out_shape=(pltpu.VMEM((rows, slots * size, si...  6.64 us
    pallas_call x1, Pallas kernels, final(): pl.pallas_call(functools.partial(final_kernel, float(states)), out_shape=...  2.65 us
    pallas_call x4, Pallas kernels, far_call(): pl.pallas_call(kernel, out_shape=outs, in_specs=in_specs, out_specs=out_s...  2.43 us
  transfers between devices with their start and end apart: 13, of which 7 were waited for; matrix products, arithmetic and copies ran while one was open for 0% of the time, Pallas kernels for 22%

profile of v3, /device:TPU:0, one launch (start us, length us, event | category | flops | bytes accessed | tf_op | source)
XLA Modules:
  0.0 84.0 jit_solution(16275024318587833463)
XLA Ops:
  0.0 0.5 collective-permute-start.5
  0.5 0.7 collective-permute-start.4
  1.1 0.7 collective-permute-start.3
  1.8 0.1 pad_add_fusion.where
  1.9 0.0 copy-start.6
  1.9 0.7 copy-done.6
  2.6 1.5 %plan.1 = s32[16,128]{1,0:T(8,128)S(4)} custom-call(s32[2]{0:T(128)S(1)} %pad_add_fusion.where, s32[5,64]{1,0:T(8,128)S(1)} %bitcast.5), custom_call_target="tpu_custom_call" | custom-call | flops 1000000 | bytes 4000 | tf_op jit(solution)/shard_map/plan/pallas_call | solution.py:139
  4.1 0.0 copy-start.4
  4.1 6.6 %prep.1 = (bf16[64,640,128]{2,1,0:T(8,128)(2,1)S(1)}, f32[64,128]{1,0:T(8,128)S(1)}) custom-call(bf16[64,5,128,128]{3,2,1,0:T(8,128)(2,1)} %tiles.1), custom_call_target="tpu_custom_call" | custom-call | flops 167772160 | bytes 20971520 | tf_op jit(solution)/shard_map/prep/pallas_call | solution.py:62
  10.8 0.0 copy-start
  10.8 0.0 collective-permute-done.5.mate
  10.8 0.0 copy-done.4
  10.8 2.4 %near_rows.4 = (bf16[192,32,128]{2,1,0:T(8,128)(2,1)S(1)}, bf16[64,32,128]{2,1,0:T(8,128)(2,1)S(1)}) custom-call(s32[16,128]{1,0:T(8,128)S(4)} %plan.1, bf16[64,640,128]{2,1,0:T(8,128)(2,1)S(1)} %get-tuple-element.44.turned, f32[64,128]{1,0:T(8,128)S(1)} %get-tuple-element.45.inverse, bf16[32,8192]{1,0:T(8,128)(2,1)S(1)} %copy-done.4, ...), custom_call_target="tpu_custom_call" | custom-call | flops 167772160 | bytes 10485760 | tf_op jit(solution)/shard_map/near_rows/pallas_call | solution.py:290
  13.3 0.0 collective-permute-done.3.theirs
  13.3 0.0 collective-permute-done.4.other
  13.3 1.5 %copy-done = bf16[64,640,128]{2,1,0:T(8,128)(2,1)} copy-done((bf16[64,640,128]{2,1,0:T(8,128)(2,1)}, bf16[64,640,128]{2,1,0:T(8,128)(2,1)S(1)}, u32[]{:S(2)}) %copy-start) | copy-done | bytes 10485784
  14.8 2.0 %far_rows.4 = (bf16[192,32,128]{2,1,0:T(8,128)(2,1)S(1)}, bf16[64,32,128]{2,1,0:T(8,128)(2,1)S(1)}, bf16[44,32,128]{2,1,0:T(8,128)(2,1)S(1)}, bf16[20,32,128]{2,...) custom-call(s32[2]{0:T(128)S(1)} %pad_add_fusion.where, ...), custom_call_target="tpu_custom_call", output_to_operand_aliasing={{0}: (6, {}), {1}: (7, {})} | custom-call | flops 167772160 | bytes 10485760 | tf_op jit(solution)/shard_map/far_rows/pallas_call | solution.py:303
  16.8 6.3 %collective-permute-start.7 = (bf16[64,32,128]{2,1,0:T(8,128)(2,1)S(1)}, bf16[64,32,128]{2,1,0:T(8,128)(2,1)S(1)}, u32[]{:S(2)}, u32[]{:S(2)}) collective-permute-start(bf16[64,32,128]{2,1,0:T(8,128)(2,1)S(1)} %get-tuple-element.52.own), channel_id=1, source_target_pairs={{0,1},{1,0},{2,3},{3,2},{4,5},{5,4},{6,7},{7,6},{8,9},{9,8},{10,11... | collective-permute-start | bytes 1572872 | tf_op jit(solution)/shard_map/ppermute | solution.py:460
  23.1 0.7 collective-permute-start.6
  24.4 0.2 collective-permute-done.7.mate
  24.6 0.0 copy-start.1
  24.6 4.0 %copy-done.1 = bf16[64,640,128]{2,1,0:T(8,128)(2,1)S(1)} copy-done((bf16[64,640,128]{2,1,0:T(8,128)(2,1)S(1)}, bf16[64,640,128]{2,1,0:T(8,128)(2,1)}, u32[]{:S(2)}) %copy-start.1) | copy-done | bytes 10485784
  28.6 2.3 %near_rows.5 = (bf16[192,32,128]{2,1,0:T(8,128)(2,1)S(1)}, bf16[64,32,128]{2,1,0:T(8,128)(2,1)S(1)}) custom-call(s32[16,128]{1,0:T(8,128)S(4)} %plan.1, bf16[64,640,128]{2,1,0:T(8,128)(2,1)S(1)} %copy-done.1, f32[64,128]{1,0:T(8,128)S(1)} %get-tuple-element.45.inverse, bf16[64,32,128]{2,1,0:T(8,128)(2,1)S(1)} %get-tuple-element.52.own, ...), custom_call_target="tpu_custom_call" | custom-call | flops 167772160 | bytes 10485760 | tf_op jit(solution)/shard_map/near_rows/pallas_call | solution.py:290
  30.9 0.0 collective-permute-done.6.other
  30.9 0.1 far_rows.5
  31.0 7.2 %collective-permute-start.9 = (bf16[64,32,128]{2,1,0:T(8,128)(2,1)S(1)}, bf16[64,32,128]{2,1,0:T(8,128)(2,1)S(1)}, u32[]{:S(2)}, u32[]{:S(2)}) collective-permute-start(bf16[64,32,128]{2,1,0:T(8,128)(2,1)S(1)} %get-tuple-element.57.own), channel_id=1, source_target_pairs={{0,1},{1,0},{2,3},{3,2},{4,5},{5,4},{6,7},{7,6},{8,9},{9,8},{10,11... | collective-permute-start | bytes 1572872 | tf_op jit(solution)/shard_map/ppermute | solution.py:460
  38.2 0.7 collective-permute-start.8
  38.9 0.8 %collective-permute-done.9.mate = bf16[64,32,128]{2,1,0:T(8,128)(2,1)S(1)} collective-permute-done((bf16[64,32,128]{2,1,0:T(8,128)(2,1)S(1)}, bf16[64,32,128]{2,1,0:T(8,128)(2,1)S(1)}, u32[]{:S(2)}, u32[]{:S(2)}) %collective-permute-start.9) | collective-permute-done | bytes 524320 | tf_op jit(solution)/shard_map/ppermute | solution.py:460
  39.7 0.0 copy-start.2
  39.7 4.0 %copy-done.2 = bf16[64,640,128]{2,1,0:T(8,128)(2,1)S(1)} copy-done((bf16[64,640,128]{2,1,0:T(8,128)(2,1)S(1)}, bf16[64,640,128]{2,1,0:T(8,128)(2,1)}, u32[]{:S(2)}) %copy-start.2) | copy-done | bytes 10485784
  43.7 2.3 %near_rows.6 = (bf16[192,32,128]{2,1,0:T(8,128)(2,1)S(1)}, bf16[64,32,128]{2,1,0:T(8,128)(2,1)S(1)}) custom-call(s32[16,128]{1,0:T(8,128)S(4)} %plan.1, bf16[64,640,128]{2,1,0:T(8,128)(2,1)S(1)} %copy-done.2, f32[64,128]{1,0:T(8,128)S(1)} %get-tuple-element.45.inverse, bf16[64,32,128]{2,1,0:T(8,128)(2,1)S(1)} %get-tuple-element.57.own, ...), custom_call_target="tpu_custom_call" | custom-call | flops 167772160 | bytes 10485760 | tf_op jit(solution)/shard_map/near_rows/pallas_call | solution.py:290
  46.0 0.0 collective-permute-done.8.other
  46.0 0.1 far_rows.6
  46.1 6.5 %collective-permute-start.11 = (bf16[64,32,128]{2,1,0:T(8,128)(2,1)S(1)}, bf16[64,32,128]{2,1,0:T(8,128)(2,1)S(1)}, u32[]{:S(2)}, u32[]{:S(2)}) collective-permute-start(bf16[64,32,128]{2,1,0:T(8,128)(2,1)S(1)} %get-tuple-element.62.own), channel_id=1, source_target_pairs={{0,1},{1,0},{2,3},{3,2},{4,5},{5,4},{6,7},{7,6},{8,9},{9,8},{10,11... | collective-permute-start | bytes 1572872 | tf_op jit(solution)/shard_map/ppermute | solution.py:460
  52.6 0.7 collective-permute-start.10
  53.3 0.8 %collective-permute-done.11.mate = bf16[64,32,128]{2,1,0:T(8,128)(2,1)S(1)} collective-permute-done((bf16[64,32,128]{2,1,0:T(8,128)(2,1)S(1)}, bf16[64,32,128]{2,1,0:T(8,128)(2,1)S(1)}, u32[]{:S(2)}, u32[]{:S(2)}) %collective-permute-start.11) | collective-permute-done | bytes 524320 | tf_op jit(solution)/shard_map/ppermute | solution.py:460
  54.2 0.0 copy-start.3
  54.2 4.0 %copy-done.3 = bf16[64,640,128]{2,1,0:T(8,128)(2,1)S(1)} copy-done((bf16[64,640,128]{2,1,0:T(8,128)(2,1)S(1)}, bf16[64,640,128]{2,1,0:T(8,128)(2,1)}, u32[]{:S(2)}) %copy-start.3) | copy-done | bytes 10485784
  58.1 3.0 %near_rows.7 = (bf16[192,32,128]{2,1,0:T(8,128)(2,1)S(1)}, bf16[64,96,128]{2,1,0:T(8,128)(2,1)S(1)}, f32[96,96]{1,0:T(8,128)S(1)}) custom-call(s32[16,128]{1,0:T(8,128)S(4)} %plan.1, bf16[64,640,128]{2,1,0:T(8,128)(2,1)S(1)} %copy-done.3, f32[64,128]{1,0:T(8,128)S(1)} %get-tuple-element.45.inverse, bf16[64,32,128]{2,1,0:T(8,128)(2,1)S(1)} %get-tuple-element.62.own, ...), custom_call_target="tpu_custom_call" | custom-call | flops 167772160 | bytes 10485760 | tf_op jit(solution)/shard_map/near_rows/pallas_call | solution.py:290
  61.2 0.0 collective-permute-done.10.other
  61.2 0.0 copy-start.5
  61.2 0.2 far_rows.7
  61.4 6.3 %collective-permute-start.12 = (f32[32,32]{1,0:T(8,128)S(1)}, f32[32,32]{1,0:T(8,128)S(1)}, u32[]{:S(2)}, u32[]{:S(2)}) collective-permute-start(f32[32,32]{1,0:T(8,128)S(1)} %get-tuple-element.66), channel_id=1, source_target_pairs={{0,1},{1,0},{2,3},{3,2},{4,5},{5,4},{6,7},{7,6},{8,9},{9,8},{10,11... | collective-permute-start | bytes 12296 | tf_op jit(solution)/shard_map/ppermute | solution.py:460
  67.7 0.8 collective-permute-done.12
  68.5 2.7 %collective-permute-start.13 = (f32[32,32]{1,0:T(8,128)S(1)}, f32[32,32]{1,0:T(8,128)S(1)}, u32[]{:S(2)}, u32[]{:S(2)}) collective-permute-start(f32[32,32]{1,0:T(8,128)S(1)} %add.14), channel_id=1, source_target_pairs={{0,2},{1,3},{2,0},{3,1},{4,6},{5,7},{6,4},{7,5},{8,10},{9,11},{10,... | collective-permute-start | bytes 12296 | tf_op jit(solution)/shard_map/ppermute | solution.py:460
  71.2 1.7 %collective-permute-done.13 = f32[32,32]{1,0:T(8,128)S(1)} collective-permute-done((f32[32,32]{1,0:T(8,128)S(1)}, f32[32,32]{1,0:T(8,128)S(1)}, u32[]{:S(2)}, u32[]{:S(2)}) %collective-permute-start.13) | collective-permute-done | bytes 4128 | tf_op jit(solution)/shard_map/ppermute | solution.py:460
  73.0 1.8 %collective-permute-start.14 = (f32[32,32]{1,0:T(8,128)S(1)}, f32[32,32]{1,0:T(8,128)S(1)}, u32[]{:S(2)}, u32[]{:S(2)}) collective-permute-start(f32[32,32]{1,0:T(8,128)S(1)} %add.15), channel_id=1, source_target_pairs={{0,4},{1,5},{2,6},{3,7},{4,0},{5,1},{6,2},{7,3},{8,12},{9,13},{10,... | collective-permute-start | bytes 12296 | tf_op jit(solution)/shard_map/ppermute | solution.py:460
  74.7 2.0 %collective-permute-done.14 = f32[32,32]{1,0:T(8,128)S(1)} collective-permute-done((f32[32,32]{1,0:T(8,128)S(1)}, f32[32,32]{1,0:T(8,128)S(1)}, u32[]{:S(2)}, u32[]{:S(2)}) %collective-permute-start.14) | collective-permute-done | bytes 4128 | tf_op jit(solution)/shard_map/ppermute | solution.py:460
  76.7 2.8 %collective-permute-start.15 = (f32[32,32]{1,0:T(8,128)S(1)}, f32[32,32]{1,0:T(8,128)S(1)}, u32[]{:S(2)}, u32[]{:S(2)}) collective-permute-start(f32[32,32]{1,0:T(8,128)S(1)} %add.16.gram_a), channel_id=1, source_target_pairs={{0,8},{1,9},{2,10},{3,11},{4,12},{5,13},{6,14},{7,15},{8,0},{9,1},... | collective-permute-start | bytes 12296 | tf_op jit(solution)/shard_map/ppermute | solution.py:460
  79.5 1.9 %collective-permute-done.15.gram_b = f32[32,32]{1,0:T(8,128)S(1)} collective-permute-done((f32[32,32]{1,0:T(8,128)S(1)}, f32[32,32]{1,0:T(8,128)S(1)}, u32[]{:S(2)}, u32[]{:S(2)}) %collective-permute-start.15) | collective-permute-done | bytes 4128 | tf_op jit(solution)/shard_map/ppermute | solution.py:460
  81.3 0.0 copy-done.5
  81.3 2.7 %memberships.1 = f32[32,8192]{1,0:T(8,128)} custom-call(f32[32,32]{1,0:T(8,128)S(1)} %add.16.gram_a, f32[32,32]{1,0:T(8,128)S(1)} %collective-permute-done.15.gram_b, f32[32,32]{1,0:T(8,128)S(1)} %copy-done.5, bf16[64,96,128]{2,1,0:T(8,128)(2,1)S(1)} %get-tuple-element.67.parts), custom_call_target="tpu_custom_call" | custom-call | flops 150994944 | bytes 3145728 | tf_op jit(solution)/shard_map/memberships/pallas_call | solution.py:435
  (6 shorter events, 0.0 us)
Async XLA Ops:
  0.0 10.8 %collective-permute-start.5 = (bf16[32,8192]{1,0:T(8,128)(2,1)}, bf16[32,8192]{1,0:T(8,128)(2,1)S(1)}, u32[]{:S(2)}, u32[]{:S(2)}) collective-permute-start(bf16[32,8192]{1,0:T(8,128)(2,1)} %own.1), channel_id=1, source_target_pairs={{0,1},{1,0},{2,3},{3,2},{4,5},{5,4},{6,7},{7,6},{8,9},{9,8},{10,11... | collective-permute-start | bytes 1572872 | tf_op jit(solution)/shard_map/ppermute | solution.py:460
  0.5 12.8 %collective-permute-start.4 = (bf16[32,8192]{1,0:T(8,128)(2,1)}, bf16[32,8192]{1,0:T(8,128)(2,1)S(1)}, u32[]{:S(2)}, u32[]{:S(2)}) collective-permute-start(bf16[32,8192]{1,0:T(8,128)(2,1)} %own.1), channel_id=1, source_target_pairs={{1,2},{2,1},{3,4},{4,3},{5,6},{6,5},{7,8},{8,7},{9,10},{10,9},{11,... | collective-permute-start | bytes 1572872 | tf_op jit(solution)/shard_map/ppermute | solution.py:460
  1.1 12.1 %collective-permute-start.3 = (s32[5,64]{1,0:T(8,128)}, s32[5,64]{1,0:T(8,128)S(1)}, u32[]{:S(2)}, u32[]{:S(2)}) collective-permute-start(s32[5,64]{1,0:T(8,128)} %bitcast.4), channel_id=1, source_target_pairs={{1,2},{2,1},{3,4},{4,3},{5,6},{6,5},{7,8},{8,7},{9,10},{10,9},{11,... | collective-permute-start | bytes 3848 | tf_op jit(solution)/shard_map/ppermute | solution.py:460
  1.9 0.7 copy-start.6
  4.1 6.7 %copy-start.4 = (bf16[32,8192]{1,0:T(8,128)(2,1)S(1)}, bf16[32,8192]{1,0:T(8,128)(2,1)}, u32[]{:S(2)}) copy-start(bf16[32,8192]{1,0:T(8,128)(2,1)} %own.1) | copy-start | bytes 1572868
  10.8 4.0 %copy-start = (bf16[64,640,128]{2,1,0:T(8,128)(2,1)}, bf16[64,640,128]{2,1,0:T(8,128)(2,1)S(1)}, u32[]{:S(2)}) copy-start(bf16[64,640,128]{2,1,0:T(8,128)(2,1)S(1)} %get-tuple-element.44.turned) | copy-start | bytes 31457284
  16.8 7.8 %collective-permute-start.7 = (bf16[64,32,128]{2,1,0:T(8,128)(2,1)S(1)}, bf16[64,32,128]{2,1,0:T(8,128)(2,1)S(1)}, u32[]{:S(2)}, u32[]{:S(2)}) collective-permute-start(bf16[64,32,128]{2,1,0:T(8,128)(2,1)S(1)} %get-tuple-element.52.own), channel_id=1, source_target_pairs={{0,1},{1,0},{2,3},{3,2},{4,5},{5,4},{6,7},{7,6},{8,9},{9,8},{10,11... | collective-permute-start | bytes 1572872 | tf_op jit(solution)/shard_map/ppermute | solution.py:460
  23.1 7.8 %collective-permute-start.6 = (bf16[44,32,128]{2,1,0:T(8,128)(2,1)S(1)}, bf16[44,32,128]{2,1,0:T(8,128)(2,1)S(1)}, u32[]{:S(2)}, u32[]{:S(2)}) collective-permute-start(bf16[44,32,128]{2,1,0:T(8,128)(2,1)S(1)} %get-tuple-element.49), channel_id=1, source_target_pairs={{1,2},{2,1},{3,4},{4,3},{5,6},{6,5},{7,8},{8,7},{9,10},{10,9},{11,... | collective-permute-start | bytes 1081352 | tf_op jit(solution)/shard_map/ppermute | solution.py:460
  24.6 4.0 %copy-start.1 = (bf16[64,640,128]{2,1,0:T(8,128)(2,1)S(1)}, bf16[64,640,128]{2,1,0:T(8,128)(2,1)}, u32[]{:S(2)}) copy-start(bf16[64,640,128]{2,1,0:T(8,128)(2,1)} %copy-done) | copy-start | bytes 31457284
  31.0 8.7 %collective-permute-start.9 = (bf16[64,32,128]{2,1,0:T(8,128)(2,1)S(1)}, bf16[64,32,128]{2,1,0:T(8,128)(2,1)S(1)}, u32[]{:S(2)}, u32[]{:S(2)}) collective-permute-start(bf16[64,32,128]{2,1,0:T(8,128)(2,1)S(1)} %get-tuple-element.57.own), channel_id=1, source_target_pairs={{0,1},{1,0},{2,3},{3,2},{4,5},{5,4},{6,7},{7,6},{8,9},{9,8},{10,11... | collective-permute-start | bytes 1572872 | tf_op jit(solution)/shard_map/ppermute | solution.py:460
  38.2 7.8 %collective-permute-start.8 = (bf16[44,32,128]{2,1,0:T(8,128)(2,1)S(1)}, bf16[44,32,128]{2,1,0:T(8,128)(2,1)S(1)}, u32[]{:S(2)}, u32[]{:S(2)}) collective-permute-start(bf16[44,32,128]{2,1,0:T(8,128)(2,1)S(1)} %get-tuple-element.55), channel_id=1, source_target_pairs={{1,2},{2,1},{3,4},{4,3},{5,6},{6,5},{7,8},{8,7},{9,10},{10,9},{11,... | collective-permute-start | bytes 1081352 | tf_op jit(solution)/shard_map/ppermute | solution.py:460
  39.7 4.0 %copy-start.2 = (bf16[64,640,128]{2,1,0:T(8,128)(2,1)S(1)}, bf16[64,640,128]{2,1,0:T(8,128)(2,1)}, u32[]{:S(2)}) copy-start(bf16[64,640,128]{2,1,0:T(8,128)(2,1)} %copy-done) | copy-start | bytes 31457284
  46.1 8.1 %collective-permute-start.11 = (bf16[64,32,128]{2,1,0:T(8,128)(2,1)S(1)}, bf16[64,32,128]{2,1,0:T(8,128)(2,1)S(1)}, u32[]{:S(2)}, u32[]{:S(2)}) collective-permute-start(bf16[64,32,128]{2,1,0:T(8,128)(2,1)S(1)} %get-tuple-element.62.own), channel_id=1, source_target_pairs={{0,1},{1,0},{2,3},{3,2},{4,5},{5,4},{6,7},{7,6},{8,9},{9,8},{10,11... | collective-permute-start | bytes 1572872 | tf_op jit(solution)/shard_map/ppermute | solution.py:460
  52.6 8.6 %collective-permute-start.10 = (bf16[44,32,128]{2,1,0:T(8,128)(2,1)S(1)}, bf16[44,32,128]{2,1,0:T(8,128)(2,1)S(1)}, u32[]{:S(2)}, u32[]{:S(2)}) collective-permute-start(bf16[44,32,128]{2,1,0:T(8,128)(2,1)S(1)} %get-tuple-element.60), channel_id=1, source_target_pairs={{1,2},{2,1},{3,4},{4,3},{5,6},{6,5},{7,8},{8,7},{9,10},{10,9},{11,... | collective-permute-start | bytes 1081352 | tf_op jit(solution)/shard_map/ppermute | solution.py:460
  54.2 4.0 %copy-start.3 = (bf16[64,640,128]{2,1,0:T(8,128)(2,1)S(1)}, bf16[64,640,128]{2,1,0:T(8,128)(2,1)}, u32[]{:S(2)}) copy-start(bf16[64,640,128]{2,1,0:T(8,128)(2,1)} %copy-done) | copy-start | bytes 31457284
  61.2 20.1 %copy-start.5 = (f32[32,32]{1,0:T(8,128)S(1)}, f32[32,32]{1,0:T(8,128)}, u32[]{:S(2)}) copy-start(f32[32,32]{1,0:T(8,128)} %mapping.1) | copy-start | bytes 12292
  61.4 7.1 %collective-permute-start.12 = (f32[32,32]{1,0:T(8,128)S(1)}, f32[32,32]{1,0:T(8,128)S(1)}, u32[]{:S(2)}, u32[]{:S(2)}) collective-permute-start(f32[32,32]{1,0:T(8,128)S(1)} %get-tuple-element.66), channel_id=1, source_target_pairs={{0,1},{1,0},{2,3},{3,2},{4,5},{5,4},{6,7},{7,6},{8,9},{9,8},{10,11... | collective-permute-start | bytes 12296 | tf_op jit(solution)/shard_map/ppermute | solution.py:460
  68.5 4.4 %collective-permute-start.13 = (f32[32,32]{1,0:T(8,128)S(1)}, f32[32,32]{1,0:T(8,128)S(1)}, u32[]{:S(2)}, u32[]{:S(2)}) collective-permute-start(f32[32,32]{1,0:T(8,128)S(1)} %add.14), channel_id=1, source_target_pairs={{0,2},{1,3},{2,0},{3,1},{4,6},{5,7},{6,4},{7,5},{8,10},{9,11},{10,... | collective-permute-start | bytes 12296 | tf_op jit(solution)/shard_map/ppermute | solution.py:460
  73.0 3.7 %collective-permute-start.14 = (f32[32,32]{1,0:T(8,128)S(1)}, f32[32,32]{1,0:T(8,128)S(1)}, u32[]{:S(2)}, u32[]{:S(2)}) collective-permute-start(f32[32,32]{1,0:T(8,128)S(1)} %add.15), channel_id=1, source_target_pairs={{0,4},{1,5},{2,6},{3,7},{4,0},{5,1},{6,2},{7,3},{8,12},{9,13},{10,... | collective-permute-start | bytes 12296 | tf_op jit(solution)/shard_map/ppermute | solution.py:460
  76.7 4.6 %collective-permute-start.15 = (f32[32,32]{1,0:T(8,128)S(1)}, f32[32,32]{1,0:T(8,128)S(1)}, u32[]{:S(2)}, u32[]{:S(2)}) collective-permute-start(f32[32,32]{1,0:T(8,128)S(1)} %add.16.gram_a), channel_id=1, source_target_pairs={{0,8},{1,9},{2,10},{3,11},{4,12},{5,13},{6,14},{7,15},{8,0},{9,1},... | collective-permute-start | bytes 12296 | tf_op jit(solution)/shard_map/ppermute | solution.py:460

commit v4 on v3

--- a/solution.py
+++ b/solution.py
@@ -24,57 +24,16 @@
     return pltpu.with_memory_space_constraint(array, pltpu.VMEM)
 
 
+def in_hbm(array):
+    return pltpu.with_memory_space_constraint(array, pltpu.HBM)
+
+
 def cost(flops, moved):
     return pl.CostEstimate(flops=flops, bytes_accessed=moved, transcendentals=0)
 
 
 def params(mib):
     return pltpu.CompilerParams(vmem_limit_bytes=mib * 2**20)
-
-
-def prep_kernel(tiles, turned, inverse, landing, arrived):
-    rows, slots, size, _ = tiles.shape
-    chunks = rows // CHUNK
-    ones = jnp.ones((16, slots * size), BF16)
-
-    def copy(i):
-        part = pl.ds(i * CHUNK, CHUNK)
-        return pltpu.make_async_copy(tiles.at[part], landing.at[part], arrived.at[i])
-
-    for i in range(chunks):
-        copy(i).start()
-
-    def step(i, carry):
-        copy(i).wait()
-        for u in range(CHUNK):
-            r = i * CHUNK + u
-            for s in range(slots):
-                turned[r, pl.ds(s * size, size), :] = landing[r, s].T
-            total = lax.dot_general(ones, turned[r], NN, preferred_element_type=F32)
-            inverse[pl.ds(r, 1), :] = 1.0 / total[0:1]
-        return carry
-
-    lax.fori_loop(0, chunks, step, 0)
-
-
-def prep(tiles):
-    rows, slots, size, _ = tiles.shape
-    return pl.pallas_call(
-        prep_kernel,
-        out_shape=(
-            pltpu.VMEM((rows, slots * size, size), BF16),
-            pltpu.VMEM((rows, size), F32),
-        ),
-        in_specs=[HB],
-        out_specs=(VM, VM),
-        scratch_shapes=[
-            pltpu.VMEM(tiles.shape, BF16),
-            pltpu.SemaphoreType.DMA((rows // CHUNK,)),
-        ],
-        compiler_params=params(14),
-        cost_estimate=cost(2 * tiles.size * 16, 4 * tiles.size),
-        name="prep",
-    )(pltpu.with_memory_space_constraint(tiles, pltpu.HBM))
 
 
 def ranks(named):
@@ -89,12 +48,11 @@
     return mark, rank
 
 
-def plan_kernel(where, columns, plan, draft, done):
+def draft_plan(first, parity, columns, draft, wanted):
     slots, rows = columns.shape
-    first, parity = where[0], where[1]
     low = jnp.where(parity == 0, 2 * rows, rows)
     high = jnp.where(parity == 0, rows, 2 * rows)
-    offset = columns[...] - first
+    offset = columns - first
     spot = jnp.where(
         offset < 0,
         offset + (rows + low),
@@ -127,25 +85,83 @@
     base = 2 * slots
     draft[base : base + 1, 0:rows] = order[0:1].astype(I32)
     draft[base + 1 : base + 2, 0:rows] = near[0:1].astype(I32)
-    draft[base + 2 : base + 3, 0:rows] = jnp.sum(mark, axis=0, keepdims=True).astype(I32)
-    copy = pltpu.make_async_copy(draft, plan, done)
-    copy.start()
-    copy.wait()
-
-
-def make_plan(where, columns):
-    slots, _ = columns.shape
+    read = jnp.sum(mark, axis=0, keepdims=True).astype(I32)
+    draft[base + 2 : base + 3, 0:rows] = read
+    here = jnp.where((mark > 0.5) & (rank.astype(I32) == lane), h, 0)
+    wanted[0:1, 0:rows] = jnp.sum(here.astype(F32), axis=0, keepdims=True).astype(I32)
+    wanted[1:2, 0:rows] = read
+
+
+def prep_kernel(
+    where, columns, tiles, turned, inverse, plan, wanted, kept,
+    landing, named, draft, arrived, left, here, done,
+):
+    rows, slots, size, _ = tiles.shape
+    chunks = rows // CHUNK
+    ones = jnp.ones((16, slots * size), BF16)
+
+    def part(i):
+        return pl.ds(i * CHUNK, CHUNK)
+
+    def copy_in(i):
+        return pltpu.make_async_copy(tiles.at[part(i)], landing.at[part(i)], arrived.at[i])
+
+    def copy_out(i):
+        return pltpu.make_async_copy(turned.at[part(i)], kept.at[part(i)], left.at[i])
+
+    copy_columns = pltpu.make_async_copy(columns, named, here)
+    copy_columns.start()
+    for i in range(chunks):
+        copy_in(i).start()
+    copy_columns.wait()
+    draft_plan(where[0], where[1], named[...], draft, wanted)
+    copy_plan = pltpu.make_async_copy(draft, plan, done)
+    copy_plan.start()
+
+    def step(i, carry):
+        copy_in(i).wait()
+        for u in range(CHUNK):
+            r = i * CHUNK + u
+            for s in range(slots):
+                turned[r, pl.ds(s * size, size), :] = landing[r, s].T
+            total = lax.dot_general(ones, turned[r], NN, preferred_element_type=F32)
+            inverse[pl.ds(r, 1), :] = 1.0 / total[0:1]
+        copy_out(i).start()
+        return carry
+
+    lax.fori_loop(0, chunks, step, 0)
+    copy_plan.wait()
+    for i in range(chunks):
+        copy_out(i).wait()
+
+
+def prep(where, columns, tiles):
+    rows, slots, size, _ = tiles.shape
     height = (2 * slots + 3 + 7) // 8 * 8
     return pl.pallas_call(
-        plan_kernel,
-        out_shape=pltpu.SMEM((height, 128), I32),
-        in_specs=[SM, VM],
-        out_specs=SM,
-        scratch_shapes=[pltpu.VMEM((height, 128), I32), pltpu.SemaphoreType.DMA],
-        compiler_params=params(2),
-        cost_estimate=cost(1000000, 4000),
-        name="plan",
-    )(where, columns)
+        prep_kernel,
+        out_shape=(
+            pltpu.VMEM((rows, slots * size, size), BF16),
+            pltpu.VMEM((rows, size), F32),
+            pltpu.SMEM((height, 128), I32),
+            pltpu.VMEM((8, 128), I32),
+            pltpu.HBM((rows, slots * size, size), BF16),
+        ),
+        in_specs=[SM, HB, HB],
+        out_specs=(VM, VM, SM, VM, HB),
+        scratch_shapes=[
+            pltpu.VMEM(tiles.shape, BF16),
+            pltpu.VMEM(columns.shape, I32),
+            pltpu.VMEM((height, 128), I32),
+            pltpu.SemaphoreType.DMA((rows // CHUNK,)),
+            pltpu.SemaphoreType.DMA((rows // CHUNK,)),
+            pltpu.SemaphoreType.DMA,
+            pltpu.SemaphoreType.DMA,
+        ],
+        compiler_params=params(14),
+        cost_estimate=cost(2 * tiles.size * 16, 4 * tiles.size),
+        name="prep",
+    )(where, in_hbm(columns), in_hbm(tiles))
 
 
 def fill(window, start, panel, tile_major):
@@ -224,29 +240,17 @@
 
 
 def far_first_kernel(
-    limit, where, theirs, plan, turned, inverse, other, w_in, i_in,
-    window, image, send, rest, sending, more, draft, done,
+    limit, asked, plan, turned, inverse, other, w_in, i_in,
+    window, image, send, rest, sending, more, done,
 ):
-    slots, rows = theirs.shape
-    offset = theirs[...] - where[0]
-    h = lax.broadcasted_iota(I32, (rows, rows), 0)
-    lane = lax.broadcasted_iota(I32, (rows, rows), 1)
-    named = functools.reduce(
-        jnp.add,
-        [jnp.where(offset[s : s + 1] == h, 1.0, 0.0) for s in range(slots)],
-    )
-    mark, rank = ranks(named)
-    here = jnp.where((mark > 0.5) & (rank.astype(I32) == lane), h, 0)
-    draft[0:1, 0:rows] = jnp.sum(here.astype(F32), axis=0, keepdims=True).astype(I32)
-    sent = jnp.sum(mark, axis=0, keepdims=True).astype(I32)
-    read = plan[2 * slots + 2, 0]
-    draft[1:2, 0:rows] = jnp.where(jnp.maximum(sent, read) > limit, 1, 0)
-    copy = pltpu.make_async_copy(draft, sending, done)
+    rows, depth, size = turned.shape
+    copy = pltpu.make_async_copy(asked, sending, done)
     copy.start()
     fill(window, 2 * rows, other, False)
     run_rows(False, 0, plan, turned, inverse, window, image, None)
     copy.wait()
-    more[0] = sending[1, 0]
+    read = plan[2 * (depth // size) + 2, 0]
+    more[0] = jnp.where(jnp.maximum(sending[1, 0], read) > limit, 1, 0)
     pack(image, sending, send, rest)
 
 
@@ -317,13 +321,13 @@
     return pltpu.VMEM(array.shape, array.dtype)
 
 
-def far_rows_first(limit, where, theirs, plan, turned, inverse, other, window, image):
+def far_rows_first(limit, asked, plan, turned, inverse, other, window, image):
     rows, vectors, size = image.shape
     return far_call(
         functools.partial(far_first_kernel, limit),
-        (where, theirs, plan, *map(in_vmem, (turned, inverse, other, window, image))),
-        [SM, VM, SM] + [VM] * 5,
-        6,
+        (in_vmem(asked), plan, *map(in_vmem, (turned, inverse, other, window, image))),
+        [VM, SM] + [VM] * 5,
+        5,
         (
             of(window),
             of(image),
@@ -334,7 +338,7 @@
         ),
         (VM, VM, VM, VM, SM, SM),
         turned,
-        [pltpu.VMEM((8, 128), I32), pltpu.SemaphoreType.DMA],
+        [pltpu.SemaphoreType.DMA],
     )[1:]
 
 
@@ -463,13 +467,13 @@
     where = jnp.stack([me * rows, me % 2]).astype(I32)
     columns = column_tiles.T
     mate, other = swap(schur_basis, mates), swap(schur_basis, others)
-    theirs = swap(columns, others)
-    plan = make_plan(where, columns)
-    turned, inverse = prep(transition_tiles)
+    turned, inverse, plan, wanted, kept = prep(where, columns, transition_tiles)
+    asked = swap(wanted, others)
     window, image = near_rows(plan, turned, inverse, schur_basis, mate, False, False)
     image, send, rest, sending, more = far_rows_first(
-        limit, where, theirs, plan, turned, inverse, other, window, image
-    )
+        limit, asked, plan, turned, inverse, other, window, image
+    )
+    turned = kept
     for step in range(1, PRODUCTS):
         last = step == PRODUCTS - 1
         mate, other = swap(image, mates), swap(send, others)

time: 84.4 us -> 84 us (level)
  local copies, waits for them, and re-layouts: 14.1 us -> 11.9 us
  Pallas kernels: 23.3 us -> 25.1 us
    pallas_call x1, Pallas kernels: 6.64 us -> 10.8 us  [prep(): pl.pallas_call(prep_kernel, out_shape=(pltpu.VMEM((rows, slots * size, si...]
    unnamed x14 -> x10, local copies, waits for them, and re-layouts: 14.1 us -> 11.9 us
    pallas_call x1 -> x0, Pallas kernels: 1.51 us -> none  [make_plan(): pl.pallas_call(plan_kernel, out_shape=pltpu.SMEM((height, 128), I32), in_...]
  transfers between devices with their start and end apart: 13 -> 13, of which waited for: 7 -> 7; matrix products, arithmetic and copies ran while one was open for 0% -> 0% of each run, Pallas kernels for 22% -> 25%
where the time goes in v4:
time: 84 us; the launch traced here: 83.6 us
  starting transfers between devices  37.4 us (45%)
  Pallas kernels  25.1 us (30%)
  local copies, waits for them, and re-layouts  11.9 us (14%)
  waiting for transfers between devices  8.2 us (10%)
  between operations  0.87 us (1%)
    ppermute x13, starting transfers between devices, swap(): return lax.ppermute(array, 'rows', pairs)  37.4 us
    unnamed x10, local copies, waits for them, and re-layouts  11.9 us
    pallas_call x1, Pallas kernels, prep(): pl.pallas_call(prep_kernel, out_shape=(pltpu.VMEM((rows, slots * size, si...  10.8 us
    pallas_call x4, Pallas kernels, near_rows(): pl.pallas_call(functools.partial(near_kernel, tile_major, last), out_shap...  10 us
    ppermute x13, waiting for transfers between devices, swap(): return lax.ppermute(array, 'rows', pairs)  8.2 us
    pallas_call x1, Pallas kernels, final(): pl.pallas_call(functools.partial(final_kernel, float(states)), out_shape=...  2.65 us
  transfers between devices with their start and end apart: 13, of which 7 were waited for; matrix products, arithmetic and copies ran while one was open for 0% of the time, Pallas kernels for 25%

profile of v4, /device:TPU:0, one launch (start us, length us, event | category | flops | bytes accessed | tf_op | source)
XLA Modules:
  0.0 83.6 jit_solution(5909765070290220766)
XLA Ops:
  0.0 0.5 collective-permute-start.5
  0.5 0.7 collective-permute-start.4
  1.2 0.1 pad_add_fusion.where
  1.2 0.0 copy-start.3
  1.2 10.8 %prep.1 = (bf16[64,640,128]{2,1,0:T(8,128)(2,1)S(1)}, f32[64,128]{1,0:T(8,128)S(1)}, s32[16,128]{1,0:T(8,128)S(4)}, s32[8,128]{1,0:T(8,128)S(1)}, bf16[64,640,128]{2,1,0:T(8,128)(2,1)}) custom-call(s32[2]{0:T(128)S(1)} %pad_add_fusion.where, s32[5,64]{1,0:T(8,128)} %bitcast.4, bf16[64,5,128,128]{3,2,1,0:T(8,128)(2,1)} %tiles.1), custom_call_target="tpu_custom_call" | custom-call | flops 167772160 | bytes 20971520 | tf_op jit(solution)/shard_map/prep/pallas_call | solution.py:141
  12.0 0.7 collective-permute-start.3
  12.7 0.0 collective-permute-done.5.mate
  12.7 0.0 copy-done.3
  12.7 2.4 %near_rows.4 = (bf16[192,32,128]{2,1,0:T(8,128)(2,1)S(1)}, bf16[64,32,128]{2,1,0:T(8,128)(2,1)S(1)}) custom-call(s32[16,128]{1,0:T(8,128)S(4)} %get-tuple-element.47.plan, bf16[64,640,128]{2,1,0:T(8,128)(2,1)S(1)} %get-tuple-element.51.turned, f32[64,128]{1,0:T(8,128)S(1)} %get-tuple-element.49.inverse, bf16[32,8192]{1,0:T(8,128)(2,1)S(1)} %copy-done.3, ...), custom_call_target="tpu_custom_call" | custom-call | flops 167772160 | bytes 10485760 | tf_op jit(solution)/shard_map/near_rows/pallas_call | solution.py:294
  15.1 0.0 collective-permute-done.3.asked
  15.1 0.0 collective-permute-done.4.other
  15.1 1.2 %far_rows.4 = (bf16[192,32,128]{2,1,0:T(8,128)(2,1)S(1)}, bf16[64,32,128]{2,1,0:T(8,128)(2,1)S(1)}, bf16[44,32,128]{2,1,0:T(8,128)(2,1)S(1)}, bf16[20,32,128]{2,...) custom-call(s32[8,128]{1,0:T(8,128)S(1)} %collective-permute-done.3.asked, ...), custom_call_target="tpu_custom_call", output_to_operand_aliasing={{0}: (5, {}), {1}: (6, {})} | custom-call | flops 167772160 | bytes 10485760 | tf_op jit(solution)/shard_map/far_rows/pallas_call | solution.py:307
  16.3 6.9 %collective-permute-start.7 = (bf16[64,32,128]{2,1,0:T(8,128)(2,1)S(1)}, bf16[64,32,128]{2,1,0:T(8,128)(2,1)S(1)}, u32[]{:S(2)}, u32[]{:S(2)}) collective-permute-start(bf16[64,32,128]{2,1,0:T(8,128)(2,1)S(1)} %get-tuple-element.58.own), channel_id=1, source_target_pairs={{0,1},{1,0},{2,3},{3,2},{4,5},{5,4},{6,7},{7,6},{8,9},{9,8},{10,11... | collective-permute-start | bytes 1572872 | tf_op jit(solution)/shard_map/ppermute | solution.py:464
  23.2 0.7 collective-permute-start.6
  24.6 0.2 collective-permute-done.7.mate
  24.7 0.0 copy-start
  24.7 4.0 %copy-done = bf16[64,640,128]{2,1,0:T(8,128)(2,1)S(1)} copy-done((bf16[64,640,128]{2,1,0:T(8,128)(2,1)S(1)}, bf16[64,640,128]{2,1,0:T(8,128)(2,1)}, u32[]{:S(2)}) %copy-start) | copy-done | bytes 10485784
  28.7 2.3 %near_rows.5 = (bf16[192,32,128]{2,1,0:T(8,128)(2,1)S(1)}, bf16[64,32,128]{2,1,0:T(8,128)(2,1)S(1)}) custom-call(s32[16,128]{1,0:T(8,128)S(4)} %get-tuple-element.47.plan, bf16[64,640,128]{2,1,0:T(8,128)(2,1)S(1)} %copy-done, f32[64,128]{1,0:T(8,128)S(1)} %get-tuple-element.49.inverse, bf16[64,32,128]{2,1,0:T(8,128)(2,1)S(1)} %get-tuple-element.58.own, ...), custom_call_target="tpu_custom_call" | custom-call | flops 167772160 | bytes 10485760 | tf_op jit(solution)/shard_map/near_rows/pallas_call | solution.py:294
  31.0 0.0 collective-permute-done.6.other
  31.0 0.1 far_rows.5
  31.2 6.0 %collective-permute-start.9 = (bf16[64,32,128]{2,1,0:T(8,128)(2,1)S(1)}, bf16[64,32,128]{2,1,0:T(8,128)(2,1)S(1)}, u32[]{:S(2)}, u32[]{:S(2)}) collective-permute-start(bf16[64,32,128]{2,1,0:T(8,128)(2,1)S(1)} %get-tuple-element.63.own), channel_id=1, source_target_pairs={{0,1},{1,0},{2,3},{3,2},{4,5},{5,4},{6,7},{7,6},{8,9},{9,8},{10,11... | collective-permute-start | bytes 1572872 | tf_op jit(solution)/shard_map/ppermute | solution.py:464
  37.2 0.7 collective-permute-start.8
  37.9 0.8 %collective-permute-done.9.mate = bf16[64,32,128]{2,1,0:T(8,128)(2,1)S(1)} collective-permute-done((bf16[64,32,128]{2,1,0:T(8,128)(2,1)S(1)}, bf16[64,32,128]{2,1,0:T(8,128)(2,1)S(1)}, u32[]{:S(2)}, u32[]{:S(2)}) %collective-permute-start.9) | collective-permute-done | bytes 524320 | tf_op jit(solution)/shard_map/ppermute | solution.py:464
  38.7 0.0 copy-start.1
  38.7 4.0 %copy-done.1 = bf16[64,640,128]{2,1,0:T(8,128)(2,1)S(1)} copy-done((bf16[64,640,128]{2,1,0:T(8,128)(2,1)S(1)}, bf16[64,640,128]{2,1,0:T(8,128)(2,1)}, u32[]{:S(2)}) %copy-start.1) | copy-done | bytes 10485784
  42.7 2.3 %near_rows.6 = (bf16[192,32,128]{2,1,0:T(8,128)(2,1)S(1)}, bf16[64,32,128]{2,1,0:T(8,128)(2,1)S(1)}) custom-call(s32[16,128]{1,0:T(8,128)S(4)} %get-tuple-element.47.plan, bf16[64,640,128]{2,1,0:T(8,128)(2,1)S(1)} %copy-done.1, f32[64,128]{1,0:T(8,128)S(1)} %get-tuple-element.49.inverse, bf16[64,32,128]{2,1,0:T(8,128)(2,1)S(1)} %get-tuple-element.63.own, ...), custom_call_target="tpu_custom_call" | custom-call | flops 167772160 | bytes 10485760 | tf_op jit(solution)/shard_map/near_rows/pallas_call | solution.py:294
  45.0 0.0 collective-permute-done.8.other
  45.0 0.1 far_rows.6
  45.1 6.5 %collective-permute-start.11 = (bf16[64,32,128]{2,1,0:T(8,128)(2,1)S(1)}, bf16[64,32,128]{2,1,0:T(8,128)(2,1)S(1)}, u32[]{:S(2)}, u32[]{:S(2)}) collective-permute-start(bf16[64,32,128]{2,1,0:T(8,128)(2,1)S(1)} %get-tuple-element.68.own), channel_id=1, source_target_pairs={{0,1},{1,0},{2,3},{3,2},{4,5},{5,4},{6,7},{7,6},{8,9},{9,8},{10,11... | collective-permute-start | bytes 1572872 | tf_op jit(solution)/shard_map/ppermute | solution.py:464
  51.6 0.7 collective-permute-start.10
  52.3 0.8 %collective-permute-done.11.mate = bf16[64,32,128]{2,1,0:T(8,128)(2,1)S(1)} collective-permute-done((bf16[64,32,128]{2,1,0:T(8,128)(2,1)S(1)}, bf16[64,32,128]{2,1,0:T(8,128)(2,1)S(1)}, u32[]{:S(2)}, u32[]{:S(2)}) %collective-permute-start.11) | collective-permute-done | bytes 524320 | tf_op jit(solution)/shard_map/ppermute | solution.py:464
  53.2 0.0 copy-start.2
  53.2 4.0 %copy-done.2 = bf16[64,640,128]{2,1,0:T(8,128)(2,1)S(1)} copy-done((bf16[64,640,128]{2,1,0:T(8,128)(2,1)S(1)}, bf16[64,640,128]{2,1,0:T(8,128)(2,1)}, u32[]{:S(2)}) %copy-start.2) | copy-done | bytes 10485784
  57.2 3.1 %near_rows.7 = (bf16[192,32,128]{2,1,0:T(8,128)(2,1)S(1)}, bf16[64,96,128]{2,1,0:T(8,128)(2,1)S(1)}, f32[96,96]{1,0:T(8,128)S(1)}) custom-call(s32[16,128]{1,0:T(8,128)S(4)} %get-tuple-element.47.plan, bf16[64,640,128]{2,1,0:T(8,128)(2,1)S(1)} %copy-done.2, f32[64,128]{1,0:T(8,128)S(1)} %get-tuple-element.49.inverse, ...), custom_call_target="tpu_custom_call" | custom-call | flops 167772160 | bytes 10485760 | tf_op jit(solution)/shard_map/near_rows/pallas_call | solution.py:294
  60.2 0.0 collective-permute-done.10.other
  60.2 0.0 copy-start.4
  60.2 0.2 far_rows.7
  60.4 6.3 %collective-permute-start.12 = (f32[32,32]{1,0:T(8,128)S(1)}, f32[32,32]{1,0:T(8,128)S(1)}, u32[]{:S(2)}, u32[]{:S(2)}) collective-permute-start(f32[32,32]{1,0:T(8,128)S(1)} %get-tuple-element.72), channel_id=1, source_target_pairs={{0,1},{1,0},{2,3},{3,2},{4,5},{5,4},{6,7},{7,6},{8,9},{9,8},{10,11... | collective-permute-start | bytes 12296 | tf_op jit(solution)/shard_map/ppermute | solution.py:464
  66.7 0.8 %collective-permute-done.12 = f32[32,32]{1,0:T(8,128)S(1)} collective-permute-done((f32[32,32]{1,0:T(8,128)S(1)}, f32[32,32]{1,0:T(8,128)S(1)}, u32[]{:S(2)}, u32[]{:S(2)}) %collective-permute-start.12) | collective-permute-done | bytes 4128 | tf_op jit(solution)/shard_map/ppermute | solution.py:464
  67.5 2.7 %collective-permute-start.13 = (f32[32,32]{1,0:T(8,128)S(1)}, f32[32,32]{1,0:T(8,128)S(1)}, u32[]{:S(2)}, u32[]{:S(2)}) collective-permute-start(f32[32,32]{1,0:T(8,128)S(1)} %add.14), channel_id=1, source_target_pairs={{0,2},{1,3},{2,0},{3,1},{4,6},{5,7},{6,4},{7,5},{8,10},{9,11},{10,... | collective-permute-start | bytes 12296 | tf_op jit(solution)/shard_map/ppermute | solution.py:464
  70.3 1.7 %collective-permute-done.13 = f32[32,32]{1,0:T(8,128)S(1)} collective-permute-done((f32[32,32]{1,0:T(8,128)S(1)}, f32[32,32]{1,0:T(8,128)S(1)}, u32[]{:S(2)}, u32[]{:S(2)}) %collective-permute-start.13) | collective-permute-done | bytes 4128 | tf_op jit(solution)/shard_map/ppermute | solution.py:464
  72.0 2.7 %collective-permute-start.14 = (f32[32,32]{1,0:T(8,128)S(1)}, f32[32,32]{1,0:T(8,128)S(1)}, u32[]{:S(2)}, u32[]{:S(2)}) collective-permute-start(f32[32,32]{1,0:T(8,128)S(1)} %add.15), channel_id=1, source_target_pairs={{0,4},{1,5},{2,6},{3,7},{4,0},{5,1},{6,2},{7,3},{8,12},{9,13},{10,... | collective-permute-start | bytes 12296 | tf_op jit(solution)/shard_map/ppermute | solution.py:464
  74.6 1.7 %collective-permute-done.14 = f32[32,32]{1,0:T(8,128)S(1)} collective-permute-done((f32[32,32]{1,0:T(8,128)S(1)}, f32[32,32]{1,0:T(8,128)S(1)}, u32[]{:S(2)}, u32[]{:S(2)}) %collective-permute-start.14) | collective-permute-done | bytes 4128 | tf_op jit(solution)/shard_map/ppermute | solution.py:464
  76.4 2.6 %collective-permute-start.15 = (f32[32,32]{1,0:T(8,128)S(1)}, f32[32,32]{1,0:T(8,128)S(1)}, u32[]{:S(2)}, u32[]{:S(2)}) collective-permute-start(f32[32,32]{1,0:T(8,128)S(1)} %add.16.gram_a), channel_id=1, source_target_pairs={{0,8},{1,9},{2,10},{3,11},{4,12},{5,13},{6,14},{7,15},{8,0},{9,1},... | collective-permute-start | bytes 12296 | tf_op jit(solution)/shard_map/ppermute | solution.py:464
  78.9 2.0 %collective-permute-done.15.gram_b = f32[32,32]{1,0:T(8,128)S(1)} collective-permute-done((f32[32,32]{1,0:T(8,128)S(1)}, f32[32,32]{1,0:T(8,128)S(1)}, u32[]{:S(2)}, u32[]{:S(2)}) %collective-permute-start.15) | collective-permute-done | bytes 4128 | tf_op jit(solution)/shard_map/ppermute | solution.py:464
  81.0 0.0 copy-done.4
  81.0 2.7 %memberships.1 = f32[32,8192]{1,0:T(8,128)} custom-call(f32[32,32]{1,0:T(8,128)S(1)} %add.16.gram_a, f32[32,32]{1,0:T(8,128)S(1)} %collective-permute-done.15.gram_b, f32[32,32]{1,0:T(8,128)S(1)} %copy-done.4, bf16[64,96,128]{2,1,0:T(8,128)(2,1)S(1)} %get-tuple-element.73.parts), custom_call_target="tpu_custom_call" | custom-call | flops 150994944 | bytes 3145728 | tf_op jit(solution)/shard_map/memberships/pallas_call | solution.py:439
  (6 shorter events, 0.0 us)
Async XLA Ops:
  0.0 12.7 %collective-permute-start.5 = (bf16[32,8192]{1,0:T(8,128)(2,1)}, bf16[32,8192]{1,0:T(8,128)(2,1)S(1)}, u32[]{:S(2)}, u32[]{:S(2)}) collective-permute-start(bf16[32,8192]{1,0:T(8,128)(2,1)} %own.1), channel_id=1, source_target_pairs={{0,1},{1,0},{2,3},{3,2},{4,5},{5,4},{6,7},{7,6},{8,9},{9,8},{10,11... | collective-permute-start | bytes 1572872 | tf_op jit(solution)/shard_map/ppermute | solution.py:464
  0.5 14.7 %collective-permute-start.4 = (bf16[32,8192]{1,0:T(8,128)(2,1)}, bf16[32,8192]{1,0:T(8,128)(2,1)S(1)}, u32[]{:S(2)}, u32[]{:S(2)}) collective-permute-start(bf16[32,8192]{1,0:T(8,128)(2,1)} %own.1), channel_id=1, source_target_pairs={{1,2},{2,1},{3,4},{4,3},{5,6},{6,5},{7,8},{8,7},{9,10},{10,9},{11,... | collective-permute-start | bytes 1572872 | tf_op jit(solution)/shard_map/ppermute | solution.py:464
  1.2 11.4 %copy-start.3 = (bf16[32,8192]{1,0:T(8,128)(2,1)S(1)}, bf16[32,8192]{1,0:T(8,128)(2,1)}, u32[]{:S(2)}) copy-start(bf16[32,8192]{1,0:T(8,128)(2,1)} %own.1) | copy-start | bytes 1572868
  12.0 3.1 %collective-permute-start.3 = (s32[8,128]{1,0:T(8,128)S(1)}, s32[8,128]{1,0:T(8,128)S(1)}, u32[]{:S(2)}, u32[]{:S(2)}) collective-permute-start(s32[8,128]{1,0:T(8,128)S(1)} %get-tuple-element.50), channel_id=1, source_target_pairs={{1,2},{2,1},{3,4},{4,3},{5,6},{6,5},{7,8},{8,7},{9,10},{10,9},{11,... | collective-permute-start | bytes 12296 | tf_op jit(solution)/shard_map/ppermute | solution.py:464
  16.3 8.4 %collective-permute-start.7 = (bf16[64,32,128]{2,1,0:T(8,128)(2,1)S(1)}, bf16[64,32,128]{2,1,0:T(8,128)(2,1)S(1)}, u32[]{:S(2)}, u32[]{:S(2)}) collective-permute-start(bf16[64,32,128]{2,1,0:T(8,128)(2,1)S(1)} %get-tuple-element.58.own), channel_id=1, source_target_pairs={{0,1},{1,0},{2,3},{3,2},{4,5},{5,4},{6,7},{7,6},{8,9},{9,8},{10,11... | collective-permute-start | bytes 1572872 | tf_op jit(solution)/shard_map/ppermute | solution.py:464
  23.2 7.8 %collective-permute-start.6 = (bf16[44,32,128]{2,1,0:T(8,128)(2,1)S(1)}, bf16[44,32,128]{2,1,0:T(8,128)(2,1)S(1)}, u32[]{:S(2)}, u32[]{:S(2)}) collective-permute-start(bf16[44,32,128]{2,1,0:T(8,128)(2,1)S(1)} %get-tuple-element.55), channel_id=1, source_target_pairs={{1,2},{2,1},{3,4},{4,3},{5,6},{6,5},{7,8},{8,7},{9,10},{10,9},{11,... | collective-permute-start | bytes 1081352 | tf_op jit(solution)/shard_map/ppermute | solution.py:464
  24.7 4.0 %copy-start = (bf16[64,640,128]{2,1,0:T(8,128)(2,1)S(1)}, bf16[64,640,128]{2,1,0:T(8,128)(2,1)}, u32[]{:S(2)}) copy-start(bf16[64,640,128]{2,1,0:T(8,128)(2,1)} %get-tuple-element.48.turned) | copy-start | bytes 31457284
  31.2 7.6 %collective-permute-start.9 = (bf16[64,32,128]{2,1,0:T(8,128)(2,1)S(1)}, bf16[64,32,128]{2,1,0:T(8,128)(2,1)S(1)}, u32[]{:S(2)}, u32[]{:S(2)}) collective-permute-start(bf16[64,32,128]{2,1,0:T(8,128)(2,1)S(1)} %get-tuple-element.63.own), channel_id=1, source_target_pairs={{0,1},{1,0},{2,3},{3,2},{4,5},{5,4},{6,7},{7,6},{8,9},{9,8},{10,11... | collective-permute-start | bytes 1572872 | tf_op jit(solution)/shard_map/ppermute | solution.py:464
  37.2 7.8 %collective-permute-start.8 = (bf16[44,32,128]{2,1,0:T(8,128)(2,1)S(1)}, bf16[44,32,128]{2,1,0:T(8,128)(2,1)S(1)}, u32[]{:S(2)}, u32[]{:S(2)}) collective-permute-start(bf16[44,32,128]{2,1,0:T(8,128)(2,1)S(1)} %get-tuple-element.61), channel_id=1, source_target_pairs={{1,2},{2,1},{3,4},{4,3},{5,6},{6,5},{7,8},{8,7},{9,10},{10,9},{11,... | collective-permute-start | bytes 1081352 | tf_op jit(solution)/shard_map/ppermute | solution.py:464
  38.7 4.0 %copy-start.1 = (bf16[64,640,128]{2,1,0:T(8,128)(2,1)S(1)}, bf16[64,640,128]{2,1,0:T(8,128)(2,1)}, u32[]{:S(2)}) copy-start(bf16[64,640,128]{2,1,0:T(8,128)(2,1)} %get-tuple-element.48.turned) | copy-start | bytes 31457284
  45.1 8.1 %collective-permute-start.11 = (bf16[64,32,128]{2,1,0:T(8,128)(2,1)S(1)}, bf16[64,32,128]{2,1,0:T(8,128)(2,1)S(1)}, u32[]{:S(2)}, u32[]{:S(2)}) collective-permute-start(bf16[64,32,128]{2,1,0:T(8,128)(2,1)S(1)} %get-tuple-element.68.own), channel_id=1, source_target_pairs={{0,1},{1,0},{2,3},{3,2},{4,5},{5,4},{6,7},{7,6},{8,9},{9,8},{10,11... | collective-permute-start | bytes 1572872 | tf_op jit(solution)/shard_map/ppermute | solution.py:464
  51.6 8.6 %collective-permute-start.10 = (bf16[44,32,128]{2,1,0:T(8,128)(2,1)S(1)}, bf16[44,32,128]{2,1,0:T(8,128)(2,1)S(1)}, u32[]{:S(2)}, u32[]{:S(2)}) collective-permute-start(bf16[44,32,128]{2,1,0:T(8,128)(2,1)S(1)} %get-tuple-element.66), channel_id=1, source_target_pairs={{1,2},{2,1},{3,4},{4,3},{5,6},{6,5},{7,8},{8,7},{9,10},{10,9},{11,... | collective-permute-start | bytes 1081352 | tf_op jit(solution)/shard_map/ppermute | solution.py:464
  53.2 4.0 %copy-start.2 = (bf16[64,640,128]{2,1,0:T(8,128)(2,1)S(1)}, bf16[64,640,128]{2,1,0:T(8,128)(2,1)}, u32[]{:S(2)}) copy-start(bf16[64,640,128]{2,1,0:T(8,128)(2,1)} %get-tuple-element.48.turned) | copy-start | bytes 31457284
  60.2 20.8 %copy-start.4 = (f32[32,32]{1,0:T(8,128)S(1)}, f32[32,32]{1,0:T(8,128)}, u32[]{:S(2)}) copy-start(f32[32,32]{1,0:T(8,128)} %mapping.1) | copy-start | bytes 12292
  60.4 7.1 %collective-permute-start.12 = (f32[32,32]{1,0:T(8,128)S(1)}, f32[32,32]{1,0:T(8,128)S(1)}, u32[]{:S(2)}, u32[]{:S(2)}) collective-permute-start(f32[32,32]{1,0:T(8,128)S(1)} %get-tuple-element.72), channel_id=1, source_target_pairs={{0,1},{1,0},{2,3},{3,2},{4,5},{5,4},{6,7},{7,6},{8,9},{9,8},{10,11... | collective-permute-start | bytes 12296 | tf_op jit(solution)/shard_map/ppermute | solution.py:464
  67.5 4.4 %collective-permute-start.13 = (f32[32,32]{1,0:T(8,128)S(1)}, f32[32,32]{1,0:T(8,128)S(1)}, u32[]{:S(2)}, u32[]{:S(2)}) collective-permute-start(f32[32,32]{1,0:T(8,128)S(1)} %add.14), channel_id=1, source_target_pairs={{0,2},{1,3},{2,0},{3,1},{4,6},{5,7},{6,4},{7,5},{8,10},{9,11},{10,... | collective-permute-start | bytes 12296 | tf_op jit(solution)/shard_map/ppermute | solution.py:464
  72.0 4.4 %collective-permute-start.14 = (f32[32,32]{1,0:T(8,128)S(1)}, f32[32,32]{1,0:T(8,128)S(1)}, u32[]{:S(2)}, u32[]{:S(2)}) collective-permute-start(f32[32,32]{1,0:T(8,128)S(1)} %add.15), channel_id=1, source_target_pairs={{0,4},{1,5},{2,6},{3,7},{4,0},{5,1},{6,2},{7,3},{8,12},{9,13},{10,... | collective-permute-start | bytes 12296 | tf_op jit(solution)/shard_map/ppermute | solution.py:464
  76.4 4.6 %collective-permute-start.15 = (f32[32,32]{1,0:T(8,128)S(1)}, f32[32,32]{1,0:T(8,128)S(1)}, u32[]{:S(2)}, u32[]{:S(2)}) collective-permute-start(f32[32,32]{1,0:T(8,128)S(1)} %add.16.gram_a), channel_id=1, source_target_pairs={{0,8},{1,9},{2,10},{3,11},{4,12},{5,13},{6,14},{7,15},{8,0},{9,1},... | collective-permute-start | bytes 12296 | tf_op jit(solution)/shard_map/ppermute | solution.py:464

commit v5 on v4

--- a/solution.py
+++ b/solution.py
@@ -93,8 +93,8 @@
 
 
 def prep_kernel(
-    where, columns, tiles, turned, inverse, plan, wanted, kept,
-    landing, named, draft, arrived, left, here, done,
+    where, columns, tiles, turned, inverse, plan, wanted,
+    landing, named, draft, arrived, here, done,
 ):
     rows, slots, size, _ = tiles.shape
     chunks = rows // CHUNK
@@ -105,9 +105,6 @@
 
     def copy_in(i):
         return pltpu.make_async_copy(tiles.at[part(i)], landing.at[part(i)], arrived.at[i])
-
-    def copy_out(i):
-        return pltpu.make_async_copy(turned.at[part(i)], kept.at[part(i)], left.at[i])
 
     copy_columns = pltpu.make_async_copy(columns, named, here)
     copy_columns.start()
@@ -126,13 +123,10 @@
                 turned[r, pl.ds(s * size, size), :] = landing[r, s].T
             total = lax.dot_general(ones, turned[r], NN, preferred_element_type=F32)
             inverse[pl.ds(r, 1), :] = 1.0 / total[0:1]
-        copy_out(i).start()
         return carry
 
     lax.fori_loop(0, chunks, step, 0)
     copy_plan.wait()
-    for i in range(chunks):
-        copy_out(i).wait()
 
 
 def prep(where, columns, tiles):
@@ -145,15 +139,13 @@
             pltpu.VMEM((rows, size), F32),
             pltpu.SMEM((height, 128), I32),
             pltpu.VMEM((8, 128), I32),
-            pltpu.HBM((rows, slots * size, size), BF16),
         ),
         in_specs=[SM, HB, HB],
-        out_specs=(VM, VM, SM, VM, HB),
+        out_specs=(VM, VM, SM, VM),
         scratch_shapes=[
             pltpu.VMEM(tiles.shape, BF16),
             pltpu.VMEM(columns.shape, I32),
             pltpu.VMEM((height, 128), I32),
-            pltpu.SemaphoreType.DMA((rows // CHUNK,)),
             pltpu.SemaphoreType.DMA((rows // CHUNK,)),
             pltpu.SemaphoreType.DMA,
             pltpu.SemaphoreType.DMA,
@@ -467,13 +459,12 @@
     where = jnp.stack([me * rows, me % 2]).astype(I32)
     columns = column_tiles.T
     mate, other = swap(schur_basis, mates), swap(schur_basis, others)
-    turned, inverse, plan, wanted, kept = prep(where, columns, transition_tiles)
+    turned, inverse, plan, wanted = prep(where, columns, transition_tiles)
     asked = swap(wanted, others)
     window, image = near_rows(plan, turned, inverse, schur_basis, mate, False, False)
     image, send, rest, sending, more = far_rows_first(
         limit, asked, plan, turned, inverse, other, window, image
     )
-    turned = kept
     for step in range(1, PRODUCTS):
         last = step == PRODUCTS - 1
         mate, other = swap(image, mates), swap(send, others)

time: 84 us -> 82.9 us (0.987)
  starting transfers between devices: 37.4 us -> 35.4 us
  Pallas kernels: 25.1 us -> 24 us
  local copies, waits for them, and re-layouts: 11.9 us -> 12.8 us
  waiting for transfers between devices: 8.2 us -> 9.08 us
    ppermute x13, starting transfers between devices: 37.4 us -> 35.4 us  [swap(): return lax.ppermute(array, 'rows', pairs)]
    pallas_call x1, Pallas kernels: 10.8 us -> 9.73 us  [prep(): pl.pallas_call(prep_kernel, out_shape=(pltpu.VMEM((rows, slots * size, si...]
    ppermute x13, waiting for transfers between devices: 8.2 us -> 9.08 us  [swap(): return lax.ppermute(array, 'rows', pairs)]
    unnamed x10 -> x12, local copies, waits for them, and re-layouts: 11.9 us -> 12.8 us
  transfers between devices with their start and end apart: 13 -> 13, of which waited for: 7 -> 7; matrix products, arithmetic and copies ran while one was open for 0% -> 0% of each run, Pallas kernels for 25% -> 24%
where the time goes in v5:
time: 82.9 us; the launch traced here: 82.3 us
  starting transfers between devices  35.4 us (43%)
  Pallas kernels  24 us (29%)
  local copies, waits for them, and re-layouts  12.8 us (15%)
  waiting for transfers between devices  9.08 us (11%)
  between operations  0.87 us (1%)
    ppermute x13, starting transfers between devices, swap(): return lax.ppermute(array, 'rows', pairs)  35.4 us
    unnamed x12, local copies, waits for them, and re-layouts  12.8 us
    pallas_call x4, Pallas kernels, near_rows(): pl.pallas_call(functools.partial(near_kernel, tile_major, last), out_shap...  10 us
    pallas_call x1, Pallas kernels, prep(): pl.pallas_call(prep_kernel, out_shape=(pltpu.VMEM((rows, slots * size, si...  9.73 us
    ppermute x13, waiting for transfers between devices, swap(): return lax.ppermute(array, 'rows', pairs)  9.08 us
    pallas_call x1, Pallas kernels, final(): pl.pallas_call(functools.partial(final_kernel, float(states)), out_shape=...  2.65 us
  transfers between devices with their start and end apart: 13, of which 7 were waited for; matrix products, arithmetic and copies ran while one was open for 0% of the time, Pallas kernels for 24%

profile of v5, /device:TPU:0, one launch (start us, length us, event | category | flops | bytes accessed | tf_op | source)
XLA Modules:
  0.0 82.3 jit_solution(5817403842380687150)
XLA Ops:
  0.0 0.5 collective-permute-start.5
  0.5 0.7 collective-permute-start.4
  1.2 0.1 pad_add_fusion.where
  1.2 0.0 copy-start.4
  1.2 9.7 %prep.1 = (bf16[64,640,128]{2,1,0:T(8,128)(2,1)S(1)}, f32[64,128]{1,0:T(8,128)S(1)}, s32[16,128]{1,0:T(8,128)S(4)}, s32[8,128]{1,0:T(8,128)S(1)}) custom-call(s32[2]{0:T(128)S(1)} %pad_add_fusion.where, s32[5,64]{1,0:T(8,128)} %bitcast.4, bf16[64,5,128,128]{3,2,1,0:T(8,128)(2,1)} %tiles.1), custom_call_target="tpu_custom_call" | custom-call | flops 167772160 | bytes 20971520 | tf_op jit(solution)/shard_map/prep/pallas_call | solution.py:135
  11.0 0.0 copy-start
  11.0 0.7 collective-permute-start.3
  11.6 0.0 collective-permute-done.5.mate
  11.7 0.0 copy-done.4
  11.7 2.4 %near_rows.4 = (bf16[192,32,128]{2,1,0:T(8,128)(2,1)S(1)}, bf16[64,32,128]{2,1,0:T(8,128)(2,1)S(1)}) custom-call(s32[16,128]{1,0:T(8,128)S(4)} %get-tuple-element.46.plan, bf16[64,640,128]{2,1,0:T(8,128)(2,1)S(1)} %get-tuple-element.47.turned, f32[64,128]{1,0:T(8,128)S(1)} %get-tuple-element.48.inverse, bf16[32,8192]{1,0:T(8,128)(2,1)S(1)} %copy-done.4, ...), custom_call_target="tpu_custom_call" | custom-call | flops 167772160 | bytes 10485760 | tf_op jit(solution)/shard_map/near_rows/pallas_call | solution.py:286
  14.1 0.0 collective-permute-done.3.asked
  14.1 0.0 collective-permute-done.4.other
  14.1 0.9 %copy-done = bf16[64,640,128]{2,1,0:T(8,128)(2,1)} copy-done((bf16[64,640,128]{2,1,0:T(8,128)(2,1)}, bf16[64,640,128]{2,1,0:T(8,128)(2,1)S(1)}, u32[]{:S(2)}) %copy-start) | copy-done | bytes 10485784
  15.0 1.2 %far_rows.4 = (bf16[192,32,128]{2,1,0:T(8,128)(2,1)S(1)}, bf16[64,32,128]{2,1,0:T(8,128)(2,1)S(1)}, bf16[44,32,128]{2,1,0:T(8,128)(2,1)S(1)}, bf16[20,32,128]{2,...) custom-call(s32[8,128]{1,0:T(8,128)S(1)} %collective-permute-done.3.asked, ...), custom_call_target="tpu_custom_call", output_to_operand_aliasing={{0}: (5, {}), {1}: (6, {})} | custom-call | flops 167772160 | bytes 10485760 | tf_op jit(solution)/shard_map/far_rows/pallas_call | solution.py:299
  16.2 6.0 %collective-permute-start.7 = (bf16[64,32,128]{2,1,0:T(8,128)(2,1)S(1)}, bf16[64,32,128]{2,1,0:T(8,128)(2,1)S(1)}, u32[]{:S(2)}, u32[]{:S(2)}) collective-permute-start(bf16[64,32,128]{2,1,0:T(8,128)(2,1)S(1)} %get-tuple-element.56.own), channel_id=1, source_target_pairs={{0,1},{1,0},{2,3},{3,2},{4,5},{5,4},{6,7},{7,6},{8,9},{9,8},{10,11... | collective-permute-start | bytes 1572872 | tf_op jit(solution)/shard_map/ppermute | solution.py:456
  22.2 0.7 collective-permute-start.6
  23.5 0.2 collective-permute-done.7.mate
  23.7 0.0 copy-start.1
  23.7 4.0 %copy-done.1 = bf16[64,640,128]{2,1,0:T(8,128)(2,1)S(1)} copy-done((bf16[64,640,128]{2,1,0:T(8,128)(2,1)S(1)}, bf16[64,640,128]{2,1,0:T(8,128)(2,1)}, u32[]{:S(2)}) %copy-start.1) | copy-done | bytes 10485784
  27.7 2.3 %near_rows.5 = (bf16[192,32,128]{2,1,0:T(8,128)(2,1)S(1)}, bf16[64,32,128]{2,1,0:T(8,128)(2,1)S(1)}) custom-call(s32[16,128]{1,0:T(8,128)S(4)} %get-tuple-element.46.plan, bf16[64,640,128]{2,1,0:T(8,128)(2,1)S(1)} %copy-done.1, f32[64,128]{1,0:T(8,128)S(1)} %get-tuple-element.48.inverse, bf16[64,32,128]{2,1,0:T(8,128)(2,1)S(1)} %get-tuple-element.56.own, ...), custom_call_target="tpu_custom_call" | custom-call | flops 167772160 | bytes 10485760 | tf_op jit(solution)/shard_map/near_rows/pallas_call | solution.py:286
  30.0 0.0 collective-permute-done.6.other
  30.0 0.1 far_rows.5
  30.1 6.0 %collective-permute-start.9 = (bf16[64,32,128]{2,1,0:T(8,128)(2,1)S(1)}, bf16[64,32,128]{2,1,0:T(8,128)(2,1)S(1)}, u32[]{:S(2)}, u32[]{:S(2)}) collective-permute-start(bf16[64,32,128]{2,1,0:T(8,128)(2,1)S(1)} %get-tuple-element.61.own), channel_id=1, source_target_pairs={{0,1},{1,0},{2,3},{3,2},{4,5},{5,4},{6,7},{7,6},{8,9},{9,8},{10,11... | collective-permute-start | bytes 1572872 | tf_op jit(solution)/shard_map/ppermute | solution.py:456
  36.2 0.7 collective-permute-start.8
  36.9 0.8 %collective-permute-done.9.mate = bf16[64,32,128]{2,1,0:T(8,128)(2,1)S(1)} collective-permute-done((bf16[64,32,128]{2,1,0:T(8,128)(2,1)S(1)}, bf16[64,32,128]{2,1,0:T(8,128)(2,1)S(1)}, u32[]{:S(2)}, u32[]{:S(2)}) %collective-permute-start.9) | collective-permute-done | bytes 524320 | tf_op jit(solution)/shard_map/ppermute | solution.py:456
  37.7 0.0 copy-start.2
  37.7 4.0 %copy-done.2 = bf16[64,640,128]{2,1,0:T(8,128)(2,1)S(1)} copy-done((bf16[64,640,128]{2,1,0:T(8,128)(2,1)S(1)}, bf16[64,640,128]{2,1,0:T(8,128)(2,1)}, u32[]{:S(2)}) %copy-start.2) | copy-done | bytes 10485784
  41.7 2.3 %near_rows.6 = (bf16[192,32,128]{2,1,0:T(8,128)(2,1)S(1)}, bf16[64,32,128]{2,1,0:T(8,128)(2,1)S(1)}) custom-call(s32[16,128]{1,0:T(8,128)S(4)} %get-tuple-element.46.plan, bf16[64,640,128]{2,1,0:T(8,128)(2,1)S(1)} %copy-done.2, f32[64,128]{1,0:T(8,128)S(1)} %get-tuple-element.48.inverse, bf16[64,32,128]{2,1,0:T(8,128)(2,1)S(1)} %get-tuple-element.61.own, ...), custom_call_target="tpu_custom_call" | custom-call | flops 167772160 | bytes 10485760 | tf_op jit(solution)/shard_map/near_rows/pallas_call | solution.py:286
  44.0 0.0 collective-permute-done.8.other
  44.0 0.1 far_rows.6
  44.1 6.5 %collective-permute-start.11 = (bf16[64,32,128]{2,1,0:T(8,128)(2,1)S(1)}, bf16[64,32,128]{2,1,0:T(8,128)(2,1)S(1)}, u32[]{:S(2)}, u32[]{:S(2)}) collective-permute-start(bf16[64,32,128]{2,1,0:T(8,128)(2,1)S(1)} %get-tuple-element.66.own), channel_id=1, source_target_pairs={{0,1},{1,0},{2,3},{3,2},{4,5},{5,4},{6,7},{7,6},{8,9},{9,8},{10,11... | collective-permute-start | bytes 1572872 | tf_op jit(solution)/shard_map/ppermute | solution.py:456
  50.6 0.7 collective-permute-start.10
  51.3 0.8 %collective-permute-done.11.mate = bf16[64,32,128]{2,1,0:T(8,128)(2,1)S(1)} collective-permute-done((bf16[64,32,128]{2,1,0:T(8,128)(2,1)S(1)}, bf16[64,32,128]{2,1,0:T(8,128)(2,1)S(1)}, u32[]{:S(2)}, u32[]{:S(2)}) %collective-permute-start.11) | collective-permute-done | bytes 524320 | tf_op jit(solution)/shard_map/ppermute | solution.py:456
  52.2 0.0 copy-start.3
  52.2 4.0 %copy-done.3 = bf16[64,640,128]{2,1,0:T(8,128)(2,1)S(1)} copy-done((bf16[64,640,128]{2,1,0:T(8,128)(2,1)S(1)}, bf16[64,640,128]{2,1,0:T(8,128)(2,1)}, u32[]{:S(2)}) %copy-start.3) | copy-done | bytes 10485784
  56.1 3.0 %near_rows.7 = (bf16[192,32,128]{2,1,0:T(8,128)(2,1)S(1)}, bf16[64,96,128]{2,1,0:T(8,128)(2,1)S(1)}, f32[96,96]{1,0:T(8,128)S(1)}) custom-call(s32[16,128]{1,0:T(8,128)S(4)} %get-tuple-element.46.plan, bf16[64,640,128]{2,1,0:T(8,128)(2,1)S(1)} %copy-done.3, f32[64,128]{1,0:T(8,128)S(1)} %get-tuple-element.48.inverse, ...), custom_call_target="tpu_custom_call" | custom-call | flops 167772160 | bytes 10485760 | tf_op jit(solution)/shard_map/near_rows/pallas_call | solution.py:286
  59.2 0.0 collective-permute-done.10.other
  59.2 0.0 copy-start.5
  59.2 0.2 far_rows.7
  59.4 6.3 %collective-permute-start.12 = (f32[32,32]{1,0:T(8,128)S(1)}, f32[32,32]{1,0:T(8,128)S(1)}, u32[]{:S(2)}, u32[]{:S(2)}) collective-permute-start(f32[32,32]{1,0:T(8,128)S(1)} %get-tuple-element.70), channel_id=1, source_target_pairs={{0,1},{1,0},{2,3},{3,2},{4,5},{5,4},{6,7},{7,6},{8,9},{9,8},{10,11... | collective-permute-start | bytes 12296 | tf_op jit(solution)/shard_map/ppermute | solution.py:456
  65.7 0.8 %collective-permute-done.12 = f32[32,32]{1,0:T(8,128)S(1)} collective-permute-done((f32[32,32]{1,0:T(8,128)S(1)}, f32[32,32]{1,0:T(8,128)S(1)}, u32[]{:S(2)}, u32[]{:S(2)}) %collective-permute-start.12) | collective-permute-done | bytes 4128 | tf_op jit(solution)/shard_map/ppermute | solution.py:456
  66.5 2.7 %collective-permute-start.13 = (f32[32,32]{1,0:T(8,128)S(1)}, f32[32,32]{1,0:T(8,128)S(1)}, u32[]{:S(2)}, u32[]{:S(2)}) collective-permute-start(f32[32,32]{1,0:T(8,128)S(1)} %add.14), channel_id=1, source_target_pairs={{0,2},{1,3},{2,0},{3,1},{4,6},{5,7},{6,4},{7,5},{8,10},{9,11},{10,... | collective-permute-start | bytes 12296 | tf_op jit(solution)/shard_map/ppermute | solution.py:456
  69.2 1.7 %collective-permute-done.13 = f32[32,32]{1,0:T(8,128)S(1)} collective-permute-done((f32[32,32]{1,0:T(8,128)S(1)}, f32[32,32]{1,0:T(8,128)S(1)}, u32[]{:S(2)}, u32[]{:S(2)}) %collective-permute-start.13) | collective-permute-done | bytes 4128 | tf_op jit(solution)/shard_map/ppermute | solution.py:456
  71.0 0.8 collective-permute-start.14
  71.8 2.9 %collective-permute-done.14 = f32[32,32]{1,0:T(8,128)S(1)} collective-permute-done((f32[32,32]{1,0:T(8,128)S(1)}, f32[32,32]{1,0:T(8,128)S(1)}, u32[]{:S(2)}, u32[]{:S(2)}) %collective-permute-start.14) | collective-permute-done | bytes 4128 | tf_op jit(solution)/shard_map/ppermute | solution.py:456
  74.7 3.2 %collective-permute-start.15 = (f32[32,32]{1,0:T(8,128)S(1)}, f32[32,32]{1,0:T(8,128)S(1)}, u32[]{:S(2)}, u32[]{:S(2)}) collective-permute-start(f32[32,32]{1,0:T(8,128)S(1)} %add.16.gram_a), channel_id=1, source_target_pairs={{0,8},{1,9},{2,10},{3,11},{4,12},{5,13},{6,14},{7,15},{8,0},{9,1},... | collective-permute-start | bytes 12296 | tf_op jit(solution)/shard_map/ppermute | solution.py:456
  77.9 1.7 %collective-permute-done.15.gram_b = f32[32,32]{1,0:T(8,128)S(1)} collective-permute-done((f32[32,32]{1,0:T(8,128)S(1)}, f32[32,32]{1,0:T(8,128)S(1)}, u32[]{:S(2)}, u32[]{:S(2)}) %collective-permute-start.15) | collective-permute-done | bytes 4128 | tf_op jit(solution)/shard_map/ppermute | solution.py:456
  79.6 0.0 copy-done.5
  79.6 2.7 %memberships.1 = f32[32,8192]{1,0:T(8,128)} custom-call(f32[32,32]{1,0:T(8,128)S(1)} %add.16.gram_a, f32[32,32]{1,0:T(8,128)S(1)} %collective-permute-done.15.gram_b, f32[32,32]{1,0:T(8,128)S(1)} %copy-done.5, bf16[64,96,128]{2,1,0:T(8,128)(2,1)S(1)} %get-tuple-element.71.parts), custom_call_target="tpu_custom_call" | custom-call | flops 150994944 | bytes 3145728 | tf_op jit(solution)/shard_map/memberships/pallas_call | solution.py:431
  (6 shorter events, 0.0 us)
Async XLA Ops:
  0.0 11.6 %collective-permute-start.5 = (bf16[32,8192]{1,0:T(8,128)(2,1)}, bf16[32,8192]{1,0:T(8,128)(2,1)S(1)}, u32[]{:S(2)}, u32[]{:S(2)}) collective-permute-start(bf16[32,8192]{1,0:T(8,128)(2,1)} %own.1), channel_id=1, source_target_pairs={{0,1},{1,0},{2,3},{3,2},{4,5},{5,4},{6,7},{7,6},{8,9},{9,8},{10,11... | collective-permute-start | bytes 1572872 | tf_op jit(solution)/shard_map/ppermute | solution.py:456
  0.5 13.6 %collective-permute-start.4 = (bf16[32,8192]{1,0:T(8,128)(2,1)}, bf16[32,8192]{1,0:T(8,128)(2,1)S(1)}, u32[]{:S(2)}, u32[]{:S(2)}) collective-permute-start(bf16[32,8192]{1,0:T(8,128)(2,1)} %own.1), channel_id=1, source_target_pairs={{1,2},{2,1},{3,4},{4,3},{5,6},{6,5},{7,8},{8,7},{9,10},{10,9},{11,... | collective-permute-start | bytes 1572872 | tf_op jit(solution)/shard_map/ppermute | solution.py:456
  1.2 10.4 %copy-start.4 = (bf16[32,8192]{1,0:T(8,128)(2,1)S(1)}, bf16[32,8192]{1,0:T(8,128)(2,1)}, u32[]{:S(2)}) copy-start(bf16[32,8192]{1,0:T(8,128)(2,1)} %own.1) | copy-start | bytes 1572868
  11.0 4.0 %copy-start = (bf16[64,640,128]{2,1,0:T(8,128)(2,1)}, bf16[64,640,128]{2,1,0:T(8,128)(2,1)S(1)}, u32[]{:S(2)}) copy-start(bf16[64,640,128]{2,1,0:T(8,128)(2,1)S(1)} %get-tuple-element.47.turned) | copy-start | bytes 31457284
  11.0 3.1 %collective-permute-start.3 = (s32[8,128]{1,0:T(8,128)S(1)}, s32[8,128]{1,0:T(8,128)S(1)}, u32[]{:S(2)}, u32[]{:S(2)}) collective-permute-start(s32[8,128]{1,0:T(8,128)S(1)} %get-tuple-element.49), channel_id=1, source_target_pairs={{1,2},{2,1},{3,4},{4,3},{5,6},{6,5},{7,8},{8,7},{9,10},{10,9},{11,... | collective-permute-start | bytes 12296 | tf_op jit(solution)/shard_map/ppermute | solution.py:456
  16.2 7.5 %collective-permute-start.7 = (bf16[64,32,128]{2,1,0:T(8,128)(2,1)S(1)}, bf16[64,32,128]{2,1,0:T(8,128)(2,1)S(1)}, u32[]{:S(2)}, u32[]{:S(2)}) collective-permute-start(bf16[64,32,128]{2,1,0:T(8,128)(2,1)S(1)} %get-tuple-element.56.own), channel_id=1, source_target_pairs={{0,1},{1,0},{2,3},{3,2},{4,5},{5,4},{6,7},{7,6},{8,9},{9,8},{10,11... | collective-permute-start | bytes 1572872 | tf_op jit(solution)/shard_map/ppermute | solution.py:456
  22.2 7.8 %collective-permute-start.6 = (bf16[44,32,128]{2,1,0:T(8,128)(2,1)S(1)}, bf16[44,32,128]{2,1,0:T(8,128)(2,1)S(1)}, u32[]{:S(2)}, u32[]{:S(2)}) collective-permute-start(bf16[44,32,128]{2,1,0:T(8,128)(2,1)S(1)} %get-tuple-element.53), channel_id=1, source_target_pairs={{1,2},{2,1},{3,4},{4,3},{5,6},{6,5},{7,8},{8,7},{9,10},{10,9},{11,... | collective-permute-start | bytes 1081352 | tf_op jit(solution)/shard_map/ppermute | solution.py:456
  23.7 4.0 %copy-start.1 = (bf16[64,640,128]{2,1,0:T(8,128)(2,1)S(1)}, bf16[64,640,128]{2,1,0:T(8,128)(2,1)}, u32[]{:S(2)}) copy-start(bf16[64,640,128]{2,1,0:T(8,128)(2,1)} %copy-done) | copy-start | bytes 31457284
  30.1 7.6 %collective-permute-start.9 = (bf16[64,32,128]{2,1,0:T(8,128)(2,1)S(1)}, bf16[64,32,128]{2,1,0:T(8,128)(2,1)S(1)}, u32[]{:S(2)}, u32[]{:S(2)}) collective-permute-start(bf16[64,32,128]{2,1,0:T(8,128)(2,1)S(1)} %get-tuple-element.61.own), channel_id=1, source_target_pairs={{0,1},{1,0},{2,3},{3,2},{4,5},{5,4},{6,7},{7,6},{8,9},{9,8},{10,11... | collective-permute-start | bytes 1572872 | tf_op jit(solution)/shard_map/ppermute | solution.py:456
  36.2 7.8 %collective-permute-start.8 = (bf16[44,32,128]{2,1,0:T(8,128)(2,1)S(1)}, bf16[44,32,128]{2,1,0:T(8,128)(2,1)S(1)}, u32[]{:S(2)}, u32[]{:S(2)}) collective-permute-start(bf16[44,32,128]{2,1,0:T(8,128)(2,1)S(1)} %get-tuple-element.59), channel_id=1, source_target_pairs={{1,2},{2,1},{3,4},{4,3},{5,6},{6,5},{7,8},{8,7},{9,10},{10,9},{11,... | collective-permute-start | bytes 1081352 | tf_op jit(solution)/shard_map/ppermute | solution.py:456
  37.7 4.0 %copy-start.2 = (bf16[64,640,128]{2,1,0:T(8,128)(2,1)S(1)}, bf16[64,640,128]{2,1,0:T(8,128)(2,1)}, u32[]{:S(2)}) copy-start(bf16[64,640,128]{2,1,0:T(8,128)(2,1)} %copy-done) | copy-start | bytes 31457284
  44.1 8.1 %collective-permute-start.11 = (bf16[64,32,128]{2,1,0:T(8,128)(2,1)S(1)}, bf16[64,32,128]{2,1,0:T(8,128)(2,1)S(1)}, u32[]{:S(2)}, u32[]{:S(2)}) collective-permute-start(bf16[64,32,128]{2,1,0:T(8,128)(2,1)S(1)} %get-tuple-element.66.own), channel_id=1, source_target_pairs={{0,1},{1,0},{2,3},{3,2},{4,5},{5,4},{6,7},{7,6},{8,9},{9,8},{10,11... | collective-permute-start | bytes 1572872 | tf_op jit(solution)/shard_map/ppermute | solution.py:456
  50.6 8.6 %collective-permute-start.10 = (bf16[44,32,128]{2,1,0:T(8,128)(2,1)S(1)}, bf16[44,32,128]{2,1,0:T(8,128)(2,1)S(1)}, u32[]{:S(2)}, u32[]{:S(2)}) collective-permute-start(bf16[44,32,128]{2,1,0:T(8,128)(2,1)S(1)} %get-tuple-element.64), channel_id=1, source_target_pairs={{1,2},{2,1},{3,4},{4,3},{5,6},{6,5},{7,8},{8,7},{9,10},{10,9},{11,... | collective-permute-start | bytes 1081352 | tf_op jit(solution)/shard_map/ppermute | solution.py:456
  52.2 4.0 %copy-start.3 = (bf16[64,640,128]{2,1,0:T(8,128)(2,1)S(1)}, bf16[64,640,128]{2,1,0:T(8,128)(2,1)}, u32[]{:S(2)}) copy-start(bf16[64,640,128]{2,1,0:T(8,128)(2,1)} %copy-done) | copy-start | bytes 31457284
  59.2 20.4 %copy-start.5 = (f32[32,32]{1,0:T(8,128)S(1)}, f32[32,32]{1,0:T(8,128)}, u32[]{:S(2)}) copy-start(f32[32,32]{1,0:T(8,128)} %mapping.1) | copy-start | bytes 12292
  59.4 7.1 %collective-permute-start.12 = (f32[32,32]{1,0:T(8,128)S(1)}, f32[32,32]{1,0:T(8,128)S(1)}, u32[]{:S(2)}, u32[]{:S(2)}) collective-permute-start(f32[32,32]{1,0:T(8,128)S(1)} %get-tuple-element.70), channel_id=1, source_target_pairs={{0,1},{1,0},{2,3},{3,2},{4,5},{5,4},{6,7},{7,6},{8,9},{9,8},{10,11... | collective-permute-start | bytes 12296 | tf_op jit(solution)/shard_map/ppermute | solution.py:456
  66.5 4.4 %collective-permute-start.13 = (f32[32,32]{1,0:T(8,128)S(1)}, f32[32,32]{1,0:T(8,128)S(1)}, u32[]{:S(2)}, u32[]{:S(2)}) collective-permute-start(f32[32,32]{1,0:T(8,128)S(1)} %add.14), channel_id=1, source_target_pairs={{0,2},{1,3},{2,0},{3,1},{4,6},{5,7},{6,4},{7,5},{8,10},{9,11},{10,... | collective-permute-start | bytes 12296 | tf_op jit(solution)/shard_map/ppermute | solution.py:456
  71.0 3.7 %collective-permute-start.14 = (f32[32,32]{1,0:T(8,128)S(1)}, f32[32,32]{1,0:T(8,128)S(1)}, u32[]{:S(2)}, u32[]{:S(2)}) collective-permute-start(f32[32,32]{1,0:T(8,128)S(1)} %add.15), channel_id=1, source_target_pairs={{0,4},{1,5},{2,6},{3,7},{4,0},{5,1},{6,2},{7,3},{8,12},{9,13},{10,... | collective-permute-start | bytes 12296 | tf_op jit(solution)/shard_map/ppermute | solution.py:456
  74.7 4.9 %collective-permute-start.15 = (f32[32,32]{1,0:T(8,128)S(1)}, f32[32,32]{1,0:T(8,128)S(1)}, u32[]{:S(2)}, u32[]{:S(2)}) collective-permute-start(f32[32,32]{1,0:T(8,128)S(1)} %add.16.gram_a), channel_id=1, source_target_pairs={{0,8},{1,9},{2,10},{3,11},{4,12},{5,13},{6,14},{7,15},{8,0},{9,1},... | collective-permute-start | bytes 12296 | tf_op jit(solution)/shard_map/ppermute | solution.py:456

commit v6 on v5

v6 whole, which is shorter than its diff:
```python
import functools

import jax
import jax.numpy as jnp
from jax import lax
from jax.experimental import pallas as pl
from jax.experimental.pallas import tpu as pltpu
from jax.sharding import PartitionSpec as P

PRODUCTS = 4
BLOCK = 16
CHUNK = 8
F32 = jnp.float32
BF16 = jnp.bfloat16
I32 = jnp.int32
NN = (((1,), (0,)), ((), ()))
NT = (((1,), (1,)), ((), ()))
VM = pl.BlockSpec(memory_space=pltpu.VMEM)
SM = pl.BlockSpec(memory_space=pltpu.SMEM)
HB = pl.BlockSpec(memory_space=pltpu.HBM)


def in_vmem(array):
    return pltpu.with_memory_space_constraint(array, pltpu.VMEM)


def in_hbm(array):
    return pltpu.with_memory_space_constraint(array, pltpu.HBM)


def cost(flops, moved):
    return pl.CostEstimate(flops=flops, bytes_accessed=moved, transcendentals=0)


def params(mib):
    return pltpu.CompilerParams(vmem_limit_bytes=mib * 2**20)


def ranks(named):
    rows = named.shape[0]
    h = lax.broadcasted_iota(I32, (rows, rows), 0)
    other = lax.broadcasted_iota(I32, (rows, rows), 1)
    before = jnp.where(other < h, 1.0, 0.0).astype(BF16)
    ones = jnp.ones((rows, rows), BF16)
    total = lax.dot_general(named.astype(BF16), ones, NN, preferred_element_type=F32)
    mark = jnp.where(total > 0.5, 1.0, 0.0)
    rank = lax.dot_general(before, mark.astype(BF16), NN, preferred_element_type=F32)
    return mark, rank


def lines(slots):
    far = slots - 1
    return slots, slots + far, slots + 2 * far, slots + 3 * far, slots + 3 * far + 1


def plan_height(slots):
    return (lines(slots)[-1] + 2 + 7) // 8 * 8


def draft_plan(first, parity, columns, draft, wanted):
    slots, rows = columns.shape
    panel, counted, slot, order, reads = lines(slots)
    low = jnp.where(parity == 0, 2 * rows, rows)
    high = jnp.where(parity == 0, rows, 2 * rows)
    offset = columns - first
    spot = jnp.where(
        offset < 0,
        offset + (rows + low),
        jnp.where(offset >= rows, offset + (high - rows), offset),
    )
    draft[0:slots, 0:rows] = jnp.minimum(spot, 2 * rows)
    h = lax.broadcasted_iota(I32, (rows, rows), 0)
    lane = lax.broadcasted_iota(I32, (rows, rows), 1)
    ones = jnp.ones((rows, rows), BF16)
    equal = [
        jnp.where(spot[s : s + 1] - 2 * rows == h, 1.0, 0.0) for s in range(slots)
    ]
    mark, rank = ranks(functools.reduce(jnp.add, equal))
    here = jnp.where((mark > 0.5) & (rank.astype(I32) == lane), h, 0)
    wanted[0:1, 0:rows] = jnp.sum(here.astype(F32), axis=0, keepdims=True).astype(I32)
    wanted[1:2, 0:rows] = jnp.sum(mark, axis=0, keepdims=True).astype(I32)
    none = jnp.zeros((1, rows), I32)
    seen = none
    tiles, places, named = [[none + start] * (slots - 1) for start in (rows, rows, 0)]
    for s in range(slots):
        place = jnp.sum(equal[s] * rank, axis=0, keepdims=True).astype(I32)
        tile = spot[s : s + 1] - 2 * rows
        far = jnp.where(tile >= 0, 1, 0)
        for j in range(min(s + 1, slots - 1)):
            hit = (far == 1) & (seen == j)
            tiles[j] = jnp.where(hit, tile, tiles[j])
            places[j] = jnp.where(hit, place, places[j])
            named[j] = jnp.where(hit, s, named[j])
        seen = seen + far
    for j in range(slots - 1):
        draft[panel + j : panel + j + 1, 0:rows] = tiles[j]
        draft[counted + j : counted + j + 1, 0:rows] = places[j]
        draft[slot + j : slot + j + 1, 0:rows] = named[j]
    along = jnp.broadcast_to(seen.astype(F32), (rows, rows))
    down = lax.dot_general(
        jnp.where(h == lane, along, 0.0).astype(BF16), ones, NN, preferred_element_type=F32
    )
    ahead = jnp.where((down < along) | ((down == along) & (h < lane)), 1.0, 0.0)
    position = jnp.sum(ahead, axis=0, keepdims=True).astype(I32)
    taken = jnp.where(position == h, 1.0, 0.0).astype(BF16)
    line = lax.broadcasted_iota(I32, (16, rows), 1).astype(BF16)
    sorted_rows = lax.dot_general(line, taken, NT, preferred_element_type=F32)
    draft[order : order + 1, 0:rows] = sorted_rows[0:1].astype(I32)
    draft[reads : reads + 1, 0:rows] = seen
    touched = jnp.sum(jnp.minimum(seen, 1).astype(F32), axis=1, keepdims=True)
    draft[reads + 1 : reads + 2, 0:rows] = jnp.broadcast_to(touched, (1, rows)).astype(I32)


def prep_kernel(
    where, columns, tiles, turned, inverse, plan, wanted,
    landing, named, draft, arrived, here, done,
):
    rows, slots, size, _ = tiles.shape
    chunks = rows // CHUNK

    def copy_in(i):
        part = pl.ds(i * CHUNK, CHUNK)
        return pltpu.make_async_copy(tiles.at[part], landing.at[part], arrived.at[i])

    copy_columns = pltpu.make_async_copy(columns, named, here)
    copy_columns.start()
    for i in range(chunks):
        copy_in(i).start()
    copy_columns.wait()
    draft_plan(where[0], where[1], named[...], draft, wanted)
    copy_plan = pltpu.make_async_copy(draft, plan, done)
    copy_plan.start()

    def step(i, carry):
        copy_in(i).wait()
        for u in range(CHUNK):
            r = i * CHUNK + u
            total = None
            for s in range(slots):
                tile = landing[r, s].T
                turned[r, pl.ds(s * size, size), :] = tile
                tile = tile.astype(F32)
                total = tile if total is None else total + tile
            inverse[pl.ds(r, 1), :] = 1.0 / jnp.sum(total, axis=0, keepdims=True)
        return carry

    lax.fori_loop(0, chunks, step, 0)
    copy_plan.wait()


def prep(where, columns, tiles):
    rows, slots, size, _ = tiles.shape
    height = plan_height(slots)
    return pl.pallas_call(
        prep_kernel,
        out_shape=(
            pltpu.VMEM((rows, slots * size, size), BF16),
            pltpu.VMEM((rows, size), F32),
            pltpu.SMEM((height, 128), I32),
            pltpu.VMEM((8, 128), I32),
        ),
        in_specs=[SM, HB, HB],
        out_specs=(VM, VM, SM, VM),
        scratch_shapes=[
            pltpu.VMEM(tiles.shape, BF16),
            pltpu.VMEM(columns.shape, I32),
            pltpu.VMEM((height, 128), I32),
            pltpu.SemaphoreType.DMA((rows // CHUNK,)),
            pltpu.SemaphoreType.DMA,
            pltpu.SemaphoreType.DMA,
        ],
        compiler_params=params(14),
        cost_estimate=cost(2 * tiles.size * 16, 4 * tiles.size),
        name="prep",
    )(where, in_hbm(columns), in_hbm(tiles))


def fill(window, start, panel, tile_major):
    size = window.shape[2]
    if tile_major:
        window[start : start + panel.shape[0]] = panel[...]
    else:
        for t in range(panel.shape[1] // size):
            window[start + t] = panel[:, t * size : (t + 1) * size]


def thirds(x):
    high = x.astype(BF16)
    rest = x - high.astype(F32)
    middle = rest.astype(BF16)
    low = (rest - middle.astype(F32)).astype(BF16)
    return high, middle, low


def fold(squares, vectors):
    total = None
    for a, b in ((2, 2), (1, 2), (2, 1), (0, 2), (2, 0), (1, 1), (0, 1), (1, 0), (0, 0)):
        part = squares[a * vectors : (a + 1) * vectors, b * vectors : (b + 1) * vectors]
        total = part if total is None else total + part
    return total


def store(image, squares, picked, results, mine):
    if squares is None:
        for r, y in zip(picked, results):
            image[r] = y.astype(BF16)
        return None
    counted = []
    for r, y, keep in zip(picked, results, mine):
        stacked = jnp.concatenate(thirds(y), axis=0)
        image[r] = stacked
        counted.append(jnp.where(keep, stacked, jnp.zeros_like(stacked)))
    wide = jnp.concatenate(counted, axis=1)
    return squares + lax.dot_general(wide, wide, NT, preferred_element_type=F32)


def near_kernel(tile_major, last, plan, turned, inverse, own, mate, image, sums, *refs):
    rows, depth, size = turned.shape
    slots = depth // size
    reads = lines(slots)[-1]
    window = refs[-1]
    fill(window, 0, own, tile_major)
    fill(window, rows, mate, tile_major)
    window[2 * rows] = jnp.zeros(window.shape[1:], BF16)

    def step(block, squares):
        picked = [block * BLOCK + u for u in range(BLOCK)]
        vectors = [
            jnp.concatenate([window[plan[s, r]] for s in range(slots)], axis=1)
            for r in picked
        ]
        products = [
            lax.dot_general(x, turned[r], NN, preferred_element_type=F32)
            for x, r in zip(vectors, picked)
        ]
        results = [y * inverse[pl.ds(r, 1), :] for r, y in zip(picked, products)]
        for r, y in zip(picked, results):
            sums[r] = y
        mine = [plan[reads, r] == 0 for r in picked]
        return store(image, squares, picked, results, mine)

    begin = jnp.zeros(refs[0].shape, F32) if last else None
    total = lax.fori_loop(0, rows // BLOCK, step, begin)
    if last:
        refs[0][...] = total


def far_part(base, plan, turned, inverse, sums, panel, image, squares):
    rows, depth, size = turned.shape
    slots = depth // size
    slot, order, reads = lines(slots)[2:]
    panel[rows] = jnp.zeros(panel.shape[1:], BF16)

    def rows_of(start, count):
        picked = [plan[order, start + u] for u in range(BLOCK)]
        products = []
        for r in picked:
            x = [panel[plan[base + j, r]] for j in range(count)]
            w = [
                turned[r, pl.ds(pl.multiple_of(plan[slot + j, r] * size, size), size), :]
                for j in range(count)
            ]
            products.append(
                lax.dot_general(
                    jnp.concatenate(x, axis=1),
                    jnp.concatenate(w, axis=0),
                    NN,
                    preferred_element_type=F32,
                )
            )
        return picked, [
            sums[r] + y * inverse[pl.ds(r, 1), :] for r, y in zip(picked, products)
        ]

    def step(block, carry):
        start = rows - (block + 1) * BLOCK
        most = plan[reads, plan[order, start + BLOCK - 1]]
        for count in range(1, slots):

            @pl.when(most == count)
            def _():
                picked, results = rows_of(start, count)
                mine = [plan[reads, r] > 0 for r in picked]
                if squares is None:
                    store(image, None, picked, results, mine)
                else:
                    squares[...] = store(image, squares[...], picked, results, mine)

        return carry

    touched = plan[reads + 1, 0]
    lax.fori_loop(0, (touched + BLOCK - 1) // BLOCK, step, 0)


def pack(image, sending, send, rest):
    limit = send.shape[0]
    for k in range(image.shape[0]):
        target = send.at[k] if k < limit else rest.at[k - limit]
        target[...] = image[sending[0, k]]


def far_first_kernel(
    asked, plan, turned, inverse, other, sums, i_in, image, send, rest, sending, panel, done
):
    rows, depth, size = turned.shape
    copy = pltpu.make_async_copy(asked, sending, done)
    copy.start()
    fill(panel, 0, other, False)
    base = lines(depth // size)[0]
    far_part(base, plan, turned, inverse, sums, panel, image, None)
    copy.wait()
    pack(image, sending, send, rest)


def far_kernel(
    sending, plan, turned, inverse, other, extra, sums, i_in, image, send, rest, panel
):
    rows, depth, size = turned.shape
    fill(panel, 0, other, True)
    fill(panel, other.shape[0], extra, True)
    base = lines(depth // size)[1]
    far_part(base, plan, turned, inverse, sums, panel, image, None)
    pack(image, sending, send, rest)


def far_last_kernel(
    plan, turned, inverse, other, extra, near, sums, i_in, image, gram, panel, squares
):
    rows, depth, size = turned.shape
    fill(panel, 0, other, True)
    fill(panel, other.shape[0], extra, True)
    squares[...] = near[...]
    base = lines(depth // size)[1]
    far_part(base, plan, turned, inverse, sums, panel, image, squares)
    gram[...] = fold(squares[...], gram.shape[0])


def near_rows(plan, turned, inverse, own, mate, tile_major, last):
    rows, depth, size = turned.shape
    vectors = own.shape[1 if tile_major else 0]
    height = 3 * vectors if last else vectors
    shapes = (
        pltpu.VMEM((rows, height, size), BF16),
        pltpu.VMEM((rows, vectors, size), F32),
    )
    if last:
        shapes += (pltpu.VMEM((height, height), F32),)
    return pl.pallas_call(
        functools.partial(near_kernel, tile_major, last),
        out_shape=shapes,
        in_specs=[SM, VM, VM, VM, VM],
        out_specs=(VM,) * len(shapes),
        scratch_shapes=[pltpu.VMEM((2 * rows + 1, vectors, size), BF16)],
        compiler_params=params(4),
        cost_estimate=cost(2 * rows * depth * size * vectors, 2 * rows * depth * size),
        name="near_rows",
    )(plan, *map(in_vmem, (turned, inverse, own, mate)))


def far_call(kernel, ins, in_specs, outs, out_specs, turned, vectors, scratch=()):
    rows, depth, size = turned.shape
    return pl.pallas_call(
        kernel,
        out_shape=outs,
        in_specs=in_specs,
        out_specs=out_specs,
        scratch_shapes=[pltpu.VMEM((rows + 1, vectors, size), BF16), *scratch],
        input_output_aliases={len(ins) - 1: 0},
        compiler_params=params(4),
        cost_estimate=cost(20 * rows * depth * size, rows * depth * size),
        name="far_rows",
    )(*ins)


def of(array):
    return pltpu.VMEM(array.shape, array.dtype)


def far_rows_first(limit, asked, plan, turned, inverse, other, sums, image):
    rows, vectors, size = image.shape
    return far_call(
        far_first_kernel,
        (in_vmem(asked), plan, *map(in_vmem, (turned, inverse, other, sums, image))),
        [VM, SM] + [VM] * 5,
        (
            of(image),
            pltpu.VMEM((limit, vectors, size), BF16),
            pltpu.VMEM((rows - limit, vectors, size), BF16),
            pltpu.SMEM((8, 128), I32),
        ),
        (VM, VM, VM, SM),
        turned,
        vectors,
        [pltpu.SemaphoreType.DMA],
    )


def far_rows(plan, turned, inverse, sending, other, extra, sums, image):
    return far_call(
        far_kernel,
        (sending, plan, *map(in_vmem, (turned, inverse, other, extra, sums, image))),
        [SM, SM] + [VM] * 6,
        (of(image), of(other), of(extra)),
        (VM,) * 3,
        turned,
        image.shape[1],
    )


def far_rows_last(plan, turned, inverse, other, extra, near, sums, image):
    vectors = near.shape[0] // 3
    return far_call(
        far_last_kernel,
        (plan, *map(in_vmem, (turned, inverse, other, extra, near, sums, image))),
        [SM] + [VM] * 7,
        (of(image), pltpu.VMEM((vectors, vectors), F32)),
        (VM,) * 2,
        turned,
        vectors,
        [pltpu.VMEM(near.shape, F32)],
    )


def inverse_factor(gram):
    count = gram.shape[0]
    step = 8
    row = lax.broadcasted_iota(I32, (count, count), 0)
    column = lax.broadcasted_iota(I32, (count, count), 1)
    work = jnp.concatenate([gram, jnp.where(row == column, 1.0, 0.0)], axis=1)
    below = lax.broadcasted_iota(I32, work.shape, 0)
    for begin in range(0, count, step):
        spread = [
            jnp.broadcast_to(work[:, k : k + 1], work.shape)
            for k in range(begin, begin + step)
        ]
        for j in range(step):
            k = begin + j
            factor = jnp.where(below > k, spread[j], 0.0)
            pivot = 1.0 / spread[j][k : k + 1]
            for q in range(j + 1, step):
                spread[q] = spread[q] - factor * (spread[q][k : k + 1] * pivot)
            work = work - factor * (work[k : k + 1] * pivot)
    pivots = jnp.sum(
        jnp.where(row == column, work[:, :count], 0.0), axis=1, keepdims=True
    )
    return work[:, count:] * lax.rsqrt(pivots)


def final_kernel(states, gram_a, gram_b, mapping, parts, out, ready, sent):
    rows, depth, size = parts.shape
    vectors = depth // 3
    factor = inverse_factor((gram_a[...] + gram_b[...]) / states)
    combined = lax.dot_general(
        mapping[...],
        factor,
        (((0,), (0,)), ((), ())),
        precision=lax.Precision.HIGHEST,
        preferred_element_type=F32,
    )
    high, middle, low = thirds(combined)
    blank = jnp.zeros_like(high)
    left = jnp.concatenate(
        [
            jnp.concatenate([high, high, high], axis=1),
            jnp.concatenate([middle, middle, blank], axis=1),
            jnp.concatenate([low, blank, blank], axis=1),
        ],
        axis=0,
    )
    copies = []
    for g in range(rows // CHUNK):
        for r in range(g * CHUNK, (g + 1) * CHUNK):
            y = lax.dot_general(left, parts[r], NN, preferred_element_type=F32)
            ready[:, r * size : (r + 1) * size] = (
                y[2 * vectors :] + y[vectors : 2 * vectors]
            ) + y[:vectors]
        part = pl.ds(g * CHUNK * size, CHUNK * size)
        copies.append(pltpu.make_async_copy(ready.at[:, part], out.at[:, part], sent.at[g]))
        copies[-1].start()
    for copy in copies:
        copy.wait()


def final(states, gram_a, gram_b, mapping, parts):
    rows, depth, size = parts.shape
    vectors = depth // 3
    return pl.pallas_call(
        functools.partial(final_kernel, float(states)),
        out_shape=jax.ShapeDtypeStruct((vectors, rows * size), F32),
        in_specs=[VM, VM, VM, VM],
        out_specs=HB,
        scratch_shapes=[
            pltpu.VMEM((vectors, rows * size), F32),
            pltpu.SemaphoreType.DMA((rows // CHUNK,)),
        ],
        compiler_params=params(8),
        cost_estimate=cost(6 * parts.size * vectors, 4 * parts.size),
        name="memberships",
    )(gram_a, gram_b, mapping, in_vmem(parts))


def body(transition_tiles, column_tiles, schur_basis, membership_map):
    rows = transition_tiles.shape[0]
    count = lax.axis_size("rows")
    me = lax.axis_index("rows")
    mates = [(i, i ^ 1) for i in range(count)]
    others = []
    for i in range(1, count - 1, 2):
        others += [(i, i + 1), (i + 1, i)]

    def swap(array, pairs):
        return lax.ppermute(array, "rows", pairs)

    limit = 11 * rows // 16
    where = jnp.stack([me * rows, me % 2]).astype(I32)
    columns = column_tiles.T
    mate, other = swap(schur_basis, mates), swap(schur_basis, others)
    turned, inverse, plan, wanted = prep(where, columns, transition_tiles)
    asked = swap(wanted, others)
    more = jnp.maximum(wanted[1, 0], asked[1, 0]) > limit
    image, sums = near_rows(plan, turned, inverse, schur_basis, mate, False, False)
    image, send, rest, sending = far_rows_first(
        limit, asked, plan, turned, inverse, other, sums, image
    )
    for step in range(1, PRODUCTS):
        last = step == PRODUCTS - 1
        mate, other = swap(image, mates), swap(send, others)
        extra = lax.cond(more, lambda x: swap(x, others), lambda x: x, rest)
        image, sums, *near = near_rows(plan, turned, inverse, image, mate, True, last)
        if last:
            parts, gram = far_rows_last(
                plan, turned, inverse, other, extra, near[0], sums, image
            )
        else:
            image, send, rest = far_rows(
                plan, turned, inverse, sending, other, extra, sums, image
            )
    distance = 1
    while distance < count:
        partner = swap(gram, [(i, i ^ distance) for i in range(count)])
        distance *= 2
        if distance < count:
            gram = gram + partner
    states = schur_basis.shape[1] * count
    return final(states, gram, partner, membership_map, parts)


def solution(mesh):
    return jax.shard_map(
        body,
        mesh=mesh,
        in_specs=(
            P(("groups", "rows"), None, None, None),
            P(("groups", "rows"), None),
            P(None, ("groups", "rows")),
            P("groups", None),
        ),
        out_specs=P(None, ("groups", "rows")),
        check_vma=False,
    )
```

time: 82.9 us -> 78.3 us (0.945)
  Pallas kernels: 24 us -> 21.4 us
  starting transfers between devices: 35.4 us -> 33.8 us
  waiting for transfers between devices: 9.08 us -> 7.95 us
    pallas_call x1, Pallas kernels: 9.73 us -> 7.59 us  [prep(): pl.pallas_call(prep_kernel, out_shape=(pltpu.VMEM((rows, slots * size, si...]
    ppermute x13, starting transfers between devices: 35.4 us -> 33.8 us  [swap(): return lax.ppermute(array, 'rows', pairs)]
    ppermute x13, waiting for transfers between devices: 9.08 us -> 7.95 us  [swap(): return lax.ppermute(array, 'rows', pairs)]
    slice x0 -> x2, local copies, waits for them, and re-layouts: none -> 1.09 us  [body(): more = jnp.maximum(wanted[1, 0], asked[1, 0]) > limit]
  transfers between devices with their start and end apart: 13 -> 13, of which waited for: 7 -> 6; matrix products, arithmetic and copies ran while one was open for 0% -> 1% of each run, Pallas kernels for 24% -> 23%
where the time goes in v6:
time: 78.3 us; the launch traced here: 78 us
  starting transfers between devices  33.8 us (43%)
  Pallas kernels  21.4 us (27%)
  local copies, waits for them, and re-layouts  13.2 us (17%)
  waiting for transfers between devices  7.95 us (10%)
  between operations  1.57 us (2%)
    ppermute x13, starting transfers between devices, swap(): return lax.ppermute(array, 'rows', pairs)  33.8 us
    unnamed x12, local copies, waits for them, and re-layouts  12.1 us
    pallas_call x4, Pallas kernels, near_rows(): pl.pallas_call(functools.partial(near_kernel, tile_major, last), out_shap...  10 us
    ppermute x13, waiting for transfers between devices, swap(): return lax.ppermute(array, 'rows', pairs)  7.95 us
    pallas_call x1, Pallas kernels, prep(): pl.pallas_call(prep_kernel, out_shape=(pltpu.VMEM((rows, slots * size, si...  7.59 us
    pallas_call x1, Pallas kernels, final(): pl.pallas_call(functools.partial(final_kernel, float(states)), out_shape=...  2.65 us
  transfers between devices with their start and end apart: 13, of which 6 were waited for; matrix products, arithmetic and copies ran while one was open for 1% of the time, Pallas kernels for 23%

profile of v6, /device:TPU:0, one launch (start us, length us, event | category | flops | bytes accessed | tf_op | source)
XLA Modules:
  0.0 78.0 jit_solution(4947398675131530846)
XLA Ops:
  0.0 0.0 copy-start.4
  0.0 0.5 collective-permute-start.5
  0.5 0.7 collective-permute-start.4
  1.2 0.1 pad_add_fusion.where
  1.2 7.6 %prep.1 = (bf16[64,640,128]{2,1,0:T(8,128)(2,1)S(1)}, f32[64,128]{1,0:T(8,128)S(1)}, s32[24,128]{1,0:T(8,128)S(4)}, s32[8,128]{1,0:T(8,128)S(1)}) custom-call(s32[2]{0:T(128)S(1)} %pad_add_fusion.where, s32[5,64]{1,0:T(8,128)} %bitcast.4, bf16[64,5,128,128]{3,2,1,0:T(8,128)(2,1)} %tiles.1), custom_call_target="tpu_custom_call" | custom-call | flops 167772160 | bytes 20971520 | tf_op jit(solution)/shard_map/prep/pallas_call | solution.py:154
  8.8 0.0 copy-start
  8.8 0.7 collective-permute-start.3
  9.5 0.0 collective-permute-done.5.mate
  9.5 0.0 copy-done.4
  9.5 2.4 %near_rows.4 = (bf16[64,32,128]{2,1,0:T(8,128)(2,1)S(1)}, f32[64,32,128]{2,1,0:T(8,128)S(1)}) custom-call(s32[24,128]{1,0:T(8,128)S(4)} %get-tuple-element.45.plan, bf16[64,640,128]{2,1,0:T(8,128)(2,1)S(1)} %get-tuple-element.46.turned, f32[64,128]{1,0:T(8,128)S(1)} %get-tuple-element.47.inverse, bf16[32,8192]{1,0:T(8,128)(2,1)S(1)} %copy-done.4, ...), custom_call_target="tpu_custom_call" | custom-call | flops 335544320 | bytes 10485760 | tf_op jit(solution)/shard_map/near_rows/pallas_call | solution.py:348
  11.9 0.0 collective-permute-done.3.asked
  11.9 0.0 collective-permute-done.4.other
  12.0 0.7 far_rows.4
  12.7 0.2 copy-done
  12.8 6.3 %collective-permute-start.7 = (bf16[64,32,128]{2,1,0:T(8,128)(2,1)S(1)}, bf16[64,32,128]{2,1,0:T(8,128)(2,1)S(1)}, u32[]{:S(2)}, u32[]{:S(2)}) collective-permute-start(bf16[64,32,128]{2,1,0:T(8,128)(2,1)S(1)} %get-tuple-element.54.own), channel_id=1, source_target_pairs={{0,1},{1,0},{2,3},{3,2},{4,5},{5,4},{6,7},{7,6},{8,9},{9,8},{10,11... | collective-permute-start | bytes 1572872 | tf_op jit(solution)/shard_map/ppermute | solution.py:512
  19.1 0.7 collective-permute-start.6
  19.8 0.5 slice.6
  20.3 0.6 slice.7
  22.2 0.0 collective-permute-done.7.mate
  22.3 0.0 copy-start.1
  22.3 4.0 %copy-done.1 = bf16[64,640,128]{2,1,0:T(8,128)(2,1)S(1)} copy-done((bf16[64,640,128]{2,1,0:T(8,128)(2,1)S(1)}, bf16[64,640,128]{2,1,0:T(8,128)(2,1)}, u32[]{:S(2)}) %copy-start.1) | copy-done | bytes 10485784
  26.2 2.3 %near_rows.5 = (bf16[64,32,128]{2,1,0:T(8,128)(2,1)S(1)}, f32[64,32,128]{2,1,0:T(8,128)S(1)}) custom-call(s32[24,128]{1,0:T(8,128)S(4)} %get-tuple-element.45.plan, bf16[64,640,128]{2,1,0:T(8,128)(2,1)S(1)} %copy-done.1, f32[64,128]{1,0:T(8,128)S(1)} %get-tuple-element.47.inverse, bf16[64,32,128]{2,1,0:T(8,128)(2,1)S(1)} %get-tuple-element.54.own, ...), custom_call_target="tpu_custom_call" | custom-call | flops 335544320 | bytes 10485760 | tf_op jit(solution)/shard_map/near_rows/pallas_call | solution.py:348
  28.5 0.0 collective-permute-done.6.other
  28.5 0.1 far_rows.5
  28.7 5.0 %collective-permute-start.9 = (bf16[64,32,128]{2,1,0:T(8,128)(2,1)S(1)}, bf16[64,32,128]{2,1,0:T(8,128)(2,1)S(1)}, u32[]{:S(2)}, u32[]{:S(2)}) collective-permute-start(bf16[64,32,128]{2,1,0:T(8,128)(2,1)S(1)} %get-tuple-element.59.own), channel_id=1, source_target_pairs={{0,1},{1,0},{2,3},{3,2},{4,5},{5,4},{6,7},{7,6},{8,9},{9,8},{10,11... | collective-permute-start | bytes 1572872 | tf_op jit(solution)/shard_map/ppermute | solution.py:512
  33.6 0.7 collective-permute-start.8
  34.3 0.8 %collective-permute-done.9.mate = bf16[64,32,128]{2,1,0:T(8,128)(2,1)S(1)} collective-permute-done((bf16[64,32,128]{2,1,0:T(8,128)(2,1)S(1)}, bf16[64,32,128]{2,1,0:T(8,128)(2,1)S(1)}, u32[]{:S(2)}, u32[]{:S(2)}) %collective-permute-start.9) | collective-permute-done | bytes 524320 | tf_op jit(solution)/shard_map/ppermute | solution.py:512
  35.2 0.0 copy-start.2
  35.2 4.0 %copy-done.2 = bf16[64,640,128]{2,1,0:T(8,128)(2,1)S(1)} copy-done((bf16[64,640,128]{2,1,0:T(8,128)(2,1)S(1)}, bf16[64,640,128]{2,1,0:T(8,128)(2,1)}, u32[]{:S(2)}) %copy-start.2) | copy-done | bytes 10485784
  39.2 2.3 %near_rows.6 = (bf16[64,32,128]{2,1,0:T(8,128)(2,1)S(1)}, f32[64,32,128]{2,1,0:T(8,128)S(1)}) custom-call(s32[24,128]{1,0:T(8,128)S(4)} %get-tuple-element.45.plan, bf16[64,640,128]{2,1,0:T(8,128)(2,1)S(1)} %copy-done.2, f32[64,128]{1,0:T(8,128)S(1)} %get-tuple-element.47.inverse, bf16[64,32,128]{2,1,0:T(8,128)(2,1)S(1)} %get-tuple-element.59.own, ...), custom_call_target="tpu_custom_call" | custom-call | flops 335544320 | bytes 10485760 | tf_op jit(solution)/shard_map/near_rows/pallas_call | solution.py:348
  41.4 0.0 collective-permute-done.8.other
  41.5 0.1 far_rows.6
  41.6 5.5 %collective-permute-start.11 = (bf16[64,32,128]{2,1,0:T(8,128)(2,1)S(1)}, bf16[64,32,128]{2,1,0:T(8,128)(2,1)S(1)}, u32[]{:S(2)}, u32[]{:S(2)}) collective-permute-start(bf16[64,32,128]{2,1,0:T(8,128)(2,1)S(1)} %get-tuple-element.64.own), channel_id=1, source_target_pairs={{0,1},{1,0},{2,3},{3,2},{4,5},{5,4},{6,7},{7,6},{8,9},{9,8},{10,11... | collective-permute-start | bytes 1572872 | tf_op jit(solution)/shard_map/ppermute | solution.py:512
  47.0 0.7 collective-permute-start.10
  47.7 0.8 %collective-permute-done.11.mate = bf16[64,32,128]{2,1,0:T(8,128)(2,1)S(1)} collective-permute-done((bf16[64,32,128]{2,1,0:T(8,128)(2,1)S(1)}, bf16[64,32,128]{2,1,0:T(8,128)(2,1)S(1)}, u32[]{:S(2)}, u32[]{:S(2)}) %collective-permute-start.11) | collective-permute-done | bytes 524320 | tf_op jit(solution)/shard_map/ppermute | solution.py:512
  48.6 0.0 copy-start.3
  48.6 4.0 %copy-done.3 = bf16[64,640,128]{2,1,0:T(8,128)(2,1)S(1)} copy-done((bf16[64,640,128]{2,1,0:T(8,128)(2,1)S(1)}, bf16[64,640,128]{2,1,0:T(8,128)(2,1)}, u32[]{:S(2)}) %copy-start.3) | copy-done | bytes 10485784
  52.6 0.0 copy-start.5
  52.6 3.0 %near_rows.7 = (bf16[64,96,128]{2,1,0:T(8,128)(2,1)S(1)}, f32[64,32,128]{2,1,0:T(8,128)S(1)}, f32[96,96]{1,0:T(8,128)S(1)}) custom-call(s32[24,128]{1,0:T(8,128)S(4)} %get-tuple-element.45.plan, bf16[64,640,128]{2,1,0:T(8,128)(2,1)S(1)} %copy-done.3, f32[64,128]{1,0:T(8,128)S(1)} %get-tuple-element.47.inverse, ...), custom_call_target="tpu_custom_call" | custom-call | flops 335544320 | bytes 10485760 | tf_op jit(solution)/shard_map/near_rows/pallas_call | solution.py:348
  55.6 0.0 collective-permute-done.10.other
  55.6 0.2 far_rows.7
  55.8 5.7 %collective-permute-start.12 = (f32[32,32]{1,0:T(8,128)S(1)}, f32[32,32]{1,0:T(8,128)S(1)}, u32[]{:S(2)}, u32[]{:S(2)}) collective-permute-start(f32[32,32]{1,0:T(8,128)S(1)} %get-tuple-element.68), channel_id=1, source_target_pairs={{0,1},{1,0},{2,3},{3,2},{4,5},{5,4},{6,7},{7,6},{8,9},{9,8},{10,11... | collective-permute-start | bytes 12296 | tf_op jit(solution)/shard_map/ppermute | solution.py:512
  61.5 0.8 %collective-permute-done.12 = f32[32,32]{1,0:T(8,128)S(1)} collective-permute-done((f32[32,32]{1,0:T(8,128)S(1)}, f32[32,32]{1,0:T(8,128)S(1)}, u32[]{:S(2)}, u32[]{:S(2)}) %collective-permute-start.12) | collective-permute-done | bytes 4128 | tf_op jit(solution)/shard_map/ppermute | solution.py:512
  62.4 2.7 %collective-permute-start.13 = (f32[32,32]{1,0:T(8,128)S(1)}, f32[32,32]{1,0:T(8,128)S(1)}, u32[]{:S(2)}, u32[]{:S(2)}) collective-permute-start(f32[32,32]{1,0:T(8,128)S(1)} %add.14), channel_id=1, source_target_pairs={{0,2},{1,3},{2,0},{3,1},{4,6},{5,7},{6,4},{7,5},{8,10},{9,11},{10,... | collective-permute-start | bytes 12296 | tf_op jit(solution)/shard_map/ppermute | solution.py:512
  65.1 1.7 %collective-permute-done.13 = f32[32,32]{1,0:T(8,128)S(1)} collective-permute-done((f32[32,32]{1,0:T(8,128)S(1)}, f32[32,32]{1,0:T(8,128)S(1)}, u32[]{:S(2)}, u32[]{:S(2)}) %collective-permute-start.13) | collective-permute-done | bytes 4128 | tf_op jit(solution)/shard_map/ppermute | solution.py:512
  66.8 1.8 %collective-permute-start.14 = (f32[32,32]{1,0:T(8,128)S(1)}, f32[32,32]{1,0:T(8,128)S(1)}, u32[]{:S(2)}, u32[]{:S(2)}) collective-permute-start(f32[32,32]{1,0:T(8,128)S(1)} %add.15), channel_id=1, source_target_pairs={{0,4},{1,5},{2,6},{3,7},{4,0},{5,1},{6,2},{7,3},{8,12},{9,13},{10,... | collective-permute-start | bytes 12296 | tf_op jit(solution)/shard_map/ppermute | solution.py:512
  68.6 2.0 %collective-permute-done.14 = f32[32,32]{1,0:T(8,128)S(1)} collective-permute-done((f32[32,32]{1,0:T(8,128)S(1)}, f32[32,32]{1,0:T(8,128)S(1)}, u32[]{:S(2)}, u32[]{:S(2)}) %collective-permute-start.14) | collective-permute-done | bytes 4128 | tf_op jit(solution)/shard_map/ppermute | solution.py:512
  70.6 3.0 %collective-permute-start.15 = (f32[32,32]{1,0:T(8,128)S(1)}, f32[32,32]{1,0:T(8,128)S(1)}, u32[]{:S(2)}, u32[]{:S(2)}) collective-permute-start(f32[32,32]{1,0:T(8,128)S(1)} %add.16.gram_a), channel_id=1, source_target_pairs={{0,8},{1,9},{2,10},{3,11},{4,12},{5,13},{6,14},{7,15},{8,0},{9,1},... | collective-permute-start | bytes 12296 | tf_op jit(solution)/shard_map/ppermute | solution.py:512
  73.6 1.7 %collective-permute-done.15.gram_b = f32[32,32]{1,0:T(8,128)S(1)} collective-permute-done((f32[32,32]{1,0:T(8,128)S(1)}, f32[32,32]{1,0:T(8,128)S(1)}, u32[]{:S(2)}, u32[]{:S(2)}) %collective-permute-start.15) | collective-permute-done | bytes 4128 | tf_op jit(solution)/shard_map/ppermute | solution.py:512
  75.3 0.0 copy-done.5
  75.3 2.7 %memberships.1 = f32[32,8192]{1,0:T(8,128)} custom-call(f32[32,32]{1,0:T(8,128)S(1)} %add.16.gram_a, f32[32,32]{1,0:T(8,128)S(1)} %collective-permute-done.15.gram_b, f32[32,32]{1,0:T(8,128)S(1)} %copy-done.5, bf16[64,96,128]{2,1,0:T(8,128)(2,1)S(1)} %get-tuple-element.69.parts), custom_call_target="tpu_custom_call" | custom-call | flops 150994944 | bytes 3145728 | tf_op jit(solution)/shard_map/memberships/pallas_call | solution.py:487
  (6 shorter events, 0.0 us)
Async XLA Ops:
  0.0 9.5 %copy-start.4 = (bf16[32,8192]{1,0:T(8,128)(2,1)S(1)}, bf16[32,8192]{1,0:T(8,128)(2,1)}, u32[]{:S(2)}) copy-start(bf16[32,8192]{1,0:T(8,128)(2,1)} %own.1) | copy-start | bytes 1572868
  0.0 9.5 %collective-permute-start.5 = (bf16[32,8192]{1,0:T(8,128)(2,1)}, bf16[32,8192]{1,0:T(8,128)(2,1)S(1)}, u32[]{:S(2)}, u32[]{:S(2)}) collective-permute-start(bf16[32,8192]{1,0:T(8,128)(2,1)} %own.1), channel_id=1, source_target_pairs={{0,1},{1,0},{2,3},{3,2},{4,5},{5,4},{6,7},{7,6},{8,9},{9,8},{10,11... | collective-permute-start | bytes 1572872 | tf_op jit(solution)/shard_map/ppermute | solution.py:512
  0.5 11.5 %collective-permute-start.4 = (bf16[32,8192]{1,0:T(8,128)(2,1)}, bf16[32,8192]{1,0:T(8,128)(2,1)S(1)}, u32[]{:S(2)}, u32[]{:S(2)}) collective-permute-start(bf16[32,8192]{1,0:T(8,128)(2,1)} %own.1), channel_id=1, source_target_pairs={{1,2},{2,1},{3,4},{4,3},{5,6},{6,5},{7,8},{8,7},{9,10},{10,9},{11,... | collective-permute-start | bytes 1572872 | tf_op jit(solution)/shard_map/ppermute | solution.py:512
  8.8 4.0 %copy-start = (bf16[64,640,128]{2,1,0:T(8,128)(2,1)}, bf16[64,640,128]{2,1,0:T(8,128)(2,1)S(1)}, u32[]{:S(2)}) copy-start(bf16[64,640,128]{2,1,0:T(8,128)(2,1)S(1)} %get-tuple-element.46.turned) | copy-start | bytes 31457284
  8.8 3.1 %collective-permute-start.3 = (s32[8,128]{1,0:T(8,128)S(1)}, s32[8,128]{1,0:T(8,128)S(1)}, u32[]{:S(2)}, u32[]{:S(2)}) collective-permute-start(s32[8,128]{1,0:T(8,128)S(1)} %get-tuple-element.48), channel_id=1, source_target_pairs={{1,2},{2,1},{3,4},{4,3},{5,6},{6,5},{7,8},{8,7},{9,10},{10,9},{11,... | collective-permute-start | bytes 12296 | tf_op jit(solution)/shard_map/ppermute | solution.py:512
  12.8 9.4 %collective-permute-start.7 = (bf16[64,32,128]{2,1,0:T(8,128)(2,1)S(1)}, bf16[64,32,128]{2,1,0:T(8,128)(2,1)S(1)}, u32[]{:S(2)}, u32[]{:S(2)}) collective-permute-start(bf16[64,32,128]{2,1,0:T(8,128)(2,1)S(1)} %get-tuple-element.54.own), channel_id=1, source_target_pairs={{0,1},{1,0},{2,3},{3,2},{4,5},{5,4},{6,7},{7,6},{8,9},{9,8},{10,11... | collective-permute-start | bytes 1572872 | tf_op jit(solution)/shard_map/ppermute | solution.py:512
  19.1 9.4 %collective-permute-start.6 = (bf16[44,32,128]{2,1,0:T(8,128)(2,1)S(1)}, bf16[44,32,128]{2,1,0:T(8,128)(2,1)S(1)}, u32[]{:S(2)}, u32[]{:S(2)}) collective-permute-start(bf16[44,32,128]{2,1,0:T(8,128)(2,1)S(1)} %get-tuple-element.52), channel_id=1, source_target_pairs={{1,2},{2,1},{3,4},{4,3},{5,6},{6,5},{7,8},{8,7},{9,10},{10,9},{11,... | collective-permute-start | bytes 1081352 | tf_op jit(solution)/shard_map/ppermute | solution.py:512
  22.3 4.0 %copy-start.1 = (bf16[64,640,128]{2,1,0:T(8,128)(2,1)S(1)}, bf16[64,640,128]{2,1,0:T(8,128)(2,1)}, u32[]{:S(2)}) copy-start(bf16[64,640,128]{2,1,0:T(8,128)(2,1)} %copy-done) | copy-start | bytes 31457284
  28.7 6.5 %collective-permute-start.9 = (bf16[64,32,128]{2,1,0:T(8,128)(2,1)S(1)}, bf16[64,32,128]{2,1,0:T(8,128)(2,1)S(1)}, u32[]{:S(2)}, u32[]{:S(2)}) collective-permute-start(bf16[64,32,128]{2,1,0:T(8,128)(2,1)S(1)} %get-tuple-element.59.own), channel_id=1, source_target_pairs={{0,1},{1,0},{2,3},{3,2},{4,5},{5,4},{6,7},{7,6},{8,9},{9,8},{10,11... | collective-permute-start | bytes 1572872 | tf_op jit(solution)/shard_map/ppermute | solution.py:512
  33.6 7.8 %collective-permute-start.8 = (bf16[44,32,128]{2,1,0:T(8,128)(2,1)S(1)}, bf16[44,32,128]{2,1,0:T(8,128)(2,1)S(1)}, u32[]{:S(2)}, u32[]{:S(2)}) collective-permute-start(bf16[44,32,128]{2,1,0:T(8,128)(2,1)S(1)} %get-tuple-element.57), channel_id=1, source_target_pairs={{1,2},{2,1},{3,4},{4,3},{5,6},{6,5},{7,8},{8,7},{9,10},{10,9},{11,... | collective-permute-start | bytes 1081352 | tf_op jit(solution)/shard_map/ppermute | solution.py:512
  35.2 4.0 %copy-start.2 = (bf16[64,640,128]{2,1,0:T(8,128)(2,1)S(1)}, bf16[64,640,128]{2,1,0:T(8,128)(2,1)}, u32[]{:S(2)}) copy-start(bf16[64,640,128]{2,1,0:T(8,128)(2,1)} %copy-done) | copy-start | bytes 31457284
  41.6 7.0 %collective-permute-start.11 = (bf16[64,32,128]{2,1,0:T(8,128)(2,1)S(1)}, bf16[64,32,128]{2,1,0:T(8,128)(2,1)S(1)}, u32[]{:S(2)}, u32[]{:S(2)}) collective-permute-start(bf16[64,32,128]{2,1,0:T(8,128)(2,1)S(1)} %get-tuple-element.64.own), channel_id=1, source_target_pairs={{0,1},{1,0},{2,3},{3,2},{4,5},{5,4},{6,7},{7,6},{8,9},{9,8},{10,11... | collective-permute-start | bytes 1572872 | tf_op jit(solution)/shard_map/ppermute | solution.py:512
  47.0 8.6 %collective-permute-start.10 = (bf16[44,32,128]{2,1,0:T(8,128)(2,1)S(1)}, bf16[44,32,128]{2,1,0:T(8,128)(2,1)S(1)}, u32[]{:S(2)}, u32[]{:S(2)}) collective-permute-start(bf16[44,32,128]{2,1,0:T(8,128)(2,1)S(1)} %get-tuple-element.62), channel_id=1, source_target_pairs={{1,2},{2,1},{3,4},{4,3},{5,6},{6,5},{7,8},{8,7},{9,10},{10,9},{11,... | collective-permute-start | bytes 1081352 | tf_op jit(solution)/shard_map/ppermute | solution.py:512
  48.6 4.0 %copy-start.3 = (bf16[64,640,128]{2,1,0:T(8,128)(2,1)S(1)}, bf16[64,640,128]{2,1,0:T(8,128)(2,1)}, u32[]{:S(2)}) copy-start(bf16[64,640,128]{2,1,0:T(8,128)(2,1)} %copy-done) | copy-start | bytes 31457284
  52.6 22.8 %copy-start.5 = (f32[32,32]{1,0:T(8,128)S(1)}, f32[32,32]{1,0:T(8,128)}, u32[]{:S(2)}) copy-start(f32[32,32]{1,0:T(8,128)} %mapping.1) | copy-start | bytes 12292
  55.8 6.6 %collective-permute-start.12 = (f32[32,32]{1,0:T(8,128)S(1)}, f32[32,32]{1,0:T(8,128)S(1)}, u32[]{:S(2)}, u32[]{:S(2)}) collective-permute-start(f32[32,32]{1,0:T(8,128)S(1)} %get-tuple-element.68), channel_id=1, source_target_pairs={{0,1},{1,0},{2,3},{3,2},{4,5},{5,4},{6,7},{7,6},{8,9},{9,8},{10,11... | collective-permute-start | bytes 12296 | tf_op jit(solution)/shard_map/ppermute | solution.py:512
  62.4 4.4 %collective-permute-start.13 = (f32[32,32]{1,0:T(8,128)S(1)}, f32[32,32]{1,0:T(8,128)S(1)}, u32[]{:S(2)}, u32[]{:S(2)}) collective-permute-start(f32[32,32]{1,0:T(8,128)S(1)} %add.14), channel_id=1, source_target_pairs={{0,2},{1,3},{2,0},{3,1},{4,6},{5,7},{6,4},{7,5},{8,10},{9,11},{10,... | collective-permute-start | bytes 12296 | tf_op jit(solution)/shard_map/ppermute | solution.py:512
  66.8 3.7 %collective-permute-start.14 = (f32[32,32]{1,0:T(8,128)S(1)}, f32[32,32]{1,0:T(8,128)S(1)}, u32[]{:S(2)}, u32[]{:S(2)}) collective-permute-start(f32[32,32]{1,0:T(8,128)S(1)} %add.15), channel_id=1, source_target_pairs={{0,4},{1,5},{2,6},{3,7},{4,0},{5,1},{6,2},{7,3},{8,12},{9,13},{10,... | collective-permute-start | bytes 12296 | tf_op jit(solution)/shard_map/ppermute | solution.py:512
  70.6 4.7 %collective-permute-start.15 = (f32[32,32]{1,0:T(8,128)S(1)}, f32[32,32]{1,0:T(8,128)S(1)}, u32[]{:S(2)}, u32[]{:S(2)}) collective-permute-start(f32[32,32]{1,0:T(8,128)S(1)} %add.16.gram_a), channel_id=1, source_target_pairs={{0,8},{1,9},{2,10},{3,11},{4,12},{5,13},{6,14},{7,15},{8,0},{9,1},... | collective-permute-start | bytes 12296 | tf_op jit(solution)/shard_map/ppermute | solution.py:512

commit v7 on v6

--- a/solution.py
+++ b/solution.py
@@ -54,7 +54,7 @@
 
 
 def plan_height(slots):
-    return (lines(slots)[-1] + 2 + 7) // 8 * 8
+    return (lines(slots)[-1] + 3 + 7) // 8 * 8
 
 
 def draft_plan(first, parity, columns, draft, wanted):
@@ -78,7 +78,9 @@
     mark, rank = ranks(functools.reduce(jnp.add, equal))
     here = jnp.where((mark > 0.5) & (rank.astype(I32) == lane), h, 0)
     wanted[0:1, 0:rows] = jnp.sum(here.astype(F32), axis=0, keepdims=True).astype(I32)
-    wanted[1:2, 0:rows] = jnp.sum(mark, axis=0, keepdims=True).astype(I32)
+    read = jnp.sum(mark, axis=0, keepdims=True).astype(I32)
+    wanted[1:2, 0:rows] = read
+    draft[reads + 2 : reads + 3, 0:rows] = read
     none = jnp.zeros((1, rows), I32)
     seen = none
     tiles, places, named = [[none + start] * (slots - 1) for start in (rows, rows, 0)]
@@ -292,15 +294,13 @@
     lax.fori_loop(0, (touched + BLOCK - 1) // BLOCK, step, 0)
 
 
-def pack(image, sending, send, rest):
-    limit = send.shape[0]
-    for k in range(image.shape[0]):
-        target = send.at[k] if k < limit else rest.at[k - limit]
-        target[...] = image[sending[0, k]]
+def pack(image, sending, send):
+    for k in range(send.shape[0]):
+        send[k] = image[sending[0, k]]
 
 
 def far_first_kernel(
-    asked, plan, turned, inverse, other, sums, i_in, image, send, rest, sending, panel, done
+    asked, plan, turned, inverse, other, sums, i_in, image, send, sending, panel, done
 ):
     rows, depth, size = turned.shape
     copy = pltpu.make_async_copy(asked, sending, done)
@@ -309,30 +309,38 @@
     base = lines(depth // size)[0]
     far_part(base, plan, turned, inverse, sums, panel, image, None)
     copy.wait()
-    pack(image, sending, send, rest)
-
-
-def far_kernel(
-    sending, plan, turned, inverse, other, extra, sums, i_in, image, send, rest, panel
-):
+    pack(image, sending, send)
+
+
+def far_kernel(sending, plan, turned, inverse, other, sums, i_in, image, send, panel):
     rows, depth, size = turned.shape
     fill(panel, 0, other, True)
-    fill(panel, other.shape[0], extra, True)
     base = lines(depth // size)[1]
     far_part(base, plan, turned, inverse, sums, panel, image, None)
-    pack(image, sending, send, rest)
+    pack(image, sending, send)
+
+
+def far_whole_kernel(tile_major, plan, turned, inverse, other, sums, i_in, image, panel):
+    rows, depth, size = turned.shape
+    fill(panel, 0, other, tile_major)
+    base = lines(depth // size)[0]
+    far_part(base, plan, turned, inverse, sums, panel, image, None)
 
 
 def far_last_kernel(
-    plan, turned, inverse, other, extra, near, sums, i_in, image, gram, panel, squares
+    whole, sending, plan, turned, inverse, other, near, sums, i_in, image, gram, panel, squares
 ):
     rows, depth, size = turned.shape
+    slots = depth // size
+    vectors = gram.shape[1]
     fill(panel, 0, other, True)
-    fill(panel, other.shape[0], extra, True)
     squares[...] = near[...]
-    base = lines(depth // size)[1]
+    base = lines(slots)[0 if whole else 1]
     far_part(base, plan, turned, inverse, sums, panel, image, squares)
-    gram[...] = fold(squares[...], gram.shape[0])
+    gram[0:vectors] = fold(squares[...], vectors)
+    read = plan[lines(slots)[-1] + 2, 0]
+    short = jnp.maximum(read, sending[1, 0]) > other.shape[0]
+    gram[vectors:] = jnp.zeros((8, vectors), F32) + jnp.where(short, 1.0, 0.0)
 
 
 def near_rows(plan, turned, inverse, own, mate, tile_major, last):
@@ -382,38 +390,45 @@
         far_first_kernel,
         (in_vmem(asked), plan, *map(in_vmem, (turned, inverse, other, sums, image))),
         [VM, SM] + [VM] * 5,
-        (
-            of(image),
-            pltpu.VMEM((limit, vectors, size), BF16),
-            pltpu.VMEM((rows - limit, vectors, size), BF16),
-            pltpu.SMEM((8, 128), I32),
-        ),
-        (VM, VM, VM, SM),
+        (of(image), pltpu.VMEM((limit, vectors, size), BF16), pltpu.SMEM((8, 128), I32)),
+        (VM, VM, SM),
         turned,
         vectors,
         [pltpu.SemaphoreType.DMA],
     )
 
 
-def far_rows(plan, turned, inverse, sending, other, extra, sums, image):
+def far_rows(plan, turned, inverse, sending, other, sums, image):
     return far_call(
         far_kernel,
-        (sending, plan, *map(in_vmem, (turned, inverse, other, extra, sums, image))),
-        [SM, SM] + [VM] * 6,
-        (of(image), of(other), of(extra)),
-        (VM,) * 3,
+        (sending, plan, *map(in_vmem, (turned, inverse, other, sums, image))),
+        [SM, SM] + [VM] * 5,
+        (of(image), of(other)),
+        (VM,) * 2,
         turned,
         image.shape[1],
     )
 
 
-def far_rows_last(plan, turned, inverse, other, extra, near, sums, image):
+def far_rows_whole(plan, turned, inverse, other, sums, image, tile_major):
+    return far_call(
+        functools.partial(far_whole_kernel, tile_major),
+        (plan, *map(in_vmem, (turned, inverse, other, sums, image))),
+        [SM] + [VM] * 5,
+        (of(image),),
+        (VM,),
+        turned,
+        image.shape[1],
+    )[0]
+
+
+def far_rows_last(whole, plan, turned, inverse, sending, other, near, sums, image):
     vectors = near.shape[0] // 3
     return far_call(
-        far_last_kernel,
-        (plan, *map(in_vmem, (turned, inverse, other, extra, near, sums, image))),
-        [SM] + [VM] * 7,
-        (of(image), pltpu.VMEM((vectors, vectors), F32)),
+        functools.partial(far_last_kernel, whole),
+        (sending, plan, *map(in_vmem, (turned, inverse, other, near, sums, image))),
+        [SM, SM] + [VM] * 6,
+        (of(image), pltpu.VMEM((vectors + 8, vectors), F32)),
         (VM,) * 2,
         turned,
         vectors,
@@ -446,10 +461,12 @@
     return work[:, count:] * lax.rsqrt(pivots)
 
 
-def final_kernel(states, gram_a, gram_b, mapping, parts, out, ready, sent):
+def final_kernel(states, gram_a, gram_b, mapping, parts, out, short, ready, sent):
     rows, depth, size = parts.shape
     vectors = depth // 3
-    factor = inverse_factor((gram_a[...] + gram_b[...]) / states)
+    total = gram_a[...] + gram_b[...]
+    short[0] = jnp.max(total[vectors:]).astype(I32)
+    factor = inverse_factor(total[:vectors] / states)
     combined = lax.dot_general(
         mapping[...],
         factor,
@@ -486,9 +503,12 @@
     vectors = depth // 3
     return pl.pallas_call(
         functools.partial(final_kernel, float(states)),
-        out_shape=jax.ShapeDtypeStruct((vectors, rows * size), F32),
+        out_shape=(
+            jax.ShapeDtypeStruct((vectors, rows * size), F32),
+            pltpu.SMEM((1,), I32),
+        ),
         in_specs=[VM, VM, VM, VM],
-        out_specs=HB,
+        out_specs=(HB, SM),
         scratch_shapes=[
             pltpu.VMEM((vectors, rows * size), F32),
             pltpu.SemaphoreType.DMA((rows // CHUNK,)),
@@ -499,7 +519,7 @@
     )(gram_a, gram_b, mapping, in_vmem(parts))
 
 
-def body(transition_tiles, column_tiles, schur_basis, membership_map):
+def memberships(whole, transition_tiles, column_tiles, schur_basis, membership_map):
     rows = transition_tiles.shape[0]
     count = lax.axis_size("rows")
     me = lax.axis_index("rows")
@@ -517,24 +537,26 @@
     mate, other = swap(schur_basis, mates), swap(schur_basis, others)
     turned, inverse, plan, wanted = prep(where, columns, transition_tiles)
     asked = swap(wanted, others)
-    more = jnp.maximum(wanted[1, 0], asked[1, 0]) > limit
     image, sums = near_rows(plan, turned, inverse, schur_basis, mate, False, False)
-    image, send, rest, sending = far_rows_first(
-        limit, asked, plan, turned, inverse, other, sums, image
-    )
+    if whole:
+        image = send = far_rows_whole(plan, turned, inverse, other, sums, image, False)
+        sending = asked
+    else:
+        image, send, sending = far_rows_first(
+            limit, asked, plan, turned, inverse, other, sums, image
+        )
     for step in range(1, PRODUCTS):
         last = step == PRODUCTS - 1
         mate, other = swap(image, mates), swap(send, others)
-        extra = lax.cond(more, lambda x: swap(x, others), lambda x: x, rest)
         image, sums, *near = near_rows(plan, turned, inverse, image, mate, True, last)
         if last:
             parts, gram = far_rows_last(
-                plan, turned, inverse, other, extra, near[0], sums, image
+                whole, plan, turned, inverse, sending, other, near[0], sums, image
             )
+        elif whole:
+            image = send = far_rows_whole(plan, turned, inverse, other, sums, image, True)
         else:
-            image, send, rest = far_rows(
-                plan, turned, inverse, sending, other, extra, sums, image
-            )
+            image, send = far_rows(plan, turned, inverse, sending, other, sums, image)
     distance = 1
     while distance < count:
         partner = swap(gram, [(i, i ^ distance) for i in range(count)])
@@ -543,6 +565,18 @@
             gram = gram + partner
     states = schur_basis.shape[1] * count
     return final(states, gram, partner, membership_map, parts)
+
+
+def body(transition_tiles, column_tiles, schur_basis, membership_map):
+    arguments = transition_tiles, column_tiles, schur_basis, membership_map
+    out, short = memberships(False, *arguments)
+    return lax.cond(
+        short[0] > 0,
+        lambda *given: memberships(True, *given[:4])[0],
+        lambda *given: given[4],
+        *arguments,
+        out,
+    )
 
 
 def solution(mesh):

time: 78.3 us -> 78.6 us (level)
  local copies, waits for them, and re-layouts: 13.2 us -> 0.01 us
  starting transfers between devices: 33.8 us -> 46.8 us
  waiting for transfers between devices: 7.95 us -> 9.35 us
  between operations: 1.57 us -> 0.38 us
    ppermute x13, starting transfers between devices: 33.8 us -> 46.8 us  [swap(): return lax.ppermute(array, 'rows', pairs)]
    unnamed x12 -> x4, local copies, waits for them, and re-layouts: 12.1 us -> 0.01 us
    ppermute x13, waiting for transfers between devices: 7.95 us -> 9.35 us  [swap(): return lax.ppermute(array, 'rows', pairs)]
    slice x2 -> x0, local copies, waits for them, and re-layouts: 1.09 us -> none  [body(): more = jnp.maximum(wanted[1, 0], asked[1, 0]) > limit]
  transfers between devices with their start and end apart: 13 -> 13, of which waited for: 6 -> 7; matrix products, arithmetic and copies ran while one was open for 1% -> 0% of each run, Pallas kernels for 23% -> 23%
where the time goes in v7:
time: 78.6 us; the launch traced here: 78.2 us
  starting transfers between devices  46.8 us (60%)
  Pallas kernels  21.3 us (27%)
  waiting for transfers between devices  9.35 us (12%)
    ppermute x13, starting transfers between devices, swap(): return lax.ppermute(array, 'rows', pairs)  46.8 us
    pallas_call x4, Pallas kernels, near_rows(): pl.pallas_call(functools.partial(near_kernel, tile_major, last), out_shap...  10 us
    ppermute x13, waiting for transfers between devices, swap(): return lax.ppermute(array, 'rows', pairs)  9.35 us
    pallas_call x1, Pallas kernels, prep(): pl.pallas_call(prep_kernel, out_shape=(pltpu.VMEM((rows, slots * size, si...  7.63 us
    pallas_call x1, Pallas kernels, final(): pl.pallas_call(functools.partial(final_kernel, float(states)), out_shape=...  2.65 us
  transfers between devices with their start and end apart: 13, of which 7 were waited for; matrix products, arithmetic and copies ran while one was open for 0% of the time, Pallas kernels for 23%

profile of v7, /device:TPU:0, one launch (start us, length us, event | category | flops | bytes accessed | tf_op | source)
XLA Modules:
  0.0 78.2 jit_solution(16882417986317270313)
XLA Ops:
  0.0 0.5 collective-permute-start.15
  0.5 0.7 collective-permute-start.14
  1.2 0.1 pad_add_fusion.1.where
  1.2 0.0 copy-start
  1.2 7.6 %prep.3 = (bf16[64,640,128]{2,1,0:T(8,128)(2,1)S(1)}, f32[64,128]{1,0:T(8,128)S(1)}, s32[24,128]{1,0:T(8,128)S(4)}, s32[8,128]{1,0:T(8,128)S(1)}) custom-call(s32[2]{0:T(128)S(1)} %pad_add_fusion.1.where, s32[5,64]{1,0:T(8,128)} %bitcast.7, bf16[64,5,128,128]{3,2,1,0:T(8,128)(2,1)} %tiles.1), custom_call_target="tpu_custom_call" | custom-call | flops 167772160 | bytes 20971520 | tf_op jit(solution)/shard_map/prep/pallas_call | solution.py:156
  8.9 0.7 collective-permute-start.13
  9.5 0.0 collective-permute-done.15.mate
  9.5 0.0 copy-done
  9.6 2.4 %near_rows.12 = (bf16[64,32,128]{2,1,0:T(8,128)(2,1)S(1)}, f32[64,32,128]{2,1,0:T(8,128)S(1)}) custom-call(s32[24,128]{1,0:T(8,128)S(4)} %get-tuple-element.62.plan, bf16[64,640,128]{2,1,0:T(8,128)(2,1)S(1)} %get-tuple-element.63.turned, f32[64,128]{1,0:T(8,128)S(1)} %get-tuple-element.64.inverse, bf16[32,8192]{1,0:T(8,128)(2,1)S(1)} %copy-done, ...), custom_call_target="tpu_custom_call" | custom-call | flops 335544320 | bytes 10485760 | tf_op jit(solution)/shard_map/near_rows/pallas_call | solution.py:356
  12.0 0.0 collective-permute-done.13.asked
  12.0 0.0 collective-permute-done.14.other
  12.0 0.7 far_rows.12
  12.7 6.3 %collective-permute-start.17 = (bf16[64,32,128]{2,1,0:T(8,128)(2,1)S(1)}, bf16[64,32,128]{2,1,0:T(8,128)(2,1)S(1)}, u32[]{:S(2)}, u32[]{:S(2)}) collective-permute-start(bf16[64,32,128]{2,1,0:T(8,128)(2,1)S(1)} %get-tuple-element.69.own), channel_id=1, source_target_pairs={{0,1},{1,0},{2,3},{3,2},{4,5},{5,4},{6,7},{7,6},{8,9},{9,8},{10,11... | collective-permute-start | bytes 1572872 | tf_op jit(solution)/shard_map/ppermute | solution.py:532
  19.0 0.7 collective-permute-start.16
  19.7 0.9 %collective-permute-done.17.mate = bf16[64,32,128]{2,1,0:T(8,128)(2,1)S(1)} collective-permute-done((bf16[64,32,128]{2,1,0:T(8,128)(2,1)S(1)}, bf16[64,32,128]{2,1,0:T(8,128)(2,1)S(1)}, u32[]{:S(2)}, u32[]{:S(2)}) %collective-permute-start.17) | collective-permute-done | bytes 524320 | tf_op jit(solution)/shard_map/ppermute | solution.py:532
  20.5 2.3 %near_rows.13 = (bf16[64,32,128]{2,1,0:T(8,128)(2,1)S(1)}, f32[64,32,128]{2,1,0:T(8,128)S(1)}) custom-call(s32[24,128]{1,0:T(8,128)S(4)} %get-tuple-element.62.plan, bf16[64,640,128]{2,1,0:T(8,128)(2,1)S(1)} %get-tuple-element.63.turned, f32[64,128]{1,0:T(8,128)S(1)} %get-tuple-element.64.inverse, bf16[64,32,128]{2,1,0:T(8,128)(2,1)S(1)} %get-tuple-element.69.own, ...), custom_call_target="tpu_custom_call" | custom-call | flops 335544320 | bytes 10485760 | tf_op jit(solution)/shard_map/near_rows/pallas_call | solution.py:356
  22.8 0.0 collective-permute-done.16.other
  22.8 0.1 far_rows.13
  22.9 10.0 %collective-permute-start.19 = (bf16[64,32,128]{2,1,0:T(8,128)(2,1)S(1)}, bf16[64,32,128]{2,1,0:T(8,128)(2,1)S(1)}, u32[]{:S(2)}, u32[]{:S(2)}) collective-permute-start(bf16[64,32,128]{2,1,0:T(8,128)(2,1)S(1)} %get-tuple-element.73.own), channel_id=1, source_target_pairs={{0,1},{1,0},{2,3},{3,2},{4,5},{5,4},{6,7},{7,6},{8,9},{9,8},{10,11... | collective-permute-start | bytes 1572872 | tf_op jit(solution)/shard_map/ppermute | solution.py:532
  33.0 0.7 collective-permute-start.18
  33.6 0.9 %collective-permute-done.19.mate = bf16[64,32,128]{2,1,0:T(8,128)(2,1)S(1)} collective-permute-done((bf16[64,32,128]{2,1,0:T(8,128)(2,1)S(1)}, bf16[64,32,128]{2,1,0:T(8,128)(2,1)S(1)}, u32[]{:S(2)}, u32[]{:S(2)}) %collective-permute-start.19) | collective-permute-done | bytes 524320 | tf_op jit(solution)/shard_map/ppermute | solution.py:532
  34.5 2.3 %near_rows.14 = (bf16[64,32,128]{2,1,0:T(8,128)(2,1)S(1)}, f32[64,32,128]{2,1,0:T(8,128)S(1)}) custom-call(s32[24,128]{1,0:T(8,128)S(4)} %get-tuple-element.62.plan, bf16[64,640,128]{2,1,0:T(8,128)(2,1)S(1)} %get-tuple-element.63.turned, f32[64,128]{1,0:T(8,128)S(1)} %get-tuple-element.64.inverse, bf16[64,32,128]{2,1,0:T(8,128)(2,1)S(1)} %get-tuple-element.73.own, ...), custom_call_target="tpu_custom_call" | custom-call | flops 335544320 | bytes 10485760 | tf_op jit(solution)/shard_map/near_rows/pallas_call | solution.py:356
  36.8 0.0 collective-permute-done.18.other
  36.8 0.1 far_rows.14
  36.9 9.9 %collective-permute-start.21 = (bf16[64,32,128]{2,1,0:T(8,128)(2,1)S(1)}, bf16[64,32,128]{2,1,0:T(8,128)(2,1)S(1)}, u32[]{:S(2)}, u32[]{:S(2)}) collective-permute-start(bf16[64,32,128]{2,1,0:T(8,128)(2,1)S(1)} %get-tuple-element.77.own), channel_id=1, source_target_pairs={{0,1},{1,0},{2,3},{3,2},{4,5},{5,4},{6,7},{7,6},{8,9},{9,8},{10,11... | collective-permute-start | bytes 1572872 | tf_op jit(solution)/shard_map/ppermute | solution.py:532
  46.8 0.7 collective-permute-start.20
  47.5 0.9 %collective-permute-done.21.mate = bf16[64,32,128]{2,1,0:T(8,128)(2,1)S(1)} collective-permute-done((bf16[64,32,128]{2,1,0:T(8,128)(2,1)S(1)}, bf16[64,32,128]{2,1,0:T(8,128)(2,1)S(1)}, u32[]{:S(2)}, u32[]{:S(2)}) %collective-permute-start.21) | collective-permute-done | bytes 524320 | tf_op jit(solution)/shard_map/ppermute | solution.py:532
  48.3 3.0 %near_rows.15 = (bf16[64,96,128]{2,1,0:T(8,128)(2,1)S(1)}, f32[64,32,128]{2,1,0:T(8,128)S(1)}, f32[96,96]{1,0:T(8,128)S(1)}) custom-call(s32[24,128]{1,0:T(8,128)S(4)} %get-tuple-element.62.plan, bf16[64,640,128]{2,1,0:T(8,128)(2,1)S(1)} %get-tuple-element.63.turned, f32[64,128]{1,0:T(8,128)S(1)} %get-tuple-element.64.inverse, ...), custom_call_target="tpu_custom_call" | custom-call | flops 335544320 | bytes 10485760 | tf_op jit(solution)/shard_map/near_rows/pallas_call | solution.py:356
  51.4 0.0 collective-permute-done.20.other
  51.4 0.0 copy-start.1
  51.4 0.2 far_rows.15
  51.6 9.6 %collective-permute-start.22 = (f32[40,32]{1,0:T(8,128)S(1)}, f32[40,32]{1,0:T(8,128)S(1)}, u32[]{:S(2)}, u32[]{:S(2)}) collective-permute-start(f32[40,32]{1,0:T(8,128)S(1)} %get-tuple-element.81), channel_id=1, source_target_pairs={{0,1},{1,0},{2,3},{3,2},{4,5},{5,4},{6,7},{7,6},{8,9},{9,8},{10,11... | collective-permute-start | bytes 15368 | tf_op jit(solution)/shard_map/ppermute | solution.py:532
  61.2 0.8 %collective-permute-done.22 = f32[40,32]{1,0:T(8,128)S(1)} collective-permute-done((f32[40,32]{1,0:T(8,128)S(1)}, f32[40,32]{1,0:T(8,128)S(1)}, u32[]{:S(2)}, u32[]{:S(2)}) %collective-permute-start.22) | collective-permute-done | bytes 5152 | tf_op jit(solution)/shard_map/ppermute | solution.py:532
  62.1 2.6 %collective-permute-start.23 = (f32[40,32]{1,0:T(8,128)S(1)}, f32[40,32]{1,0:T(8,128)S(1)}, u32[]{:S(2)}, u32[]{:S(2)}) collective-permute-start(f32[40,32]{1,0:T(8,128)S(1)} %add.26), channel_id=1, source_target_pairs={{0,2},{1,3},{2,0},{3,1},{4,6},{5,7},{6,4},{7,5},{8,10},{9,11},{10,... | collective-permute-start | bytes 15368 | tf_op jit(solution)/shard_map/ppermute | solution.py:532
  64.7 1.8 %collective-permute-done.23 = f32[40,32]{1,0:T(8,128)S(1)} collective-permute-done((f32[40,32]{1,0:T(8,128)S(1)}, f32[40,32]{1,0:T(8,128)S(1)}, u32[]{:S(2)}, u32[]{:S(2)}) %collective-permute-start.23) | collective-permute-done | bytes 5152 | tf_op jit(solution)/shard_map/ppermute | solution.py:532
  66.5 2.2 %collective-permute-start.24 = (f32[40,32]{1,0:T(8,128)S(1)}, f32[40,32]{1,0:T(8,128)S(1)}, u32[]{:S(2)}, u32[]{:S(2)}) collective-permute-start(f32[40,32]{1,0:T(8,128)S(1)} %add.27), channel_id=1, source_target_pairs={{0,4},{1,5},{2,6},{3,7},{4,0},{5,1},{6,2},{7,3},{8,12},{9,13},{10,... | collective-permute-start | bytes 15368 | tf_op jit(solution)/shard_map/ppermute | solution.py:532
  68.7 1.8 %collective-permute-done.24 = f32[40,32]{1,0:T(8,128)S(1)} collective-permute-done((f32[40,32]{1,0:T(8,128)S(1)}, f32[40,32]{1,0:T(8,128)S(1)}, u32[]{:S(2)}, u32[]{:S(2)}) %collective-permute-start.24) | collective-permute-done | bytes 5152 | tf_op jit(solution)/shard_map/ppermute | solution.py:532
  70.4 2.3 %collective-permute-start.25 = (f32[40,32]{1,0:T(8,128)S(1)}, f32[40,32]{1,0:T(8,128)S(1)}, u32[]{:S(2)}, u32[]{:S(2)}) collective-permute-start(f32[40,32]{1,0:T(8,128)S(1)} %add.28.gram_a), channel_id=1, source_target_pairs={{0,8},{1,9},{2,10},{3,11},{4,12},{5,13},{6,14},{7,15},{8,0},{9,1},... | collective-permute-start | bytes 15368 | tf_op jit(solution)/shard_map/ppermute | solution.py:532
  72.7 2.4 %collective-permute-done.25.gram_b = f32[40,32]{1,0:T(8,128)S(1)} collective-permute-done((f32[40,32]{1,0:T(8,128)S(1)}, f32[40,32]{1,0:T(8,128)S(1)}, u32[]{:S(2)}, u32[]{:S(2)}) %collective-permute-start.25) | collective-permute-done | bytes 5152 | tf_op jit(solution)/shard_map/ppermute | solution.py:532
  75.1 0.0 copy-done.1
  75.1 2.7 %memberships.3 = (f32[32,8192]{1,0:T(8,128)}, s32[1]{0:T(128)S(4)}) custom-call(f32[40,32]{1,0:T(8,128)S(1)} %add.28.gram_a, f32[40,32]{1,0:T(8,128)S(1)} %collective-permute-done.25.gram_b, f32[32,32]{1,0:T(8,128)S(1)} %copy-done.1, bf16[64,96,128]{2,1,0:T(8,128)(2,1)S(1)} %get-tuple-element.82.parts), custom_call_target="tpu_custom_call" | custom-call | flops 150994944 | bytes 3145728 | tf_op jit(solution)/shard_map/memberships/pallas_call | solution.py:504
  77.8 0.2 conditional.1
  (3 shorter events, 0.0 us)
Async XLA Ops:
  0.0 9.5 %collective-permute-start.15 = (bf16[32,8192]{1,0:T(8,128)(2,1)}, bf16[32,8192]{1,0:T(8,128)(2,1)S(1)}, u32[]{:S(2)}, u32[]{:S(2)}) collective-permute-start(bf16[32,8192]{1,0:T(8,128)(2,1)} %own.1), channel_id=1, source_target_pairs={{0,1},{1,0},{2,3},{3,2},{4,5},{5,4},{6,7},{7,6},{8,9},{9,8},{10,11... | collective-permute-start | bytes 1572872 | tf_op jit(solution)/shard_map/ppermute | solution.py:532
  0.5 11.5 %collective-permute-start.14 = (bf16[32,8192]{1,0:T(8,128)(2,1)}, bf16[32,8192]{1,0:T(8,128)(2,1)S(1)}, u32[]{:S(2)}, u32[]{:S(2)}) collective-permute-start(bf16[32,8192]{1,0:T(8,128)(2,1)} %own.1), channel_id=1, source_target_pairs={{1,2},{2,1},{3,4},{4,3},{5,6},{6,5},{7,8},{8,7},{9,10},{10,9},{11,... | collective-permute-start | bytes 1572872 | tf_op jit(solution)/shard_map/ppermute | solution.py:532
  1.2 8.3 %copy-start = (bf16[32,8192]{1,0:T(8,128)(2,1)S(1)}, bf16[32,8192]{1,0:T(8,128)(2,1)}, u32[]{:S(2)}) copy-start(bf16[32,8192]{1,0:T(8,128)(2,1)} %own.1) | copy-start | bytes 1572868
  8.9 3.1 %collective-permute-start.13 = (s32[8,128]{1,0:T(8,128)S(1)}, s32[8,128]{1,0:T(8,128)S(1)}, u32[]{:S(2)}, u32[]{:S(2)}) collective-permute-start(s32[8,128]{1,0:T(8,128)S(1)} %get-tuple-element.61), channel_id=1, source_target_pairs={{1,2},{2,1},{3,4},{4,3},{5,6},{6,5},{7,8},{8,7},{9,10},{10,9},{11,... | collective-permute-start | bytes 12296 | tf_op jit(solution)/shard_map/ppermute | solution.py:532
  12.7 7.9 %collective-permute-start.17 = (bf16[64,32,128]{2,1,0:T(8,128)(2,1)S(1)}, bf16[64,32,128]{2,1,0:T(8,128)(2,1)S(1)}, u32[]{:S(2)}, u32[]{:S(2)}) collective-permute-start(bf16[64,32,128]{2,1,0:T(8,128)(2,1)S(1)} %get-tuple-element.69.own), channel_id=1, source_target_pairs={{0,1},{1,0},{2,3},{3,2},{4,5},{5,4},{6,7},{7,6},{8,9},{9,8},{10,11... | collective-permute-start | bytes 1572872 | tf_op jit(solution)/shard_map/ppermute | solution.py:532
  19.0 3.8 %collective-permute-start.16 = (bf16[44,32,128]{2,1,0:T(8,128)(2,1)S(1)}, bf16[44,32,128]{2,1,0:T(8,128)(2,1)S(1)}, u32[]{:S(2)}, u32[]{:S(2)}) collective-permute-start(bf16[44,32,128]{2,1,0:T(8,128)(2,1)S(1)} %get-tuple-element.68), channel_id=1, source_target_pairs={{1,2},{2,1},{3,4},{4,3},{5,6},{6,5},{7,8},{8,7},{9,10},{10,9},{11,... | collective-permute-start | bytes 1081352 | tf_op jit(solution)/shard_map/ppermute | solution.py:532
  22.9 11.6 %collective-permute-start.19 = (bf16[64,32,128]{2,1,0:T(8,128)(2,1)S(1)}, bf16[64,32,128]{2,1,0:T(8,128)(2,1)S(1)}, u32[]{:S(2)}, u32[]{:S(2)}) collective-permute-start(bf16[64,32,128]{2,1,0:T(8,128)(2,1)S(1)} %get-tuple-element.73.own), channel_id=1, source_target_pairs={{0,1},{1,0},{2,3},{3,2},{4,5},{5,4},{6,7},{7,6},{8,9},{9,8},{10,11... | collective-permute-start | bytes 1572872 | tf_op jit(solution)/shard_map/ppermute | solution.py:532
  33.0 3.8 %collective-permute-start.18 = (bf16[44,32,128]{2,1,0:T(8,128)(2,1)S(1)}, bf16[44,32,128]{2,1,0:T(8,128)(2,1)S(1)}, u32[]{:S(2)}, u32[]{:S(2)}) collective-permute-start(bf16[44,32,128]{2,1,0:T(8,128)(2,1)S(1)} %get-tuple-element.72), channel_id=1, source_target_pairs={{1,2},{2,1},{3,4},{4,3},{5,6},{6,5},{7,8},{8,7},{9,10},{10,9},{11,... | collective-permute-start | bytes 1081352 | tf_op jit(solution)/shard_map/ppermute | solution.py:532
  36.9 11.4 %collective-permute-start.21 = (bf16[64,32,128]{2,1,0:T(8,128)(2,1)S(1)}, bf16[64,32,128]{2,1,0:T(8,128)(2,1)S(1)}, u32[]{:S(2)}, u32[]{:S(2)}) collective-permute-start(bf16[64,32,128]{2,1,0:T(8,128)(2,1)S(1)} %get-tuple-element.77.own), channel_id=1, source_target_pairs={{0,1},{1,0},{2,3},{3,2},{4,5},{5,4},{6,7},{7,6},{8,9},{9,8},{10,11... | collective-permute-start | bytes 1572872 | tf_op jit(solution)/shard_map/ppermute | solution.py:532
  46.8 4.6 %collective-permute-start.20 = (bf16[44,32,128]{2,1,0:T(8,128)(2,1)S(1)}, bf16[44,32,128]{2,1,0:T(8,128)(2,1)S(1)}, u32[]{:S(2)}, u32[]{:S(2)}) collective-permute-start(bf16[44,32,128]{2,1,0:T(8,128)(2,1)S(1)} %get-tuple-element.76), channel_id=1, source_target_pairs={{1,2},{2,1},{3,4},{4,3},{5,6},{6,5},{7,8},{8,7},{9,10},{10,9},{11,... | collective-permute-start | bytes 1081352 | tf_op jit(solution)/shard_map/ppermute | solution.py:532
  51.4 23.7 %copy-start.1 = (f32[32,32]{1,0:T(8,128)S(1)}, f32[32,32]{1,0:T(8,128)}, u32[]{:S(2)}) copy-start(f32[32,32]{1,0:T(8,128)} %mapping.1) | copy-start | bytes 12292
  51.6 10.5 %collective-permute-start.22 = (f32[40,32]{1,0:T(8,128)S(1)}, f32[40,32]{1,0:T(8,128)S(1)}, u32[]{:S(2)}, u32[]{:S(2)}) collective-permute-start(f32[40,32]{1,0:T(8,128)S(1)} %get-tuple-element.81), channel_id=1, source_target_pairs={{0,1},{1,0},{2,3},{3,2},{4,5},{5,4},{6,7},{7,6},{8,9},{9,8},{10,11... | collective-permute-start | bytes 15368 | tf_op jit(solution)/shard_map/ppermute | solution.py:532
  62.1 4.4 %collective-permute-start.23 = (f32[40,32]{1,0:T(8,128)S(1)}, f32[40,32]{1,0:T(8,128)S(1)}, u32[]{:S(2)}, u32[]{:S(2)}) collective-permute-start(f32[40,32]{1,0:T(8,128)S(1)} %add.26), channel_id=1, source_target_pairs={{0,2},{1,3},{2,0},{3,1},{4,6},{5,7},{6,4},{7,5},{8,10},{9,11},{10,... | collective-permute-start | bytes 15368 | tf_op jit(solution)/shard_map/ppermute | solution.py:532
  66.5 3.9 %collective-permute-start.24 = (f32[40,32]{1,0:T(8,128)S(1)}, f32[40,32]{1,0:T(8,128)S(1)}, u32[]{:S(2)}, u32[]{:S(2)}) collective-permute-start(f32[40,32]{1,0:T(8,128)S(1)} %add.27), channel_id=1, source_target_pairs={{0,4},{1,5},{2,6},{3,7},{4,0},{5,1},{6,2},{7,3},{8,12},{9,13},{10,... | collective-permute-start | bytes 15368 | tf_op jit(solution)/shard_map/ppermute | solution.py:532
  70.4 4.7 %collective-permute-start.25 = (f32[40,32]{1,0:T(8,128)S(1)}, f32[40,32]{1,0:T(8,128)S(1)}, u32[]{:S(2)}, u32[]{:S(2)}) collective-permute-start(f32[40,32]{1,0:T(8,128)S(1)} %add.28.gram_a), channel_id=1, source_target_pairs={{0,8},{1,9},{2,10},{3,11},{4,12},{5,13},{6,14},{7,15},{8,0},{9,1},... | collective-permute-start | bytes 15368 | tf_op jit(solution)/shard_map/ppermute | solution.py:532

commit v8 on v7

--- a/solution.py
+++ b/solution.py
@@ -216,13 +216,17 @@
     return squares + lax.dot_general(wide, wide, NT, preferred_element_type=F32)
 
 
-def near_kernel(tile_major, last, plan, turned, inverse, own, mate, image, sums, *refs):
+def near_kernel(tile_major, last, count, plan, turned, inverse, own, *refs):
+    mate, (image, sums, *refs) = refs[:count], refs[count:]
     rows, depth, size = turned.shape
     slots = depth // size
     reads = lines(slots)[-1]
     window = refs[-1]
     fill(window, 0, own, tile_major)
-    fill(window, rows, mate, tile_major)
+    start = rows
+    for panel in mate:
+        fill(window, start, panel, tile_major)
+        start += panel.shape[0]
     window[2 * rows] = jnp.zeros(window.shape[1:], BF16)
 
     def step(block, squares):
@@ -299,8 +303,14 @@
         send[k] = image[sending[0, k]]
 
 
+def halve(image, halves):
+    half = halves[0].shape[0]
+    for i, part in enumerate(halves):
+        part[...] = image[i * half : (i + 1) * half]
+
+
 def far_first_kernel(
-    asked, plan, turned, inverse, other, sums, i_in, image, send, sending, panel, done
+    asked, plan, turned, inverse, other, sums, i_in, image, left, right, send, sending, panel, done
 ):
     rows, depth, size = turned.shape
     copy = pltpu.make_async_copy(asked, sending, done)
@@ -310,21 +320,26 @@
     far_part(base, plan, turned, inverse, sums, panel, image, None)
     copy.wait()
     pack(image, sending, send)
-
-
-def far_kernel(sending, plan, turned, inverse, other, sums, i_in, image, send, panel):
+    halve(image, (left, right))
+
+
+def far_kernel(sending, plan, turned, inverse, other, sums, i_in, image, left, right, send, panel):
     rows, depth, size = turned.shape
     fill(panel, 0, other, True)
     base = lines(depth // size)[1]
     far_part(base, plan, turned, inverse, sums, panel, image, None)
     pack(image, sending, send)
-
-
-def far_whole_kernel(tile_major, plan, turned, inverse, other, sums, i_in, image, panel):
+    halve(image, (left, right))
+
+
+def far_whole_kernel(
+    tile_major, plan, turned, inverse, other, sums, i_in, image, left, right, panel
+):
     rows, depth, size = turned.shape
     fill(panel, 0, other, tile_major)
     base = lines(depth // size)[0]
     far_part(base, plan, turned, inverse, sums, panel, image, None)
+    halve(image, (left, right))
 
 
 def far_last_kernel(
@@ -354,15 +369,15 @@
     if last:
         shapes += (pltpu.VMEM((height, height), F32),)
     return pl.pallas_call(
-        functools.partial(near_kernel, tile_major, last),
+        functools.partial(near_kernel, tile_major, last, len(mate)),
         out_shape=shapes,
-        in_specs=[SM, VM, VM, VM, VM],
+        in_specs=[SM, VM, VM, VM] + [VM] * len(mate),
         out_specs=(VM,) * len(shapes),
         scratch_shapes=[pltpu.VMEM((2 * rows + 1, vectors, size), BF16)],
         compiler_params=params(4),
-        cost_estimate=cost(2 * rows * depth * size * vectors, 2 * rows * depth * size),
+        cost_estimate=cost(0, 1024),
         name="near_rows",
-    )(plan, *map(in_vmem, (turned, inverse, own, mate)))
+    )(plan, *map(in_vmem, (turned, inverse, own, *mate)))
 
 
 def far_call(kernel, ins, in_specs, outs, out_specs, turned, vectors, scratch=()):
@@ -384,14 +399,24 @@
     return pltpu.VMEM(array.shape, array.dtype)
 
 
+def halves_of(image):
+    rows, vectors, size = image.shape
+    return (pltpu.VMEM((rows // 2, vectors, size), BF16),) * 2
+
+
 def far_rows_first(limit, asked, plan, turned, inverse, other, sums, image):
     rows, vectors, size = image.shape
     return far_call(
         far_first_kernel,
         (in_vmem(asked), plan, *map(in_vmem, (turned, inverse, other, sums, image))),
         [VM, SM] + [VM] * 5,
-        (of(image), pltpu.VMEM((limit, vectors, size), BF16), pltpu.SMEM((8, 128), I32)),
-        (VM, VM, SM),
+        (
+            of(image),
+            *halves_of(image),
+            pltpu.VMEM((limit, vectors, size), BF16),
+            pltpu.SMEM((8, 128), I32),
+        ),
+        (VM, VM, VM, VM, SM),
         turned,
         vectors,
         [pltpu.SemaphoreType.DMA],
@@ -403,8 +428,8 @@
         far_kernel,
         (sending, plan, *map(in_vmem, (turned, inverse, other, sums, image))),
         [SM, SM] + [VM] * 5,
-        (of(image), of(other)),
-        (VM,) * 2,
+        (of(image), *halves_of(image), of(other)),
+        (VM,) * 4,
         turned,
         image.shape[1],
     )
@@ -415,11 +440,11 @@
         functools.partial(far_whole_kernel, tile_major),
         (plan, *map(in_vmem, (turned, inverse, other, sums, image))),
         [SM] + [VM] * 5,
-        (of(image),),
-        (VM,),
+        (of(image), *halves_of(image)),
+        (VM,) * 3,
         turned,
         image.shape[1],
-    )[0]
+    )
 
 
 def far_rows_last(whole, plan, turned, inverse, sending, other, near, sums, image):
@@ -537,26 +562,28 @@
     mate, other = swap(schur_basis, mates), swap(schur_basis, others)
     turned, inverse, plan, wanted = prep(where, columns, transition_tiles)
     asked = swap(wanted, others)
-    image, sums = near_rows(plan, turned, inverse, schur_basis, mate, False, False)
+    image, sums = near_rows(plan, turned, inverse, schur_basis, (mate,), False, False)
     if whole:
-        image = send = far_rows_whole(plan, turned, inverse, other, sums, image, False)
-        sending = asked
+        image, *halves = far_rows_whole(plan, turned, inverse, other, sums, image, False)
+        send, sending = image, asked
     else:
-        image, send, sending = far_rows_first(
+        image, *halves, send, sending = far_rows_first(
             limit, asked, plan, turned, inverse, other, sums, image
         )
     for step in range(1, PRODUCTS):
         last = step == PRODUCTS - 1
-        mate, other = swap(image, mates), swap(send, others)
+        other = swap(send, others)
+        mate = [swap(half, mates) for half in halves]
         image, sums, *near = near_rows(plan, turned, inverse, image, mate, True, last)
         if last:
             parts, gram = far_rows_last(
                 whole, plan, turned, inverse, sending, other, near[0], sums, image
             )
         elif whole:
-            image = send = far_rows_whole(plan, turned, inverse, other, sums, image, True)
+            image, *halves = far_rows_whole(plan, turned, inverse, other, sums, image, True)
+            send = image
         else:
-            image, send = far_rows(plan, turned, inverse, sending, other, sums, image)
+            image, *halves, send = far_rows(plan, turned, inverse, sending, other, sums, image)
     distance = 1
     while distance < count:
         partner = swap(gram, [(i, i ^ distance) for i in range(count)])

time: 78.6 us -> 73.3 us (0.933)
  starting transfers between devices: 46.8 us -> 39.4 us
  waiting for transfers between devices: 9.35 us -> 11.9 us
    ppermute x13 -> x16, starting transfers between devices: 46.8 us -> 39.4 us  [swap(): return lax.ppermute(array, 'rows', pairs)]
    ppermute x13 -> x16, waiting for transfers between devices: 9.35 us -> 11.9 us  [swap(): return lax.ppermute(array, 'rows', pairs)]
  transfers between devices with their start and end apart: 13 -> 16, of which waited for: 7 -> 10; matrix products, arithmetic and copies ran while one was open for 0% -> 0% of each run, Pallas kernels for 23% -> 24%
where the time goes in v8:
time: 73.3 us; the launch traced here: 73.4 us
  starting transfers between devices  39.4 us (54%)
  Pallas kernels  21.4 us (29%)
  waiting for transfers between devices  11.9 us (16%)
    ppermute x16, starting transfers between devices, swap(): return lax.ppermute(array, 'rows', pairs)  39.4 us
    ppermute x16, waiting for transfers between devices, swap(): return lax.ppermute(array, 'rows', pairs)  11.9 us
    pallas_call x4, Pallas kernels, near_rows(): pl.pallas_call(functools.partial(near_kernel, tile_major, last, len(mate)...  10 us
    pallas_call x1, Pallas kernels, prep(): pl.pallas_call(prep_kernel, out_shape=(pltpu.VMEM((rows, slots * size, si...  7.63 us
    pallas_call x1, Pallas kernels, final(): pl.pallas_call(functools.partial(final_kernel, float(states)), out_shape=...  2.65 us
  transfers between devices with their start and end apart: 16, of which 10 were waited for; matrix products, arithmetic and copies ran while one was open for 0% of the time, Pallas kernels for 24%

profile of v8, /device:TPU:0, one launch (start us, length us, event | category | flops | bytes accessed | tf_op | source)
XLA Modules:
  0.0 73.4 jit_solution(14731868957632552407)
XLA Ops:
  0.0 0.5 collective-permute-start.18
  0.5 0.7 collective-permute-start.17
  1.2 0.1 pad_add_fusion.1.where
  1.2 0.0 copy-start
  1.2 7.6 %prep.3 = (bf16[64,640,128]{2,1,0:T(8,128)(2,1)S(1)}, f32[64,128]{1,0:T(8,128)S(1)}, s32[24,128]{1,0:T(8,128)S(4)}, s32[8,128]{1,0:T(8,128)S(1)}) custom-call(s32[2]{0:T(128)S(1)} %pad_add_fusion.1.where, s32[5,64]{1,0:T(8,128)} %bitcast.7, bf16[64,5,128,128]{3,2,1,0:T(8,128)(2,1)} %tiles.1), custom_call_target="tpu_custom_call" | custom-call | flops 167772160 | bytes 20971520 | tf_op jit(solution)/shard_map/prep/pallas_call | solution.py:156
  8.9 0.7 collective-permute-start.16
  9.5 0.0 collective-permute-done.18.refs_0_
  9.5 0.0 copy-done
  9.6 2.4 %near_rows.12 = (bf16[64,32,128]{2,1,0:T(8,128)(2,1)S(1)}, f32[64,32,128]{2,1,0:T(8,128)S(1)}) custom-call(s32[24,128]{1,0:T(8,128)S(4)} %get-tuple-element.77.plan, bf16[64,640,128]{2,1,0:T(8,128)(2,1)S(1)} %get-tuple-element.78.turned, f32[64,128]{1,0:T(8,128)S(1)} %get-tuple-element.79.inverse, bf16[32,8192]{1,0:T(8,128)(2,1)S(1)} %copy-done, ...), custom_call_target="tpu_custom_call" | custom-call | bytes 1024 | tf_op jit(solution)/shard_map/near_rows/pallas_call | solution.py:371
  12.0 0.0 collective-permute-done.16.asked
  12.0 0.0 collective-permute-done.17.other
  12.0 0.7 far_rows.12
  12.7 0.7 collective-permute-start.19
  13.4 9.3 %collective-permute-start.20 = (bf16[32,32,128]{2,1,0:T(8,128)(2,1)S(1)}, bf16[32,32,128]{2,1,0:T(8,128)(2,1)S(1)}, u32[]{:S(2)}, u32[]{:S(2)}) collective-permute-start(bf16[32,32,128]{2,1,0:T(8,128)(2,1)S(1)} %get-tuple-element.85), channel_id=1, source_target_pairs={{0,1},{1,0},{2,3},{3,2},{4,5},{5,4},{6,7},{7,6},{8,9},{9,8},{10,11... | collective-permute-start | bytes 786440 | tf_op jit(solution)/shard_map/ppermute | solution.py:557
  22.7 0.1 collective-permute-start.21
  22.7 1.1 %collective-permute-done.20.refs_0_ = bf16[32,32,128]{2,1,0:T(8,128)(2,1)S(1)} collective-permute-done((bf16[32,32,128]{2,1,0:T(8,128)(2,1)S(1)}, bf16[32,32,128]{2,1,0:T(8,128)(2,1)S(1)}, u32[]{:S(2)}, u32[]{:S(2)}) %collective-permute-start.20) | collective-permute-done | bytes 262176 | tf_op jit(solution)/shard_map/ppermute | solution.py:557
  23.8 0.4 collective-permute-done.21.refs_1_
  24.2 2.3 %near_rows.13 = (bf16[64,32,128]{2,1,0:T(8,128)(2,1)S(1)}, f32[64,32,128]{2,1,0:T(8,128)S(1)}) custom-call(s32[24,128]{1,0:T(8,128)S(4)} %get-tuple-element.77.plan, bf16[64,640,128]{2,1,0:T(8,128)(2,1)S(1)} %get-tuple-element.78.turned, f32[64,128]{1,0:T(8,128)S(1)} %get-tuple-element.79.inverse, bf16[64,32,128]{2,1,0:T(8,128)(2,1)S(1)} %get-tuple-element.84.own, ...), custom_call_target="tpu_custom_call" | custom-call | bytes 1024 | tf_op jit(solution)/shard_map/near_rows/pallas_call | solution.py:371
  26.5 0.0 collective-permute-done.19.other
  26.5 0.1 far_rows.13
  26.6 0.7 collective-permute-start.22
  27.3 9.1 %collective-permute-start.23 = (bf16[32,32,128]{2,1,0:T(8,128)(2,1)S(1)}, bf16[32,32,128]{2,1,0:T(8,128)(2,1)S(1)}, u32[]{:S(2)}, u32[]{:S(2)}) collective-permute-start(bf16[32,32,128]{2,1,0:T(8,128)(2,1)S(1)} %get-tuple-element.91), channel_id=1, source_target_pairs={{0,1},{1,0},{2,3},{3,2},{4,5},{5,4},{6,7},{7,6},{8,9},{9,8},{10,11... | collective-permute-start | bytes 786440 | tf_op jit(solution)/shard_map/ppermute | solution.py:557
  36.4 0.1 collective-permute-start.24
  36.5 1.1 %collective-permute-done.23.refs_0_ = bf16[32,32,128]{2,1,0:T(8,128)(2,1)S(1)} collective-permute-done((bf16[32,32,128]{2,1,0:T(8,128)(2,1)S(1)}, bf16[32,32,128]{2,1,0:T(8,128)(2,1)S(1)}, u32[]{:S(2)}, u32[]{:S(2)}) %collective-permute-start.23) | collective-permute-done | bytes 262176 | tf_op jit(solution)/shard_map/ppermute | solution.py:557
  37.6 0.4 collective-permute-done.24.refs_1_
  38.0 2.3 %near_rows.14 = (bf16[64,32,128]{2,1,0:T(8,128)(2,1)S(1)}, f32[64,32,128]{2,1,0:T(8,128)S(1)}) custom-call(s32[24,128]{1,0:T(8,128)S(4)} %get-tuple-element.77.plan, bf16[64,640,128]{2,1,0:T(8,128)(2,1)S(1)} %get-tuple-element.78.turned, f32[64,128]{1,0:T(8,128)S(1)} %get-tuple-element.79.inverse, bf16[64,32,128]{2,1,0:T(8,128)(2,1)S(1)} %get-tuple-element.90.own, ...), custom_call_target="tpu_custom_call" | custom-call | bytes 1024 | tf_op jit(solution)/shard_map/near_rows/pallas_call | solution.py:371
  40.3 0.0 collective-permute-done.22.other
  40.3 0.1 far_rows.14
  40.4 0.7 collective-permute-start.25
  41.1 8.3 %collective-permute-start.26 = (bf16[32,32,128]{2,1,0:T(8,128)(2,1)S(1)}, bf16[32,32,128]{2,1,0:T(8,128)(2,1)S(1)}, u32[]{:S(2)}, u32[]{:S(2)}) collective-permute-start(bf16[32,32,128]{2,1,0:T(8,128)(2,1)S(1)} %get-tuple-element.97), channel_id=1, source_target_pairs={{0,1},{1,0},{2,3},{3,2},{4,5},{5,4},{6,7},{7,6},{8,9},{9,8},{10,11... | collective-permute-start | bytes 786440 | tf_op jit(solution)/shard_map/ppermute | solution.py:557
  49.3 0.1 collective-permute-start.27
  49.4 1.1 %collective-permute-done.26.refs_0_ = bf16[32,32,128]{2,1,0:T(8,128)(2,1)S(1)} collective-permute-done((bf16[32,32,128]{2,1,0:T(8,128)(2,1)S(1)}, bf16[32,32,128]{2,1,0:T(8,128)(2,1)S(1)}, u32[]{:S(2)}, u32[]{:S(2)}) %collective-permute-start.26) | collective-permute-done | bytes 262176 | tf_op jit(solution)/shard_map/ppermute | solution.py:557
  50.5 0.4 collective-permute-done.27.refs_1_
  50.9 3.0 %near_rows.15 = (bf16[64,96,128]{2,1,0:T(8,128)(2,1)S(1)}, f32[64,32,128]{2,1,0:T(8,128)S(1)}, f32[96,96]{1,0:T(8,128)S(1)}) custom-call(s32[24,128]{1,0:T(8,128)S(4)} %get-tuple-element.77.plan, bf16[64,640,128]{2,1,0:T(8,128)(2,1)S(1)} %get-tuple-element.78.turned, f32[64,128]{1,0:T(8,128)S(1)} %get-tuple-element.79.inverse, ...), custom_call_target="tpu_custom_call" | custom-call | bytes 1024 | tf_op jit(solution)/shard_map/near_rows/pallas_call | solution.py:371
  53.9 0.0 collective-permute-done.25.other
  53.9 0.0 copy-start.1
  53.9 0.2 far_rows.15
  54.1 1.9 %collective-permute-start.28 = (f32[40,32]{1,0:T(8,128)S(1)}, f32[40,32]{1,0:T(8,128)S(1)}, u32[]{:S(2)}, u32[]{:S(2)}) collective-permute-start(f32[40,32]{1,0:T(8,128)S(1)} %get-tuple-element.102), channel_id=1, source_target_pairs={{0,1},{1,0},{2,3},{3,2},{4,5},{5,4},{6,7},{7,6},{8,9},{9,8},{10,11... | collective-permute-start | bytes 15368 | tf_op jit(solution)/shard_map/ppermute | solution.py:557
  56.0 0.8 %collective-permute-done.28 = f32[40,32]{1,0:T(8,128)S(1)} collective-permute-done((f32[40,32]{1,0:T(8,128)S(1)}, f32[40,32]{1,0:T(8,128)S(1)}, u32[]{:S(2)}, u32[]{:S(2)}) %collective-permute-start.28) | collective-permute-done | bytes 5152 | tf_op jit(solution)/shard_map/ppermute | solution.py:557
  56.9 3.2 %collective-permute-start.29 = (f32[40,32]{1,0:T(8,128)S(1)}, f32[40,32]{1,0:T(8,128)S(1)}, u32[]{:S(2)}, u32[]{:S(2)}) collective-permute-start(f32[40,32]{1,0:T(8,128)S(1)} %add.26), channel_id=1, source_target_pairs={{0,2},{1,3},{2,0},{3,1},{4,6},{5,7},{6,4},{7,5},{8,10},{9,11},{10,... | collective-permute-start | bytes 15368 | tf_op jit(solution)/shard_map/ppermute | solution.py:557
  60.0 1.8 %collective-permute-done.29 = f32[40,32]{1,0:T(8,128)S(1)} collective-permute-done((f32[40,32]{1,0:T(8,128)S(1)}, f32[40,32]{1,0:T(8,128)S(1)}, u32[]{:S(2)}, u32[]{:S(2)}) %collective-permute-start.29) | collective-permute-done | bytes 5152 | tf_op jit(solution)/shard_map/ppermute | solution.py:557
  61.8 1.1 %collective-permute-start.30 = (f32[40,32]{1,0:T(8,128)S(1)}, f32[40,32]{1,0:T(8,128)S(1)}, u32[]{:S(2)}, u32[]{:S(2)}) collective-permute-start(f32[40,32]{1,0:T(8,128)S(1)} %add.27), channel_id=1, source_target_pairs={{0,4},{1,5},{2,6},{3,7},{4,0},{5,1},{6,2},{7,3},{8,12},{9,13},{10,... | collective-permute-start | bytes 15368 | tf_op jit(solution)/shard_map/ppermute | solution.py:557
  62.9 2.7 %collective-permute-done.30 = f32[40,32]{1,0:T(8,128)S(1)} collective-permute-done((f32[40,32]{1,0:T(8,128)S(1)}, f32[40,32]{1,0:T(8,128)S(1)}, u32[]{:S(2)}, u32[]{:S(2)}) %collective-permute-start.30) | collective-permute-done | bytes 5152 | tf_op jit(solution)/shard_map/ppermute | solution.py:557
  65.6 2.5 %collective-permute-start.31 = (f32[40,32]{1,0:T(8,128)S(1)}, f32[40,32]{1,0:T(8,128)S(1)}, u32[]{:S(2)}, u32[]{:S(2)}) collective-permute-start(f32[40,32]{1,0:T(8,128)S(1)} %add.28.gram_a), channel_id=1, source_target_pairs={{0,8},{1,9},{2,10},{3,11},{4,12},{5,13},{6,14},{7,15},{8,0},{9,1},... | collective-permute-start | bytes 15368 | tf_op jit(solution)/shard_map/ppermute | solution.py:557
  68.1 2.2 %collective-permute-done.31.gram_b = f32[40,32]{1,0:T(8,128)S(1)} collective-permute-done((f32[40,32]{1,0:T(8,128)S(1)}, f32[40,32]{1,0:T(8,128)S(1)}, u32[]{:S(2)}, u32[]{:S(2)}) %collective-permute-start.31) | collective-permute-done | bytes 5152 | tf_op jit(solution)/shard_map/ppermute | solution.py:557
  70.3 0.0 copy-done.1
  70.3 2.7 %memberships.3 = (f32[32,8192]{1,0:T(8,128)}, s32[1]{0:T(128)S(4)}) custom-call(f32[40,32]{1,0:T(8,128)S(1)} %add.28.gram_a, f32[40,32]{1,0:T(8,128)S(1)} %collective-permute-done.31.gram_b, f32[32,32]{1,0:T(8,128)S(1)} %copy-done.1, bf16[64,96,128]{2,1,0:T(8,128)(2,1)S(1)} %get-tuple-element.103.parts), custom_call_target="tpu_custom_call" | custom-call | flops 150994944 | bytes 3145728 | tf_op jit(solution)/shard_map/memberships/pallas_call | solution.py:529
  72.9 0.2 conditional.1
  (3 shorter events, 0.0 us)
Async XLA Ops:
  0.0 9.5 %collective-permute-start.18 = (bf16[32,8192]{1,0:T(8,128)(2,1)}, bf16[32,8192]{1,0:T(8,128)(2,1)S(1)}, u32[]{:S(2)}, u32[]{:S(2)}) collective-permute-start(bf16[32,8192]{1,0:T(8,128)(2,1)} %own.1), channel_id=1, source_target_pairs={{0,1},{1,0},{2,3},{3,2},{4,5},{5,4},{6,7},{7,6},{8,9},{9,8},{10,11... | collective-permute-start | bytes 1572872 | tf_op jit(solution)/shard_map/ppermute | solution.py:557
  0.5 11.5 %collective-permute-start.17 = (bf16[32,8192]{1,0:T(8,128)(2,1)}, bf16[32,8192]{1,0:T(8,128)(2,1)S(1)}, u32[]{:S(2)}, u32[]{:S(2)}) collective-permute-start(bf16[32,8192]{1,0:T(8,128)(2,1)} %own.1), channel_id=1, source_target_pairs={{1,2},{2,1},{3,4},{4,3},{5,6},{6,5},{7,8},{8,7},{9,10},{10,9},{11,... | collective-permute-start | bytes 1572872 | tf_op jit(solution)/shard_map/ppermute | solution.py:557
  1.2 8.3 %copy-start = (bf16[32,8192]{1,0:T(8,128)(2,1)S(1)}, bf16[32,8192]{1,0:T(8,128)(2,1)}, u32[]{:S(2)}) copy-start(bf16[32,8192]{1,0:T(8,128)(2,1)} %own.1) | copy-start | bytes 1572868
  8.9 3.1 %collective-permute-start.16 = (s32[8,128]{1,0:T(8,128)S(1)}, s32[8,128]{1,0:T(8,128)S(1)}, u32[]{:S(2)}, u32[]{:S(2)}) collective-permute-start(s32[8,128]{1,0:T(8,128)S(1)} %get-tuple-element.76), channel_id=1, source_target_pairs={{1,2},{2,1},{3,4},{4,3},{5,6},{6,5},{7,8},{8,7},{9,10},{10,9},{11,... | collective-permute-start | bytes 12296 | tf_op jit(solution)/shard_map/ppermute | solution.py:557
  12.7 13.8 %collective-permute-start.19 = (bf16[44,32,128]{2,1,0:T(8,128)(2,1)S(1)}, bf16[44,32,128]{2,1,0:T(8,128)(2,1)S(1)}, u32[]{:S(2)}, u32[]{:S(2)}) collective-permute-start(bf16[44,32,128]{2,1,0:T(8,128)(2,1)S(1)} %get-tuple-element.83), channel_id=1, source_target_pairs={{1,2},{2,1},{3,4},{4,3},{5,6},{6,5},{7,8},{8,7},{9,10},{10,9},{11,... | collective-permute-start | bytes 1081352 | tf_op jit(solution)/shard_map/ppermute | solution.py:557
  13.4 10.5 %collective-permute-start.20 = (bf16[32,32,128]{2,1,0:T(8,128)(2,1)S(1)}, bf16[32,32,128]{2,1,0:T(8,128)(2,1)S(1)}, u32[]{:S(2)}, u32[]{:S(2)}) collective-permute-start(bf16[32,32,128]{2,1,0:T(8,128)(2,1)S(1)} %get-tuple-element.85), channel_id=1, source_target_pairs={{0,1},{1,0},{2,3},{3,2},{4,5},{5,4},{6,7},{7,6},{8,9},{9,8},{10,11... | collective-permute-start | bytes 786440 | tf_op jit(solution)/shard_map/ppermute | solution.py:557
  22.7 1.5 %collective-permute-start.21 = (bf16[32,32,128]{2,1,0:T(8,128)(2,1)S(1)}, bf16[32,32,128]{2,1,0:T(8,128)(2,1)S(1)}, u32[]{:S(2)}, u32[]{:S(2)}) collective-permute-start(bf16[32,32,128]{2,1,0:T(8,128)(2,1)S(1)} %get-tuple-element.86), channel_id=1, source_target_pairs={{0,1},{1,0},{2,3},{3,2},{4,5},{5,4},{6,7},{7,6},{8,9},{9,8},{10,11... | collective-permute-start | bytes 786440 | tf_op jit(solution)/shard_map/ppermute | solution.py:557
  26.6 13.7 %collective-permute-start.22 = (bf16[44,32,128]{2,1,0:T(8,128)(2,1)S(1)}, bf16[44,32,128]{2,1,0:T(8,128)(2,1)S(1)}, u32[]{:S(2)}, u32[]{:S(2)}) collective-permute-start(bf16[44,32,128]{2,1,0:T(8,128)(2,1)S(1)} %get-tuple-element.89), channel_id=1, source_target_pairs={{1,2},{2,1},{3,4},{4,3},{5,6},{6,5},{7,8},{8,7},{9,10},{10,9},{11,... | collective-permute-start | bytes 1081352 | tf_op jit(solution)/shard_map/ppermute | solution.py:557
  27.3 10.3 %collective-permute-start.23 = (bf16[32,32,128]{2,1,0:T(8,128)(2,1)S(1)}, bf16[32,32,128]{2,1,0:T(8,128)(2,1)S(1)}, u32[]{:S(2)}, u32[]{:S(2)}) collective-permute-start(bf16[32,32,128]{2,1,0:T(8,128)(2,1)S(1)} %get-tuple-element.91), channel_id=1, source_target_pairs={{0,1},{1,0},{2,3},{3,2},{4,5},{5,4},{6,7},{7,6},{8,9},{9,8},{10,11... | collective-permute-start | bytes 786440 | tf_op jit(solution)/shard_map/ppermute | solution.py:557
  36.4 1.5 %collective-permute-start.24 = (bf16[32,32,128]{2,1,0:T(8,128)(2,1)S(1)}, bf16[32,32,128]{2,1,0:T(8,128)(2,1)S(1)}, u32[]{:S(2)}, u32[]{:S(2)}) collective-permute-start(bf16[32,32,128]{2,1,0:T(8,128)(2,1)S(1)} %get-tuple-element.92), channel_id=1, source_target_pairs={{0,1},{1,0},{2,3},{3,2},{4,5},{5,4},{6,7},{7,6},{8,9},{9,8},{10,11... | collective-permute-start | bytes 786440 | tf_op jit(solution)/shard_map/ppermute | solution.py:557
  40.4 13.5 %collective-permute-start.25 = (bf16[44,32,128]{2,1,0:T(8,128)(2,1)S(1)}, bf16[44,32,128]{2,1,0:T(8,128)(2,1)S(1)}, u32[]{:S(2)}, u32[]{:S(2)}) collective-permute-start(bf16[44,32,128]{2,1,0:T(8,128)(2,1)S(1)} %get-tuple-element.95), channel_id=1, source_target_pairs={{1,2},{2,1},{3,4},{4,3},{5,6},{6,5},{7,8},{8,7},{9,10},{10,9},{11,... | collective-permute-start | bytes 1081352 | tf_op jit(solution)/shard_map/ppermute | solution.py:557
  41.1 9.4 %collective-permute-start.26 = (bf16[32,32,128]{2,1,0:T(8,128)(2,1)S(1)}, bf16[32,32,128]{2,1,0:T(8,128)(2,1)S(1)}, u32[]{:S(2)}, u32[]{:S(2)}) collective-permute-start(bf16[32,32,128]{2,1,0:T(8,128)(2,1)S(1)} %get-tuple-element.97), channel_id=1, source_target_pairs={{0,1},{1,0},{2,3},{3,2},{4,5},{5,4},{6,7},{7,6},{8,9},{9,8},{10,11... | collective-permute-start | bytes 786440 | tf_op jit(solution)/shard_map/ppermute | solution.py:557
  49.3 1.5 %collective-permute-start.27 = (bf16[32,32,128]{2,1,0:T(8,128)(2,1)S(1)}, bf16[32,32,128]{2,1,0:T(8,128)(2,1)S(1)}, u32[]{:S(2)}, u32[]{:S(2)}) collective-permute-start(bf16[32,32,128]{2,1,0:T(8,128)(2,1)S(1)} %get-tuple-element.98), channel_id=1, source_target_pairs={{0,1},{1,0},{2,3},{3,2},{4,5},{5,4},{6,7},{7,6},{8,9},{9,8},{10,11... | collective-permute-start | bytes 786440 | tf_op jit(solution)/shard_map/ppermute | solution.py:557
  53.9 16.4 %copy-start.1 = (f32[32,32]{1,0:T(8,128)S(1)}, f32[32,32]{1,0:T(8,128)}, u32[]{:S(2)}) copy-start(f32[32,32]{1,0:T(8,128)} %mapping.1) | copy-start | bytes 12292
  54.1 2.7 %collective-permute-start.28 = (f32[40,32]{1,0:T(8,128)S(1)}, f32[40,32]{1,0:T(8,128)S(1)}, u32[]{:S(2)}, u32[]{:S(2)}) collective-permute-start(f32[40,32]{1,0:T(8,128)S(1)} %get-tuple-element.102), channel_id=1, source_target_pairs={{0,1},{1,0},{2,3},{3,2},{4,5},{5,4},{6,7},{7,6},{8,9},{9,8},{10,11... | collective-permute-start | bytes 15368 | tf_op jit(solution)/shard_map/ppermute | solution.py:557
  56.9 4.9 %collective-permute-start.29 = (f32[40,32]{1,0:T(8,128)S(1)}, f32[40,32]{1,0:T(8,128)S(1)}, u32[]{:S(2)}, u32[]{:S(2)}) collective-permute-start(f32[40,32]{1,0:T(8,128)S(1)} %add.26), channel_id=1, source_target_pairs={{0,2},{1,3},{2,0},{3,1},{4,6},{5,7},{6,4},{7,5},{8,10},{9,11},{10,... | collective-permute-start | bytes 15368 | tf_op jit(solution)/shard_map/ppermute | solution.py:557
  61.8 3.8 %collective-permute-start.30 = (f32[40,32]{1,0:T(8,128)S(1)}, f32[40,32]{1,0:T(8,128)S(1)}, u32[]{:S(2)}, u32[]{:S(2)}) collective-permute-start(f32[40,32]{1,0:T(8,128)S(1)} %add.27), channel_id=1, source_target_pairs={{0,4},{1,5},{2,6},{3,7},{4,0},{5,1},{6,2},{7,3},{8,12},{9,13},{10,... | collective-permute-start | bytes 15368 | tf_op jit(solution)/shard_map/ppermute | solution.py:557
  65.6 4.7 %collective-permute-start.31 = (f32[40,32]{1,0:T(8,128)S(1)}, f32[40,32]{1,0:T(8,128)S(1)}, u32[]{:S(2)}, u32[]{:S(2)}) collective-permute-start(f32[40,32]{1,0:T(8,128)S(1)} %add.28.gram_a), channel_id=1, source_target_pairs={{0,8},{1,9},{2,10},{3,11},{4,12},{5,13},{6,14},{7,15},{8,0},{9,1},... | collective-permute-start | bytes 15368 | tf_op jit(solution)/shard_map/ppermute | solution.py:557

commit v9 on v8

--- a/solution.py
+++ b/solution.py
@@ -128,10 +128,7 @@
     copy_columns.start()
     for i in range(chunks):
         copy_in(i).start()
-    copy_columns.wait()
-    draft_plan(where[0], where[1], named[...], draft, wanted)
     copy_plan = pltpu.make_async_copy(draft, plan, done)
-    copy_plan.start()
 
     def step(i, carry):
         copy_in(i).wait()
@@ -146,7 +143,11 @@
             inverse[pl.ds(r, 1), :] = 1.0 / jnp.sum(total, axis=0, keepdims=True)
         return carry
 
-    lax.fori_loop(0, chunks, step, 0)
+    lax.fori_loop(0, chunks // 2, step, 0)
+    copy_columns.wait()
+    draft_plan(where[0], where[1], named[...], draft, wanted)
+    copy_plan.start()
+    lax.fori_loop(chunks // 2, chunks, step, 0)
     copy_plan.wait()
 
 
@@ -196,7 +197,7 @@
 
 def fold(squares, vectors):
     total = None
-    for a, b in ((2, 2), (1, 2), (2, 1), (0, 2), (2, 0), (1, 1), (0, 1), (1, 0), (0, 0)):
+    for a, b in ((1, 1), (0, 1), (1, 0), (0, 0)):
         part = squares[a * vectors : (a + 1) * vectors, b * vectors : (b + 1) * vectors]
         total = part if total is None else total + part
     return total
@@ -209,7 +210,7 @@
         return None
     counted = []
     for r, y, keep in zip(picked, results, mine):
-        stacked = jnp.concatenate(thirds(y), axis=0)
+        stacked = jnp.concatenate(thirds(y)[:2], axis=0)
         image[r] = stacked
         counted.append(jnp.where(keep, stacked, jnp.zeros_like(stacked)))
     wide = jnp.concatenate(counted, axis=1)
@@ -361,7 +362,7 @@
 def near_rows(plan, turned, inverse, own, mate, tile_major, last):
     rows, depth, size = turned.shape
     vectors = own.shape[1 if tile_major else 0]
-    height = 3 * vectors if last else vectors
+    height = 2 * vectors if last else vectors
     shapes = (
         pltpu.VMEM((rows, height, size), BF16),
         pltpu.VMEM((rows, vectors, size), F32),
@@ -448,7 +449,7 @@
 
 
 def far_rows_last(whole, plan, turned, inverse, sending, other, near, sums, image):
-    vectors = near.shape[0] // 3
+    vectors = near.shape[0] // 2
     return far_call(
         functools.partial(far_last_kernel, whole),
         (sending, plan, *map(in_vmem, (turned, inverse, other, near, sums, image))),
@@ -488,7 +489,7 @@
 
 def final_kernel(states, gram_a, gram_b, mapping, parts, out, short, ready, sent):
     rows, depth, size = parts.shape
-    vectors = depth // 3
+    vectors = depth // 2
     total = gram_a[...] + gram_b[...]
     short[0] = jnp.max(total[vectors:]).astype(I32)
     factor = inverse_factor(total[:vectors] / states)
@@ -503,9 +504,9 @@
     blank = jnp.zeros_like(high)
     left = jnp.concatenate(
         [
-            jnp.concatenate([high, high, high], axis=1),
-            jnp.concatenate([middle, middle, blank], axis=1),
-            jnp.concatenate([low, blank, blank], axis=1),
+            jnp.concatenate([high, high], axis=1),
+            jnp.concatenate([middle, middle], axis=1),
+            jnp.concatenate([low, blank], axis=1),
         ],
         axis=0,
     )
@@ -525,7 +526,7 @@
 
 def final(states, gram_a, gram_b, mapping, parts):
     rows, depth, size = parts.shape
-    vectors = depth // 3
+    vectors = depth // 2
     return pl.pallas_call(
         functools.partial(final_kernel, float(states)),
         out_shape=(

time: 73.3 us -> 72.5 us (0.989)
  starting transfers between devices: 39.4 us -> 41.2 us
  Pallas kernels: 21.4 us -> 19.7 us
  waiting for transfers between devices: 11.9 us -> 10.6 us
    ppermute x16, starting transfers between devices: 39.4 us -> 41.2 us  [swap(): return lax.ppermute(array, 'rows', pairs)]
    pallas_call x1, Pallas kernels: 7.63 us -> 5.99 us  [prep(): pl.pallas_call(prep_kernel, out_shape=(pltpu.VMEM((rows, slots * size, si...]
    ppermute x16, waiting for transfers between devices: 11.9 us -> 10.6 us  [swap(): return lax.ppermute(array, 'rows', pairs)]
  transfers between devices with their start and end apart: 16 -> 16, of which waited for: 10 -> 10; matrix products, arithmetic and copies ran while one was open for 0% -> 0% of each run, Pallas kernels for 24% -> 22%
where the time goes in v9:
time: 72.5 us; the launch traced here: 71.9 us
  starting transfers between devices  41.2 us (57%)
  Pallas kernels  19.7 us (27%)
  waiting for transfers between devices  10.6 us (15%)
    ppermute x16, starting transfers between devices, swap(): return lax.ppermute(array, 'rows', pairs)  41.2 us
    ppermute x16, waiting for transfers between devices, swap(): return lax.ppermute(array, 'rows', pairs)  10.6 us
    pallas_call x4, Pallas kernels, near_rows(): pl.pallas_call(functools.partial(near_kernel, tile_major, last, len(mate)...  9.87 us
    pallas_call x1, Pallas kernels, prep(): pl.pallas_call(prep_kernel, out_shape=(pltpu.VMEM((rows, slots * size, si...  5.99 us
    pallas_call x1, Pallas kernels, final(): pl.pallas_call(functools.partial(final_kernel, float(states)), out_shape=...  2.6 us
  transfers between devices with their start and end apart: 16, of which 10 were waited for; matrix products, arithmetic and copies ran while one was open for 0% of the time, Pallas kernels for 22%

profile of v9, /device:TPU:0, one launch (start us, length us, event | category | flops | bytes accessed | tf_op | source)
XLA Modules:
  0.0 71.9 jit_solution(1239739253916575574)
XLA Ops:
  0.0 0.0 copy-start
  0.0 0.5 collective-permute-start.18
  0.5 0.7 collective-permute-start.17
  1.2 0.1 pad_add_fusion.1.where
  1.2 6.0 %prep.3 = (bf16[64,640,128]{2,1,0:T(8,128)(2,1)S(1)}, f32[64,128]{1,0:T(8,128)S(1)}, s32[24,128]{1,0:T(8,128)S(4)}, s32[8,128]{1,0:T(8,128)S(1)}) custom-call(s32[2]{0:T(128)S(1)} %pad_add_fusion.1.where, s32[5,64]{1,0:T(8,128)} %bitcast.7, bf16[64,5,128,128]{3,2,1,0:T(8,128)(2,1)} %tiles.1), custom_call_target="tpu_custom_call" | custom-call | flops 167772160 | bytes 20971520 | tf_op jit(solution)/shard_map/prep/pallas_call | solution.py:157
  7.2 0.7 collective-permute-start.16
  7.9 0.0 collective-permute-done.18.refs_0_
  7.9 0.0 copy-done
  7.9 2.4 %near_rows.12 = (bf16[64,32,128]{2,1,0:T(8,128)(2,1)S(1)}, f32[64,32,128]{2,1,0:T(8,128)S(1)}) custom-call(s32[24,128]{1,0:T(8,128)S(4)} %get-tuple-element.77.plan, bf16[64,640,128]{2,1,0:T(8,128)(2,1)S(1)} %get-tuple-element.78.turned, f32[64,128]{1,0:T(8,128)S(1)} %get-tuple-element.79.inverse, bf16[32,8192]{1,0:T(8,128)(2,1)S(1)} %copy-done, ...), custom_call_target="tpu_custom_call" | custom-call | bytes 1024 | tf_op jit(solution)/shard_map/near_rows/pallas_call | solution.py:372
  10.3 0.0 collective-permute-done.16.asked
  10.3 0.0 collective-permute-done.17.other
  10.4 0.7 far_rows.12
  11.0 0.7 collective-permute-start.19
  11.7 10.9 %collective-permute-start.20 = (bf16[32,32,128]{2,1,0:T(8,128)(2,1)S(1)}, bf16[32,32,128]{2,1,0:T(8,128)(2,1)S(1)}, u32[]{:S(2)}, u32[]{:S(2)}) collective-permute-start(bf16[32,32,128]{2,1,0:T(8,128)(2,1)S(1)} %get-tuple-element.85), channel_id=1, source_target_pairs={{0,1},{1,0},{2,3},{3,2},{4,5},{5,4},{6,7},{7,6},{8,9},{9,8},{10,11... | collective-permute-start | bytes 786440 | tf_op jit(solution)/shard_map/ppermute | solution.py:558
  22.6 0.1 collective-permute-start.21
  22.7 1.1 %collective-permute-done.20.refs_0_ = bf16[32,32,128]{2,1,0:T(8,128)(2,1)S(1)} collective-permute-done((bf16[32,32,128]{2,1,0:T(8,128)(2,1)S(1)}, bf16[32,32,128]{2,1,0:T(8,128)(2,1)S(1)}, u32[]{:S(2)}, u32[]{:S(2)}) %collective-permute-start.20) | collective-permute-done | bytes 262176 | tf_op jit(solution)/shard_map/ppermute | solution.py:558
  23.8 0.4 collective-permute-done.21.refs_1_
  24.1 2.3 %near_rows.13 = (bf16[64,32,128]{2,1,0:T(8,128)(2,1)S(1)}, f32[64,32,128]{2,1,0:T(8,128)S(1)}) custom-call(s32[24,128]{1,0:T(8,128)S(4)} %get-tuple-element.77.plan, bf16[64,640,128]{2,1,0:T(8,128)(2,1)S(1)} %get-tuple-element.78.turned, f32[64,128]{1,0:T(8,128)S(1)} %get-tuple-element.79.inverse, bf16[64,32,128]{2,1,0:T(8,128)(2,1)S(1)} %get-tuple-element.84.own, ...), custom_call_target="tpu_custom_call" | custom-call | bytes 1024 | tf_op jit(solution)/shard_map/near_rows/pallas_call | solution.py:372
  26.4 0.0 collective-permute-done.19.other
  26.4 0.1 far_rows.13
  26.5 0.7 collective-permute-start.22
  27.2 8.9 %collective-permute-start.23 = (bf16[32,32,128]{2,1,0:T(8,128)(2,1)S(1)}, bf16[32,32,128]{2,1,0:T(8,128)(2,1)S(1)}, u32[]{:S(2)}, u32[]{:S(2)}) collective-permute-start(bf16[32,32,128]{2,1,0:T(8,128)(2,1)S(1)} %get-tuple-element.91), channel_id=1, source_target_pairs={{0,1},{1,0},{2,3},{3,2},{4,5},{5,4},{6,7},{7,6},{8,9},{9,8},{10,11... | collective-permute-start | bytes 786440 | tf_op jit(solution)/shard_map/ppermute | solution.py:558
  36.1 0.1 collective-permute-start.24
  36.2 1.1 %collective-permute-done.23.refs_0_ = bf16[32,32,128]{2,1,0:T(8,128)(2,1)S(1)} collective-permute-done((bf16[32,32,128]{2,1,0:T(8,128)(2,1)S(1)}, bf16[32,32,128]{2,1,0:T(8,128)(2,1)S(1)}, u32[]{:S(2)}, u32[]{:S(2)}) %collective-permute-start.23) | collective-permute-done | bytes 262176 | tf_op jit(solution)/shard_map/ppermute | solution.py:558
  37.3 0.4 collective-permute-done.24.refs_1_
  37.7 2.3 %near_rows.14 = (bf16[64,32,128]{2,1,0:T(8,128)(2,1)S(1)}, f32[64,32,128]{2,1,0:T(8,128)S(1)}) custom-call(s32[24,128]{1,0:T(8,128)S(4)} %get-tuple-element.77.plan, bf16[64,640,128]{2,1,0:T(8,128)(2,1)S(1)} %get-tuple-element.78.turned, f32[64,128]{1,0:T(8,128)S(1)} %get-tuple-element.79.inverse, bf16[64,32,128]{2,1,0:T(8,128)(2,1)S(1)} %get-tuple-element.90.own, ...), custom_call_target="tpu_custom_call" | custom-call | bytes 1024 | tf_op jit(solution)/shard_map/near_rows/pallas_call | solution.py:372
  40.0 0.0 collective-permute-done.22.other
  40.0 0.1 far_rows.14
  40.1 0.7 collective-permute-start.25
  40.8 6.2 %collective-permute-start.26 = (bf16[32,32,128]{2,1,0:T(8,128)(2,1)S(1)}, bf16[32,32,128]{2,1,0:T(8,128)(2,1)S(1)}, u32[]{:S(2)}, u32[]{:S(2)}) collective-permute-start(bf16[32,32,128]{2,1,0:T(8,128)(2,1)S(1)} %get-tuple-element.97), channel_id=1, source_target_pairs={{0,1},{1,0},{2,3},{3,2},{4,5},{5,4},{6,7},{7,6},{8,9},{9,8},{10,11... | collective-permute-start | bytes 786440 | tf_op jit(solution)/shard_map/ppermute | solution.py:558
  46.9 0.1 collective-permute-start.27
  47.0 1.1 %collective-permute-done.26.refs_0_ = bf16[32,32,128]{2,1,0:T(8,128)(2,1)S(1)} collective-permute-done((bf16[32,32,128]{2,1,0:T(8,128)(2,1)S(1)}, bf16[32,32,128]{2,1,0:T(8,128)(2,1)S(1)}, u32[]{:S(2)}, u32[]{:S(2)}) %collective-permute-start.26) | collective-permute-done | bytes 262176 | tf_op jit(solution)/shard_map/ppermute | solution.py:558
  48.1 0.4 collective-permute-done.27.refs_1_
  48.5 0.0 copy-start.1
  48.5 2.9 %near_rows.15 = (bf16[64,64,128]{2,1,0:T(8,128)(2,1)S(1)}, f32[64,32,128]{2,1,0:T(8,128)S(1)}, f32[64,64]{1,0:T(8,128)S(1)}) custom-call(s32[24,128]{1,0:T(8,128)S(4)} %get-tuple-element.77.plan, bf16[64,640,128]{2,1,0:T(8,128)(2,1)S(1)} %get-tuple-element.78.turned, f32[64,128]{1,0:T(8,128)S(1)} %get-tuple-element.79.inverse, ...), custom_call_target="tpu_custom_call" | custom-call | bytes 1024 | tf_op jit(solution)/shard_map/near_rows/pallas_call | solution.py:372
  51.4 0.0 collective-permute-done.25.other
  51.4 0.4 far_rows.15
  51.7 3.7 %collective-permute-start.28 = (f32[40,32]{1,0:T(8,128)S(1)}, f32[40,32]{1,0:T(8,128)S(1)}, u32[]{:S(2)}, u32[]{:S(2)}) collective-permute-start(f32[40,32]{1,0:T(8,128)S(1)} %get-tuple-element.102), channel_id=1, source_target_pairs={{0,1},{1,0},{2,3},{3,2},{4,5},{5,4},{6,7},{7,6},{8,9},{9,8},{10,11... | collective-permute-start | bytes 15368 | tf_op jit(solution)/shard_map/ppermute | solution.py:558
  55.4 0.8 %collective-permute-done.28 = f32[40,32]{1,0:T(8,128)S(1)} collective-permute-done((f32[40,32]{1,0:T(8,128)S(1)}, f32[40,32]{1,0:T(8,128)S(1)}, u32[]{:S(2)}, u32[]{:S(2)}) %collective-permute-start.28) | collective-permute-done | bytes 5152 | tf_op jit(solution)/shard_map/ppermute | solution.py:558
  56.3 2.2 %collective-permute-start.29 = (f32[40,32]{1,0:T(8,128)S(1)}, f32[40,32]{1,0:T(8,128)S(1)}, u32[]{:S(2)}, u32[]{:S(2)}) collective-permute-start(f32[40,32]{1,0:T(8,128)S(1)} %add.26), channel_id=1, source_target_pairs={{0,2},{1,3},{2,0},{3,1},{4,6},{5,7},{6,4},{7,5},{8,10},{9,11},{10,... | collective-permute-start | bytes 15368 | tf_op jit(solution)/shard_map/ppermute | solution.py:558
  58.5 1.8 %collective-permute-done.29 = f32[40,32]{1,0:T(8,128)S(1)} collective-permute-done((f32[40,32]{1,0:T(8,128)S(1)}, f32[40,32]{1,0:T(8,128)S(1)}, u32[]{:S(2)}, u32[]{:S(2)}) %collective-permute-start.29) | collective-permute-done | bytes 5152 | tf_op jit(solution)/shard_map/ppermute | solution.py:558
  60.3 2.4 %collective-permute-start.30 = (f32[40,32]{1,0:T(8,128)S(1)}, f32[40,32]{1,0:T(8,128)S(1)}, u32[]{:S(2)}, u32[]{:S(2)}) collective-permute-start(f32[40,32]{1,0:T(8,128)S(1)} %add.27), channel_id=1, source_target_pairs={{0,4},{1,5},{2,6},{3,7},{4,0},{5,1},{6,2},{7,3},{8,12},{9,13},{10,... | collective-permute-start | bytes 15368 | tf_op jit(solution)/shard_map/ppermute | solution.py:558
  62.7 1.8 %collective-permute-done.30 = f32[40,32]{1,0:T(8,128)S(1)} collective-permute-done((f32[40,32]{1,0:T(8,128)S(1)}, f32[40,32]{1,0:T(8,128)S(1)}, u32[]{:S(2)}, u32[]{:S(2)}) %collective-permute-start.30) | collective-permute-done | bytes 5152 | tf_op jit(solution)/shard_map/ppermute | solution.py:558
  64.4 2.9 %collective-permute-start.31 = (f32[40,32]{1,0:T(8,128)S(1)}, f32[40,32]{1,0:T(8,128)S(1)}, u32[]{:S(2)}, u32[]{:S(2)}) collective-permute-start(f32[40,32]{1,0:T(8,128)S(1)} %add.28.gram_a), channel_id=1, source_target_pairs={{0,8},{1,9},{2,10},{3,11},{4,12},{5,13},{6,14},{7,15},{8,0},{9,1},... | collective-permute-start | bytes 15368 | tf_op jit(solution)/shard_map/ppermute | solution.py:558
  67.3 1.8 %collective-permute-done.31.gram_b = f32[40,32]{1,0:T(8,128)S(1)} collective-permute-done((f32[40,32]{1,0:T(8,128)S(1)}, f32[40,32]{1,0:T(8,128)S(1)}, u32[]{:S(2)}, u32[]{:S(2)}) %collective-permute-start.31) | collective-permute-done | bytes 5152 | tf_op jit(solution)/shard_map/ppermute | solution.py:558
  69.1 0.0 copy-done.1
  69.1 2.6 %memberships.3 = (f32[32,8192]{1,0:T(8,128)}, s32[1]{0:T(128)S(4)}) custom-call(f32[40,32]{1,0:T(8,128)S(1)} %add.28.gram_a, f32[40,32]{1,0:T(8,128)S(1)} %collective-permute-done.31.gram_b, f32[32,32]{1,0:T(8,128)S(1)} %copy-done.1, bf16[64,64,128]{2,1,0:T(8,128)(2,1)S(1)} %get-tuple-element.103.parts), custom_call_target="tpu_custom_call" | custom-call | flops 100663296 | bytes 2097152 | tf_op jit(solution)/shard_map/memberships/pallas_call | solution.py:530
  (4 shorter events, 0.0 us)
Async XLA Ops:
  0.0 7.9 %copy-start = (bf16[32,8192]{1,0:T(8,128)(2,1)S(1)}, bf16[32,8192]{1,0:T(8,128)(2,1)}, u32[]{:S(2)}) copy-start(bf16[32,8192]{1,0:T(8,128)(2,1)} %own.1) | copy-start | bytes 1572868
  0.0 7.9 %collective-permute-start.18 = (bf16[32,8192]{1,0:T(8,128)(2,1)}, bf16[32,8192]{1,0:T(8,128)(2,1)S(1)}, u32[]{:S(2)}, u32[]{:S(2)}) collective-permute-start(bf16[32,8192]{1,0:T(8,128)(2,1)} %own.1), channel_id=1, source_target_pairs={{0,1},{1,0},{2,3},{3,2},{4,5},{5,4},{6,7},{7,6},{8,9},{9,8},{10,11... | collective-permute-start | bytes 1572872 | tf_op jit(solution)/shard_map/ppermute | solution.py:558
  0.5 9.9 %collective-permute-start.17 = (bf16[32,8192]{1,0:T(8,128)(2,1)}, bf16[32,8192]{1,0:T(8,128)(2,1)S(1)}, u32[]{:S(2)}, u32[]{:S(2)}) collective-permute-start(bf16[32,8192]{1,0:T(8,128)(2,1)} %own.1), channel_id=1, source_target_pairs={{1,2},{2,1},{3,4},{4,3},{5,6},{6,5},{7,8},{8,7},{9,10},{10,9},{11,... | collective-permute-start | bytes 1572872 | tf_op jit(solution)/shard_map/ppermute | solution.py:558
  7.2 3.1 %collective-permute-start.16 = (s32[8,128]{1,0:T(8,128)S(1)}, s32[8,128]{1,0:T(8,128)S(1)}, u32[]{:S(2)}, u32[]{:S(2)}) collective-permute-start(s32[8,128]{1,0:T(8,128)S(1)} %get-tuple-element.76), channel_id=1, source_target_pairs={{1,2},{2,1},{3,4},{4,3},{5,6},{6,5},{7,8},{8,7},{9,10},{10,9},{11,... | collective-permute-start | bytes 12296 | tf_op jit(solution)/shard_map/ppermute | solution.py:558
  11.0 15.4 %collective-permute-start.19 = (bf16[44,32,128]{2,1,0:T(8,128)(2,1)S(1)}, bf16[44,32,128]{2,1,0:T(8,128)(2,1)S(1)}, u32[]{:S(2)}, u32[]{:S(2)}) collective-permute-start(bf16[44,32,128]{2,1,0:T(8,128)(2,1)S(1)} %get-tuple-element.83), channel_id=1, source_target_pairs={{1,2},{2,1},{3,4},{4,3},{5,6},{6,5},{7,8},{8,7},{9,10},{10,9},{11,... | collective-permute-start | bytes 1081352 | tf_op jit(solution)/shard_map/ppermute | solution.py:558
  11.7 12.0 %collective-permute-start.20 = (bf16[32,32,128]{2,1,0:T(8,128)(2,1)S(1)}, bf16[32,32,128]{2,1,0:T(8,128)(2,1)S(1)}, u32[]{:S(2)}, u32[]{:S(2)}) collective-permute-start(bf16[32,32,128]{2,1,0:T(8,128)(2,1)S(1)} %get-tuple-element.85), channel_id=1, source_target_pairs={{0,1},{1,0},{2,3},{3,2},{4,5},{5,4},{6,7},{7,6},{8,9},{9,8},{10,11... | collective-permute-start | bytes 786440 | tf_op jit(solution)/shard_map/ppermute | solution.py:558
  22.6 1.5 %collective-permute-start.21 = (bf16[32,32,128]{2,1,0:T(8,128)(2,1)S(1)}, bf16[32,32,128]{2,1,0:T(8,128)(2,1)S(1)}, u32[]{:S(2)}, u32[]{:S(2)}) collective-permute-start(bf16[32,32,128]{2,1,0:T(8,128)(2,1)S(1)} %get-tuple-element.86), channel_id=1, source_target_pairs={{0,1},{1,0},{2,3},{3,2},{4,5},{5,4},{6,7},{7,6},{8,9},{9,8},{10,11... | collective-permute-start | bytes 786440 | tf_op jit(solution)/shard_map/ppermute | solution.py:558
  26.5 13.4 %collective-permute-start.22 = (bf16[44,32,128]{2,1,0:T(8,128)(2,1)S(1)}, bf16[44,32,128]{2,1,0:T(8,128)(2,1)S(1)}, u32[]{:S(2)}, u32[]{:S(2)}) collective-permute-start(bf16[44,32,128]{2,1,0:T(8,128)(2,1)S(1)} %get-tuple-element.89), channel_id=1, source_target_pairs={{1,2},{2,1},{3,4},{4,3},{5,6},{6,5},{7,8},{8,7},{9,10},{10,9},{11,... | collective-permute-start | bytes 1081352 | tf_op jit(solution)/shard_map/ppermute | solution.py:558
  27.2 10.0 %collective-permute-start.23 = (bf16[32,32,128]{2,1,0:T(8,128)(2,1)S(1)}, bf16[32,32,128]{2,1,0:T(8,128)(2,1)S(1)}, u32[]{:S(2)}, u32[]{:S(2)}) collective-permute-start(bf16[32,32,128]{2,1,0:T(8,128)(2,1)S(1)} %get-tuple-element.91), channel_id=1, source_target_pairs={{0,1},{1,0},{2,3},{3,2},{4,5},{5,4},{6,7},{7,6},{8,9},{9,8},{10,11... | collective-permute-start | bytes 786440 | tf_op jit(solution)/shard_map/ppermute | solution.py:558
  36.1 1.5 %collective-permute-start.24 = (bf16[32,32,128]{2,1,0:T(8,128)(2,1)S(1)}, bf16[32,32,128]{2,1,0:T(8,128)(2,1)S(1)}, u32[]{:S(2)}, u32[]{:S(2)}) collective-permute-start(bf16[32,32,128]{2,1,0:T(8,128)(2,1)S(1)} %get-tuple-element.92), channel_id=1, source_target_pairs={{0,1},{1,0},{2,3},{3,2},{4,5},{5,4},{6,7},{7,6},{8,9},{9,8},{10,11... | collective-permute-start | bytes 786440 | tf_op jit(solution)/shard_map/ppermute | solution.py:558
  40.1 11.3 %collective-permute-start.25 = (bf16[44,32,128]{2,1,0:T(8,128)(2,1)S(1)}, bf16[44,32,128]{2,1,0:T(8,128)(2,1)S(1)}, u32[]{:S(2)}, u32[]{:S(2)}) collective-permute-start(bf16[44,32,128]{2,1,0:T(8,128)(2,1)S(1)} %get-tuple-element.95), channel_id=1, source_target_pairs={{1,2},{2,1},{3,4},{4,3},{5,6},{6,5},{7,8},{8,7},{9,10},{10,9},{11,... | collective-permute-start | bytes 1081352 | tf_op jit(solution)/shard_map/ppermute | solution.py:558
  40.8 7.3 %collective-permute-start.26 = (bf16[32,32,128]{2,1,0:T(8,128)(2,1)S(1)}, bf16[32,32,128]{2,1,0:T(8,128)(2,1)S(1)}, u32[]{:S(2)}, u32[]{:S(2)}) collective-permute-start(bf16[32,32,128]{2,1,0:T(8,128)(2,1)S(1)} %get-tuple-element.97), channel_id=1, source_target_pairs={{0,1},{1,0},{2,3},{3,2},{4,5},{5,4},{6,7},{7,6},{8,9},{9,8},{10,11... | collective-permute-start | bytes 786440 | tf_op jit(solution)/shard_map/ppermute | solution.py:558
  46.9 1.5 %collective-permute-start.27 = (bf16[32,32,128]{2,1,0:T(8,128)(2,1)S(1)}, bf16[32,32,128]{2,1,0:T(8,128)(2,1)S(1)}, u32[]{:S(2)}, u32[]{:S(2)}) collective-permute-start(bf16[32,32,128]{2,1,0:T(8,128)(2,1)S(1)} %get-tuple-element.98), channel_id=1, source_target_pairs={{0,1},{1,0},{2,3},{3,2},{4,5},{5,4},{6,7},{7,6},{8,9},{9,8},{10,11... | collective-permute-start | bytes 786440 | tf_op jit(solution)/shard_map/ppermute | solution.py:558
  48.5 20.7 %copy-start.1 = (f32[32,32]{1,0:T(8,128)S(1)}, f32[32,32]{1,0:T(8,128)}, u32[]{:S(2)}) copy-start(f32[32,32]{1,0:T(8,128)} %mapping.1) | copy-start | bytes 12292
  51.7 4.5 %collective-permute-start.28 = (f32[40,32]{1,0:T(8,128)S(1)}, f32[40,32]{1,0:T(8,128)S(1)}, u32[]{:S(2)}, u32[]{:S(2)}) collective-permute-start(f32[40,32]{1,0:T(8,128)S(1)} %get-tuple-element.102), channel_id=1, source_target_pairs={{0,1},{1,0},{2,3},{3,2},{4,5},{5,4},{6,7},{7,6},{8,9},{9,8},{10,11... | collective-permute-start | bytes 15368 | tf_op jit(solution)/shard_map/ppermute | solution.py:558
  56.3 4.0 %collective-permute-start.29 = (f32[40,32]{1,0:T(8,128)S(1)}, f32[40,32]{1,0:T(8,128)S(1)}, u32[]{:S(2)}, u32[]{:S(2)}) collective-permute-start(f32[40,32]{1,0:T(8,128)S(1)} %add.26), channel_id=1, source_target_pairs={{0,2},{1,3},{2,0},{3,1},{4,6},{5,7},{6,4},{7,5},{8,10},{9,11},{10,... | collective-permute-start | bytes 15368 | tf_op jit(solution)/shard_map/ppermute | solution.py:558
  60.3 4.1 %collective-permute-start.30 = (f32[40,32]{1,0:T(8,128)S(1)}, f32[40,32]{1,0:T(8,128)S(1)}, u32[]{:S(2)}, u32[]{:S(2)}) collective-permute-start(f32[40,32]{1,0:T(8,128)S(1)} %add.27), channel_id=1, source_target_pairs={{0,4},{1,5},{2,6},{3,7},{4,0},{5,1},{6,2},{7,3},{8,12},{9,13},{10,... | collective-permute-start | bytes 15368 | tf_op jit(solution)/shard_map/ppermute | solution.py:558
  64.4 4.7 %collective-permute-start.31 = (f32[40,32]{1,0:T(8,128)S(1)}, f32[40,32]{1,0:T(8,128)S(1)}, u32[]{:S(2)}, u32[]{:S(2)}) collective-permute-start(f32[40,32]{1,0:T(8,128)S(1)} %add.28.gram_a), channel_id=1, source_target_pairs={{0,8},{1,9},{2,10},{3,11},{4,12},{5,13},{6,14},{7,15},{8,0},{9,1},... | collective-permute-start | bytes 15368 | tf_op jit(solution)/shard_map/ppermute | solution.py:558

commit v10 on v9

--- a/solution.py
+++ b/solution.py
@@ -140,7 +140,8 @@
                 turned[r, pl.ds(s * size, size), :] = tile
                 tile = tile.astype(F32)
                 total = tile if total is None else total + tile
-            inverse[pl.ds(r, 1), :] = 1.0 / jnp.sum(total, axis=0, keepdims=True)
+            total = jnp.sum(total, axis=0, keepdims=True)
+            inverse[r] = jnp.broadcast_to(1.0 / total, inverse.shape[1:])
         return carry
 
     lax.fori_loop(0, chunks // 2, step, 0)
@@ -158,7 +159,7 @@
         prep_kernel,
         out_shape=(
             pltpu.VMEM((rows, slots * size, size), BF16),
-            pltpu.VMEM((rows, size), F32),
+            pltpu.VMEM((rows, 8, size), F32),
             pltpu.SMEM((height, 128), I32),
             pltpu.VMEM((8, 128), I32),
         ),
@@ -203,6 +204,10 @@
     return total
 
 
+def scaled(y, factor):
+    return (y.reshape(-1, *factor.shape) * factor[None]).reshape(y.shape)
+
+
 def store(image, squares, picked, results, mine):
     if squares is None:
         for r, y in zip(picked, results):
@@ -240,7 +245,7 @@
             lax.dot_general(x, turned[r], NN, preferred_element_type=F32)
             for x, r in zip(vectors, picked)
         ]
-        results = [y * inverse[pl.ds(r, 1), :] for r, y in zip(picked, products)]
+        results = [scaled(y, inverse[r]) for r, y in zip(picked, products)]
         for r, y in zip(picked, results):
             sums[r] = y
         mine = [plan[reads, r] == 0 for r in picked]
@@ -276,7 +281,7 @@
                 )
             )
         return picked, [
-            sums[r] + y * inverse[pl.ds(r, 1), :] for r, y in zip(picked, products)
+            sums[r] + scaled(y, inverse[r]) for r, y in zip(picked, products)
         ]
 
     def step(block, carry):

time: 72.5 us -> 72.3 us (level)
  no operation moved by 1% of the time
where the time goes in v10:
time: 72.3 us; the launch traced here: 72.2 us
  starting transfers between devices  41.6 us (58%)
  Pallas kernels  19.7 us (27%)
  waiting for transfers between devices  10.5 us (15%)
    ppermute x16, starting transfers between devices, swap(): return lax.ppermute(array, 'rows', pairs)  41.6 us
    ppermute x16, waiting for transfers between devices, swap(): return lax.ppermute(array, 'rows', pairs)  10.5 us
    pallas_call x4, Pallas kernels, near_rows(): pl.pallas_call(functools.partial(near_kernel, tile_major, last, len(mate)...  9.87 us
    pallas_call x1, Pallas kernels, prep(): pl.pallas_call(prep_kernel, out_shape=(pltpu.VMEM((rows, slots * size, si...  5.99 us
    pallas_call x1, Pallas kernels, final(): pl.pallas_call(functools.partial(final_kernel, float(states)), out_shape=...  2.6 us
  transfers between devices with their start and end apart: 16, of which 10 were waited for; matrix products, arithmetic and copies ran while one was open for 0% of the time, Pallas kernels for 22%

profile of v10, /device:TPU:0, one launch (start us, length us, event | category | flops | bytes accessed | tf_op | source)
XLA Modules:
  0.0 72.2 jit_solution(2057294167991282485)
XLA Ops:
  0.0 0.0 copy-start
  0.0 0.5 collective-permute-start.18
  0.5 0.7 collective-permute-start.17
  1.2 0.1 pad_add_fusion.1.where
  1.2 6.0 %prep.3 = (bf16[64,640,128]{2,1,0:T(8,128)(2,1)S(1)}, f32[64,8,128]{2,1,0:T(8,128)S(1)}, s32[24,128]{1,0:T(8,128)S(4)}, s32[8,128]{1,0:T(8,128)S(1)}) custom-call(s32[2]{0:T(128)S(1)} %pad_add_fusion.1.where, s32[5,64]{1,0:T(8,128)} %bitcast.7, bf16[64,5,128,128]{3,2,1,0:T(8,128)(2,1)} %tiles.1), custom_call_target="tpu_custom_call" | custom-call | flops 167772160 | bytes 20971520 | tf_op jit(solution)/shard_map/prep/pallas_call | solution.py:158
  7.2 0.7 collective-permute-start.16
  7.9 0.0 collective-permute-done.18.refs_0_
  7.9 0.0 copy-done
  7.9 2.4 %near_rows.12 = (bf16[64,32,128]{2,1,0:T(8,128)(2,1)S(1)}, f32[64,32,128]{2,1,0:T(8,128)S(1)}) custom-call(s32[24,128]{1,0:T(8,128)S(4)} %get-tuple-element.77.plan, bf16[64,640,128]{2,1,0:T(8,128)(2,1)S(1)} %get-tuple-element.78.turned, f32[64,8,128]{2,1,0:T(8,128)S(1)} %get-tuple-element.79.inverse, bf16[32,8192]{1,0:T(8,128)(2,1)S(1)} %copy-done, ...), custom_call_target="tpu_custom_call" | custom-call | bytes 1024 | tf_op jit(solution)/shard_map/near_rows/pallas_call | solution.py:377
  10.3 0.0 collective-permute-done.16.asked
  10.3 0.0 collective-permute-done.17.other
  10.3 0.7 far_rows.12
  11.0 0.7 collective-permute-start.19
  11.7 11.1 %collective-permute-start.20 = (bf16[32,32,128]{2,1,0:T(8,128)(2,1)S(1)}, bf16[32,32,128]{2,1,0:T(8,128)(2,1)S(1)}, u32[]{:S(2)}, u32[]{:S(2)}) collective-permute-start(bf16[32,32,128]{2,1,0:T(8,128)(2,1)S(1)} %get-tuple-element.85), channel_id=1, source_target_pairs={{0,1},{1,0},{2,3},{3,2},{4,5},{5,4},{6,7},{7,6},{8,9},{9,8},{10,11... | collective-permute-start | bytes 786440 | tf_op jit(solution)/shard_map/ppermute | solution.py:563
  22.8 0.1 collective-permute-start.21
  22.9 1.1 %collective-permute-done.20.refs_0_ = bf16[32,32,128]{2,1,0:T(8,128)(2,1)S(1)} collective-permute-done((bf16[32,32,128]{2,1,0:T(8,128)(2,1)S(1)}, bf16[32,32,128]{2,1,0:T(8,128)(2,1)S(1)}, u32[]{:S(2)}, u32[]{:S(2)}) %collective-permute-start.20) | collective-permute-done | bytes 262176 | tf_op jit(solution)/shard_map/ppermute | solution.py:563
  24.0 0.4 collective-permute-done.21.refs_1_
  24.4 2.3 %near_rows.13 = (bf16[64,32,128]{2,1,0:T(8,128)(2,1)S(1)}, f32[64,32,128]{2,1,0:T(8,128)S(1)}) custom-call(s32[24,128]{1,0:T(8,128)S(4)} %get-tuple-element.77.plan, bf16[64,640,128]{2,1,0:T(8,128)(2,1)S(1)} %get-tuple-element.78.turned, f32[64,8,128]{2,1,0:T(8,128)S(1)} %get-tuple-element.79.inverse, bf16[64,32,128]{2,1,0:T(8,128)(2,1)S(1)} %get-tuple-element.84.own, ...), custom_call_target="tpu_custom_call" | custom-call | bytes 1024 | tf_op jit(solution)/shard_map/near_rows/pallas_call | solution.py:377
  26.7 0.0 collective-permute-done.19.other
  26.7 0.1 far_rows.13
  26.8 0.7 collective-permute-start.22
  27.5 9.1 %collective-permute-start.23 = (bf16[32,32,128]{2,1,0:T(8,128)(2,1)S(1)}, bf16[32,32,128]{2,1,0:T(8,128)(2,1)S(1)}, u32[]{:S(2)}, u32[]{:S(2)}) collective-permute-start(bf16[32,32,128]{2,1,0:T(8,128)(2,1)S(1)} %get-tuple-element.91), channel_id=1, source_target_pairs={{0,1},{1,0},{2,3},{3,2},{4,5},{5,4},{6,7},{7,6},{8,9},{9,8},{10,11... | collective-permute-start | bytes 786440 | tf_op jit(solution)/shard_map/ppermute | solution.py:563
  36.6 0.1 collective-permute-start.24
  36.6 1.1 %collective-permute-done.23.refs_0_ = bf16[32,32,128]{2,1,0:T(8,128)(2,1)S(1)} collective-permute-done((bf16[32,32,128]{2,1,0:T(8,128)(2,1)S(1)}, bf16[32,32,128]{2,1,0:T(8,128)(2,1)S(1)}, u32[]{:S(2)}, u32[]{:S(2)}) %collective-permute-start.23) | collective-permute-done | bytes 262176 | tf_op jit(solution)/shard_map/ppermute | solution.py:563
  37.7 0.4 collective-permute-done.24.refs_1_
  38.1 2.3 %near_rows.14 = (bf16[64,32,128]{2,1,0:T(8,128)(2,1)S(1)}, f32[64,32,128]{2,1,0:T(8,128)S(1)}) custom-call(s32[24,128]{1,0:T(8,128)S(4)} %get-tuple-element.77.plan, bf16[64,640,128]{2,1,0:T(8,128)(2,1)S(1)} %get-tuple-element.78.turned, f32[64,8,128]{2,1,0:T(8,128)S(1)} %get-tuple-element.79.inverse, bf16[64,32,128]{2,1,0:T(8,128)(2,1)S(1)} %get-tuple-element.90.own, ...), custom_call_target="tpu_custom_call" | custom-call | bytes 1024 | tf_op jit(solution)/shard_map/near_rows/pallas_call | solution.py:377
  40.4 0.0 collective-permute-done.22.other
  40.4 0.1 far_rows.14
  40.5 0.7 collective-permute-start.25
  41.2 6.0 %collective-permute-start.26 = (bf16[32,32,128]{2,1,0:T(8,128)(2,1)S(1)}, bf16[32,32,128]{2,1,0:T(8,128)(2,1)S(1)}, u32[]{:S(2)}, u32[]{:S(2)}) collective-permute-start(bf16[32,32,128]{2,1,0:T(8,128)(2,1)S(1)} %get-tuple-element.97), channel_id=1, source_target_pairs={{0,1},{1,0},{2,3},{3,2},{4,5},{5,4},{6,7},{7,6},{8,9},{9,8},{10,11... | collective-permute-start | bytes 786440 | tf_op jit(solution)/shard_map/ppermute | solution.py:563
  47.2 0.1 collective-permute-start.27
  47.3 1.1 %collective-permute-done.26.refs_0_ = bf16[32,32,128]{2,1,0:T(8,128)(2,1)S(1)} collective-permute-done((bf16[32,32,128]{2,1,0:T(8,128)(2,1)S(1)}, bf16[32,32,128]{2,1,0:T(8,128)(2,1)S(1)}, u32[]{:S(2)}, u32[]{:S(2)}) %collective-permute-start.26) | collective-permute-done | bytes 262176 | tf_op jit(solution)/shard_map/ppermute | solution.py:563
  48.3 0.4 collective-permute-done.27.refs_1_
  48.7 0.0 copy-start.1
  48.7 2.9 %near_rows.15 = (bf16[64,64,128]{2,1,0:T(8,128)(2,1)S(1)}, f32[64,32,128]{2,1,0:T(8,128)S(1)}, f32[64,64]{1,0:T(8,128)S(1)}) custom-call(s32[24,128]{1,0:T(8,128)S(4)} %get-tuple-element.77.plan, bf16[64,640,128]{2,1,0:T(8,128)(2,1)S(1)} %get-tuple-element.78.turned, f32[64,8,128]{2,1,0:T(8,128)S(1)} %get-tuple-element.79.inverse, ...), custom_call_target="tpu_custom_call" | custom-call | bytes 1024 | tf_op jit(solution)/shard_map/near_rows/pallas_call | solution.py:377
  51.6 0.0 collective-permute-done.25.other
  51.7 0.4 far_rows.15
  52.0 3.0 %collective-permute-start.28 = (f32[40,32]{1,0:T(8,128)S(1)}, f32[40,32]{1,0:T(8,128)S(1)}, u32[]{:S(2)}, u32[]{:S(2)}) collective-permute-start(f32[40,32]{1,0:T(8,128)S(1)} %get-tuple-element.102), channel_id=1, source_target_pairs={{0,1},{1,0},{2,3},{3,2},{4,5},{5,4},{6,7},{7,6},{8,9},{9,8},{10,11... | collective-permute-start | bytes 15368 | tf_op jit(solution)/shard_map/ppermute | solution.py:563
  55.1 0.8 %collective-permute-done.28 = f32[40,32]{1,0:T(8,128)S(1)} collective-permute-done((f32[40,32]{1,0:T(8,128)S(1)}, f32[40,32]{1,0:T(8,128)S(1)}, u32[]{:S(2)}, u32[]{:S(2)}) %collective-permute-start.28) | collective-permute-done | bytes 5152 | tf_op jit(solution)/shard_map/ppermute | solution.py:563
  55.9 2.7 %collective-permute-start.29 = (f32[40,32]{1,0:T(8,128)S(1)}, f32[40,32]{1,0:T(8,128)S(1)}, u32[]{:S(2)}, u32[]{:S(2)}) collective-permute-start(f32[40,32]{1,0:T(8,128)S(1)} %add.26), channel_id=1, source_target_pairs={{0,2},{1,3},{2,0},{3,1},{4,6},{5,7},{6,4},{7,5},{8,10},{9,11},{10,... | collective-permute-start | bytes 15368 | tf_op jit(solution)/shard_map/ppermute | solution.py:563
  58.6 1.8 %collective-permute-done.29 = f32[40,32]{1,0:T(8,128)S(1)} collective-permute-done((f32[40,32]{1,0:T(8,128)S(1)}, f32[40,32]{1,0:T(8,128)S(1)}, u32[]{:S(2)}, u32[]{:S(2)}) %collective-permute-start.29) | collective-permute-done | bytes 5152 | tf_op jit(solution)/shard_map/ppermute | solution.py:563
  60.3 2.4 %collective-permute-start.30 = (f32[40,32]{1,0:T(8,128)S(1)}, f32[40,32]{1,0:T(8,128)S(1)}, u32[]{:S(2)}, u32[]{:S(2)}) collective-permute-start(f32[40,32]{1,0:T(8,128)S(1)} %add.27), channel_id=1, source_target_pairs={{0,4},{1,5},{2,6},{3,7},{4,0},{5,1},{6,2},{7,3},{8,12},{9,13},{10,... | collective-permute-start | bytes 15368 | tf_op jit(solution)/shard_map/ppermute | solution.py:563
  62.7 1.8 %collective-permute-done.30 = f32[40,32]{1,0:T(8,128)S(1)} collective-permute-done((f32[40,32]{1,0:T(8,128)S(1)}, f32[40,32]{1,0:T(8,128)S(1)}, u32[]{:S(2)}, u32[]{:S(2)}) %collective-permute-start.30) | collective-permute-done | bytes 5152 | tf_op jit(solution)/shard_map/ppermute | solution.py:563
  64.5 3.2 %collective-permute-start.31 = (f32[40,32]{1,0:T(8,128)S(1)}, f32[40,32]{1,0:T(8,128)S(1)}, u32[]{:S(2)}, u32[]{:S(2)}) collective-permute-start(f32[40,32]{1,0:T(8,128)S(1)} %add.28.gram_a), channel_id=1, source_target_pairs={{0,8},{1,9},{2,10},{3,11},{4,12},{5,13},{6,14},{7,15},{8,0},{9,1},... | collective-permute-start | bytes 15368 | tf_op jit(solution)/shard_map/ppermute | solution.py:563
  67.7 1.8 %collective-permute-done.31.gram_b = f32[40,32]{1,0:T(8,128)S(1)} collective-permute-done((f32[40,32]{1,0:T(8,128)S(1)}, f32[40,32]{1,0:T(8,128)S(1)}, u32[]{:S(2)}, u32[]{:S(2)}) %collective-permute-start.31) | collective-permute-done | bytes 5152 | tf_op jit(solution)/shard_map/ppermute | solution.py:563
  69.4 0.0 copy-done.1
  69.4 2.6 %memberships.3 = (f32[32,8192]{1,0:T(8,128)}, s32[1]{0:T(128)S(4)}) custom-call(f32[40,32]{1,0:T(8,128)S(1)} %add.28.gram_a, f32[40,32]{1,0:T(8,128)S(1)} %collective-permute-done.31.gram_b, f32[32,32]{1,0:T(8,128)S(1)} %copy-done.1, bf16[64,64,128]{2,1,0:T(8,128)(2,1)S(1)} %get-tuple-element.103.parts), custom_call_target="tpu_custom_call" | custom-call | flops 100663296 | bytes 2097152 | tf_op jit(solution)/shard_map/memberships/pallas_call | solution.py:535
  (4 shorter events, 0.0 us)
Async XLA Ops:
  0.0 7.9 %copy-start = (bf16[32,8192]{1,0:T(8,128)(2,1)S(1)}, bf16[32,8192]{1,0:T(8,128)(2,1)}, u32[]{:S(2)}) copy-start(bf16[32,8192]{1,0:T(8,128)(2,1)} %own.1) | copy-start | bytes 1572868
  0.0 7.9 %collective-permute-start.18 = (bf16[32,8192]{1,0:T(8,128)(2,1)}, bf16[32,8192]{1,0:T(8,128)(2,1)S(1)}, u32[]{:S(2)}, u32[]{:S(2)}) collective-permute-start(bf16[32,8192]{1,0:T(8,128)(2,1)} %own.1), channel_id=1, source_target_pairs={{0,1},{1,0},{2,3},{3,2},{4,5},{5,4},{6,7},{7,6},{8,9},{9,8},{10,11... | collective-permute-start | bytes 1572872 | tf_op jit(solution)/shard_map/ppermute | solution.py:563
  0.5 9.9 %collective-permute-start.17 = (bf16[32,8192]{1,0:T(8,128)(2,1)}, bf16[32,8192]{1,0:T(8,128)(2,1)S(1)}, u32[]{:S(2)}, u32[]{:S(2)}) collective-permute-start(bf16[32,8192]{1,0:T(8,128)(2,1)} %own.1), channel_id=1, source_target_pairs={{1,2},{2,1},{3,4},{4,3},{5,6},{6,5},{7,8},{8,7},{9,10},{10,9},{11,... | collective-permute-start | bytes 1572872 | tf_op jit(solution)/shard_map/ppermute | solution.py:563
  7.2 3.1 %collective-permute-start.16 = (s32[8,128]{1,0:T(8,128)S(1)}, s32[8,128]{1,0:T(8,128)S(1)}, u32[]{:S(2)}, u32[]{:S(2)}) collective-permute-start(s32[8,128]{1,0:T(8,128)S(1)} %get-tuple-element.76), channel_id=1, source_target_pairs={{1,2},{2,1},{3,4},{4,3},{5,6},{6,5},{7,8},{8,7},{9,10},{10,9},{11,... | collective-permute-start | bytes 12296 | tf_op jit(solution)/shard_map/ppermute | solution.py:563
  11.0 15.6 %collective-permute-start.19 = (bf16[44,32,128]{2,1,0:T(8,128)(2,1)S(1)}, bf16[44,32,128]{2,1,0:T(8,128)(2,1)S(1)}, u32[]{:S(2)}, u32[]{:S(2)}) collective-permute-start(bf16[44,32,128]{2,1,0:T(8,128)(2,1)S(1)} %get-tuple-element.83), channel_id=1, source_target_pairs={{1,2},{2,1},{3,4},{4,3},{5,6},{6,5},{7,8},{8,7},{9,10},{10,9},{11,... | collective-permute-start | bytes 1081352 | tf_op jit(solution)/shard_map/ppermute | solution.py:563
  11.7 12.3 %collective-permute-start.20 = (bf16[32,32,128]{2,1,0:T(8,128)(2,1)S(1)}, bf16[32,32,128]{2,1,0:T(8,128)(2,1)S(1)}, u32[]{:S(2)}, u32[]{:S(2)}) collective-permute-start(bf16[32,32,128]{2,1,0:T(8,128)(2,1)S(1)} %get-tuple-element.85), channel_id=1, source_target_pairs={{0,1},{1,0},{2,3},{3,2},{4,5},{5,4},{6,7},{7,6},{8,9},{9,8},{10,11... | collective-permute-start | bytes 786440 | tf_op jit(solution)/shard_map/ppermute | solution.py:563
  22.8 1.5 %collective-permute-start.21 = (bf16[32,32,128]{2,1,0:T(8,128)(2,1)S(1)}, bf16[32,32,128]{2,1,0:T(8,128)(2,1)S(1)}, u32[]{:S(2)}, u32[]{:S(2)}) collective-permute-start(bf16[32,32,128]{2,1,0:T(8,128)(2,1)S(1)} %get-tuple-element.86), channel_id=1, source_target_pairs={{0,1},{1,0},{2,3},{3,2},{4,5},{5,4},{6,7},{7,6},{8,9},{9,8},{10,11... | collective-permute-start | bytes 786440 | tf_op jit(solution)/shard_map/ppermute | solution.py:563
  26.8 13.6 %collective-permute-start.22 = (bf16[44,32,128]{2,1,0:T(8,128)(2,1)S(1)}, bf16[44,32,128]{2,1,0:T(8,128)(2,1)S(1)}, u32[]{:S(2)}, u32[]{:S(2)}) collective-permute-start(bf16[44,32,128]{2,1,0:T(8,128)(2,1)S(1)} %get-tuple-element.89), channel_id=1, source_target_pairs={{1,2},{2,1},{3,4},{4,3},{5,6},{6,5},{7,8},{8,7},{9,10},{10,9},{11,... | collective-permute-start | bytes 1081352 | tf_op jit(solution)/shard_map/ppermute | solution.py:563
  27.5 10.3 %collective-permute-start.23 = (bf16[32,32,128]{2,1,0:T(8,128)(2,1)S(1)}, bf16[32,32,128]{2,1,0:T(8,128)(2,1)S(1)}, u32[]{:S(2)}, u32[]{:S(2)}) collective-permute-start(bf16[32,32,128]{2,1,0:T(8,128)(2,1)S(1)} %get-tuple-element.91), channel_id=1, source_target_pairs={{0,1},{1,0},{2,3},{3,2},{4,5},{5,4},{6,7},{7,6},{8,9},{9,8},{10,11... | collective-permute-start | bytes 786440 | tf_op jit(solution)/shard_map/ppermute | solution.py:563
  36.6 1.5 %collective-permute-start.24 = (bf16[32,32,128]{2,1,0:T(8,128)(2,1)S(1)}, bf16[32,32,128]{2,1,0:T(8,128)(2,1)S(1)}, u32[]{:S(2)}, u32[]{:S(2)}) collective-permute-start(bf16[32,32,128]{2,1,0:T(8,128)(2,1)S(1)} %get-tuple-element.92), channel_id=1, source_target_pairs={{0,1},{1,0},{2,3},{3,2},{4,5},{5,4},{6,7},{7,6},{8,9},{9,8},{10,11... | collective-permute-start | bytes 786440 | tf_op jit(solution)/shard_map/ppermute | solution.py:563
  40.5 11.2 %collective-permute-start.25 = (bf16[44,32,128]{2,1,0:T(8,128)(2,1)S(1)}, bf16[44,32,128]{2,1,0:T(8,128)(2,1)S(1)}, u32[]{:S(2)}, u32[]{:S(2)}) collective-permute-start(bf16[44,32,128]{2,1,0:T(8,128)(2,1)S(1)} %get-tuple-element.95), channel_id=1, source_target_pairs={{1,2},{2,1},{3,4},{4,3},{5,6},{6,5},{7,8},{8,7},{9,10},{10,9},{11,... | collective-permute-start | bytes 1081352 | tf_op jit(solution)/shard_map/ppermute | solution.py:563
  41.2 7.1 %collective-permute-start.26 = (bf16[32,32,128]{2,1,0:T(8,128)(2,1)S(1)}, bf16[32,32,128]{2,1,0:T(8,128)(2,1)S(1)}, u32[]{:S(2)}, u32[]{:S(2)}) collective-permute-start(bf16[32,32,128]{2,1,0:T(8,128)(2,1)S(1)} %get-tuple-element.97), channel_id=1, source_target_pairs={{0,1},{1,0},{2,3},{3,2},{4,5},{5,4},{6,7},{7,6},{8,9},{9,8},{10,11... | collective-permute-start | bytes 786440 | tf_op jit(solution)/shard_map/ppermute | solution.py:563
  47.2 1.5 %collective-permute-start.27 = (bf16[32,32,128]{2,1,0:T(8,128)(2,1)S(1)}, bf16[32,32,128]{2,1,0:T(8,128)(2,1)S(1)}, u32[]{:S(2)}, u32[]{:S(2)}) collective-permute-start(bf16[32,32,128]{2,1,0:T(8,128)(2,1)S(1)} %get-tuple-element.98), channel_id=1, source_target_pairs={{0,1},{1,0},{2,3},{3,2},{4,5},{5,4},{6,7},{7,6},{8,9},{9,8},{10,11... | collective-permute-start | bytes 786440 | tf_op jit(solution)/shard_map/ppermute | solution.py:563
  48.7 20.7 %copy-start.1 = (f32[32,32]{1,0:T(8,128)S(1)}, f32[32,32]{1,0:T(8,128)}, u32[]{:S(2)}) copy-start(f32[32,32]{1,0:T(8,128)} %mapping.1) | copy-start | bytes 12292
  52.0 3.9 %collective-permute-start.28 = (f32[40,32]{1,0:T(8,128)S(1)}, f32[40,32]{1,0:T(8,128)S(1)}, u32[]{:S(2)}, u32[]{:S(2)}) collective-permute-start(f32[40,32]{1,0:T(8,128)S(1)} %get-tuple-element.102), channel_id=1, source_target_pairs={{0,1},{1,0},{2,3},{3,2},{4,5},{5,4},{6,7},{7,6},{8,9},{9,8},{10,11... | collective-permute-start | bytes 15368 | tf_op jit(solution)/shard_map/ppermute | solution.py:563
  55.9 4.4 %collective-permute-start.29 = (f32[40,32]{1,0:T(8,128)S(1)}, f32[40,32]{1,0:T(8,128)S(1)}, u32[]{:S(2)}, u32[]{:S(2)}) collective-permute-start(f32[40,32]{1,0:T(8,128)S(1)} %add.26), channel_id=1, source_target_pairs={{0,2},{1,3},{2,0},{3,1},{4,6},{5,7},{6,4},{7,5},{8,10},{9,11},{10,... | collective-permute-start | bytes 15368 | tf_op jit(solution)/shard_map/ppermute | solution.py:563
  60.3 4.1 %collective-permute-start.30 = (f32[40,32]{1,0:T(8,128)S(1)}, f32[40,32]{1,0:T(8,128)S(1)}, u32[]{:S(2)}, u32[]{:S(2)}) collective-permute-start(f32[40,32]{1,0:T(8,128)S(1)} %add.27), channel_id=1, source_target_pairs={{0,4},{1,5},{2,6},{3,7},{4,0},{5,1},{6,2},{7,3},{8,12},{9,13},{10,... | collective-permute-start | bytes 15368 | tf_op jit(solution)/shard_map/ppermute | solution.py:563
  64.5 5.0 %collective-permute-start.31 = (f32[40,32]{1,0:T(8,128)S(1)}, f32[40,32]{1,0:T(8,128)S(1)}, u32[]{:S(2)}, u32[]{:S(2)}) collective-permute-start(f32[40,32]{1,0:T(8,128)S(1)} %add.28.gram_a), channel_id=1, source_target_pairs={{0,8},{1,9},{2,10},{3,11},{4,12},{5,13},{6,14},{7,15},{8,0},{9,1},... | collective-permute-start | bytes 15368 | tf_op jit(solution)/shard_map/ppermute | solution.py:563

commit v11 on v10

--- a/solution.py
+++ b/solution.py
@@ -232,7 +232,7 @@
     start = rows
     for panel in mate:
         fill(window, start, panel, tile_major)
-        start += panel.shape[0]
+        start += panel.shape[0] if tile_major else panel.shape[1] // size
     window[2 * rows] = jnp.zeros(window.shape[1:], BF16)
 
     def step(block, squares):
@@ -565,10 +565,11 @@
     limit = 11 * rows // 16
     where = jnp.stack([me * rows, me % 2]).astype(I32)
     columns = column_tiles.T
-    mate, other = swap(schur_basis, mates), swap(schur_basis, others)
+    other = swap(schur_basis, others)
+    mate = [swap(half, mates) for half in jnp.split(schur_basis, 2, axis=1)]
     turned, inverse, plan, wanted = prep(where, columns, transition_tiles)
     asked = swap(wanted, others)
-    image, sums = near_rows(plan, turned, inverse, schur_basis, (mate,), False, False)
+    image, sums = near_rows(plan, turned, inverse, schur_basis, mate, False, False)
     if whole:
         image, *halves = far_rows_whole(plan, turned, inverse, other, sums, image, False)
         send, sending = image, asked

time: 72.3 us -> 74.2 us (1.026)
  local copies, waits for them, and re-layouts: 0.01 us -> 2.04 us
  starting transfers between devices: 41.6 us -> 40.6 us
    split x0 -> x1, local copies, waits for them, and re-layouts: none -> 1.07 us  [memberships(): mate = [swap(half, mates) for half in jnp.split(schur_basis, 2, axis=1)]]
    unnamed x4 -> x6, local copies, waits for them, and re-layouts: 0.01 us -> 0.97 us
    ppermute x16 -> x17, starting transfers between devices: 41.6 us -> 40.6 us  [swap(): return lax.ppermute(array, 'rows', pairs)]
    ppermute x16 -> x17, waiting for transfers between devices: 10.5 us -> 10.6 us  [swap(): return lax.ppermute(array, 'rows', pairs)]
  transfers between devices with their start and end apart: 16 -> 17, of which waited for: 10 -> 10; matrix products, arithmetic and copies ran while one was open for 0% -> 2% of each run, Pallas kernels for 22% -> 21%
where the time goes in v11:
time: 74.2 us; the launch traced here: 73.8 us
  starting transfers between devices  40.6 us (55%)
  Pallas kernels  20.2 us (27%)
  waiting for transfers between devices  10.6 us (14%)
  local copies, waits for them, and re-layouts  2.04 us (3%)
    ppermute x17, starting transfers between devices, swap(): return lax.ppermute(array, 'rows', pairs)  40.6 us
    ppermute x17, waiting for transfers between devices, swap(): return lax.ppermute(array, 'rows', pairs)  10.6 us
    pallas_call x4, Pallas kernels, near_rows(): pl.pallas_call(functools.partial(near_kernel, tile_major, last, len(mate)...  9.86 us
    pallas_call x1, Pallas kernels, prep(): pl.pallas_call(prep_kernel, out_shape=(pltpu.VMEM((rows, slots * size, si...  5.99 us
    pallas_call x1, Pallas kernels, final(): pl.pallas_call(functools.partial(final_kernel, float(states)), out_shape=...  3.15 us
  transfers between devices with their start and end apart: 17, of which 10 were waited for; matrix products, arithmetic and copies ran while one was open for 2% of the time, Pallas kernels for 21%

profile of v11, /device:TPU:0, one launch (start us, length us, event | category | flops | bytes accessed | tf_op | source)
XLA Modules:
  0.0 73.8 jit_solution(3638616805867301787)
XLA Ops:
  0.0 0.0 copy-start
  0.0 0.8 %collective-permute-start.18 = (bf16[32,8192]{1,0:T(8,128)(2,1)}, bf16[32,8192]{1,0:T(8,128)(2,1)S(1)}, u32[]{:S(2)}, u32[]{:S(2)}) collective-permute-start(bf16[32,8192]{1,0:T(8,128)(2,1)} %own.1), channel_id=1, source_target_pairs={{1,2},{2,1},{3,4},{4,3},{5,6},{6,5},{7,8},{8,7},{9,10},{10,9},{11,... | collective-permute-start | bytes 1572872 | tf_op jit(solution)/shard_map/ppermute | solution.py:563
  0.8 1.1 %fusion.1 = (bf16[32,4096]{1,0:T(8,128)(2,1)S(1)}, bf16[32,4096]{1,0:T(8,128)(2,1)S(1)}) fusion(bf16[32,8192]{1,0:T(8,128)(2,1)} %own.1), kind=kLoop, calls=%fused_computation.3 | loop fusion | bytes 1048576 | tf_op jit(solution)/shard_map/split | solution.py:569
  1.9 4.3 %collective-permute-start.20 = (bf16[32,4096]{1,0:T(8,128)(2,1)S(1)}, bf16[32,4096]{1,0:T(8,128)(2,1)S(1)}, u32[]{:S(2)}, u32[]{:S(2)}) collective-permute-start(bf16[32,4096]{1,0:T(8,128)(2,1)S(1)} %get-tuple-element.109), channel_id=1, source_target_pairs={{0,1},{1,0},{2,3},{3,2},{4,5},{5,4},{6,7},{7,6},{8,9},{9,8},{10,11... | collective-permute-start | bytes 786440 | tf_op jit(solution)/shard_map/ppermute | solution.py:563
  6.2 0.1 collective-permute-start.19
  6.3 0.1 pad_add_fusion.1.where
  6.4 6.0 %prep.3 = (bf16[64,640,128]{2,1,0:T(8,128)(2,1)S(1)}, f32[64,8,128]{2,1,0:T(8,128)S(1)}, s32[24,128]{1,0:T(8,128)S(4)}, s32[8,128]{1,0:T(8,128)S(1)}) custom-call(s32[2]{0:T(128)S(1)} %pad_add_fusion.1.where, s32[5,64]{1,0:T(8,128)} %bitcast.7, bf16[64,5,128,128]{3,2,1,0:T(8,128)(2,1)} %tiles.1), custom_call_target="tpu_custom_call" | custom-call | flops 167772160 | bytes 20971520 | tf_op jit(solution)/shard_map/prep/pallas_call | solution.py:158
  12.4 0.7 collective-permute-start.17
  13.0 0.0 collective-permute-done.20.refs_1_
  13.1 0.0 collective-permute-done.19.refs_0_
  13.1 0.0 copy-done
  13.1 2.4 %near_rows.12 = (bf16[64,32,128]{2,1,0:T(8,128)(2,1)S(1)}, f32[64,32,128]{2,1,0:T(8,128)S(1)}) custom-call(s32[24,128]{1,0:T(8,128)S(4)} %get-tuple-element.77.plan, bf16[64,640,128]{2,1,0:T(8,128)(2,1)S(1)} %get-tuple-element.78.turned, f32[64,8,128]{2,1,0:T(8,128)S(1)} %get-tuple-element.79.inverse, bf16[32,8192]{1,0:T(8,128)(2,1)S(1)} %copy-done, ...), custom_call_target="tpu_custom_call" | custom-call | bytes 1024 | tf_op jit(solution)/shard_map/near_rows/pallas_call | solution.py:377
  15.5 0.0 collective-permute-done.17.asked
  15.5 0.0 collective-permute-done.18.other
  15.5 0.7 far_rows.12
  16.2 0.7 collective-permute-start.21
  16.9 6.0 %collective-permute-start.22 = (bf16[32,32,128]{2,1,0:T(8,128)(2,1)S(1)}, bf16[32,32,128]{2,1,0:T(8,128)(2,1)S(1)}, u32[]{:S(2)}, u32[]{:S(2)}) collective-permute-start(bf16[32,32,128]{2,1,0:T(8,128)(2,1)S(1)} %get-tuple-element.85), channel_id=1, source_target_pairs={{0,1},{1,0},{2,3},{3,2},{4,5},{5,4},{6,7},{7,6},{8,9},{9,8},{10,11... | collective-permute-start | bytes 786440 | tf_op jit(solution)/shard_map/ppermute | solution.py:563
  22.8 0.1 collective-permute-start.23
  22.9 1.1 %collective-permute-done.22.refs_0_ = bf16[32,32,128]{2,1,0:T(8,128)(2,1)S(1)} collective-permute-done((bf16[32,32,128]{2,1,0:T(8,128)(2,1)S(1)}, bf16[32,32,128]{2,1,0:T(8,128)(2,1)S(1)}, u32[]{:S(2)}, u32[]{:S(2)}) %collective-permute-start.22) | collective-permute-done | bytes 262176 | tf_op jit(solution)/shard_map/ppermute | solution.py:563
  24.0 0.4 collective-permute-done.23.refs_1_
  24.4 2.3 %near_rows.13 = (bf16[64,32,128]{2,1,0:T(8,128)(2,1)S(1)}, f32[64,32,128]{2,1,0:T(8,128)S(1)}) custom-call(s32[24,128]{1,0:T(8,128)S(4)} %get-tuple-element.77.plan, bf16[64,640,128]{2,1,0:T(8,128)(2,1)S(1)} %get-tuple-element.78.turned, f32[64,8,128]{2,1,0:T(8,128)S(1)} %get-tuple-element.79.inverse, bf16[64,32,128]{2,1,0:T(8,128)(2,1)S(1)} %get-tuple-element.84.own, ...), custom_call_target="tpu_custom_call" | custom-call | bytes 1024 | tf_op jit(solution)/shard_map/near_rows/pallas_call | solution.py:377
  26.7 0.0 collective-permute-done.21.other
  26.7 0.1 far_rows.13
  26.8 0.7 collective-permute-start.24
  27.5 9.2 %collective-permute-start.25 = (bf16[32,32,128]{2,1,0:T(8,128)(2,1)S(1)}, bf16[32,32,128]{2,1,0:T(8,128)(2,1)S(1)}, u32[]{:S(2)}, u32[]{:S(2)}) collective-permute-start(bf16[32,32,128]{2,1,0:T(8,128)(2,1)S(1)} %get-tuple-element.91), channel_id=1, source_target_pairs={{0,1},{1,0},{2,3},{3,2},{4,5},{5,4},{6,7},{7,6},{8,9},{9,8},{10,11... | collective-permute-start | bytes 786440 | tf_op jit(solution)/shard_map/ppermute | solution.py:563
  36.7 0.1 collective-permute-start.26
  36.8 1.1 %collective-permute-done.25.refs_0_ = bf16[32,32,128]{2,1,0:T(8,128)(2,1)S(1)} collective-permute-done((bf16[32,32,128]{2,1,0:T(8,128)(2,1)S(1)}, bf16[32,32,128]{2,1,0:T(8,128)(2,1)S(1)}, u32[]{:S(2)}, u32[]{:S(2)}) %collective-permute-start.25) | collective-permute-done | bytes 262176 | tf_op jit(solution)/shard_map/ppermute | solution.py:563
  37.8 0.4 collective-permute-done.26.refs_1_
  38.2 2.3 %near_rows.14 = (bf16[64,32,128]{2,1,0:T(8,128)(2,1)S(1)}, f32[64,32,128]{2,1,0:T(8,128)S(1)}) custom-call(s32[24,128]{1,0:T(8,128)S(4)} %get-tuple-element.77.plan, bf16[64,640,128]{2,1,0:T(8,128)(2,1)S(1)} %get-tuple-element.78.turned, f32[64,8,128]{2,1,0:T(8,128)S(1)} %get-tuple-element.79.inverse, bf16[64,32,128]{2,1,0:T(8,128)(2,1)S(1)} %get-tuple-element.90.own, ...), custom_call_target="tpu_custom_call" | custom-call | bytes 1024 | tf_op jit(solution)/shard_map/near_rows/pallas_call | solution.py:377
  40.5 0.0 collective-permute-done.24.other
  40.5 0.1 far_rows.14
  40.6 0.7 collective-permute-start.27
  41.3 7.6 %collective-permute-start.28 = (bf16[32,32,128]{2,1,0:T(8,128)(2,1)S(1)}, bf16[32,32,128]{2,1,0:T(8,128)(2,1)S(1)}, u32[]{:S(2)}, u32[]{:S(2)}) collective-permute-start(bf16[32,32,128]{2,1,0:T(8,128)(2,1)S(1)} %get-tuple-element.97), channel_id=1, source_target_pairs={{0,1},{1,0},{2,3},{3,2},{4,5},{5,4},{6,7},{7,6},{8,9},{9,8},{10,11... | collective-permute-start | bytes 786440 | tf_op jit(solution)/shard_map/ppermute | solution.py:563
  48.9 0.1 collective-permute-start.29
  49.0 1.1 %collective-permute-done.28.refs_0_ = bf16[32,32,128]{2,1,0:T(8,128)(2,1)S(1)} collective-permute-done((bf16[32,32,128]{2,1,0:T(8,128)(2,1)S(1)}, bf16[32,32,128]{2,1,0:T(8,128)(2,1)S(1)}, u32[]{:S(2)}, u32[]{:S(2)}) %collective-permute-start.28) | collective-permute-done | bytes 262176 | tf_op jit(solution)/shard_map/ppermute | solution.py:563
  50.0 0.4 collective-permute-done.29.refs_1_
  50.4 0.0 copy-start.1
  50.4 2.9 %near_rows.15 = (bf16[64,64,128]{2,1,0:T(8,128)(2,1)S(1)}, f32[64,32,128]{2,1,0:T(8,128)S(1)}, f32[64,64]{1,0:T(8,128)S(1)}) custom-call(s32[24,128]{1,0:T(8,128)S(4)} %get-tuple-element.77.plan, bf16[64,640,128]{2,1,0:T(8,128)(2,1)S(1)} %get-tuple-element.78.turned, f32[64,8,128]{2,1,0:T(8,128)S(1)} %get-tuple-element.79.inverse, ...), custom_call_target="tpu_custom_call" | custom-call | bytes 1024 | tf_op jit(solution)/shard_map/near_rows/pallas_call | solution.py:377
  53.4 0.0 collective-permute-done.27.other
  53.4 0.4 far_rows.15
  53.7 1.6 %collective-permute-start.30 = (f32[40,32]{1,0:T(8,128)S(1)}, f32[40,32]{1,0:T(8,128)S(1)}, u32[]{:S(2)}, u32[]{:S(2)}) collective-permute-start(f32[40,32]{1,0:T(8,128)S(1)} %get-tuple-element.102), channel_id=1, source_target_pairs={{0,1},{1,0},{2,3},{3,2},{4,5},{5,4},{6,7},{7,6},{8,9},{9,8},{10,11... | collective-permute-start | bytes 15368 | tf_op jit(solution)/shard_map/ppermute | solution.py:563
  55.3 0.8 %collective-permute-done.30 = f32[40,32]{1,0:T(8,128)S(1)} collective-permute-done((f32[40,32]{1,0:T(8,128)S(1)}, f32[40,32]{1,0:T(8,128)S(1)}, u32[]{:S(2)}, u32[]{:S(2)}) %collective-permute-start.30) | collective-permute-done | bytes 5152 | tf_op jit(solution)/shard_map/ppermute | solution.py:563
  56.2 3.2 %collective-permute-start.31 = (f32[40,32]{1,0:T(8,128)S(1)}, f32[40,32]{1,0:T(8,128)S(1)}, u32[]{:S(2)}, u32[]{:S(2)}) collective-permute-start(f32[40,32]{1,0:T(8,128)S(1)} %add.26), channel_id=1, source_target_pairs={{0,2},{1,3},{2,0},{3,1},{4,6},{5,7},{6,4},{7,5},{8,10},{9,11},{10,... | collective-permute-start | bytes 15368 | tf_op jit(solution)/shard_map/ppermute | solution.py:563
  59.4 1.8 %collective-permute-done.31 = f32[40,32]{1,0:T(8,128)S(1)} collective-permute-done((f32[40,32]{1,0:T(8,128)S(1)}, f32[40,32]{1,0:T(8,128)S(1)}, u32[]{:S(2)}, u32[]{:S(2)}) %collective-permute-start.31) | collective-permute-done | bytes 5152 | tf_op jit(solution)/shard_map/ppermute | solution.py:563
  61.1 2.0 %collective-permute-start.32 = (f32[40,32]{1,0:T(8,128)S(1)}, f32[40,32]{1,0:T(8,128)S(1)}, u32[]{:S(2)}, u32[]{:S(2)}) collective-permute-start(f32[40,32]{1,0:T(8,128)S(1)} %add.27), channel_id=1, source_target_pairs={{0,4},{1,5},{2,6},{3,7},{4,0},{5,1},{6,2},{7,3},{8,12},{9,13},{10,... | collective-permute-start | bytes 15368 | tf_op jit(solution)/shard_map/ppermute | solution.py:563
  63.2 1.8 %collective-permute-done.32 = f32[40,32]{1,0:T(8,128)S(1)} collective-permute-done((f32[40,32]{1,0:T(8,128)S(1)}, f32[40,32]{1,0:T(8,128)S(1)}, u32[]{:S(2)}, u32[]{:S(2)}) %collective-permute-start.32) | collective-permute-done | bytes 5152 | tf_op jit(solution)/shard_map/ppermute | solution.py:563
  64.9 2.8 %collective-permute-start.33 = (f32[40,32]{1,0:T(8,128)S(1)}, f32[40,32]{1,0:T(8,128)S(1)}, u32[]{:S(2)}, u32[]{:S(2)}) collective-permute-start(f32[40,32]{1,0:T(8,128)S(1)} %add.28.gram_a), channel_id=1, source_target_pairs={{0,8},{1,9},{2,10},{3,11},{4,12},{5,13},{6,14},{7,15},{8,0},{9,1},... | collective-permute-start | bytes 15368 | tf_op jit(solution)/shard_map/ppermute | solution.py:563
  67.8 1.8 %collective-permute-done.33.gram_b = f32[40,32]{1,0:T(8,128)S(1)} collective-permute-done((f32[40,32]{1,0:T(8,128)S(1)}, f32[40,32]{1,0:T(8,128)S(1)}, u32[]{:S(2)}, u32[]{:S(2)}) %collective-permute-start.33) | collective-permute-done | bytes 5152 | tf_op jit(solution)/shard_map/ppermute | solution.py:563
  69.6 0.0 copy-done.1
  69.6 3.1 %memberships.3 = (f32[32,8192]{1,0:T(8,128)S(1)}, s32[1]{0:T(128)S(4)}) custom-call(f32[40,32]{1,0:T(8,128)S(1)} %add.28.gram_a, f32[40,32]{1,0:T(8,128)S(1)} %collective-permute-done.33.gram_b, f32[32,32]{1,0:T(8,128)S(1)} %copy-done.1, bf16[64,64,128]{2,1,0:T(8,128)(2,1)S(1)} %get-tuple-element.103.parts), custom_call_target="tpu_custom_call" | custom-call | flops 100663296 | bytes 2097152 | tf_op jit(solution)/shard_map/memberships/pallas_call | solution.py:535
  72.8 0.0 copy-start.2
  72.8 1.0 %copy-done.2 = f32[32,8192]{1,0:T(8,128)} copy-done((f32[32,8192]{1,0:T(8,128)}, f32[32,8192]{1,0:T(8,128)S(1)}, u32[]{:S(2)}) %copy-start.2) | copy-done | bytes 1048600
  (4 shorter events, 0.0 us)
Async XLA Ops:
  0.0 13.1 %copy-start = (bf16[32,8192]{1,0:T(8,128)(2,1)S(1)}, bf16[32,8192]{1,0:T(8,128)(2,1)}, u32[]{:S(2)}) copy-start(bf16[32,8192]{1,0:T(8,128)(2,1)} %own.1) | copy-start | bytes 1572868
  0.0 15.5 %collective-permute-start.18 = (bf16[32,8192]{1,0:T(8,128)(2,1)}, bf16[32,8192]{1,0:T(8,128)(2,1)S(1)}, u32[]{:S(2)}, u32[]{:S(2)}) collective-permute-start(bf16[32,8192]{1,0:T(8,128)(2,1)} %own.1), channel_id=1, source_target_pairs={{1,2},{2,1},{3,4},{4,3},{5,6},{6,5},{7,8},{8,7},{9,10},{10,9},{11,... | collective-permute-start | bytes 1572872 | tf_op jit(solution)/shard_map/ppermute | solution.py:563
  1.9 11.2 %collective-permute-start.20 = (bf16[32,4096]{1,0:T(8,128)(2,1)S(1)}, bf16[32,4096]{1,0:T(8,128)(2,1)S(1)}, u32[]{:S(2)}, u32[]{:S(2)}) collective-permute-start(bf16[32,4096]{1,0:T(8,128)(2,1)S(1)} %get-tuple-element.109), channel_id=1, source_target_pairs={{0,1},{1,0},{2,3},{3,2},{4,5},{5,4},{6,7},{7,6},{8,9},{9,8},{10,11... | collective-permute-start | bytes 786440 | tf_op jit(solution)/shard_map/ppermute | solution.py:563
  6.2 6.8 %collective-permute-start.19 = (bf16[32,4096]{1,0:T(8,128)(2,1)S(1)}, bf16[32,4096]{1,0:T(8,128)(2,1)S(1)}, u32[]{:S(2)}, u32[]{:S(2)}) collective-permute-start(bf16[32,4096]{1,0:T(8,128)(2,1)S(1)} %get-tuple-element.110), channel_id=1, source_target_pairs={{0,1},{1,0},{2,3},{3,2},{4,5},{5,4},{6,7},{7,6},{8,9},{9,8},{10,11... | collective-permute-start | bytes 786440 | tf_op jit(solution)/shard_map/ppermute | solution.py:563
  12.4 3.1 %collective-permute-start.17 = (s32[8,128]{1,0:T(8,128)S(1)}, s32[8,128]{1,0:T(8,128)S(1)}, u32[]{:S(2)}, u32[]{:S(2)}) collective-permute-start(s32[8,128]{1,0:T(8,128)S(1)} %get-tuple-element.76), channel_id=1, source_target_pairs={{1,2},{2,1},{3,4},{4,3},{5,6},{6,5},{7,8},{8,7},{9,10},{10,9},{11,... | collective-permute-start | bytes 12296 | tf_op jit(solution)/shard_map/ppermute | solution.py:563
  16.2 10.5 %collective-permute-start.21 = (bf16[44,32,128]{2,1,0:T(8,128)(2,1)S(1)}, bf16[44,32,128]{2,1,0:T(8,128)(2,1)S(1)}, u32[]{:S(2)}, u32[]{:S(2)}) collective-permute-start(bf16[44,32,128]{2,1,0:T(8,128)(2,1)S(1)} %get-tuple-element.83), channel_id=1, source_target_pairs={{1,2},{2,1},{3,4},{4,3},{5,6},{6,5},{7,8},{8,7},{9,10},{10,9},{11,... | collective-permute-start | bytes 1081352 | tf_op jit(solution)/shard_map/ppermute | solution.py:563
  16.9 7.1 %collective-permute-start.22 = (bf16[32,32,128]{2,1,0:T(8,128)(2,1)S(1)}, bf16[32,32,128]{2,1,0:T(8,128)(2,1)S(1)}, u32[]{:S(2)}, u32[]{:S(2)}) collective-permute-start(bf16[32,32,128]{2,1,0:T(8,128)(2,1)S(1)} %get-tuple-element.85), channel_id=1, source_target_pairs={{0,1},{1,0},{2,3},{3,2},{4,5},{5,4},{6,7},{7,6},{8,9},{9,8},{10,11... | collective-permute-start | bytes 786440 | tf_op jit(solution)/shard_map/ppermute | solution.py:563
  22.8 1.5 %collective-permute-start.23 = (bf16[32,32,128]{2,1,0:T(8,128)(2,1)S(1)}, bf16[32,32,128]{2,1,0:T(8,128)(2,1)S(1)}, u32[]{:S(2)}, u32[]{:S(2)}) collective-permute-start(bf16[32,32,128]{2,1,0:T(8,128)(2,1)S(1)} %get-tuple-element.86), channel_id=1, source_target_pairs={{0,1},{1,0},{2,3},{3,2},{4,5},{5,4},{6,7},{7,6},{8,9},{9,8},{10,11... | collective-permute-start | bytes 786440 | tf_op jit(solution)/shard_map/ppermute | solution.py:563
  26.8 13.7 %collective-permute-start.24 = (bf16[44,32,128]{2,1,0:T(8,128)(2,1)S(1)}, bf16[44,32,128]{2,1,0:T(8,128)(2,1)S(1)}, u32[]{:S(2)}, u32[]{:S(2)}) collective-permute-start(bf16[44,32,128]{2,1,0:T(8,128)(2,1)S(1)} %get-tuple-element.89), channel_id=1, source_target_pairs={{1,2},{2,1},{3,4},{4,3},{5,6},{6,5},{7,8},{8,7},{9,10},{10,9},{11,... | collective-permute-start | bytes 1081352 | tf_op jit(solution)/shard_map/ppermute | solution.py:563
  27.5 10.4 %collective-permute-start.25 = (bf16[32,32,128]{2,1,0:T(8,128)(2,1)S(1)}, bf16[32,32,128]{2,1,0:T(8,128)(2,1)S(1)}, u32[]{:S(2)}, u32[]{:S(2)}) collective-permute-start(bf16[32,32,128]{2,1,0:T(8,128)(2,1)S(1)} %get-tuple-element.91), channel_id=1, source_target_pairs={{0,1},{1,0},{2,3},{3,2},{4,5},{5,4},{6,7},{7,6},{8,9},{9,8},{10,11... | collective-permute-start | bytes 786440 | tf_op jit(solution)/shard_map/ppermute | solution.py:563
  36.7 1.5 %collective-permute-start.26 = (bf16[32,32,128]{2,1,0:T(8,128)(2,1)S(1)}, bf16[32,32,128]{2,1,0:T(8,128)(2,1)S(1)}, u32[]{:S(2)}, u32[]{:S(2)}) collective-permute-start(bf16[32,32,128]{2,1,0:T(8,128)(2,1)S(1)} %get-tuple-element.92), channel_id=1, source_target_pairs={{0,1},{1,0},{2,3},{3,2},{4,5},{5,4},{6,7},{7,6},{8,9},{9,8},{10,11... | collective-permute-start | bytes 786440 | tf_op jit(solution)/shard_map/ppermute | solution.py:563
  40.6 12.7 %collective-permute-start.27 = (bf16[44,32,128]{2,1,0:T(8,128)(2,1)S(1)}, bf16[44,32,128]{2,1,0:T(8,128)(2,1)S(1)}, u32[]{:S(2)}, u32[]{:S(2)}) collective-permute-start(bf16[44,32,128]{2,1,0:T(8,128)(2,1)S(1)} %get-tuple-element.95), channel_id=1, source_target_pairs={{1,2},{2,1},{3,4},{4,3},{5,6},{6,5},{7,8},{8,7},{9,10},{10,9},{11,... | collective-permute-start | bytes 1081352 | tf_op jit(solution)/shard_map/ppermute | solution.py:563
  41.3 8.7 %collective-permute-start.28 = (bf16[32,32,128]{2,1,0:T(8,128)(2,1)S(1)}, bf16[32,32,128]{2,1,0:T(8,128)(2,1)S(1)}, u32[]{:S(2)}, u32[]{:S(2)}) collective-permute-start(bf16[32,32,128]{2,1,0:T(8,128)(2,1)S(1)} %get-tuple-element.97), channel_id=1, source_target_pairs={{0,1},{1,0},{2,3},{3,2},{4,5},{5,4},{6,7},{7,6},{8,9},{9,8},{10,11... | collective-permute-start | bytes 786440 | tf_op jit(solution)/shard_map/ppermute | solution.py:563
  48.9 1.5 %collective-permute-start.29 = (bf16[32,32,128]{2,1,0:T(8,128)(2,1)S(1)}, bf16[32,32,128]{2,1,0:T(8,128)(2,1)S(1)}, u32[]{:S(2)}, u32[]{:S(2)}) collective-permute-start(bf16[32,32,128]{2,1,0:T(8,128)(2,1)S(1)} %get-tuple-element.98), channel_id=1, source_target_pairs={{0,1},{1,0},{2,3},{3,2},{4,5},{5,4},{6,7},{7,6},{8,9},{9,8},{10,11... | collective-permute-start | bytes 786440 | tf_op jit(solution)/shard_map/ppermute | solution.py:563
  50.4 19.2 %copy-start.1 = (f32[32,32]{1,0:T(8,128)S(1)}, f32[32,32]{1,0:T(8,128)}, u32[]{:S(2)}) copy-start(f32[32,32]{1,0:T(8,128)} %mapping.1) | copy-start | bytes 12292
  53.7 2.5 %collective-permute-start.30 = (f32[40,32]{1,0:T(8,128)S(1)}, f32[40,32]{1,0:T(8,128)S(1)}, u32[]{:S(2)}, u32[]{:S(2)}) collective-permute-start(f32[40,32]{1,0:T(8,128)S(1)} %get-tuple-element.102), channel_id=1, source_target_pairs={{0,1},{1,0},{2,3},{3,2},{4,5},{5,4},{6,7},{7,6},{8,9},{9,8},{10,11... | collective-permute-start | bytes 15368 | tf_op jit(solution)/shard_map/ppermute | solution.py:563
  56.2 4.9 %collective-permute-start.31 = (f32[40,32]{1,0:T(8,128)S(1)}, f32[40,32]{1,0:T(8,128)S(1)}, u32[]{:S(2)}, u32[]{:S(2)}) collective-permute-start(f32[40,32]{1,0:T(8,128)S(1)} %add.26), channel_id=1, source_target_pairs={{0,2},{1,3},{2,0},{3,1},{4,6},{5,7},{6,4},{7,5},{8,10},{9,11},{10,... | collective-permute-start | bytes 15368 | tf_op jit(solution)/shard_map/ppermute | solution.py:563
  61.1 3.8 %collective-permute-start.32 = (f32[40,32]{1,0:T(8,128)S(1)}, f32[40,32]{1,0:T(8,128)S(1)}, u32[]{:S(2)}, u32[]{:S(2)}) collective-permute-start(f32[40,32]{1,0:T(8,128)S(1)} %add.27), channel_id=1, source_target_pairs={{0,4},{1,5},{2,6},{3,7},{4,0},{5,1},{6,2},{7,3},{8,12},{9,13},{10,... | collective-permute-start | bytes 15368 | tf_op jit(solution)/shard_map/ppermute | solution.py:563
  64.9 4.7 %collective-permute-start.33 = (f32[40,32]{1,0:T(8,128)S(1)}, f32[40,32]{1,0:T(8,128)S(1)}, u32[]{:S(2)}, u32[]{:S(2)}) collective-permute-start(f32[40,32]{1,0:T(8,128)S(1)} %add.28.gram_a), channel_id=1, source_target_pairs={{0,8},{1,9},{2,10},{3,11},{4,12},{5,13},{6,14},{7,15},{8,0},{9,1},... | collective-permute-start | bytes 15368 | tf_op jit(solution)/shard_map/ppermute | solution.py:563
  72.8 1.0 %copy-start.2 = (f32[32,8192]{1,0:T(8,128)}, f32[32,8192]{1,0:T(8,128)S(1)}, u32[]{:S(2)}) copy-start(f32[32,8192]{1,0:T(8,128)S(1)} %get-tuple-element.181) | copy-start | bytes 3145732

commit v12 on v10

--- a/solution.py
+++ b/solution.py
@@ -146,9 +146,10 @@
 
     lax.fori_loop(0, chunks // 2, step, 0)
     copy_columns.wait()
+    step(chunks // 2, 0)
     draft_plan(where[0], where[1], named[...], draft, wanted)
     copy_plan.start()
-    lax.fori_loop(chunks // 2, chunks, step, 0)
+    lax.fori_loop(chunks // 2 + 1, chunks, step, 0)
     copy_plan.wait()
 
 

time: 72.3 us -> 72.3 us (level)
  no operation moved by 1% of the time
where the time goes in v12:
time: 72.3 us; the launch traced here: 72.1 us
  starting transfers between devices  41.7 us (58%)
  Pallas kernels  19.4 us (27%)
  waiting for transfers between devices  10.5 us (15%)
    ppermute x16, starting transfers between devices, swap(): return lax.ppermute(array, 'rows', pairs)  41.7 us
    ppermute x16, waiting for transfers between devices, swap(): return lax.ppermute(array, 'rows', pairs)  10.5 us
    pallas_call x4, Pallas kernels, near_rows(): pl.pallas_call(functools.partial(near_kernel, tile_major, last, len(mate)...  9.88 us
    pallas_call x1, Pallas kernels, prep(): pl.pallas_call(prep_kernel, out_shape=(pltpu.VMEM((rows, slots * size, si...  5.75 us
    pallas_call x1, Pallas kernels, final(): pl.pallas_call(functools.partial(final_kernel, float(states)), out_shape=...  2.6 us
  transfers between devices with their start and end apart: 16, of which 10 were waited for; matrix products, arithmetic and copies ran while one was open for 0% of the time, Pallas kernels for 22%

profile of v12, /device:TPU:0, one launch (start us, length us, event | category | flops | bytes accessed | tf_op | source)
XLA Modules:
  0.0 72.1 jit_solution(17289987834146392270)
XLA Ops:
  0.0 0.0 copy-start
  0.0 0.5 collective-permute-start.18
  0.5 0.7 collective-permute-start.17
  1.2 0.1 pad_add_fusion.1.where
  1.2 5.7 %prep.3 = (bf16[64,640,128]{2,1,0:T(8,128)(2,1)S(1)}, f32[64,8,128]{2,1,0:T(8,128)S(1)}, s32[24,128]{1,0:T(8,128)S(4)}, s32[8,128]{1,0:T(8,128)S(1)}) custom-call(s32[2]{0:T(128)S(1)} %pad_add_fusion.1.where, s32[5,64]{1,0:T(8,128)} %bitcast.7, bf16[64,5,128,128]{3,2,1,0:T(8,128)(2,1)} %tiles.1), custom_call_target="tpu_custom_call" | custom-call | flops 167772160 | bytes 20971520 | tf_op jit(solution)/shard_map/prep/pallas_call | solution.py:159
  7.0 0.7 collective-permute-start.16
  7.7 0.0 collective-permute-done.18.refs_0_
  7.7 0.0 copy-done
  7.7 2.4 %near_rows.12 = (bf16[64,32,128]{2,1,0:T(8,128)(2,1)S(1)}, f32[64,32,128]{2,1,0:T(8,128)S(1)}) custom-call(s32[24,128]{1,0:T(8,128)S(4)} %get-tuple-element.77.plan, bf16[64,640,128]{2,1,0:T(8,128)(2,1)S(1)} %get-tuple-element.78.turned, f32[64,8,128]{2,1,0:T(8,128)S(1)} %get-tuple-element.79.inverse, bf16[32,8192]{1,0:T(8,128)(2,1)S(1)} %copy-done, ...), custom_call_target="tpu_custom_call" | custom-call | bytes 1024 | tf_op jit(solution)/shard_map/near_rows/pallas_call | solution.py:378
  10.1 0.0 collective-permute-done.16.asked
  10.1 0.0 collective-permute-done.17.other
  10.1 0.7 far_rows.12
  10.8 0.7 collective-permute-start.19
  11.5 11.1 %collective-permute-start.20 = (bf16[32,32,128]{2,1,0:T(8,128)(2,1)S(1)}, bf16[32,32,128]{2,1,0:T(8,128)(2,1)S(1)}, u32[]{:S(2)}, u32[]{:S(2)}) collective-permute-start(bf16[32,32,128]{2,1,0:T(8,128)(2,1)S(1)} %get-tuple-element.85), channel_id=1, source_target_pairs={{0,1},{1,0},{2,3},{3,2},{4,5},{5,4},{6,7},{7,6},{8,9},{9,8},{10,11... | collective-permute-start | bytes 786440 | tf_op jit(solution)/shard_map/ppermute | solution.py:564
  22.5 0.1 collective-permute-start.21
  22.6 1.1 %collective-permute-done.20.refs_0_ = bf16[32,32,128]{2,1,0:T(8,128)(2,1)S(1)} collective-permute-done((bf16[32,32,128]{2,1,0:T(8,128)(2,1)S(1)}, bf16[32,32,128]{2,1,0:T(8,128)(2,1)S(1)}, u32[]{:S(2)}, u32[]{:S(2)}) %collective-permute-start.20) | collective-permute-done | bytes 262176 | tf_op jit(solution)/shard_map/ppermute | solution.py:564
  23.7 0.4 collective-permute-done.21.refs_1_
  24.1 2.3 %near_rows.13 = (bf16[64,32,128]{2,1,0:T(8,128)(2,1)S(1)}, f32[64,32,128]{2,1,0:T(8,128)S(1)}) custom-call(s32[24,128]{1,0:T(8,128)S(4)} %get-tuple-element.77.plan, bf16[64,640,128]{2,1,0:T(8,128)(2,1)S(1)} %get-tuple-element.78.turned, f32[64,8,128]{2,1,0:T(8,128)S(1)} %get-tuple-element.79.inverse, bf16[64,32,128]{2,1,0:T(8,128)(2,1)S(1)} %get-tuple-element.84.own, ...), custom_call_target="tpu_custom_call" | custom-call | bytes 1024 | tf_op jit(solution)/shard_map/near_rows/pallas_call | solution.py:378
  26.4 0.0 collective-permute-done.19.other
  26.4 0.1 far_rows.13
  26.5 0.7 collective-permute-start.22
  27.2 8.8 %collective-permute-start.23 = (bf16[32,32,128]{2,1,0:T(8,128)(2,1)S(1)}, bf16[32,32,128]{2,1,0:T(8,128)(2,1)S(1)}, u32[]{:S(2)}, u32[]{:S(2)}) collective-permute-start(bf16[32,32,128]{2,1,0:T(8,128)(2,1)S(1)} %get-tuple-element.91), channel_id=1, source_target_pairs={{0,1},{1,0},{2,3},{3,2},{4,5},{5,4},{6,7},{7,6},{8,9},{9,8},{10,11... | collective-permute-start | bytes 786440 | tf_op jit(solution)/shard_map/ppermute | solution.py:564
  36.0 0.1 collective-permute-start.24
  36.1 1.1 %collective-permute-done.23.refs_0_ = bf16[32,32,128]{2,1,0:T(8,128)(2,1)S(1)} collective-permute-done((bf16[32,32,128]{2,1,0:T(8,128)(2,1)S(1)}, bf16[32,32,128]{2,1,0:T(8,128)(2,1)S(1)}, u32[]{:S(2)}, u32[]{:S(2)}) %collective-permute-start.23) | collective-permute-done | bytes 262176 | tf_op jit(solution)/shard_map/ppermute | solution.py:564
  37.2 0.4 collective-permute-done.24.refs_1_
  37.5 2.3 %near_rows.14 = (bf16[64,32,128]{2,1,0:T(8,128)(2,1)S(1)}, f32[64,32,128]{2,1,0:T(8,128)S(1)}) custom-call(s32[24,128]{1,0:T(8,128)S(4)} %get-tuple-element.77.plan, bf16[64,640,128]{2,1,0:T(8,128)(2,1)S(1)} %get-tuple-element.78.turned, f32[64,8,128]{2,1,0:T(8,128)S(1)} %get-tuple-element.79.inverse, bf16[64,32,128]{2,1,0:T(8,128)(2,1)S(1)} %get-tuple-element.90.own, ...), custom_call_target="tpu_custom_call" | custom-call | bytes 1024 | tf_op jit(solution)/shard_map/near_rows/pallas_call | solution.py:378
  39.8 0.0 collective-permute-done.22.other
  39.8 0.1 far_rows.14
  39.9 0.7 collective-permute-start.25
  40.6 6.6 %collective-permute-start.26 = (bf16[32,32,128]{2,1,0:T(8,128)(2,1)S(1)}, bf16[32,32,128]{2,1,0:T(8,128)(2,1)S(1)}, u32[]{:S(2)}, u32[]{:S(2)}) collective-permute-start(bf16[32,32,128]{2,1,0:T(8,128)(2,1)S(1)} %get-tuple-element.97), channel_id=1, source_target_pairs={{0,1},{1,0},{2,3},{3,2},{4,5},{5,4},{6,7},{7,6},{8,9},{9,8},{10,11... | collective-permute-start | bytes 786440 | tf_op jit(solution)/shard_map/ppermute | solution.py:564
  47.2 0.1 collective-permute-start.27
  47.3 1.1 %collective-permute-done.26.refs_0_ = bf16[32,32,128]{2,1,0:T(8,128)(2,1)S(1)} collective-permute-done((bf16[32,32,128]{2,1,0:T(8,128)(2,1)S(1)}, bf16[32,32,128]{2,1,0:T(8,128)(2,1)S(1)}, u32[]{:S(2)}, u32[]{:S(2)}) %collective-permute-start.26) | collective-permute-done | bytes 262176 | tf_op jit(solution)/shard_map/ppermute | solution.py:564
  48.4 0.4 collective-permute-done.27.refs_1_
  48.8 0.0 copy-start.1
  48.8 2.9 %near_rows.15 = (bf16[64,64,128]{2,1,0:T(8,128)(2,1)S(1)}, f32[64,32,128]{2,1,0:T(8,128)S(1)}, f32[64,64]{1,0:T(8,128)S(1)}) custom-call(s32[24,128]{1,0:T(8,128)S(4)} %get-tuple-element.77.plan, bf16[64,640,128]{2,1,0:T(8,128)(2,1)S(1)} %get-tuple-element.78.turned, f32[64,8,128]{2,1,0:T(8,128)S(1)} %get-tuple-element.79.inverse, ...), custom_call_target="tpu_custom_call" | custom-call | bytes 1024 | tf_op jit(solution)/shard_map/near_rows/pallas_call | solution.py:378
  51.7 0.0 collective-permute-done.25.other
  51.7 0.4 far_rows.15
  52.1 3.2 %collective-permute-start.28 = (f32[40,32]{1,0:T(8,128)S(1)}, f32[40,32]{1,0:T(8,128)S(1)}, u32[]{:S(2)}, u32[]{:S(2)}) collective-permute-start(f32[40,32]{1,0:T(8,128)S(1)} %get-tuple-element.102), channel_id=1, source_target_pairs={{0,1},{1,0},{2,3},{3,2},{4,5},{5,4},{6,7},{7,6},{8,9},{9,8},{10,11... | collective-permute-start | bytes 15368 | tf_op jit(solution)/shard_map/ppermute | solution.py:564
  55.2 0.8 %collective-permute-done.28 = f32[40,32]{1,0:T(8,128)S(1)} collective-permute-done((f32[40,32]{1,0:T(8,128)S(1)}, f32[40,32]{1,0:T(8,128)S(1)}, u32[]{:S(2)}, u32[]{:S(2)}) %collective-permute-start.28) | collective-permute-done | bytes 5152 | tf_op jit(solution)/shard_map/ppermute | solution.py:564
  56.1 2.2 %collective-permute-start.29 = (f32[40,32]{1,0:T(8,128)S(1)}, f32[40,32]{1,0:T(8,128)S(1)}, u32[]{:S(2)}, u32[]{:S(2)}) collective-permute-start(f32[40,32]{1,0:T(8,128)S(1)} %add.26), channel_id=1, source_target_pairs={{0,2},{1,3},{2,0},{3,1},{4,6},{5,7},{6,4},{7,5},{8,10},{9,11},{10,... | collective-permute-start | bytes 15368 | tf_op jit(solution)/shard_map/ppermute | solution.py:564
  58.3 1.8 %collective-permute-done.29 = f32[40,32]{1,0:T(8,128)S(1)} collective-permute-done((f32[40,32]{1,0:T(8,128)S(1)}, f32[40,32]{1,0:T(8,128)S(1)}, u32[]{:S(2)}, u32[]{:S(2)}) %collective-permute-start.29) | collective-permute-done | bytes 5152 | tf_op jit(solution)/shard_map/ppermute | solution.py:564
  60.0 2.8 %collective-permute-start.30 = (f32[40,32]{1,0:T(8,128)S(1)}, f32[40,32]{1,0:T(8,128)S(1)}, u32[]{:S(2)}, u32[]{:S(2)}) collective-permute-start(f32[40,32]{1,0:T(8,128)S(1)} %add.27), channel_id=1, source_target_pairs={{0,4},{1,5},{2,6},{3,7},{4,0},{5,1},{6,2},{7,3},{8,12},{9,13},{10,... | collective-permute-start | bytes 15368 | tf_op jit(solution)/shard_map/ppermute | solution.py:564
  62.9 1.8 %collective-permute-done.30 = f32[40,32]{1,0:T(8,128)S(1)} collective-permute-done((f32[40,32]{1,0:T(8,128)S(1)}, f32[40,32]{1,0:T(8,128)S(1)}, u32[]{:S(2)}, u32[]{:S(2)}) %collective-permute-start.30) | collective-permute-done | bytes 5152 | tf_op jit(solution)/shard_map/ppermute | solution.py:564
  64.6 3.0 %collective-permute-start.31 = (f32[40,32]{1,0:T(8,128)S(1)}, f32[40,32]{1,0:T(8,128)S(1)}, u32[]{:S(2)}, u32[]{:S(2)}) collective-permute-start(f32[40,32]{1,0:T(8,128)S(1)} %add.28.gram_a), channel_id=1, source_target_pairs={{0,8},{1,9},{2,10},{3,11},{4,12},{5,13},{6,14},{7,15},{8,0},{9,1},... | collective-permute-start | bytes 15368 | tf_op jit(solution)/shard_map/ppermute | solution.py:564
  67.6 1.8 %collective-permute-done.31.gram_b = f32[40,32]{1,0:T(8,128)S(1)} collective-permute-done((f32[40,32]{1,0:T(8,128)S(1)}, f32[40,32]{1,0:T(8,128)S(1)}, u32[]{:S(2)}, u32[]{:S(2)}) %collective-permute-start.31) | collective-permute-done | bytes 5152 | tf_op jit(solution)/shard_map/ppermute | solution.py:564
  69.4 0.0 copy-done.1
  69.4 2.6 %memberships.3 = (f32[32,8192]{1,0:T(8,128)}, s32[1]{0:T(128)S(4)}) custom-call(f32[40,32]{1,0:T(8,128)S(1)} %add.28.gram_a, f32[40,32]{1,0:T(8,128)S(1)} %collective-permute-done.31.gram_b, f32[32,32]{1,0:T(8,128)S(1)} %copy-done.1, bf16[64,64,128]{2,1,0:T(8,128)(2,1)S(1)} %get-tuple-element.103.parts), custom_call_target="tpu_custom_call" | custom-call | flops 100663296 | bytes 2097152 | tf_op jit(solution)/shard_map/memberships/pallas_call | solution.py:536
  (4 shorter events, 0.0 us)
Async XLA Ops:
  0.0 7.7 %copy-start = (bf16[32,8192]{1,0:T(8,128)(2,1)S(1)}, bf16[32,8192]{1,0:T(8,128)(2,1)}, u32[]{:S(2)}) copy-start(bf16[32,8192]{1,0:T(8,128)(2,1)} %own.1) | copy-start | bytes 1572868
  0.0 7.7 %collective-permute-start.18 = (bf16[32,8192]{1,0:T(8,128)(2,1)}, bf16[32,8192]{1,0:T(8,128)(2,1)S(1)}, u32[]{:S(2)}, u32[]{:S(2)}) collective-permute-start(bf16[32,8192]{1,0:T(8,128)(2,1)} %own.1), channel_id=1, source_target_pairs={{0,1},{1,0},{2,3},{3,2},{4,5},{5,4},{6,7},{7,6},{8,9},{9,8},{10,11... | collective-permute-start | bytes 1572872 | tf_op jit(solution)/shard_map/ppermute | solution.py:564
  0.5 9.6 %collective-permute-start.17 = (bf16[32,8192]{1,0:T(8,128)(2,1)}, bf16[32,8192]{1,0:T(8,128)(2,1)S(1)}, u32[]{:S(2)}, u32[]{:S(2)}) collective-permute-start(bf16[32,8192]{1,0:T(8,128)(2,1)} %own.1), channel_id=1, source_target_pairs={{1,2},{2,1},{3,4},{4,3},{5,6},{6,5},{7,8},{8,7},{9,10},{10,9},{11,... | collective-permute-start | bytes 1572872 | tf_op jit(solution)/shard_map/ppermute | solution.py:564
  7.0 3.1 %collective-permute-start.16 = (s32[8,128]{1,0:T(8,128)S(1)}, s32[8,128]{1,0:T(8,128)S(1)}, u32[]{:S(2)}, u32[]{:S(2)}) collective-permute-start(s32[8,128]{1,0:T(8,128)S(1)} %get-tuple-element.76), channel_id=1, source_target_pairs={{1,2},{2,1},{3,4},{4,3},{5,6},{6,5},{7,8},{8,7},{9,10},{10,9},{11,... | collective-permute-start | bytes 12296 | tf_op jit(solution)/shard_map/ppermute | solution.py:564
  10.8 15.6 %collective-permute-start.19 = (bf16[44,32,128]{2,1,0:T(8,128)(2,1)S(1)}, bf16[44,32,128]{2,1,0:T(8,128)(2,1)S(1)}, u32[]{:S(2)}, u32[]{:S(2)}) collective-permute-start(bf16[44,32,128]{2,1,0:T(8,128)(2,1)S(1)} %get-tuple-element.83), channel_id=1, source_target_pairs={{1,2},{2,1},{3,4},{4,3},{5,6},{6,5},{7,8},{8,7},{9,10},{10,9},{11,... | collective-permute-start | bytes 1081352 | tf_op jit(solution)/shard_map/ppermute | solution.py:564
  11.5 12.2 %collective-permute-start.20 = (bf16[32,32,128]{2,1,0:T(8,128)(2,1)S(1)}, bf16[32,32,128]{2,1,0:T(8,128)(2,1)S(1)}, u32[]{:S(2)}, u32[]{:S(2)}) collective-permute-start(bf16[32,32,128]{2,1,0:T(8,128)(2,1)S(1)} %get-tuple-element.85), channel_id=1, source_target_pairs={{0,1},{1,0},{2,3},{3,2},{4,5},{5,4},{6,7},{7,6},{8,9},{9,8},{10,11... | collective-permute-start | bytes 786440 | tf_op jit(solution)/shard_map/ppermute | solution.py:564
  22.5 1.5 %collective-permute-start.21 = (bf16[32,32,128]{2,1,0:T(8,128)(2,1)S(1)}, bf16[32,32,128]{2,1,0:T(8,128)(2,1)S(1)}, u32[]{:S(2)}, u32[]{:S(2)}) collective-permute-start(bf16[32,32,128]{2,1,0:T(8,128)(2,1)S(1)} %get-tuple-element.86), channel_id=1, source_target_pairs={{0,1},{1,0},{2,3},{3,2},{4,5},{5,4},{6,7},{7,6},{8,9},{9,8},{10,11... | collective-permute-start | bytes 786440 | tf_op jit(solution)/shard_map/ppermute | solution.py:564
  26.5 13.4 %collective-permute-start.22 = (bf16[44,32,128]{2,1,0:T(8,128)(2,1)S(1)}, bf16[44,32,128]{2,1,0:T(8,128)(2,1)S(1)}, u32[]{:S(2)}, u32[]{:S(2)}) collective-permute-start(bf16[44,32,128]{2,1,0:T(8,128)(2,1)S(1)} %get-tuple-element.89), channel_id=1, source_target_pairs={{1,2},{2,1},{3,4},{4,3},{5,6},{6,5},{7,8},{8,7},{9,10},{10,9},{11,... | collective-permute-start | bytes 1081352 | tf_op jit(solution)/shard_map/ppermute | solution.py:564
  27.2 10.0 %collective-permute-start.23 = (bf16[32,32,128]{2,1,0:T(8,128)(2,1)S(1)}, bf16[32,32,128]{2,1,0:T(8,128)(2,1)S(1)}, u32[]{:S(2)}, u32[]{:S(2)}) collective-permute-start(bf16[32,32,128]{2,1,0:T(8,128)(2,1)S(1)} %get-tuple-element.91), channel_id=1, source_target_pairs={{0,1},{1,0},{2,3},{3,2},{4,5},{5,4},{6,7},{7,6},{8,9},{9,8},{10,11... | collective-permute-start | bytes 786440 | tf_op jit(solution)/shard_map/ppermute | solution.py:564
  36.0 1.5 %collective-permute-start.24 = (bf16[32,32,128]{2,1,0:T(8,128)(2,1)S(1)}, bf16[32,32,128]{2,1,0:T(8,128)(2,1)S(1)}, u32[]{:S(2)}, u32[]{:S(2)}) collective-permute-start(bf16[32,32,128]{2,1,0:T(8,128)(2,1)S(1)} %get-tuple-element.92), channel_id=1, source_target_pairs={{0,1},{1,0},{2,3},{3,2},{4,5},{5,4},{6,7},{7,6},{8,9},{9,8},{10,11... | collective-permute-start | bytes 786440 | tf_op jit(solution)/shard_map/ppermute | solution.py:564
  39.9 11.8 %collective-permute-start.25 = (bf16[44,32,128]{2,1,0:T(8,128)(2,1)S(1)}, bf16[44,32,128]{2,1,0:T(8,128)(2,1)S(1)}, u32[]{:S(2)}, u32[]{:S(2)}) collective-permute-start(bf16[44,32,128]{2,1,0:T(8,128)(2,1)S(1)} %get-tuple-element.95), channel_id=1, source_target_pairs={{1,2},{2,1},{3,4},{4,3},{5,6},{6,5},{7,8},{8,7},{9,10},{10,9},{11,... | collective-permute-start | bytes 1081352 | tf_op jit(solution)/shard_map/ppermute | solution.py:564
  40.6 7.8 %collective-permute-start.26 = (bf16[32,32,128]{2,1,0:T(8,128)(2,1)S(1)}, bf16[32,32,128]{2,1,0:T(8,128)(2,1)S(1)}, u32[]{:S(2)}, u32[]{:S(2)}) collective-permute-start(bf16[32,32,128]{2,1,0:T(8,128)(2,1)S(1)} %get-tuple-element.97), channel_id=1, source_target_pairs={{0,1},{1,0},{2,3},{3,2},{4,5},{5,4},{6,7},{7,6},{8,9},{9,8},{10,11... | collective-permute-start | bytes 786440 | tf_op jit(solution)/shard_map/ppermute | solution.py:564
  47.2 1.5 %collective-permute-start.27 = (bf16[32,32,128]{2,1,0:T(8,128)(2,1)S(1)}, bf16[32,32,128]{2,1,0:T(8,128)(2,1)S(1)}, u32[]{:S(2)}, u32[]{:S(2)}) collective-permute-start(bf16[32,32,128]{2,1,0:T(8,128)(2,1)S(1)} %get-tuple-element.98), channel_id=1, source_target_pairs={{0,1},{1,0},{2,3},{3,2},{4,5},{5,4},{6,7},{7,6},{8,9},{9,8},{10,11... | collective-permute-start | bytes 786440 | tf_op jit(solution)/shard_map/ppermute | solution.py:564
  48.8 20.6 %copy-start.1 = (f32[32,32]{1,0:T(8,128)S(1)}, f32[32,32]{1,0:T(8,128)}, u32[]{:S(2)}) copy-start(f32[32,32]{1,0:T(8,128)} %mapping.1) | copy-start | bytes 12292
  52.1 4.0 %collective-permute-start.28 = (f32[40,32]{1,0:T(8,128)S(1)}, f32[40,32]{1,0:T(8,128)S(1)}, u32[]{:S(2)}, u32[]{:S(2)}) collective-permute-start(f32[40,32]{1,0:T(8,128)S(1)} %get-tuple-element.102), channel_id=1, source_target_pairs={{0,1},{1,0},{2,3},{3,2},{4,5},{5,4},{6,7},{7,6},{8,9},{9,8},{10,11... | collective-permute-start | bytes 15368 | tf_op jit(solution)/shard_map/ppermute | solution.py:564
  56.1 4.0 %collective-permute-start.29 = (f32[40,32]{1,0:T(8,128)S(1)}, f32[40,32]{1,0:T(8,128)S(1)}, u32[]{:S(2)}, u32[]{:S(2)}) collective-permute-start(f32[40,32]{1,0:T(8,128)S(1)} %add.26), channel_id=1, source_target_pairs={{0,2},{1,3},{2,0},{3,1},{4,6},{5,7},{6,4},{7,5},{8,10},{9,11},{10,... | collective-permute-start | bytes 15368 | tf_op jit(solution)/shard_map/ppermute | solution.py:564
  60.0 4.6 %collective-permute-start.30 = (f32[40,32]{1,0:T(8,128)S(1)}, f32[40,32]{1,0:T(8,128)S(1)}, u32[]{:S(2)}, u32[]{:S(2)}) collective-permute-start(f32[40,32]{1,0:T(8,128)S(1)} %add.27), channel_id=1, source_target_pairs={{0,4},{1,5},{2,6},{3,7},{4,0},{5,1},{6,2},{7,3},{8,12},{9,13},{10,... | collective-permute-start | bytes 15368 | tf_op jit(solution)/shard_map/ppermute | solution.py:564
  64.6 4.7 %collective-permute-start.31 = (f32[40,32]{1,0:T(8,128)S(1)}, f32[40,32]{1,0:T(8,128)S(1)}, u32[]{:S(2)}, u32[]{:S(2)}) collective-permute-start(f32[40,32]{1,0:T(8,128)S(1)} %add.28.gram_a), channel_id=1, source_target_pairs={{0,8},{1,9},{2,10},{3,11},{4,12},{5,13},{6,14},{7,15},{8,0},{9,1},... | collective-permute-start | bytes 15368 | tf_op jit(solution)/shard_map/ppermute | solution.py:564
